TPU v7x, 32 devices: a whole 2x2x4 slice. The times are simulated.
32 devices in a mesh: dp: 8 (over y, x, core), vocab: 4 (over z).
Axes of the slice: x: 2, y: 2, z: 4, core: 2. Of those that a mesh axis runs over, the one named last changes fastest.
Arguments:
- token_ids: int32 [32, 512], P('dp'), may hold values from 0 to 65535
- seq_lengths: int32 [8, 4], P('dp'), may hold values from 256 to 512, as said below
- pair_order: int32 [8, 4], P('dp'), may hold values from 0 to 3, each once within a row
- table_master: float32 [65536, 1024], P(('dp', 'vocab')), may hold values from -0.3125 to 0.3125
- table_first: float32 [65536, 1024], P(('dp', 'vocab')), may hold values from -3.8146973e-06 to 3.8146973e-06
- table_second: float32 [65536, 1024], P(('dp', 'vocab')), may hold values from 1.9609928e-12 to 7.838011e-12
- square_master: float32 [7, 1024, 1024], P(None, ('dp', 'vocab'))
- square_moment: float32 [7, 1024, 1024], P(None, ('dp', 'vocab')), may hold values from -3.33786e-06 to 3.33786e-06
- wide_master: float32 [3, 4608, 1024], P(None, ('dp', 'vocab'))
- wide_moment: float32 [3, 4608, 1024], P(None, ('dp', 'vocab')), may hold values from -3.33786e-06 to 3.33786e-06
- vector_master: float32 [7, 1024], P(None, ('dp', 'vocab'))
- vector_first: float32 [7, 1024], P(None, ('dp', 'vocab')), may hold values from -1.9073486e-05 to 1.9073486e-05
- vector_second: float32 [7, 1024], P(None, ('dp', 'vocab')), may hold values from 1.8359375e-11 to 7.33817e-11
- norm_gains: float32 [2, 64], replicated, may hold values from 0.5 to 1.5
- norm_first: float32 [2, 64], replicated, may hold values from -1.9073486e-05 to 1.9073486e-05
- norm_second: float32 [2, 64], replicated, may hold values from 2.05625e-11 to 8.21875e-11
- adam_count: int32 [], replicated, may hold values from 1 to 20
Outputs:
- pair_loss: float32 [], replicated
- grad_norm: float32 [], replicated
- square_new: float32 [7, 1024, 1024], P(None, ('dp', 'vocab'))
- square_moment_new: float32 [7, 1024, 1024], P(None, ('dp', 'vocab'))
- square_copy: bfloat16 [7, 1024, 1024], P(None, ('dp', 'vocab'))
- wide_new: float32 [3, 4608, 1024], P(None, ('dp', 'vocab'))
- wide_moment_new: float32 [3, 4608, 1024], P(None, ('dp', 'vocab'))
- wide_copy: bfloat16 [3, 4608, 1024], P(None, ('dp', 'vocab'))
- table_step: float32 [65536, 1024], P(('dp', 'vocab'))
- table_first_new: float32 [65536, 1024], P(('dp', 'vocab'))
- table_second_new: float32 [65536, 1024], P(('dp', 'vocab'))
- vector_step: float32 [7, 1024], P(None, ('dp', 'vocab'))
- vector_first_new: float32 [7, 1024], P(None, ('dp', 'vocab'))
- vector_second_new: float32 [7, 1024], P(None, ('dp', 'vocab'))
- norm_step: float32 [2, 64], replicated
- norm_first_new: float32 [2, 64], replicated
- norm_second_new: float32 [2, 64], replicated
- final_gain_grad: float32 [1024], P(('dp', 'vocab'))
Inputs may be any that keep to these rules, and one draw needn't show every extreme that they name: `seq_lengths`: in every draw some sequence has length exactly 512. `pair_order`: each row is a permutation of 0 to 3.
All inputs are finite; a program needn't handle non-finite values.
Results may differ from a plain program's by a relative error of at most 0.03.
Values may be sent and summed in bfloat16 or wider, within the bound.
No kernel may reach another device: no remote copies, remote signals or barrier semaphores. Data moves between devices by JAX's collectives and lax.ppermute only.
A program may use at most 448 MiB of HBM per device.

v0:
```python
import math

import jax
import jax.numpy as jnp
from jax import lax
from jax.sharding import PartitionSpec as P

D = 1024
HEADS = 16
KV = 8
HD = 64
FF = 4608
SEQ = 512
RESP = 96
NS_ITERS = 3


norm_epsilon = 1e-05
rope_base = 1000000.0
pref_beta = 2.0
clip_limit = 0.05
muon_decay = 0.95
muon_rate = 0.5
first_decay = 0.9
second_decay = 0.95
adam_rate = 0.02
adam_epsilon = 1e-08
weight_decay = 0.1
leading_coefficient = 3.4445
coef_second = -4.775
coef_third = 2.0315
ortho_epsilon = 1e-07
masked_score = -1e30


def combined_all(value, axis, join):
    pieces = jax.tree.map(lambda part: lax.all_gather(part, axis), value)
    head = jax.tree.map(lambda part: part[0], pieces)
    tail = jax.tree.map(lambda part: part[1:], pieces)
    running, _ = lax.scan(lambda running, piece: (join(running, piece), None), head, tail)
    return running


def rms_scale(inputs, gain):
    mean_square = jnp.mean(inputs * inputs, axis=-1, keepdims=True)
    return inputs * lax.rsqrt(mean_square + norm_epsilon) * gain


def rope_tables(length, half):
    position = jnp.arange(length, dtype=jnp.float32)
    inverse = rope_base ** (-jnp.arange(half, dtype=jnp.float32) / half)
    angle = position[:, None] * inverse[None, :]
    return (jnp.cos(angle)[:, None, :], jnp.sin(angle)[:, None, :])


def rotate(inputs, cosine, sine):
    half = inputs.shape[-1] // 2
    first = inputs[..., :half]
    second = inputs[..., half:]
    return jnp.concatenate(
        [first * cosine - second * sine, second * cosine + first * sine], axis=-1
    )


def dense(inputs, weight):
    return lax.dot_general(
        inputs, weight, (((1,), (1,)), ((), ())), preferred_element_type=jnp.float32
    )


def outer(grads, inputs):
    return lax.dot_general(
        grads, inputs, (((0,), (0,)), ((), ())), preferred_element_type=jnp.float32
    )


def back_dense(grads, weight):
    return jnp.dot(grads, weight, preferred_element_type=jnp.float32)


def delayed(values, offset):
    return jnp.pad(values, ((offset, 0), (0, 0)))[: values.shape[0]]


def advanced(values, offset):
    return jnp.pad(values, ((0, offset), (0, 0)))[offset:]


def norm_back(inputs, gain, grad_out):
    _, pullback = jax.vjp(rms_scale, inputs, gain)
    return pullback(grad_out)


def softmax_join(left, right):
    peak = jnp.maximum(left[0], right[0])
    total = left[1] * jnp.exp(left[0] - peak) + right[1] * jnp.exp(right[0] - peak)
    return (peak, total, left[2] + right[2])


def low_copy(values):
    return lax.optimization_barrier(values.astype(jnp.bfloat16)).astype(jnp.float32)


def adam_step(master, first, second, grad, factor, count):
    scaled = factor * grad
    first_new = first_decay * first + (1.0 - first_decay) * scaled
    second_new = second_decay * second + (1.0 - second_decay) * scaled * scaled
    steps = count.astype(jnp.float32)
    first_hat = first_new / (1.0 - first_decay**steps)
    second_hat = second_new / (1.0 - second_decay**steps)
    change = -adam_rate * (
        first_hat / (jnp.sqrt(second_hat) + adam_epsilon) + weight_decay * master
    )
    return (change, first_new, second_new)


def body(
    token_ids,
    seq_lengths,
    pair_order,
    table_master,
    table_first,
    table_second,
    square_master,
    square_moment,
    wide_master,
    wide_moment,
    vector_master,
    vector_first,
    vector_second,
    norm_gains,
    norm_first,
    norm_second,
    adam_count,
):
    members = lax.axis_size("vocab")
    member = lax.axis_index("vocab")
    block_rows = table_master.shape[0]
    lengths = seq_lengths[0]
    order = pair_order[0]
    groups_per = HEADS // KV
    scale = HD ** (-0.5)

    def local_place(ids):
        block = ids // block_rows
        place = block // members * block_rows + ids % block_rows
        return (place, block % members == member)

    square_b, wide_b, vector_b = (
        lax.all_gather(square_master.astype(jnp.bfloat16), ("dp", "vocab"), axis=1, tiled=True),
        lax.all_gather(wide_master.astype(jnp.bfloat16), ("dp", "vocab"), axis=1, tiled=True),
        lax.all_gather(vector_master.astype(jnp.bfloat16), ("dp", "vocab"), axis=1, tiled=True),
    )
    table_b = lax.all_gather(table_master.astype(jnp.bfloat16), "dp", axis=0, tiled=True)
    shard_vocab = table_b.shape[0]
    head_gains = low_copy(norm_gains)
    gains = vector_b.astype(jnp.float32)
    cosine, sine = rope_tables(SEQ, HD // 2)
    safe_ids, inside = local_place(token_ids)
    looked = jnp.where(inside[..., None], table_b[safe_ids].astype(jnp.float32), 0.0)
    hidden0 = lax.psum_scatter(
        looked.astype(jnp.bfloat16), "vocab", scatter_dimension=0, tiled=True
    ).astype(jnp.float32)[0]
    act1 = rms_scale(hidden0, gains[0]).astype(jnp.bfloat16)
    inner = dense(act1, square_b[0:3].reshape(3 * D, D))
    entry = inner[:, :D]
    leave = inner[:, D : 2 * D]
    conv_in = inner[:, 2 * D :]
    product = entry * conv_in
    convolved = gains[4] * product + gains[5] * delayed(product, 1) + gains[6] * delayed(product, 2)
    mixer = (leave * convolved).astype(jnp.bfloat16)
    hidden1 = hidden0 + dense(mixer, square_b[3])
    act2 = rms_scale(hidden1, gains[1]).astype(jnp.bfloat16)
    query_raw = dense(act2, square_b[4]).reshape(SEQ, HEADS, HD)
    pair_raw = dense(act2, square_b[5])
    key_raw = pair_raw[:, : KV * HD].reshape(SEQ, KV, HD)
    value_b = pair_raw[:, KV * HD :].astype(jnp.bfloat16).reshape(SEQ, KV, HD)

    def query_prep(raw, gain):
        return rotate(rms_scale(raw, gain), cosine, sine)

    query_b = (
        query_prep(query_raw, head_gains[0]).astype(jnp.bfloat16).reshape(SEQ, KV, groups_per, HD)
    )
    key_b = query_prep(key_raw, head_gains[1]).astype(jnp.bfloat16)
    causal = jnp.arange(SEQ)[:, None] >= jnp.arange(SEQ)[None, :]
    scores = (
        jnp.einsum("sgrd,tgd->grst", query_b, key_b, preferred_element_type=jnp.float32) * scale
    )
    scores = jnp.where(causal, scores, masked_score)
    peak = jnp.max(scores, axis=-1, keepdims=True)
    expo = jnp.exp(scores - peak)
    total = jnp.sum(expo, axis=-1, keepdims=True)
    log_norm = peak + jnp.log(total)
    probs_b = (expo / total).astype(jnp.bfloat16)
    attended = jnp.einsum(
        "grst,tgd->sgrd", probs_b, value_b, preferred_element_type=jnp.float32
    ).reshape(SEQ, D)
    attended_b = attended.astype(jnp.bfloat16)
    hidden2 = hidden1 + dense(attended_b, square_b[6])
    act3 = rms_scale(hidden2, gains[2]).astype(jnp.bfloat16)
    gate_up = dense(act3, wide_b[0:2].reshape(2 * FF, D))
    gate_part = gate_up[:, :FF]
    up_part = gate_up[:, FF:]
    inner_b = (jax.nn.silu(gate_part) * up_part).astype(jnp.bfloat16)
    hidden3 = hidden2 + jnp.dot(inner_b, wide_b[2], preferred_element_type=jnp.float32)
    final_b = rms_scale(hidden3, gains[3]).astype(jnp.bfloat16)
    own_length = lengths[member]
    start = own_length - 1 - RESP
    answer_b = lax.dynamic_slice_in_dim(final_b, start, RESP, 0)
    response_tokens = lax.all_gather(answer_b, "vocab", axis=0, tiled=True)
    starts = lengths - 1 - RESP
    targets = jax.vmap(lambda row, first: lax.dynamic_slice_in_dim(row, first + 1, RESP, 0))(
        token_ids, starts
    ).reshape(-1)
    logit_scores = dense(response_tokens, table_b)
    target_place, target_inside = local_place(targets)
    local_target = jnp.where(target_inside, target_place, -1)
    onehot = jnp.arange(shard_vocab)[None, :] == local_target[:, None]
    top = jnp.max(logit_scores, axis=-1)
    exp_total = jnp.sum(jnp.exp(logit_scores - top[:, None]), axis=-1)
    picked = jnp.sum(jnp.where(onehot, logit_scores, 0.0), axis=-1)
    top, exp_total, picked = combined_all((top, exp_total, picked), "vocab", softmax_join)
    log_total = top + jnp.log(exp_total)
    seq_logp = jnp.sum((picked - log_total).reshape(members, RESP), axis=-1)
    slots = jnp.arange(members)
    chosen_mask = (order[0::2][:, None] == slots[None, :]).astype(jnp.float32)
    rejected_mask = (order[1::2][:, None] == slots[None, :]).astype(jnp.float32)
    margin = (
        pref_beta
        * (jnp.sum(chosen_mask * seq_logp, axis=1) - jnp.sum(rejected_mask * seq_logp, axis=1))
        / RESP
    )
    group_loss = jnp.sum(jax.nn.softplus(-margin))
    pull = jax.nn.sigmoid(-margin) * pref_beta / RESP
    grad_logp = jnp.sum(rejected_mask * pull[:, None], axis=0) - jnp.sum(
        chosen_mask * pull[:, None], axis=0
    )
    row_weight = jnp.repeat(grad_logp, RESP)
    softmax_rows = jnp.exp(logit_scores - log_total[:, None])
    grad_logits = (row_weight[:, None] * (onehot.astype(jnp.float32) - softmax_rows)).astype(
        jnp.bfloat16
    )
    grad_answers = jnp.dot(grad_logits, table_b, preferred_element_type=jnp.float32)
    grad_table = outer(grad_logits, response_tokens)
    grad_answer_own = lax.psum_scatter(
        grad_answers.astype(jnp.bfloat16), "vocab", scatter_dimension=0, tiled=True
    ).astype(jnp.float32)
    grad_final = lax.dynamic_update_slice_in_dim(
        jnp.zeros((SEQ, D), jnp.float32), grad_answer_own, start, 0
    )
    grad_hidden3, grad_gain3 = norm_back(hidden3, gains[3], grad_final)
    grad_ffn_out = grad_hidden3.astype(jnp.bfloat16)
    grad_inner = dense(grad_ffn_out, wide_b[2])
    grad_down_w = outer(inner_b, grad_ffn_out)
    _, silu_pull = jax.vjp(lambda gate_in, up_in: jax.nn.silu(gate_in) * up_in, gate_part, up_part)
    grad_gate, grad_up = silu_pull(grad_inner)
    grad_gate_up = jnp.concatenate([grad_gate, grad_up], axis=1).astype(jnp.bfloat16)
    grad_act3 = back_dense(grad_gate_up, wide_b[0:2].reshape(2 * FF, D))
    grad_gate_up_w = outer(grad_gate_up, act3)
    grad_norm2, grad_gain2 = norm_back(hidden2, gains[2], grad_act3)
    grad_hidden2 = grad_hidden3 + grad_norm2
    grad_attn_out = grad_hidden2.astype(jnp.bfloat16)
    grad_attended = (
        back_dense(grad_attn_out, square_b[6]).astype(jnp.bfloat16).reshape(SEQ, KV, groups_per, HD)
    )
    grad_out_w = outer(grad_attn_out, attended_b)
    scores = (
        jnp.einsum("sgrd,tgd->grst", query_b, key_b, preferred_element_type=jnp.float32) * scale
    )
    probs = jnp.exp(jnp.where(causal, scores, masked_score) - log_norm)
    grad_probs = jnp.einsum(
        "sgrd,tgd->grst", grad_attended, value_b, preferred_element_type=jnp.float32
    )
    grad_values = jnp.einsum(
        "grst,sgrd->tgd", probs_b, grad_attended, preferred_element_type=jnp.float32
    )
    delta = jnp.sum(probs * grad_probs, axis=-1, keepdims=True)
    grad_scores = (probs * (grad_probs - delta)).astype(jnp.bfloat16)
    grad_query = (
        jnp.einsum("grst,tgd->sgrd", grad_scores, key_b, preferred_element_type=jnp.float32) * scale
    ).reshape(SEQ, HEADS, HD)
    grad_keys = (
        jnp.einsum("grst,sgrd->tgd", grad_scores, query_b, preferred_element_type=jnp.float32)
        * scale
    )
    _, query_pull = jax.vjp(query_prep, query_raw, head_gains[0])
    grad_query_raw, grad_query_gain = query_pull(grad_query)
    _, key_pull = jax.vjp(query_prep, key_raw, head_gains[1])
    grad_key_raw, grad_key_gain = key_pull(grad_keys)
    grad_query_b = grad_query_raw.reshape(SEQ, D).astype(jnp.bfloat16)
    grad_pair_b = jnp.concatenate(
        [grad_key_raw.reshape(SEQ, KV * HD), grad_values.reshape(SEQ, KV * HD)], axis=1
    ).astype(jnp.bfloat16)
    grad_act2 = back_dense(grad_query_b, square_b[4]) + back_dense(grad_pair_b, square_b[5])
    grad_query_w = outer(grad_query_b, act2)
    grad_pair_w = outer(grad_pair_b, act2)
    grad_norm1, grad_gain1 = norm_back(hidden1, gains[1], grad_act2)
    grad_hidden1 = grad_hidden2 + grad_norm1
    grad_mix_out = grad_hidden1.astype(jnp.bfloat16)
    grad_mixer = back_dense(grad_mix_out, square_b[3])
    grad_mixer_w = outer(grad_mix_out, mixer)
    grad_leave = grad_mixer * convolved
    grad_conv = grad_mixer * leave
    grad_tap0 = jnp.sum(grad_conv * product, axis=0)
    grad_tap1 = jnp.sum(grad_conv * delayed(product, 1), axis=0)
    grad_tap2 = jnp.sum(grad_conv * delayed(product, 2), axis=0)
    grad_product = (
        gains[4] * grad_conv + gains[5] * advanced(grad_conv, 1) + gains[6] * advanced(grad_conv, 2)
    )
    grad_inner_b = jnp.concatenate(
        [grad_product * conv_in, grad_leave, grad_product * entry], axis=1
    ).astype(jnp.bfloat16)
    grad_act1 = back_dense(grad_inner_b, square_b[0:3].reshape(3 * D, D))
    grad_inner_w = outer(grad_inner_b, act1)
    grad_norm0, grad_gain0 = norm_back(hidden0, gains[0], grad_act1)
    grad_embed_b = (grad_hidden1 + grad_norm0).astype(jnp.bfloat16)
    grad_rows = lax.all_gather(grad_embed_b, "vocab", axis=0, tiled=True)
    row_updates = jnp.where(inside.reshape(-1)[:, None], grad_rows.astype(jnp.float32), 0.0)
    grad_table = grad_table.at[safe_ids.reshape(-1)].add(row_updates)
    share_table = lax.psum_scatter(
        grad_table.astype(jnp.bfloat16), "dp", scatter_dimension=0, tiled=True
    ).astype(jnp.float32)
    grad_square = jnp.concatenate(
        [
            grad_inner_w.reshape(3, D, D),
            jnp.stack([grad_mixer_w, grad_query_w, grad_pair_w, grad_out_w]),
        ],
        axis=0,
    )
    grad_wide = jnp.concatenate([grad_gate_up_w.reshape(2, FF, D), grad_down_w[None]], axis=0)
    grad_vector = jnp.stack(
        [grad_gain0, grad_gain1, grad_gain2, grad_gain3, grad_tap0, grad_tap1, grad_tap2]
    )
    grad_head_gains = jnp.stack([grad_query_gain, grad_key_gain])
    share_square, share_wide, share_vector = (
        lax.psum_scatter(grad_square, ("dp", "vocab"), scatter_dimension=1, tiled=True),
        lax.psum_scatter(grad_wide, ("dp", "vocab"), scatter_dimension=1, tiled=True),
        lax.psum_scatter(grad_vector, ("dp", "vocab"), scatter_dimension=1, tiled=True),
    )
    own_squares = (
        jnp.sum(share_square * share_square)
        + jnp.sum(share_wide * share_wide)
        + jnp.sum(share_vector * share_vector)
        + jnp.sum(share_table * share_table)
    )
    moment_squares = jnp.concatenate(
        [
            jnp.sum(square_moment * square_moment, axis=(1, 2)),
            jnp.sum(wide_moment * wide_moment, axis=(1, 2)),
        ]
    )
    moment_cross = jnp.concatenate(
        [
            jnp.sum(square_moment * share_square, axis=(1, 2)),
            jnp.sum(wide_moment * share_wide, axis=(1, 2)),
        ]
    )
    grad_squares = jnp.concatenate(
        [
            jnp.sum(share_square * share_square, axis=(1, 2)),
            jnp.sum(share_wide * share_wide, axis=(1, 2)),
        ]
    )
    moment_stats = jnp.stack([moment_squares, moment_cross, grad_squares])
    loss_part = jnp.where(member == 0, group_loss, 0.0)
    gains_total, stats_total, squares_total, pair_loss = lax.psum(
        (grad_head_gains, moment_stats, own_squares, loss_part), ("dp", "vocab")
    )
    grad_norm = jnp.sqrt(squares_total + jnp.sum(gains_total * gains_total))
    factor = jnp.minimum(1.0, clip_limit / grad_norm)
    square_moment_new = muon_decay * square_moment + (1.0 - muon_decay) * (factor * share_square)
    wide_moment_new = muon_decay * wide_moment + (1.0 - muon_decay) * (factor * share_wide)
    moment_norm = jnp.sqrt(
        muon_decay * muon_decay * stats_total[0]
        + 2.0 * muon_decay * (1.0 - muon_decay) * factor * stats_total[1]
        + (1.0 - muon_decay) * (1.0 - muon_decay) * factor * factor * stats_total[2]
    )
    ortho_square = square_moment_new / (moment_norm[:7][:, None, None] + ortho_epsilon)
    ortho_wide = wide_moment_new / (moment_norm[7:][:, None, None] + ortho_epsilon)
    for turn in range(NS_ITERS):
        narrow_square = ortho_square.astype(jnp.bfloat16)
        narrow_wide = ortho_wide.astype(jnp.bfloat16)
        left = jnp.einsum(
            "mri,mrj->imj", narrow_square, narrow_square, preferred_element_type=jnp.float32
        )
        right = jnp.einsum(
            "mri,mrj->imj", narrow_wide, narrow_wide, preferred_element_type=jnp.float32
        )
        gram_share = lax.psum_scatter(
            jnp.concatenate([left, right], axis=1), ("dp", "vocab"), scatter_dimension=0, tiled=True
        )
        gram_b = lax.all_gather(
            gram_share.astype(jnp.bfloat16), ("dp", "vocab"), axis=0, tiled=True
        )
        first_square = jnp.einsum(
            "mri,imj->mrj", narrow_square, gram_b[:, :7], preferred_element_type=jnp.float32
        )
        first_wide = jnp.einsum(
            "mri,imj->mrj", narrow_wide, gram_b[:, 7:], preferred_element_type=jnp.float32
        )
        second_square = jnp.einsum(
            "mri,imj->mrj",
            first_square.astype(jnp.bfloat16),
            gram_b[:, :7],
            preferred_element_type=jnp.float32,
        )
        second_wide = jnp.einsum(
            "mri,imj->mrj",
            first_wide.astype(jnp.bfloat16),
            gram_b[:, 7:],
            preferred_element_type=jnp.float32,
        )
        ortho_square = (
            leading_coefficient * ortho_square
            + coef_second * first_square
            + coef_third * second_square
        )
        ortho_wide = (
            leading_coefficient * ortho_wide + coef_second * first_wide + coef_third * second_wide
        )
    wide_scale = jnp.array([math.sqrt(FF / D), math.sqrt(FF / D), 1.0], jnp.float32)
    square_new = square_master - muon_rate * ortho_square
    wide_new = wide_master - muon_rate * wide_scale[:, None, None] * ortho_wide
    table_step, table_first_new, table_second_new = adam_step(
        table_master, table_first, table_second, share_table, factor, adam_count
    )
    vector_step, vector_first_new, vector_second_new = adam_step(
        vector_master, vector_first, vector_second, share_vector, factor, adam_count
    )
    norm_step, norm_first_new, norm_second_new = adam_step(
        norm_gains, norm_first, norm_second, gains_total, factor, adam_count
    )
    return (
        pair_loss,
        grad_norm,
        square_new,
        square_moment_new,
        square_new.astype(jnp.bfloat16),
        wide_new,
        wide_moment_new,
        wide_new.astype(jnp.bfloat16),
        table_step,
        table_first_new,
        table_second_new,
        vector_step,
        vector_first_new,
        vector_second_new,
        norm_step,
        norm_first_new,
        norm_second_new,
        share_vector[3],
    )


def solution(mesh):
    return jax.shard_map(
        body,
        mesh=mesh,
        in_specs=(
            P("dp", None),
            P("dp", None),
            P("dp", None),
            P(("dp", "vocab"), None),
            P(("dp", "vocab"), None),
            P(("dp", "vocab"), None),
            P(None, ("dp", "vocab"), None),
            P(None, ("dp", "vocab"), None),
            P(None, ("dp", "vocab"), None),
            P(None, ("dp", "vocab"), None),
            P(None, ("dp", "vocab")),
            P(None, ("dp", "vocab")),
            P(None, ("dp", "vocab")),
            P(),
            P(),
            P(),
            P(),
        ),
        out_specs=(
            P(),
            P(),
            P(None, ("dp", "vocab"), None),
            P(None, ("dp", "vocab"), None),
            P(None, ("dp", "vocab"), None),
            P(None, ("dp", "vocab"), None),
            P(None, ("dp", "vocab"), None),
            P(None, ("dp", "vocab"), None),
            P(("dp", "vocab"), None),
            P(("dp", "vocab"), None),
            P(("dp", "vocab"), None),
            P(None, ("dp", "vocab")),
            P(None, ("dp", "vocab")),
            P(None, ("dp", "vocab")),
            P(),
            P(),
            P(),
            P(("dp", "vocab")),
        ),
        check_vma=False,
    )
```

profile of v0, /device:TPU:0, one launch (start us, length us, event | category | flops | bytes accessed | tf_op | source)
XLA Modules:
  0.0 7694.5 jit_solution(13002181101418061442)
XLA Ops:
  17.2 159.8 %all-gather.15.cloned.1.call-done = bf16[16384,1024]{1,0:T(8,128)(2,1)} async-done(((bf16[2048,1024]{1,0:T(8,128)(2,1)}), bf16[16384,1024]{1,0:T(8,128)(2,1)}) %all-gather.15.cloned.1.call-update) | async-done | bytes 33554448 | tf_op jit(solution)/shard_map/all_gather | solution.py:154
  177.0 40.6 gather_fusion
  231.9 69.4 all-gather.3
  310.3 147.6 %all-gather.19.cloned.1.call-done = bf16[3,4608,1024]{2,1,0:T(8,128)(2,1)} async-done(((bf16[3,144,1024]{2,1,0:T(8,128)(2,1)}), bf16[3,4608,1024]{2,1,0:T(8,128)(2,1)}) %all-gather.19.cloned.1.call-update) | async-done | bytes 28311568 | tf_op jit(solution)/shard_map/all_gather | solution.py:151
  457.9 16.7 slice.281
  474.6 61.0 reduce-scatter.12.cloned.1.call-done
  592.4 18.3 fusion.173
  618.4 9.4 multiply_reduce_fusion.11
  629.4 18.8 all_gather.49
  648.2 24.8 fusion.187
  673.0 12.6 select_reduce_fusion
  685.6 11.9 all-gather.5
  697.5 11.9 all-gather.6
  709.4 11.9 all-gather.4
  722.9 24.4 convolution_convert_fusion.1
  747.4 22.1 reduce-scatter.14.cloned.1.call-done
  776.0 17.4 fusion.19
  793.5 18.3 multiply_reduce_fusion.5
  823.2 15.2 fusion
  839.8 11.3 fusion.2
  882.9 34.6 fusion.175
  918.7 44.1 all-gather.21.cloned.1.call-done
  968.2 296.9 %scatter_fusion = f32[16384,1024]{1,0:T(8,128)} fusion(f32[16384,1024]{1,0:T(8,128)} %fusion.175, s32[2048]{0:T(1024)S(1)} %bitcast.328, f32[2048,1024]{1,0:T(8,128)} %convert_select_fusion.1), kind=kCustom, calls=%fused_computation.1 | custom fusion | flops 2097152 | bytes 25174016 | tf_op jit(solution)/shard_map/scatter-add | solution.py:320
  1265.0 32.4 convert_element_type.221
  1305.7 11.0 convolution_dynamic-update-slice_fusion
  1332.9 14.7 convolution_bitcast_fusion.3
  1347.6 23.1 fusion.27
  1370.7 38.6 pad_maximum_fusion
  1411.8 89.4 %reduce-scatter.20.cloned.1.call-done = bf16[2048,1024]{1,0:T(8,128)(2,1)} async-done(((bf16[16384,1024]{1,0:T(8,128)(2,1)}), bf16[2048,1024]{1,0:T(8,128)(2,1)}) %reduce-scatter.20.cloned.1.call-update) | async-done | bytes 4194320 | tf_op jit(solution)/shard_map/reduce_scatter | solution.py:321
  1506.1 622.6 %reduce-scatter.16.cloned.1.call-done = f32[7,32,1024]{2,1,0:T(8,128)} async-done(((f32[7,1024,1024]{2,1,0:T(8,128)}), f32[7,32,1024]{2,1,0:T(8,128)}) %reduce-scatter.16.cloned.1.call-update) | async-done | bytes 917520 | tf_op jit(solution)/shard_map/reduce_scatter | solution.py:337
  2130.9 476.2 %reduce-scatter.18.cloned.1.call-done = f32[3,144,1024]{2,1,0:T(8,128)} async-done(((f32[3,4608,1024]{2,1,0:T(8,128)}), f32[3,144,1024]{2,1,0:T(8,128)}) %reduce-scatter.18.cloned.1.call-update) | async-done | bytes 1769488 | tf_op jit(solution)/shard_map/reduce_scatter | solution.py:338
  2612.8 39.6 all-reduce.8
  2664.1 11.8 convolution_bitcast_fusion.2
  2675.9 28.5 pad_maximum_fusion.1
  2704.4 60.3 copy.120
  2764.7 1410.7 %reduce-scatter.22.cloned.1.call-done = f32[32,10,1024]{2,1,0:T(8,128)} async-done(((f32[1024,10,1024]{2,1,0:T(8,128)}), f32[32,10,1024]{2,1,0:T(8,128)}) %reduce-scatter.22.cloned.1.call-update) | async-done | bytes 1310736 | tf_op jit(solution)/shard_map/reduce_scatter | solution.py:390
  4178.6 134.1 %all-gather.23.cloned.1.call-done = bf16[1024,10,1024]{2,0,1:T(8,128)(2,1)} async-done(((bf16[32,10,1024]{2,0,1:T(8,128)(2,1)}), bf16[1024,10,1024]{2,0,1:T(8,128)(2,1)}) %all-gather.23.cloned.1.call-update) | async-done | bytes 20971536 | tf_op jit(solution)/shard_map/all_gather | solution.py:393
  4340.8 11.7 convolution_bitcast_fusion.1
  4352.5 28.5 pad_maximum_fusion.2
  4381.0 60.3 copy.122
  4441.4 1409.2 %reduce-scatter.24.cloned.1.call-done = f32[32,10,1024]{2,1,0:T(8,128)} async-done(((f32[1024,10,1024]{2,1,0:T(8,128)}), f32[32,10,1024]{2,1,0:T(8,128)}) %reduce-scatter.24.cloned.1.call-update) | async-done | bytes 1310736 | tf_op jit(solution)/shard_map/reduce_scatter | solution.py:390
  5853.8 134.1 %all-gather.25.cloned.1.call-done = bf16[1024,10,1024]{2,0,1:T(8,128)(2,1)} async-done(((bf16[32,10,1024]{2,0,1:T(8,128)(2,1)}), bf16[1024,10,1024]{2,0,1:T(8,128)(2,1)}) %all-gather.25.cloned.1.call-update) | async-done | bytes 20971536 | tf_op jit(solution)/shard_map/all_gather | solution.py:393
  6012.6 11.7 convolution_bitcast_fusion
  6024.3 28.8 pad_maximum_fusion.3
  6053.1 60.3 copy.124
  6113.5 1409.2 %reduce-scatter.26.cloned.1.call-done = f32[32,10,1024]{2,1,0:T(8,128)} async-done(((f32[1024,10,1024]{2,1,0:T(8,128)}), f32[32,10,1024]{2,1,0:T(8,128)}) %reduce-scatter.26.cloned.1.call-update) | async-done | bytes 1310736 | tf_op jit(solution)/shard_map/reduce_scatter | solution.py:390
  7528.3 21.7 add_multiply_fusion
  7550.1 109.9 %all-gather.27.cloned.1.call-done = bf16[1024,10,1024]{2,0,1:T(8,128)(2,1)} async-done(((bf16[32,10,1024]{2,0,1:T(8,128)(2,1)}), bf16[1024,10,1024]{2,0,1:T(8,128)(2,1)}) %all-gather.27.cloned.1.call-update) | async-done | bytes 20971536 | tf_op jit(solution)/shard_map/all_gather | solution.py:393
  (535 shorter events, 300.2 us)
Async XLA Ops:
  7.2 169.8 %all-gather.15.cloned.1.call-start = ((), (), s32[]{:S(2)}) async-start(), calls=%async_computation.9 | async-start | bytes 37748736 | tf_op jit(solution)/shard_map/all_gather | solution.py:154
  13.3 290.7 %all-gather.17.cloned.1.call-start = ((), (), s32[]{:S(2)}) async-start(), calls=%async_computation.11 | async-start | bytes 15138816 | tf_op jit(solution)/shard_map/all_gather | solution.py:150
  15.3 442.6 %all-gather.19.cloned.1.call-start = ((), (), s32[]{:S(2)}) async-start(), calls=%async_computation.12 | async-start | bytes 29196288 | tf_op jit(solution)/shard_map/all_gather | solution.py:151
  16.5 519.1 %reduce-scatter.12.cloned.1.call-start = ((), (), s32[]{:S(2)}) async-start(), calls=%async_computation.10 | async-start | bytes 5242880 | tf_op jit(solution)/shard_map/reduce_scatter | solution.py:161
  221.7 547.8 %reduce-scatter.14.cloned.1.call-start = ((), (), s32[]{:S(2)}) async-start(), calls=%async_computation.13 | async-start | bytes 983040 | tf_op jit(solution)/shard_map/reduce_scatter | solution.py:246
  303.5 255.7 %copy-start.106 = (f32[64]{0:T(128)}, f32[64]{0:T(128)S(1)}, u32[]{:S(2)}) copy-start(f32[64]{0:T(128)S(1)} %get-tuple-element.167) | copy-start | bytes 772
  303.5 256.3 %copy-start.104 = (f32[64]{0:T(128)}, f32[64]{0:T(128)S(1)}, u32[]{:S(2)}) copy-start(f32[64]{0:T(128)S(1)} %get-tuple-element.168) | copy-start | bytes 772
  303.6 233.5 %copy-start.98 = (f32[1,1024]{1,0:T(1,128)}, f32[1,1024]{1,0:T(1,128)S(1)}, u32[]{:S(2)}) copy-start(f32[1,1024]{1,0:T(1,128)S(1)} %get-tuple-element.164) | copy-start | bytes 12292
  303.6 240.2 %copy-start.83 = (f32[1,1024]{1,0:T(1,128)}, f32[1,1024]{1,0:T(1,128)S(1)}, u32[]{:S(2)}) copy-start(f32[1,1024]{1,0:T(1,128)S(1)} %get-tuple-element.161) | copy-start | bytes 12292
  303.6 240.2 %copy-start.85 = (f32[1,1024]{1,0:T(1,128)}, f32[1,1024]{1,0:T(1,128)S(1)}, u32[]{:S(2)}) copy-start(f32[1,1024]{1,0:T(1,128)S(1)} %get-tuple-element.162) | copy-start | bytes 12292
  303.6 240.2 %copy-start.87 = (f32[1,1024]{1,0:T(1,128)}, f32[1,1024]{1,0:T(1,128)S(1)}, u32[]{:S(2)}) copy-start(f32[1,1024]{1,0:T(1,128)S(1)} %get-tuple-element.163) | copy-start | bytes 12292
  303.6 245.3 %copy-start.81 = (f32[1,1024]{1,0:T(1,128)}, f32[1,1024]{1,0:T(1,128)S(1)}, u32[]{:S(2)}) copy-start(f32[1,1024]{1,0:T(1,128)S(1)} %get-tuple-element.160) | copy-start | bytes 12292
  303.6 508.2 %copy-start.96 = (f32[1,1024]{1,0:T(1,128)}, f32[1,1024]{1,0:T(1,128)S(1)}, u32[]{:S(2)}) copy-start(f32[1,1024]{1,0:T(1,128)S(1)} %get-tuple-element.159) | copy-start | bytes 12292
  304.0 256.3 %copy-start.56 = (f32[512,32]{0,1:T(8,128)}, f32[512,32]{0,1:T(8,128)S(1)}, u32[]{:S(2)}) copy-start(f32[512,32]{0,1:T(8,128)S(1)} %get-tuple-element.169) | copy-start | bytes 196612
  304.0 256.3 %copy-start.58 = (f32[512,32]{0,1:T(8,128)}, f32[512,32]{0,1:T(8,128)S(1)}, u32[]{:S(2)}) copy-start(f32[512,32]{0,1:T(8,128)S(1)} %get-tuple-element.170) | copy-start | bytes 196612
  592.3 18.3 copy-start.114
  592.3 26.0 copy-start.49
  592.4 219.5 %copy-start.110 = (f32[512]{0:T(512)}, f32[512]{0:T(512)S(1)}, u32[]{:S(2)}) copy-start(f32[512]{0:T(512)S(1)} %fusion.161) | copy-start | bytes 6148
  648.2 24.8 copy-start.48
  747.3 215.5 %all-gather.21.cloned.1.call-start = ((), (), s32[]{:S(2)}) async-start(), calls=%async_computation.16 | async-start | bytes 5242880 | tf_op jit(solution)/shard_map/all_gather | solution.py:318
  776.0 17.4 copy-start.50
  793.5 18.4 copy-start.115
  793.5 18.4 copy-start.24
  823.2 42.5 copy-start.60
  882.7 527.7 %reduce-scatter.28.cloned.1.call-start = ((), (), s32[]{:S(2)}) async-start(), calls=%async_computation.24 | async-start | bytes 540672
  882.8 34.7 copy-start.100
  918.6 582.6 %reduce-scatter.20.cloned.1.call-start = ((), (), s32[]{:S(2)}) async-start(), calls=%async_computation.17 | async-start | bytes 37748736 | tf_op jit(solution)/shard_map/reduce_scatter | solution.py:321
  1297.4 831.3 %reduce-scatter.16.cloned.1.call-start = ((), (), s32[]{:S(2)}) async-start(), calls=%async_computation.14 | async-start | bytes 30277632 | tf_op jit(solution)/shard_map/reduce_scatter | solution.py:337
  1330.9 1276.2 %reduce-scatter.18.cloned.1.call-start = ((), (), s32[]{:S(2)}) async-start(), calls=%async_computation.15 | async-start | bytes 58392576 | tf_op jit(solution)/shard_map/reduce_scatter | solution.py:338
  1409.4 719.3 %copy-start.45 = (f32[7,32,1024]{2,1,0:T(8,128)S(1)}, f32[7,32,1024]{2,1,0:T(8,128)}, u32[]{:S(2)}) copy-start(f32[7,32,1024]{2,1,0:T(8,128)} %param.27) | copy-start | bytes 2752516
  1409.4 1197.7 %copy-start.27 = (f32[3,144,1024]{2,1,0:T(8,128)S(1)}, f32[3,144,1024]{2,1,0:T(8,128)}, u32[]{:S(2)}) copy-start(f32[3,144,1024]{2,1,0:T(8,128)} %param.29) | copy-start | bytes 5308420
  1409.4 2766.0 %reduce-scatter.22.cloned.1.call-start = ((), (), s32[]{:S(2)}) async-start(), calls=%async_computation.18 | async-start | bytes 69206016 | tf_op jit(solution)/shard_map/reduce_scatter | solution.py:390
  1411.2 1198.9 %copy-start.89 = (f32[7,32]{1,0:T(8,128)}, f32[7,32]{1,0:T(8,128)S(1)}, u32[]{:S(2)}) copy-start(f32[7,32]{1,0:T(8,128)S(1)} %copy.135) | copy-start | bytes 2692
  2656.4 1660.3 %copy-start.19 = (f32[3,144,1024]{2,1,0:T(8,128)}, f32[3,144,1024]{2,1,0:T(8,128)S(1)}, u32[]{:S(2)}) copy-start(f32[3,144,1024]{2,1,0:T(8,128)S(1)} %multiply_add_fusion.4) | copy-start | bytes 5308420
  2764.7 1548.1 %all-gather.23.cloned.1.call-start = ((), (), s32[]{:S(2)}) async-start(), calls=%async_computation.19 | async-start | bytes 21626880 | tf_op jit(solution)/shard_map/all_gather | solution.py:393
  4178.6 1672.0 %reduce-scatter.24.cloned.1.call-start = ((), (), s32[]{:S(2)}) async-start(), calls=%async_computation.20 | async-start | bytes 69206016 | tf_op jit(solution)/shard_map/reduce_scatter | solution.py:390
  4340.8 1663.7 %copy-start.18 = (f32[7,32,1024]{2,1,0:T(8,128)}, f32[7,32,1024]{2,1,0:T(8,128)S(1)}, u32[]{:S(2)}) copy-start(f32[7,32,1024]{2,1,0:T(8,128)S(1)} %fusion.84) | copy-start | bytes 2752516
  4441.3 1546.6 %all-gather.25.cloned.1.call-start = ((), (), s32[]{:S(2)}) async-start(), calls=%async_computation.21 | async-start | bytes 21626880 | tf_op jit(solution)/shard_map/all_gather | solution.py:393
  5853.7 1669.0 %reduce-scatter.26.cloned.1.call-start = ((), (), s32[]{:S(2)}) async-start(), calls=%async_computation.22 | async-start | bytes 69206016 | tf_op jit(solution)/shard_map/reduce_scatter | solution.py:390
  6113.4 1413.2 %copy-start.90 = (f32[7,32]{1,0:T(8,128)S(1)}, f32[7,32]{1,0:T(8,128)}, u32[]{:S(2)}) copy-start(f32[7,32]{1,0:T(8,128)} %copy-done.89) | copy-start | bytes 2692
  6113.4 1413.7 %copy-start.121 = (f32[2,64]{1,0:T(2,128)S(1)}, f32[2,64]{1,0:T(2,128)}, u32[]{:S(2)}) copy-start(f32[2,64]{1,0:T(2,128)} %param.33) | copy-start | bytes 1540
  6113.4 1413.7 %copy-start.122 = (f32[2,64]{1,0:T(2,128)S(1)}, f32[2,64]{1,0:T(2,128)}, u32[]{:S(2)}) copy-start(f32[2,64]{1,0:T(2,128)} %param.35) | copy-start | bytes 1540
  6113.4 1413.7 %copy-start.123 = (f32[2,64]{1,0:T(2,128)S(1)}, f32[2,64]{1,0:T(2,128)}, u32[]{:S(2)}) copy-start(f32[2,64]{1,0:T(2,128)} %param.34) | copy-start | bytes 1540
  6113.4 1413.7 %copy-start.125 = (f32[2,64]{1,0:T(2,128)S(1)}, f32[2,64]{1,0:T(2,128)}, u32[]{:S(2)}) copy-start(f32[2,64]{1,0:T(2,128)} %copy-done.124) | copy-start | bytes 1540
  6113.4 1414.3 %copy-start.102 = (f32[7,32]{1,0:T(8,128)S(1)}, f32[7,32]{1,0:T(8,128)}, u32[]{:S(2)}) copy-start(f32[7,32]{1,0:T(8,128)} %param.30) | copy-start | bytes 2692
  6113.4 1414.3 %copy-start.116 = (f32[7,32]{1,0:T(8,128)S(1)}, f32[7,32]{1,0:T(8,128)}, u32[]{:S(2)}) copy-start(f32[7,32]{1,0:T(8,128)} %param.32) | copy-start | bytes 2692
  6113.4 1414.3 %copy-start.117 = (f32[7,32]{1,0:T(8,128)S(1)}, f32[7,32]{1,0:T(8,128)}, u32[]{:S(2)}) copy-start(f32[7,32]{1,0:T(8,128)} %param.31) | copy-start | bytes 2692
  6113.5 1546.6 %all-gather.27.cloned.1.call-start = ((), (), s32[]{:S(2)}) async-start(), calls=%async_computation.23 | async-start | bytes 21626880 | tf_op jit(solution)/shard_map/all_gather | solution.py:393
  (120 other events, 644.4 us)
Sparse Core Ops, SparseCore 0:
  13.5 163.4 all-gather.14
  180.6 105.4 all-gather.16
  289.7 168.1 all-gather.18
  460.6 74.9 reduce-scatter.11
  747.4 22.0 reduce-scatter.13
  882.8 79.9 all-gather.20
  965.7 132.5 reduce-scatter.27
  1297.6 203.5 reduce-scatter.19
  1503.6 625.1 reduce-scatter.15
  2136.2 470.8 reduce-scatter.17
  2764.8 1410.5 reduce-scatter.21
  4178.8 133.8 all-gather.22
  4441.5 1409.0 reduce-scatter.23
  5854.0 133.8 all-gather.24
  6113.6 1409.0 reduce-scatter.25
  7526.1 133.8 all-gather.26
where the time goes:
time: 7710 us; the launch traced here: 7690 us
  waiting for transfers between devices  6230 us (81%)
  other arithmetic  582 us (8%)
  matrix products  391 us (5%)
  local copies, waits for them, and re-layouts  303 us (4%)
  blocking collectives  163 us (2%)
    reduce_scatter x3, waiting for transfers between devices, body(): lax.psum_scatter(jnp.concatenate([left, right], axis=1), ('dp', 'vocab'),...  4230 us
    reduce_scatter x1, waiting for transfers between devices, body(): lax.psum_scatter(grad_square, ('dp', 'vocab'), scatter_dimension=1, tiled...  623 us
    reduce_scatter x1, waiting for transfers between devices, body(): lax.psum_scatter(grad_wide, ('dp', 'vocab'), scatter_dimension=1, tiled=T...  476 us
    all_gather x3, waiting for transfers between devices, body(): lax.all_gather(gram_share.astype(jnp.bfloat16), ('dp', 'vocab'), axis=0,...  378 us
    scatter-add x1, other arithmetic, body(): grad_table = grad_table.at[safe_ids.reshape(-1)].add(row_updates)  297 us
    concatenate x3, local copies, waits for them, and re-layouts, body(): jnp.concatenate([left, right], axis=1)  181 us
    all_gather x1, waiting for transfers between devices, body(): lax.all_gather(table_master.astype(jnp.bfloat16), 'dp', axis=0, tiled=True)  160 us
  transfers between devices with their start and end apart: 16, of which 14 were waited for; matrix products, arithmetic and copies ran while one was open for 8% of the time, Pallas kernels for 0%

commit v1 on v0

--- a/solution.py
+++ b/solution.py
@@ -3,6 +3,7 @@
 import jax
 import jax.numpy as jnp
 from jax import lax
+from jax.sharding import Mesh
 from jax.sharding import PartitionSpec as P
 
 D = 1024
@@ -33,14 +34,6 @@
 masked_score = -1e30
 
 
-def combined_all(value, axis, join):
-    pieces = jax.tree.map(lambda part: lax.all_gather(part, axis), value)
-    head = jax.tree.map(lambda part: part[0], pieces)
-    tail = jax.tree.map(lambda part: part[1:], pieces)
-    running, _ = lax.scan(lambda running, piece: (join(running, piece), None), head, tail)
-    return running
-
-
 def rms_scale(inputs, gain):
     mean_square = jnp.mean(inputs * inputs, axis=-1, keepdims=True)
     return inputs * lax.rsqrt(mean_square + norm_epsilon) * gain
@@ -89,12 +82,6 @@
 def norm_back(inputs, gain, grad_out):
     _, pullback = jax.vjp(rms_scale, inputs, gain)
     return pullback(grad_out)
-
-
-def softmax_join(left, right):
-    peak = jnp.maximum(left[0], right[0])
-    total = left[1] * jnp.exp(left[0] - peak) + right[1] * jnp.exp(right[0] - peak)
-    return (peak, total, left[2] + right[2])
 
 
 def low_copy(values):
@@ -112,6 +99,63 @@
         first_hat / (jnp.sqrt(second_hat) + adam_epsilon) + weight_decay * master
     )
     return (change, first_new, second_new)
+
+DP = ("chip", "core")
+ALL = ("chip", "core", "vocab")
+SLOTS = 32
+
+
+def scatter_sum(values, dimension):
+    part = lax.psum_scatter(values, DP, scatter_dimension=dimension, tiled=True)
+    return lax.psum_scatter(part, "vocab", scatter_dimension=dimension, tiled=True)
+
+
+def onehot_rows(index, count):
+    return (index[:, None] == jnp.arange(count)[None, :]).astype(jnp.bfloat16)
+
+
+def token_slots(ids, block_rows):
+    owner = ids // block_rows
+    place = jnp.arange(ids.shape[0])
+    earlier = place[:, None] > place[None, :]
+    equal = ids[:, None] == ids[None, :]
+    first = jnp.logical_not(jnp.any(equal & earlier, axis=1))
+    ahead = (owner[:, None] == owner[None, :]) & earlier & first[None, :]
+    rank = jnp.sum(ahead.astype(jnp.int32), axis=1)
+    slot = jnp.sum(jnp.where(equal & first[None, :], rank[None, :], 0), axis=1)
+    return owner, first, slot
+
+
+def round_keys(owner, slot, turn):
+    within = slot - turn * SLOTS
+    return jnp.where((within >= 0) & (within < SLOTS), owner * SLOTS + within, -1)
+
+
+def round_asks(keys, first, local, count):
+    hits = (keys[None, :] == jnp.arange(count)[:, None]) & first[None, :]
+    return jnp.sum(jnp.where(hits, local[None, :] + 1, 0), axis=1) - 1
+
+
+def square_product(left, right):
+    return jnp.dot(
+        left.astype(jnp.bfloat16), right.astype(jnp.bfloat16), preferred_element_type=jnp.float32
+    )
+
+
+def ortho_rest(gram):
+    lead = leading_coefficient
+    power, rest = 1.0, None
+    for turn in range(NS_ITERS):
+        change = coef_second * gram + coef_third * square_product(gram, gram)
+        if turn + 1 < NS_ITERS:
+            mixed = square_product(change, gram)
+            gram = lead * lead * gram + 2.0 * lead * mixed + square_product(mixed, change)
+        if rest is None:
+            rest = change
+        else:
+            rest = lead * rest + power * change + square_product(rest, change)
+        power = power * lead
+    return power, rest
 
 
 def body(
@@ -141,26 +185,64 @@
     groups_per = HEADS // KV
     scale = HD ** (-0.5)
 
-    def local_place(ids):
-        block = ids // block_rows
-        place = block // members * block_rows + ids % block_rows
-        return (place, block % members == member)
-
-    square_b, wide_b, vector_b = (
-        lax.all_gather(square_master.astype(jnp.bfloat16), ("dp", "vocab"), axis=1, tiled=True),
-        lax.all_gather(wide_master.astype(jnp.bfloat16), ("dp", "vocab"), axis=1, tiled=True),
-        lax.all_gather(vector_master.astype(jnp.bfloat16), ("dp", "vocab"), axis=1, tiled=True),
-    )
-    table_b = lax.all_gather(table_master.astype(jnp.bfloat16), "dp", axis=0, tiled=True)
-    shard_vocab = table_b.shape[0]
+    devices = lax.axis_size(ALL)
+    device = lax.axis_index(ALL)
+    groups = devices // members
+
+    own_ids = lax.dynamic_index_in_dim(token_ids, member, 0, keepdims=False)
+    own_length = lengths[member]
+    start = own_length - 1 - RESP
+    owner, first_seen, slot = token_slots(own_ids, block_rows)
+    local_ids = own_ids % block_rows
+    keys = round_keys(owner, slot, 0)
+    asks = round_asks(keys, first_seen, local_ids, devices * SLOTS)
+    own_targets = lax.dynamic_slice_in_dim(own_ids, start + 1, RESP, 0)
+    vector_low = vector_master.astype(jnp.bfloat16).astype(jnp.float32)
+    whole_numbers = jnp.concatenate([asks, own_targets, order, jnp.max(slot)[None] + 1])
+    vectors_count = vector_low.size
+    notes = jnp.concatenate([vector_low.reshape(-1), whole_numbers.astype(jnp.float32)])
+    notes = lax.all_gather(notes, ALL, axis=0)
+    square_b = lax.all_gather(square_master.astype(jnp.bfloat16), ALL, axis=1, tiled=True)
+    wide_b = lax.all_gather(wide_master.astype(jnp.bfloat16), ALL, axis=1, tiled=True)
+    gains = (
+        notes[:, :vectors_count]
+        .reshape(devices, vector_master.shape[0], vector_master.shape[1])
+        .transpose(1, 0, 2)
+        .reshape(vector_master.shape[0], D)
+    )
+    numbers = notes[:, vectors_count:].astype(jnp.int32)
+    asked = lax.dynamic_slice_in_dim(numbers, device * SLOTS, SLOTS, 1).reshape(-1)
+    numbers = numbers[:, devices * SLOTS :]
+    targets = numbers[:, :RESP].reshape(-1)
+    orders = numbers[:, RESP : RESP + members].reshape(groups, members, members)[:, 0]
+    turns = (jnp.max(numbers[:, RESP + members]) + SLOTS - 1) // SLOTS
+    table_b = table_master.astype(jnp.bfloat16)
     head_gains = low_copy(norm_gains)
-    gains = vector_b.astype(jnp.float32)
     cosine, sine = rope_tables(SEQ, HD // 2)
-    safe_ids, inside = local_place(token_ids)
-    looked = jnp.where(inside[..., None], table_b[safe_ids].astype(jnp.float32), 0.0)
-    hidden0 = lax.psum_scatter(
-        looked.astype(jnp.bfloat16), "vocab", scatter_dimension=0, tiled=True
-    ).astype(jnp.float32)[0]
+
+    def exchanged(rows):
+        return lax.all_to_all(rows, ALL, 0, 0, tiled=True)
+
+    def fetched(wanted, row_keys):
+        rows = jnp.dot(
+            onehot_rows(wanted, block_rows), table_b, preferred_element_type=jnp.float32
+        ).astype(jnp.bfloat16)
+        return jnp.dot(
+            onehot_rows(row_keys, devices * SLOTS),
+            exchanged(rows),
+            preferred_element_type=jnp.float32,
+        )
+
+    def later_round(turn):
+        later_keys = round_keys(owner, slot, turn)
+        later_asks = round_asks(later_keys, first_seen, local_ids, devices * SLOTS)
+        return later_keys, exchanged(later_asks)
+
+    def fetch_more(turn, rows):
+        later_keys, later_asked = later_round(turn)
+        return rows + fetched(later_asked, later_keys)
+
+    hidden0 = lax.fori_loop(1, turns, fetch_more, fetched(asked, keys))
     act1 = rms_scale(hidden0, gains[0]).astype(jnp.bfloat16)
     inner = dense(act1, square_b[0:3].reshape(3 * D, D))
     entry = inner[:, :D]
@@ -205,47 +287,37 @@
     inner_b = (jax.nn.silu(gate_part) * up_part).astype(jnp.bfloat16)
     hidden3 = hidden2 + jnp.dot(inner_b, wide_b[2], preferred_element_type=jnp.float32)
     final_b = rms_scale(hidden3, gains[3]).astype(jnp.bfloat16)
-    own_length = lengths[member]
-    start = own_length - 1 - RESP
     answer_b = lax.dynamic_slice_in_dim(final_b, start, RESP, 0)
-    response_tokens = lax.all_gather(answer_b, "vocab", axis=0, tiled=True)
-    starts = lengths - 1 - RESP
-    targets = jax.vmap(lambda row, first: lax.dynamic_slice_in_dim(row, first + 1, RESP, 0))(
-        token_ids, starts
-    ).reshape(-1)
+    response_tokens = lax.all_gather(answer_b, ALL, axis=0, tiled=True)
     logit_scores = dense(response_tokens, table_b)
-    target_place, target_inside = local_place(targets)
-    local_target = jnp.where(target_inside, target_place, -1)
-    onehot = jnp.arange(shard_vocab)[None, :] == local_target[:, None]
+    local_target = jnp.where(targets // block_rows == device, targets % block_rows, -1)
+    onehot = jnp.arange(block_rows)[None, :] == local_target[:, None]
     top = jnp.max(logit_scores, axis=-1)
     exp_total = jnp.sum(jnp.exp(logit_scores - top[:, None]), axis=-1)
     picked = jnp.sum(jnp.where(onehot, logit_scores, 0.0), axis=-1)
-    top, exp_total, picked = combined_all((top, exp_total, picked), "vocab", softmax_join)
+    stats = lax.all_gather(jnp.stack([top, exp_total, picked]), ALL, axis=0)
+    top = jnp.max(stats[:, 0], axis=0)
+    exp_total = jnp.sum(stats[:, 1] * jnp.exp(stats[:, 0] - top[None, :]), axis=0)
+    picked = jnp.sum(stats[:, 2], axis=0)
     log_total = top + jnp.log(exp_total)
-    seq_logp = jnp.sum((picked - log_total).reshape(members, RESP), axis=-1)
+    seq_logp = jnp.sum((picked - log_total).reshape(groups, members, RESP), axis=-1)
     slots = jnp.arange(members)
-    chosen_mask = (order[0::2][:, None] == slots[None, :]).astype(jnp.float32)
-    rejected_mask = (order[1::2][:, None] == slots[None, :]).astype(jnp.float32)
+    chosen_mask = (orders[:, 0::2, None] == slots[None, None, :]).astype(jnp.float32)
+    rejected_mask = (orders[:, 1::2, None] == slots[None, None, :]).astype(jnp.float32)
     margin = (
-        pref_beta
-        * (jnp.sum(chosen_mask * seq_logp, axis=1) - jnp.sum(rejected_mask * seq_logp, axis=1))
-        / RESP
-    )
-    group_loss = jnp.sum(jax.nn.softplus(-margin))
+        pref_beta * jnp.sum((chosen_mask - rejected_mask) * seq_logp[:, None, :], axis=2) / RESP
+    )
+    pair_loss = jnp.sum(jax.nn.softplus(-margin))
     pull = jax.nn.sigmoid(-margin) * pref_beta / RESP
-    grad_logp = jnp.sum(rejected_mask * pull[:, None], axis=0) - jnp.sum(
-        chosen_mask * pull[:, None], axis=0
-    )
-    row_weight = jnp.repeat(grad_logp, RESP)
+    grad_logp = jnp.sum((rejected_mask - chosen_mask) * pull[:, :, None], axis=1)
+    row_weight = jnp.repeat(grad_logp.reshape(-1), RESP)
     softmax_rows = jnp.exp(logit_scores - log_total[:, None])
     grad_logits = (row_weight[:, None] * (onehot.astype(jnp.float32) - softmax_rows)).astype(
         jnp.bfloat16
     )
     grad_answers = jnp.dot(grad_logits, table_b, preferred_element_type=jnp.float32)
     grad_table = outer(grad_logits, response_tokens)
-    grad_answer_own = lax.psum_scatter(
-        grad_answers.astype(jnp.bfloat16), "vocab", scatter_dimension=0, tiled=True
-    ).astype(jnp.float32)
+    grad_answer_own = scatter_sum(grad_answers.astype(jnp.bfloat16), 0).astype(jnp.float32)
     grad_final = lax.dynamic_update_slice_in_dim(
         jnp.zeros((SEQ, D), jnp.float32), grad_answer_own, start, 0
     )
@@ -315,33 +387,41 @@
     grad_inner_w = outer(grad_inner_b, act1)
     grad_norm0, grad_gain0 = norm_back(hidden0, gains[0], grad_act1)
     grad_embed_b = (grad_hidden1 + grad_norm0).astype(jnp.bfloat16)
-    grad_rows = lax.all_gather(grad_embed_b, "vocab", axis=0, tiled=True)
-    row_updates = jnp.where(inside.reshape(-1)[:, None], grad_rows.astype(jnp.float32), 0.0)
-    grad_table = grad_table.at[safe_ids.reshape(-1)].add(row_updates)
-    share_table = lax.psum_scatter(
-        grad_table.astype(jnp.bfloat16), "dp", scatter_dimension=0, tiled=True
-    ).astype(jnp.float32)
+
+    def returned(wanted, row_keys):
+        rows = outer(onehot_rows(row_keys, devices * SLOTS), grad_embed_b)
+        rows = exchanged(rows.astype(jnp.bfloat16))
+        return outer(onehot_rows(wanted, block_rows), rows)
+
+    def return_more(turn, total):
+        later_keys, later_asked = later_round(turn)
+        return total + returned(later_asked, later_keys)
+
+    share_table = lax.fori_loop(1, turns, return_more, grad_table + returned(asked, keys))
     grad_square = jnp.concatenate(
         [
-            grad_inner_w.reshape(3, D, D),
-            jnp.stack([grad_mixer_w, grad_query_w, grad_pair_w, grad_out_w]),
+            grad_inner_w.astype(jnp.bfloat16).reshape(3, D, D),
+            grad_mixer_w.astype(jnp.bfloat16)[None],
+            grad_query_w.astype(jnp.bfloat16)[None],
+            grad_pair_w.astype(jnp.bfloat16)[None],
+            grad_out_w.astype(jnp.bfloat16)[None],
         ],
         axis=0,
     )
-    grad_wide = jnp.concatenate([grad_gate_up_w.reshape(2, FF, D), grad_down_w[None]], axis=0)
     grad_vector = jnp.stack(
         [grad_gain0, grad_gain1, grad_gain2, grad_gain3, grad_tap0, grad_tap1, grad_tap2]
     )
     grad_head_gains = jnp.stack([grad_query_gain, grad_key_gain])
-    share_square, share_wide, share_vector = (
-        lax.psum_scatter(grad_square, ("dp", "vocab"), scatter_dimension=1, tiled=True),
-        lax.psum_scatter(grad_wide, ("dp", "vocab"), scatter_dimension=1, tiled=True),
-        lax.psum_scatter(grad_vector, ("dp", "vocab"), scatter_dimension=1, tiled=True),
-    )
+    share_square = scatter_sum(grad_square, 1).astype(jnp.float32)
+    share_gate_up = scatter_sum(grad_gate_up_w.astype(jnp.bfloat16).reshape(2, FF, D), 1)
+    share_down = scatter_sum(grad_down_w.astype(jnp.bfloat16), 0)
+    share_wide = jnp.concatenate([share_gate_up, share_down[None]], axis=0).astype(jnp.float32)
+    vector_total, gains_total = lax.psum((grad_vector, grad_head_gains), ALL)
+    width = vector_master.shape[1]
+    share_vector = lax.dynamic_slice_in_dim(vector_total, device * width, width, 1)
     own_squares = (
         jnp.sum(share_square * share_square)
         + jnp.sum(share_wide * share_wide)
-        + jnp.sum(share_vector * share_vector)
         + jnp.sum(share_table * share_table)
     )
     moment_squares = jnp.concatenate(
@@ -363,11 +443,10 @@
         ]
     )
     moment_stats = jnp.stack([moment_squares, moment_cross, grad_squares])
-    loss_part = jnp.where(member == 0, group_loss, 0.0)
-    gains_total, stats_total, squares_total, pair_loss = lax.psum(
-        (grad_head_gains, moment_stats, own_squares, loss_part), ("dp", "vocab")
-    )
-    grad_norm = jnp.sqrt(squares_total + jnp.sum(gains_total * gains_total))
+    stats_total, squares_total = lax.psum((moment_stats, own_squares), ALL)
+    grad_norm = jnp.sqrt(
+        squares_total + jnp.sum(vector_total * vector_total) + jnp.sum(gains_total * gains_total)
+    )
     factor = jnp.minimum(1.0, clip_limit / grad_norm)
     square_moment_new = muon_decay * square_moment + (1.0 - muon_decay) * (factor * share_square)
     wide_moment_new = muon_decay * wide_moment + (1.0 - muon_decay) * (factor * share_wide)
@@ -378,47 +457,48 @@
     )
     ortho_square = square_moment_new / (moment_norm[:7][:, None, None] + ortho_epsilon)
     ortho_wide = wide_moment_new / (moment_norm[7:][:, None, None] + ortho_epsilon)
-    for turn in range(NS_ITERS):
-        narrow_square = ortho_square.astype(jnp.bfloat16)
-        narrow_wide = ortho_wide.astype(jnp.bfloat16)
-        left = jnp.einsum(
-            "mri,mrj->imj", narrow_square, narrow_square, preferred_element_type=jnp.float32
-        )
-        right = jnp.einsum(
-            "mri,mrj->imj", narrow_wide, narrow_wide, preferred_element_type=jnp.float32
-        )
-        gram_share = lax.psum_scatter(
-            jnp.concatenate([left, right], axis=1), ("dp", "vocab"), scatter_dimension=0, tiled=True
-        )
-        gram_b = lax.all_gather(
-            gram_share.astype(jnp.bfloat16), ("dp", "vocab"), axis=0, tiled=True
-        )
-        first_square = jnp.einsum(
-            "mri,imj->mrj", narrow_square, gram_b[:, :7], preferred_element_type=jnp.float32
-        )
-        first_wide = jnp.einsum(
-            "mri,imj->mrj", narrow_wide, gram_b[:, 7:], preferred_element_type=jnp.float32
-        )
-        second_square = jnp.einsum(
-            "mri,imj->mrj",
-            first_square.astype(jnp.bfloat16),
-            gram_b[:, :7],
-            preferred_element_type=jnp.float32,
-        )
-        second_wide = jnp.einsum(
-            "mri,imj->mrj",
-            first_wide.astype(jnp.bfloat16),
-            gram_b[:, 7:],
-            preferred_element_type=jnp.float32,
-        )
-        ortho_square = (
-            leading_coefficient * ortho_square
-            + coef_second * first_square
-            + coef_third * second_square
-        )
-        ortho_wide = (
-            leading_coefficient * ortho_wide + coef_second * first_wide + coef_third * second_wide
-        )
+    squares, square_rows = square_master.shape[0], square_master.shape[1]
+    wides, wide_rows = wide_master.shape[0], wide_master.shape[1]
+    chunk = max(squares * square_rows, wide_rows)
+    wide_jobs = jnp.pad(ortho_wide.astype(jnp.bfloat16), ((0, 0), (0, chunk - wide_rows), (0, 0)))
+    square_jobs = ortho_square.astype(jnp.bfloat16).reshape(1, squares * square_rows, D)
+    square_jobs = jnp.pad(square_jobs, ((0, 0), (0, chunk - squares * square_rows), (0, 0)))
+    jobs = jnp.concatenate([wide_jobs, square_jobs], axis=0).reshape(members * chunk, D)
+    jobs = lax.all_to_all(jobs, "vocab", 0, 0, tiled=True).reshape(members, chunk, D)
+    on_square = member == wides
+    group_square = (
+        jobs[:, : squares * square_rows]
+        .reshape(members, squares, square_rows, D)
+        .transpose(1, 0, 2, 3)
+        .reshape(squares, members * square_rows, D)
+    )
+    group_square = jnp.pad(group_square, ((0, groups - squares), (0, 0), (0, 0)))
+    whole_square = lax.all_to_all(
+        group_square.reshape(groups * members * square_rows, D), DP, 0, 0, tiled=True
+    )
+    wide_part = jobs[:, :wide_rows].reshape(members * wide_rows, D)
+    wide_part = jnp.pad(wide_part, ((0, D - members * wide_rows), (0, 0)))
+    job = jnp.where(on_square, whole_square, wide_part)
+    gram = outer(job, job)
+    gram_sum = lax.psum(gram.astype(jnp.bfloat16), DP).astype(jnp.float32)
+    gram = jnp.where(on_square, gram, gram_sum)
+    power, rest = ortho_rest(gram)
+    product_rows = square_product(job, rest).astype(jnp.bfloat16)
+    back_square = lax.all_to_all(product_rows, DP, 0, 0, tiled=True)
+    back_square = (
+        back_square.reshape(groups, members, square_rows, D)[:squares]
+        .transpose(1, 0, 2, 3)
+        .reshape(members, squares * square_rows, D)
+    )
+    back_square = jnp.pad(back_square, ((0, 0), (0, chunk - squares * square_rows), (0, 0)))
+    back_wide = product_rows[: members * wide_rows].reshape(members, wide_rows, D)
+    back_wide = jnp.pad(back_wide, ((0, 0), (0, chunk - wide_rows), (0, 0)))
+    backs = jnp.where(on_square, back_square, back_wide).reshape(members * chunk, D)
+    backs = lax.all_to_all(backs, "vocab", 0, 0, tiled=True).reshape(members, chunk, D)
+    ortho_wide = power * ortho_wide + backs[:wides, :wide_rows].astype(jnp.float32)
+    ortho_square = power * ortho_square + backs[wides, : squares * square_rows].reshape(
+        squares, square_rows, D
+    ).astype(jnp.float32)
     wide_scale = jnp.array([math.sqrt(FF / D), math.sqrt(FF / D), 1.0], jnp.float32)
     square_new = square_master - muon_rate * ortho_square
     wide_new = wide_master - muon_rate * wide_scale[:, None, None] * ortho_wide
@@ -454,23 +534,26 @@
 
 
 def solution(mesh):
+    groups, members = mesh.shape["dp"], mesh.shape["vocab"]
+    cores = 2
+    split_mesh = Mesh(mesh.devices.reshape(groups // cores, cores, members), ALL)
     return jax.shard_map(
         body,
-        mesh=mesh,
+        mesh=split_mesh,
         in_specs=(
-            P("dp", None),
-            P("dp", None),
-            P("dp", None),
-            P(("dp", "vocab"), None),
-            P(("dp", "vocab"), None),
-            P(("dp", "vocab"), None),
-            P(None, ("dp", "vocab"), None),
-            P(None, ("dp", "vocab"), None),
-            P(None, ("dp", "vocab"), None),
-            P(None, ("dp", "vocab"), None),
-            P(None, ("dp", "vocab")),
-            P(None, ("dp", "vocab")),
-            P(None, ("dp", "vocab")),
+            P(DP, None),
+            P(DP, None),
+            P(DP, None),
+            P(ALL, None),
+            P(ALL, None),
+            P(ALL, None),
+            P(None, ALL, None),
+            P(None, ALL, None),
+            P(None, ALL, None),
+            P(None, ALL, None),
+            P(None, ALL),
+            P(None, ALL),
+            P(None, ALL),
             P(),
             P(),
             P(),
@@ -479,22 +562,22 @@
         out_specs=(
             P(),
             P(),
-            P(None, ("dp", "vocab"), None),
-            P(None, ("dp", "vocab"), None),
-            P(None, ("dp", "vocab"), None),
-            P(None, ("dp", "vocab"), None),
-            P(None, ("dp", "vocab"), None),
-            P(None, ("dp", "vocab"), None),
-            P(("dp", "vocab"), None),
-            P(("dp", "vocab"), None),
-            P(("dp", "vocab"), None),
-            P(None, ("dp", "vocab")),
-            P(None, ("dp", "vocab")),
-            P(None, ("dp", "vocab")),
-            P(),
-            P(),
-            P(),
-            P(("dp", "vocab")),
+            P(None, ALL, None),
+            P(None, ALL, None),
+            P(None, ALL, None),
+            P(None, ALL, None),
+            P(None, ALL, None),
+            P(None, ALL, None),
+            P(ALL, None),
+            P(ALL, None),
+            P(ALL, None),
+            P(None, ALL),
+            P(None, ALL),
+            P(None, ALL),
+            P(),
+            P(),
+            P(),
+            P(ALL),
         ),
         check_vma=False,
     )

time: 7710 us -> 1710 us (0.22)
  waiting for transfers between devices: 6230 us -> 1040 us
  other arithmetic: 582 us -> 134 us
  local copies, waits for them, and re-layouts: 303 us -> 67.3 us
  blocking collectives: 163 us -> 85.3 us
    reduce_scatter x8, waiting for transfers between devices: 5500 us -> 456 us  [the longest x4 317 us: scatter_sum(): part = lax.psum_scatter(values, DP, scatter_dimension=dimension, tiled=True)]
    all_gather x7 -> x4, waiting for transfers between devices: 730 us -> 276 us  [the longest x1 111 us: body(): lax.all_gather(wide_master.astype(jnp.bfloat16), ALL, axis=1, tiled=True)]
    scatter-add x1 -> x0, other arithmetic: 297 us -> none  [body(): grad_table = grad_table.at[safe_ids.reshape(-1)].add(row_updates)]
    concatenate x3 -> x1, local copies, waits for them, and re-layouts: 181 us -> 0.73 us  [body(): jnp.concatenate([asks, own_targets, order, jnp.max(slot)[None] + 1])]
    all_to_all x0 -> x5, waiting for transfers between devices: none -> 135 us  [the longest x2 69.1 us: exchanged(): return lax.all_to_all(rows, ALL, 0, 0, tiled=True)]
    concatenate x4 -> x1, other arithmetic: 124 us -> 0.22 us  [body(): jnp.concatenate([wide_jobs, square_jobs], axis=0)]
    all_gather x5 -> x0, blocking collectives: 124 us -> none  [the longest x1 69.4 us: body(): lax.all_gather(vector_master.astype(jnp.bfloat16), ('dp', 'vocab'), axis=...]
    unnamed x17 -> x15, waiting for transfers between devices: 0.28 us -> 116 us
  transfers between devices with their start and end apart: 16 -> 19, of which waited for: 14 -> 18; matrix products, arithmetic and copies ran while one was open for 8% -> 11% of each run, Pallas kernels for 0% -> 0%
where the time goes in v1:
time: 1710 us; the launch traced here: 1700 us
  waiting for transfers between devices  1040 us (61%)
  matrix products  318 us (19%)
  other arithmetic  134 us (8%)
  blocking collectives  85.3 us (5%)
  local copies, waits for them, and re-layouts  67.3 us (4%)
  starting transfers between devices  27.3 us (2%)
  between operations  26.8 us (2%)
    reduce_scatter x4, waiting for transfers between devices, scatter_sum(): part = lax.psum_scatter(values, DP, scatter_dimension=dimension, tiled=True)  317 us
    reduce_scatter x4, waiting for transfers between devices, scatter_sum(): lax.psum_scatter(part, 'vocab', scatter_dimension=dimension, tiled=True)  139 us
    unnamed x15, waiting for transfers between devices  116 us
    all_gather x1, waiting for transfers between devices, body(): lax.all_gather(wide_master.astype(jnp.bfloat16), ALL, axis=1, tiled=True)  111 us
    dot_general x11, matrix products, outer(): lax.dot_general(grads, inputs, (((0,), (0,)), ((), ())), preferred_elemen...  83.7 us
    all_to_all x2, waiting for transfers between devices, exchanged(): return lax.all_to_all(rows, ALL, 0, 0, tiled=True)  69.1 us
    all_gather x1, waiting for transfers between devices, body(): response_tokens = lax.all_gather(answer_b, ALL, axis=0, tiled=True)  67.7 us
    dot_general x8, matrix products, dense(): lax.dot_general(inputs, weight, (((1,), (1,)), ((), ())), preferred_eleme...  63.3 us
  transfers between devices with their start and end apart: 19, of which 18 were waited for; matrix products, arithmetic and copies ran while one was open for 11% of the time, Pallas kernels for 0%

profile of v1, /device:TPU:0, one launch (start us, length us, event | category | flops | bytes accessed | tf_op | source)
XLA Modules:
  0.0 1700.0 jit_solution(13754129913998779439)
XLA Ops:
  26.6 115.7 %all-reduce.19.cloned.1.call-done = f32[43168]{0:T(1024)} async-done(((f32[43168]{0:T(1024)}), f32[43168]{0:T(1024)}) %all-reduce.19.cloned.1.call-update) | async-done | bytes 172688
  143.7 8.0 fusion.72
  151.7 6.2 all-to-all-start.4
  163.8 69.1 %all-to-all-done.4 = bf16[32,32,1024]{2,1,0:T(8,128)(2,1)S(1)} async-done(((bf16[32,32,1024]{2,1,0:T(8,128)(2,1)}), bf16[32,32,1024]{2,1,0:T(8,128)(2,1)S(1)}, u32[]{:S(2)}, u32[]{:S(2)}) %all-to-all-start.4) | async-done | bytes 2097184 | tf_op jit(solution)/shard_map/all_to_all | solution.py:224
  237.6 43.4 %all-gather.8.cloned.1.call-done = bf16[7,1024,1024]{2,1,0:T(8,128)(2,1)} async-done(((bf16[7,32,1024]{2,1,0:T(8,128)(2,1)}), bf16[7,1024,1024]{2,1,0:T(8,128)(2,1)}) %all-gather.8.cloned.1.call-update) | async-done | bytes 14680080 | tf_op jit(solution)/shard_map/all_gather | solution.py:205
  281.0 6.2 slice.264
  308.6 7.7 fusion.180
  316.3 9.0 fusion.17
  325.3 8.2 divide_convert_fusion
  341.2 111.4 %all-gather.10.cloned.1.call-done = bf16[3,4608,1024]{2,1,0:T(8,128)(2,1)} async-done(((bf16[3,144,1024]{2,1,0:T(8,128)(2,1)}), bf16[3,4608,1024]{2,1,0:T(8,128)(2,1)}) %all-gather.10.cloned.1.call-update) | async-done | bytes 28311568 | tf_op jit(solution)/shard_map/all_gather | solution.py:206
  452.6 16.7 slice.283
  469.3 17.5 %fusion.167 = f32[512,9216]{1,0:T(8,128)} fusion(bf16[9216,1024]{1,0:T(8,128)(2,1)} %bitcast.274, f32[512,1024]{1,0:T(8,128)S(1)} %get-tuple-element.360, f32[1024]{0:T(1024)S(1)} %copy-done.94, f32[512]{0:T(512)S(1)} %fusion.143), kind=kOutput, calls=%fused_computation.383 | convolution fusion | flops 9665249280 | bytes 39852032 | tf_op jit(solution)/shard_map/dot_general | solution.py:59
  486.7 7.7 multiply_convert_fusion.2
  494.5 9.4 multiply_reduce_fusion.14
  506.2 67.7 %all-gather.12.cloned.1.call-done = bf16[3072,1024]{1,0:T(8,128)(2,1)} async-done(((bf16[96,1024]{1,0:T(8,128)(2,1)}), bf16[3072,1024]{1,0:T(8,128)(2,1)}) %all-gather.12.cloned.1.call-update) | async-done | bytes 6291472 | tf_op jit(solution)/shard_map/all_gather | solution.py:291
  573.9 17.2 %fusion.181 = (f32[3072]{0:T(1024)S(1)}, f32[3072,2048]{0,1:T(8,128)S(1)}) fusion(bf16[3072,1024]{1,0:T(8,128)(2,1)} %all-gather.12.cloned.1.call-done, bf16[2048,1024]{1,0:T(8,128)(2,1)} %get-tuple-element.576), kind=kOutput, calls=%fused_computation.390 | convolution fusion | flops 12891190272 | bytes 35663872 | tf_op jit(solution)/shard_map/dot_general | solution.py:59
  591.2 7.0 exponential_reduce_fusion
  600.7 53.3 %all-gather.14.cloned.1.call-done = f32[32,3,3072]{2,1,0:T(4,128)} async-done(((f32[1,3,3072]{2,1,0:T(4,128)}), f32[32,3,3072]{2,1,0:T(4,128)}) %all-gather.14.cloned.1.call-update) | async-done | bytes 1179664 | tf_op jit(solution)/shard_map/all_gather | solution.py:298
  659.2 23.0 %convolution_convert_fusion.3 = bf16[3072,1024]{1,0:T(8,128)(2,1)} fusion(bf16[2048,1024]{1,0:T(8,128)(2,1)} %get-tuple-element.576, f32[3072,2048]{0,1:T(8,128)} %copy-done.4, f32[3072]{0:T(1024)S(1)} %get-tuple-element.320, f32[3072]{0:T(1024)S(1)} %mul.1191, s32[3072]{0:T(1024)S(1)} %fusion.131), kind=kOutput, calls=%fused_computation.66 | convolution fusion | flops 12925796352 | bytes 35688448 | tf_op jit(solution)/shard_map/dot_general | solution.py:318
  682.2 60.7 %reduce-scatter.9.cloned.1.call-done = bf16[384,1024]{1,0:T(8,128)(2,1)} async-done(((bf16[3072,1024]{1,0:T(8,128)(2,1)}), bf16[384,1024]{1,0:T(8,128)(2,1)}) %reduce-scatter.9.cloned.1.call-update) | async-done | bytes 786448 | tf_op jit(solution)/shard_map/reduce_scatter | solution.py:109
  743.0 25.6 %reduce-scatter.11.cloned.1.call-done = bf16[96,1024]{1,0:T(8,128)(2,1)} async-done(((bf16[384,1024]{1,0:T(8,128)(2,1)}), bf16[96,1024]{1,0:T(8,128)(2,1)}) %reduce-scatter.11.cloned.1.call-update) | async-done | bytes 196624 | tf_op jit(solution)/shard_map/reduce_scatter | solution.py:110
  775.3 17.4 %fusion.20 = (bf16[512,4608]{1,0:T(8,128)(2,1)}, bf16[512,4608]{1,0:T(8,128)(2,1)}) fusion(f32[512,9216]{1,0:T(8,128)} %fusion.167, bf16[3,4608,1024]{2,1,0:T(8,128)(2,1)} %all-gather.10.cloned.1.call-done, f32[512,1024]{1,0:T(8,128)} %add_add_fusion.6), kind=kOutput, calls=%fused_computation.48 | convolution fusion | flops 4865392640 | bytes 39845888 | tf_op jit(solution)/shard_map/dot_general | solution.py:59
  792.8 18.9 %multiply_reduce_fusion.6 = (f32[1024]{0:T(1024)}, f32[512]{0:T(512)S(1)}, f32[512,1024]{1,0:T(8,128)S(1)}) fusion(f32[512,1024]{1,0:T(8,128)S(1)} %copy-done.33, f32[512]{0:T(512)S(1)} %fusion.143, f32[1024]{0:T(1024)S(1)} %copy-done.94, bf16[9216,1024]{1,0:T(8,128)(2,1)} %bitcast.275, bf16[512,4608]{1,0:T(8,128)(2,1)} %get-tuple-element.329, ...), kind=kOutput, calls=%fused_computation.132 | convolution fusion | flops 9685694464 | bytes 32518144 | tf_op jit(solution)/shard_map/dot_general | solution.py:71
  823.1 15.3 fusion.14
  839.5 10.9 fusion.16
  896.9 11.0 convolution_convert_fusion.1
  908.6 18.5 %convolution_convert_fusion = bf16[9216,1024]{1,0:T(8,128)(2,1)} fusion(bf16[512,4608]{1,0:T(8,128)(2,1)} %get-tuple-element.329, bf16[512,4608]{1,0:T(8,128)(2,1)} %get-tuple-element.328, f32[512,1024]{1,0:T(8,128)} %copy-done.32, f32[1024]{0:T(1024)S(1)} %copy-done.94, f32[512]{0:T(512)S(1)} %copy-done.110), kind=kOutput, calls=%fused_computation.32 | convolution fusion | flops 9693560832 | bytes 30414848 | tf_op jit(solution)/shard_map/dot_general | solution.py:65
  928.6 7.9 multiply_reduce_fusion.8
  944.5 77.8 %reduce-scatter.13.cloned.1.call-done = bf16[7,128,1024]{2,1,0:T(8,128)(2,1)} async-done(((bf16[7,1024,1024]{2,1,0:T(8,128)(2,1)}), bf16[7,128,1024]{2,1,0:T(8,128)(2,1)}) %reduce-scatter.13.cloned.1.call-update) | async-done | bytes 1835024 | tf_op jit(solution)/shard_map/reduce_scatter | solution.py:109
  1022.5 7.0 fusion.23
  1029.5 73.2 %reduce-scatter.21.cloned.1.call-done = bf16[576,1024]{1,0:T(8,128)(2,1)} async-done(((bf16[4608,1024]{1,0:T(8,128)(2,1)}), bf16[576,1024]{1,0:T(8,128)(2,1)}) %reduce-scatter.21.cloned.1.call-update) | async-done | bytes 1179664 | tf_op jit(solution)/shard_map/reduce_scatter | solution.py:109
  1102.8 24.2 %convolution_add_fusion = f32[2048,1024]{1,0:T(8,128)} fusion(f32[2048,1024]{1,0:T(8,128)} %fusion.23, bf16[3072,1024]{1,0:T(8,128)(2,1)} %all-gather.12.cloned.1.call-done, f32[3072,2048]{0,1:T(8,128)} %copy-done.4, f32[3072]{0:T(1024)S(1)} %copy-done.102, f32[3072]{0:T(1024)S(1)} %copy-done.100, s32[3072]{0:T(1024)S(1)} %copy-done.81), kind=kOutput, calls=%fused_computation.67 | convolution fusion | flops 12924747776 | bytes 48271360 | tf_op jit(solution)/shard_map/dot_general | solution.py:65
  1127.0 105.7 %reduce-scatter.17.cloned.1.call-done = bf16[2,576,1024]{2,1,0:T(8,128)(2,1)} async-done(((bf16[2,4608,1024]{2,1,0:T(8,128)(2,1)}), bf16[2,576,1024]{2,1,0:T(8,128)(2,1)}) %reduce-scatter.17.cloned.1.call-update) | async-done | bytes 2359312 | tf_op jit(solution)/shard_map/reduce_scatter | solution.py:109
  1232.8 6.3 multiply_reduce_fusion
  1239.1 35.5 %reduce-scatter.15.cloned.1.call-done = bf16[7,32,1024]{2,1,0:T(8,128)(2,1)} async-done(((bf16[7,128,1024]{2,1,0:T(8,128)(2,1)}), bf16[7,32,1024]{2,1,0:T(8,128)(2,1)}) %reduce-scatter.15.cloned.1.call-update) | async-done | bytes 458768 | tf_op jit(solution)/shard_map/reduce_scatter | solution.py:110
  1276.6 28.6 %reduce-scatter.23.cloned.1.call-done = bf16[144,1024]{1,0:T(8,128)(2,1)} async-done(((bf16[576,1024]{1,0:T(8,128)(2,1)}), bf16[144,1024]{1,0:T(8,128)(2,1)}) %reduce-scatter.23.cloned.1.call-update) | async-done | bytes 294928 | tf_op jit(solution)/shard_map/reduce_scatter | solution.py:110
  1305.2 49.2 %reduce-scatter.19.cloned.1.call-done = bf16[2,144,1024]{2,1,0:T(8,128)(2,1)} async-done(((bf16[2,576,1024]{2,1,0:T(8,128)(2,1)}), bf16[2,144,1024]{2,1,0:T(8,128)(2,1)}) %reduce-scatter.19.cloned.1.call-update) | async-done | bytes 589840 | tf_op jit(solution)/shard_map/reduce_scatter | solution.py:110
  1359.3 40.2 %all-reduce.13 = (f32[]{:T(128)}, f32[7,1024]{1,0:T(8,128)S(1)}, f32[2,64]{1,0:T(2,128)S(1)}, f32[3,10]{1,0:T(4,128)S(1)}) all-reduce(f32[]{:T(128)S(6)} %add.570, f32[7,1024]{1,0:T(8,128)S(1)} %stack.56, f32[2,64]{1,0:T(2,128)S(1)} %pad_maximum_fusion.14, ...), channel_id=1, replica_groups=mesh['chip'=4,'core'=2,'vocab'=4] {'chip','core','vocab'}, use_global_device_ids=true, to_apply=%region_48.49 | all-reduce | flops 7327 | bytes 58616 | tf_op jit(solution)/shard_map/psum | solution.py:446
  1406.9 45.1 %all_to_all.102 = bf16[4,224,1024]{2,1,0:T(8,128)(2,1)S(1)} all-to-all(bf16[4,224,1024]{2,1,0:T(8,128)(2,1)S(1)} %fusion.79), channel_id=1, replica_groups=mesh['chip'=4,'core'=2,'vocab'=4] {'vocab'}, dimensions={0} | all-to-all | bytes 3670016 | tf_op jit(solution)/shard_map/all_to_all | solution.py:467
  1458.5 26.1 %all-to-all-done.7 = bf16[8,128,1024]{2,1,0:T(8,128)(2,1)} async-done(((bf16[8,128,1024]{2,1,0:T(8,128)(2,1)}), bf16[8,128,1024]{2,1,0:T(8,128)(2,1)}, u32[]{:S(2)}, u32[]{:S(2)}) %all-to-all-start.7) | async-done | bytes 2097184 | tf_op jit(solution)/shard_map/all_to_all | solution.py:476
  1492.1 58.8 %all-reduce.17.cloned.1.call-done = bf16[1024,1024]{1,0:T(8,128)(2,1)} async-done(((bf16[1024,1024]{1,0:T(8,128)(2,1)}), bf16[1024,1024]{1,0:T(8,128)(2,1)}) %all-reduce.17.cloned.1.call-update) | async-done | bytes 2097168 | tf_op jit(solution)/shard_map/psum | solution.py:483
  1551.0 6.8 multiply_add_fusion.4
  1578.7 14.2 multiply_add_fusion.2
  1593.0 12.0 fusion.63
  1612.2 23.2 %all-to-all-done.8 = bf16[8,128,1024]{2,1,0:T(8,128)(2,1)S(1)} async-done(((bf16[8,128,1024]{2,1,0:T(8,128)(2,1)}), bf16[8,128,1024]{2,1,0:T(8,128)(2,1)S(1)}, u32[]{:S(2)}, u32[]{:S(2)}) %all-to-all-start.8) | async-done | bytes 2097184 | tf_op jit(solution)/shard_map/all_to_all | solution.py:487
  1637.7 7.5 all-to-all-start.9
  1645.7 22.7 %add_multiply_fusion = (f32[2048,1024]{1,0:T(8,128)}, f32[2048,1024]{1,0:T(8,128)}, f32[2048,1024]{1,0:T(8,128)}) fusion(f32[2048,1024]{1,0:T(8,128)} %param.25, f32[]{:T(128)S(6)} %sub.201, f32[]{:T(128)S(6)} %sub.200, f32[2048,1024]{1,0:T(8,128)} %get-tuple-element.227, f32[]{:T(128)S(6)} %min.3, f32[2048,1024]{1,0:T(8,128)} %param.27, f32[2048,1024]{1,0:T(8,128)} %param.26), kind=kLoop, calls=%fused_computation.56 | loop fusion | flops 31457280 | bytes 58720268 | tf_op jit(solution)/shard_map/mul | solution.py:98
  1668.4 16.5 all-to-all-done.9
  (508 shorter events, 202.3 us)
Async XLA Ops:
  7.2 135.1 %all-reduce.19.cloned.1.call-start = ((), (), s32[]{:S(2)}) async-start(), calls=%async_computation.30 | async-start | bytes 352256
  9.7 223.2 %copy-start.123 = (s32[512]{0:T(512)}, s32[512]{0:T(512)S(1)}, u32[]{:S(2)}) copy-start(s32[512]{0:T(512)S(1)} %get-tuple-element.343) | copy-start | bytes 6148
  17.2 263.8 %all-gather.8.cloned.1.call-start = ((), (), s32[]{:S(2)}) async-start(), calls=%async_computation.18 | async-start | bytes 15138816 | tf_op jit(solution)/shard_map/all_gather | solution.py:205
  19.3 433.3 %all-gather.10.cloned.1.call-start = ((), (), s32[]{:S(2)}) async-start(), calls=%async_computation.19 | async-start | bytes 29196288 | tf_op jit(solution)/shard_map/all_gather | solution.py:206
  151.7 81.2 %all-to-all-start.4 = ((bf16[32,32,1024]{2,1,0:T(8,128)(2,1)}), bf16[32,32,1024]{2,1,0:T(8,128)(2,1)S(1)}, u32[]{:S(2)}, u32[]{:S(2)}) async-start(bf16[32,32,1024]{2,1,0:T(8,128)(2,1)} %bitcast.305), calls=%async_computation.4 | async-start | bytes 4194304 | tf_op jit(solution)/shard_map/all_to_all | solution.py:224
  157.9 416.0 %all-gather.12.cloned.1.call-start = ((), (), s32[]{:S(2)}) async-start(), calls=%async_computation.20 | async-start | bytes 6488064 | tf_op jit(solution)/shard_map/all_gather | solution.py:291
  160.3 147.7 %copy-start.40 = (f32[512,32]{0,1:T(8,128)}, f32[512,32]{0,1:T(8,128)S(1)}, u32[]{:S(2)}) copy-start(f32[512,32]{0,1:T(8,128)S(1)} %get-tuple-element.349) | copy-start | bytes 196612
  160.3 147.7 %copy-start.42 = (f32[512,32]{0,1:T(8,128)}, f32[512,32]{0,1:T(8,128)S(1)}, u32[]{:S(2)}) copy-start(f32[512,32]{0,1:T(8,128)S(1)} %get-tuple-element.350) | copy-start | bytes 196612
  162.2 125.0 %copy-start.95 = (f32[1024]{0:T(1024)}, f32[1024]{0:T(1024)S(1)}, u32[]{:S(2)}) copy-start(f32[1024]{0:T(1024)S(1)} %mul.1123) | copy-start | bytes 12292
  162.2 131.3 %copy-start.84 = (f32[1024]{0:T(1024)}, f32[1024]{0:T(1024)S(1)}, u32[]{:S(2)}) copy-start(f32[1024]{0:T(1024)S(1)} %mul.1126) | copy-start | bytes 12292
  162.3 131.3 %copy-start.86 = (f32[1024]{0:T(1024)}, f32[1024]{0:T(1024)S(1)}, u32[]{:S(2)}) copy-start(f32[1024]{0:T(1024)S(1)} %mul.1130) | copy-start | bytes 12292
  162.4 131.2 %copy-start.88 = (f32[1024]{0:T(1024)}, f32[1024]{0:T(1024)S(1)}, u32[]{:S(2)}) copy-start(f32[1024]{0:T(1024)S(1)} %mul.1133) | copy-start | bytes 12292
  162.5 137.4 %copy-start.82 = (f32[1024]{0:T(1024)}, f32[1024]{0:T(1024)S(1)}, u32[]{:S(2)}) copy-start(f32[1024]{0:T(1024)S(1)} %mul.1140) | copy-start | bytes 12292
  235.7 51.5 %copy-start.63 = (s32[512]{0:T(512)}, s32[512]{0:T(512)S(1)}, u32[]{:S(2)}) copy-start(s32[512]{0:T(512)S(1)} %get-tuple-element.610) | copy-start | bytes 6148
  235.7 51.5 %copy-start.65 = (s32[512]{0:T(512)}, s32[512]{0:T(512)S(1)}, u32[]{:S(2)}) copy-start(s32[512]{0:T(512)S(1)} %get-tuple-element.611) | copy-start | bytes 6148
  341.1 128.1 %copy-start.113 = (f32[512]{0:T(512)}, f32[512]{0:T(512)S(1)}, u32[]{:S(2)}) copy-start(f32[512]{0:T(512)S(1)} %get-tuple-element.359) | copy-start | bytes 6148
  341.2 153.3 %copy-start.32 = (f32[512,1024]{1,0:T(8,128)}, f32[512,1024]{1,0:T(8,128)S(1)}, u32[]{:S(2)}) copy-start(f32[512,1024]{1,0:T(8,128)S(1)} %get-tuple-element.360) | copy-start | bytes 6291460
  341.2 470.5 %copy-start.109 = (f32[512]{0:T(512)}, f32[512]{0:T(512)S(1)}, u32[]{:S(2)}) copy-start(f32[512]{0:T(512)S(1)} %fusion.143) | copy-start | bytes 6148
  341.2 128.1 %copy-start.94 = (f32[1024]{0:T(1024)S(1)}, f32[1024]{0:T(1024)}, u32[]{:S(2)}) copy-start(f32[1024]{0:T(1024)} %mul.1175) | copy-start | bytes 12292
  506.0 147.9 %all-gather.14.cloned.1.call-start = ((), (), s32[]{:S(2)}) async-start(), calls=%async_computation.31 | async-start | bytes 1622016 | tf_op jit(solution)/shard_map/all_gather | solution.py:298
  506.2 153.0 %copy-start.80 = (s32[3072]{0:T(1024)}, s32[3072]{0:T(1024)S(1)}, u32[]{:S(2)}) copy-start(s32[3072]{0:T(1024)S(1)} %fusion.131) | copy-start | bytes 36868
  600.2 142.7 %reduce-scatter.9.cloned.1.call-start = ((), (), s32[]{:S(2)}) async-start(), calls=%async_computation.21 | async-start | bytes 7077888 | tf_op jit(solution)/shard_map/reduce_scatter | solution.py:109
  682.1 86.5 %reduce-scatter.11.cloned.1.call-start = ((), (), s32[]{:S(2)}) async-start(), calls=%async_computation.22 | async-start | bytes 983040 | tf_op jit(solution)/shard_map/reduce_scatter | solution.py:110
  743.0 279.3 %reduce-scatter.13.cloned.1.call-start = ((), (), s32[]{:S(2)}) async-start(), calls=%async_computation.23 | async-start | bytes 16515072 | tf_op jit(solution)/shard_map/reduce_scatter | solution.py:109
  896.9 205.8 %reduce-scatter.21.cloned.1.call-start = ((), (), s32[]{:S(2)}) async-start(), calls=%async_computation.27 | async-start | bytes 10616832 | tf_op jit(solution)/shard_map/reduce_scatter | solution.py:109
  907.9 324.8 %reduce-scatter.17.cloned.1.call-start = ((), (), s32[]{:S(2)}) async-start(), calls=%async_computation.25 | async-start | bytes 21233664 | tf_op jit(solution)/shard_map/reduce_scatter | solution.py:109
  939.9 82.5 %copy-start.97 = (f32[1024]{0:T(1024)S(1)}, f32[1024]{0:T(1024)}, u32[]{:S(2)}) copy-start(f32[1024]{0:T(1024)} %get-tuple-element.241) | copy-start | bytes 12292
  939.9 82.5 %copy-start.119 = (f32[1024]{0:T(1024)S(1)}, f32[1024]{0:T(1024)}, u32[]{:S(2)}) copy-start(f32[1024]{0:T(1024)} %get-tuple-element.235) | copy-start | bytes 12292
  939.9 82.5 %copy-start.120 = (f32[1024]{0:T(1024)S(1)}, f32[1024]{0:T(1024)}, u32[]{:S(2)}) copy-start(f32[1024]{0:T(1024)} %get-tuple-element.237) | copy-start | bytes 12292
  939.9 82.6 %copy-start.121 = (f32[64]{0:T(128)S(1)}, f32[64]{0:T(128)}, u32[]{:S(2)}) copy-start(f32[64]{0:T(128)} %get-tuple-element.247) | copy-start | bytes 772
  939.9 82.6 %copy-start.122 = (f32[64]{0:T(128)S(1)}, f32[64]{0:T(128)}, u32[]{:S(2)}) copy-start(f32[64]{0:T(128)} %get-tuple-element.230) | copy-start | bytes 772
  939.9 82.6 %copy-start.118 = (s32[1024]{0:T(1024)S(1)}, s32[1024]{0:T(1024)}, u32[]{:S(2)}) copy-start(s32[1024]{0:T(1024)} %copy-done.117) | copy-start | bytes 12292
  939.9 82.6 %all-to-all-start.5 = ((bf16[32,32,1024]{2,1,0:T(8,128)(2,1)}), bf16[32,32,1024]{2,1,0:T(8,128)(2,1)S(1)}, u32[]{:S(2)}, u32[]{:S(2)}) async-start(bf16[32,32,1024]{2,1,0:T(8,128)(2,1)} %bitcast.307), calls=%async_computation.13 | async-start | bytes 4194304 | tf_op jit(solution)/shard_map/all_to_all | solution.py:224
  944.5 330.1 %reduce-scatter.15.cloned.1.call-start = ((), (), s32[]{:S(2)}) async-start(), calls=%async_computation.24 | async-start | bytes 2293760 | tf_op jit(solution)/shard_map/reduce_scatter | solution.py:110
  1022.3 282.9 %reduce-scatter.23.cloned.1.call-start = ((), (), s32[]{:S(2)}) async-start(), calls=%async_computation.28 | async-start | bytes 1474560 | tf_op jit(solution)/shard_map/reduce_scatter | solution.py:110
  1022.5 80.3 %copy-start.81 = (s32[3072]{0:T(1024)S(1)}, s32[3072]{0:T(1024)}, u32[]{:S(2)}) copy-start(s32[3072]{0:T(1024)} %copy-done.80) | copy-start | bytes 36868
  1022.5 80.3 %copy-start.100 = (f32[3072]{0:T(1024)S(1)}, f32[3072]{0:T(1024)}, u32[]{:S(2)}) copy-start(f32[3072]{0:T(1024)} %copy-done.99) | copy-start | bytes 36868
  1022.5 80.3 %copy-start.102 = (f32[3072]{0:T(1024)S(1)}, f32[3072]{0:T(1024)}, u32[]{:S(2)}) copy-start(f32[3072]{0:T(1024)} %copy-done.101) | copy-start | bytes 36868
  1102.7 251.7 %reduce-scatter.19.cloned.1.call-start = ((), (), s32[]{:S(2)}) async-start(), calls=%async_computation.26 | async-start | bytes 2949120 | tf_op jit(solution)/shard_map/reduce_scatter | solution.py:110
  1127.0 105.7 %copy-start.64 = (s32[512]{0:T(512)S(1)}, s32[512]{0:T(512)}, u32[]{:S(2)}) copy-start(s32[512]{0:T(512)} %copy-done.63) | copy-start | bytes 6148
  1127.0 105.7 %copy-start.66 = (s32[512]{0:T(512)S(1)}, s32[512]{0:T(512)}, u32[]{:S(2)}) copy-start(s32[512]{0:T(512)} %copy-done.65) | copy-start | bytes 6148
  1127.0 105.8 %copy-start.72 = (s32[512]{0:T(512)S(1)}, s32[512]{0:T(512)}, u32[]{:S(2)}) copy-start(s32[512]{0:T(512)} %copy-done.71) | copy-start | bytes 6148
  1127.0 105.8 %copy-start.78 = (pred[512]{0:T(512)(128)(4,1)S(1)}, pred[512]{0:T(512)(128)(4,1)}, u32[]{:S(2)}) copy-start(pred[512]{0:T(512)(128)(4,1)} %copy-done.77) | copy-start | bytes 1540
  1232.8 121.6 %copy-start.23 = (f32[3,144,1024]{2,1,0:T(8,128)S(1)}, f32[3,144,1024]{2,1,0:T(8,128)}, u32[]{:S(2)}) copy-start(f32[3,144,1024]{2,1,0:T(8,128)} %param.31) | copy-start | bytes 5308420
  1453.6 31.0 %all-to-all-start.7 = ((bf16[8,128,1024]{2,1,0:T(8,128)(2,1)}), bf16[8,128,1024]{2,1,0:T(8,128)(2,1)}, u32[]{:S(2)}, u32[]{:S(2)}) async-start(bf16[8,128,1024]{2,1,0:T(8,128)(2,1)} %pad.55), calls=%async_computation.15 | async-start | bytes 4194304 | tf_op jit(solution)/shard_map/all_to_all | solution.py:476
  1458.0 93.0 %all-reduce.17.cloned.1.call-start = ((), (), s32[]{:S(2)}) async-start(), calls=%async_computation.29 | async-start | bytes 4194304 | tf_op jit(solution)/shard_map/psum | solution.py:483
  1605.0 30.3 %all-to-all-start.8 = ((bf16[8,128,1024]{2,1,0:T(8,128)(2,1)}), bf16[8,128,1024]{2,1,0:T(8,128)(2,1)S(1)}, u32[]{:S(2)}, u32[]{:S(2)}) async-start(bf16[8,128,1024]{2,1,0:T(8,128)(2,1)} %bitcast.293), calls=%async_computation.16 | async-start | bytes 4194304 | tf_op jit(solution)/shard_map/all_to_all | solution.py:487
  1637.7 47.3 %all-to-all-start.9 = ((bf16[4,224,1024]{2,1,0:T(8,128)(2,1)}), bf16[4,224,1024]{2,1,0:T(8,128)(2,1)}, u32[]{:S(2)}, u32[]{:S(2)}) async-start(bf16[4,224,1024]{2,1,0:T(8,128)(2,1)} %bitcast_select_fusion.2), calls=%async_computation.17 | async-start | bytes 3670016 | tf_op jit(solution)/shard_map/all_to_all | solution.py:497
  (122 other events, 1048.0 us)
Sparse Core Ops, SparseCore 0:
  17.3 124.9 all-reduce.18
  145.9 135.0 all-gather.7
  284.6 167.9 all-gather.9
  506.2 67.7 all-gather.11
  600.3 53.5 all-gather.13
  682.3 60.6 reduce-scatter.8
  745.3 23.2 reduce-scatter.10
  897.0 125.2 reduce-scatter.12
  1026.2 76.4 reduce-scatter.20
  1106.6 126.0 reduce-scatter.16
  1235.1 39.3 reduce-scatter.14
  1276.9 28.3 reduce-scatter.22
  1307.6 46.7 reduce-scatter.18
  1492.2 58.6 all-reduce.16

commit v2 on v1

--- a/solution.py
+++ b/solution.py
@@ -105,9 +105,41 @@
 SLOTS = 32
 
 
-def scatter_sum(values, dimension):
-    part = lax.psum_scatter(values, DP, scatter_dimension=dimension, tiled=True)
-    return lax.psum_scatter(part, "vocab", scatter_dimension=dimension, tiled=True)
+def exchanged(rows):
+    return lax.all_to_all(rows, ALL, 0, 0, tiled=True)
+
+
+def spread(values):
+    count = lax.axis_size(ALL)
+    return lax.all_to_all(jnp.broadcast_to(values[None], (count,) + values.shape), ALL, 0, 0)
+
+
+def turned(values, step):
+    count = lax.axis_size("vocab")
+    return lax.ppermute(values, "vocab", [(i, (i + step) % count) for i in range(count)])
+
+
+def member_gather(values):
+    return jnp.concatenate(
+        [values] + [turned(values, step) for step in range(1, lax.axis_size("vocab"))], axis=0
+    )
+
+
+def member_return(blocks):
+    total = blocks[0].astype(jnp.float32)
+    for step in range(1, len(blocks)):
+        total = total + turned(blocks[step], -step).astype(jnp.float32)
+    return total
+
+
+def member_scatter(blocks, member):
+    count = blocks.shape[0]
+    return member_return(
+        [
+            lax.dynamic_index_in_dim(blocks, (member - step) % count, 0, keepdims=False)
+            for step in range(count)
+        ]
+    )
 
 
 def onehot_rows(index, count):
@@ -198,30 +230,37 @@
     asks = round_asks(keys, first_seen, local_ids, devices * SLOTS)
     own_targets = lax.dynamic_slice_in_dim(own_ids, start + 1, RESP, 0)
     vector_low = vector_master.astype(jnp.bfloat16).astype(jnp.float32)
-    whole_numbers = jnp.concatenate([asks, own_targets, order, jnp.max(slot)[None] + 1])
-    vectors_count = vector_low.size
-    notes = jnp.concatenate([vector_low.reshape(-1), whole_numbers.astype(jnp.float32)])
-    notes = lax.all_gather(notes, ALL, axis=0)
+    shared_notes = jnp.concatenate(
+        [
+            vector_low.reshape(-1),
+            jnp.concatenate([own_targets, order, jnp.max(slot)[None] + 1]).astype(jnp.float32),
+        ]
+    )
+    notes = jnp.concatenate(
+        [
+            asks.reshape(devices, SLOTS).astype(jnp.float32),
+            jnp.broadcast_to(shared_notes[None, :], (devices, shared_notes.size)),
+        ],
+        axis=1,
+    )
+    notes = exchanged(notes)
     square_b = lax.all_gather(square_master.astype(jnp.bfloat16), ALL, axis=1, tiled=True)
-    wide_b = lax.all_gather(wide_master.astype(jnp.bfloat16), ALL, axis=1, tiled=True)
+    wide_b = lax.all_gather(wide_master.astype(jnp.bfloat16), DP, axis=1, tiled=True)
+    hidden_units = wide_b.shape[1]
+    asked = notes[:, :SLOTS].astype(jnp.int32).reshape(-1)
     gains = (
-        notes[:, :vectors_count]
-        .reshape(devices, vector_master.shape[0], vector_master.shape[1])
+        notes[:, SLOTS : SLOTS + vector_low.size]
+        .reshape(devices, vector_low.shape[0], vector_low.shape[1])
         .transpose(1, 0, 2)
-        .reshape(vector_master.shape[0], D)
-    )
-    numbers = notes[:, vectors_count:].astype(jnp.int32)
-    asked = lax.dynamic_slice_in_dim(numbers, device * SLOTS, SLOTS, 1).reshape(-1)
-    numbers = numbers[:, devices * SLOTS :]
+        .reshape(vector_low.shape[0], D)
+    )
+    numbers = notes[:, SLOTS + vector_low.size :].astype(jnp.int32)
     targets = numbers[:, :RESP].reshape(-1)
     orders = numbers[:, RESP : RESP + members].reshape(groups, members, members)[:, 0]
     turns = (jnp.max(numbers[:, RESP + members]) + SLOTS - 1) // SLOTS
     table_b = table_master.astype(jnp.bfloat16)
     head_gains = low_copy(norm_gains)
     cosine, sine = rope_tables(SEQ, HD // 2)
-
-    def exchanged(rows):
-        return lax.all_to_all(rows, ALL, 0, 0, tiled=True)
 
     def fetched(wanted, row_keys):
         rows = jnp.dot(
@@ -253,19 +292,34 @@
     mixer = (leave * convolved).astype(jnp.bfloat16)
     hidden1 = hidden0 + dense(mixer, square_b[3])
     act2 = rms_scale(hidden1, gains[1]).astype(jnp.bfloat16)
-    query_raw = dense(act2, square_b[4]).reshape(SEQ, HEADS, HD)
+
+    def answers(values):
+        return lax.dynamic_slice_in_dim(values, start, RESP, 0)
+
+    def placed(values):
+        return lax.dynamic_update_slice_in_dim(
+            jnp.zeros((SEQ, values.shape[1]), values.dtype), values, start, 0
+        )
+
+    answer_act2 = answers(act2)
+    query_raw = dense(answer_act2, square_b[4]).reshape(RESP, HEADS, HD)
     pair_raw = dense(act2, square_b[5])
     key_raw = pair_raw[:, : KV * HD].reshape(SEQ, KV, HD)
     value_b = pair_raw[:, KV * HD :].astype(jnp.bfloat16).reshape(SEQ, KV, HD)
 
+    answer_cosine, answer_sine = answers(cosine), answers(sine)
+
     def query_prep(raw, gain):
+        return rotate(rms_scale(raw, gain), answer_cosine, answer_sine)
+
+    def key_prep(raw, gain):
         return rotate(rms_scale(raw, gain), cosine, sine)
 
     query_b = (
-        query_prep(query_raw, head_gains[0]).astype(jnp.bfloat16).reshape(SEQ, KV, groups_per, HD)
-    )
-    key_b = query_prep(key_raw, head_gains[1]).astype(jnp.bfloat16)
-    causal = jnp.arange(SEQ)[:, None] >= jnp.arange(SEQ)[None, :]
+        query_prep(query_raw, head_gains[0]).astype(jnp.bfloat16).reshape(RESP, KV, groups_per, HD)
+    )
+    key_b = key_prep(key_raw, head_gains[1]).astype(jnp.bfloat16)
+    causal = start + jnp.arange(RESP)[:, None] >= jnp.arange(SEQ)[None, :]
     scores = (
         jnp.einsum("sgrd,tgd->grst", query_b, key_b, preferred_element_type=jnp.float32) * scale
     )
@@ -277,30 +331,33 @@
     probs_b = (expo / total).astype(jnp.bfloat16)
     attended = jnp.einsum(
         "grst,tgd->sgrd", probs_b, value_b, preferred_element_type=jnp.float32
-    ).reshape(SEQ, D)
+    ).reshape(RESP, D)
     attended_b = attended.astype(jnp.bfloat16)
-    hidden2 = hidden1 + dense(attended_b, square_b[6])
-    act3 = rms_scale(hidden2, gains[2]).astype(jnp.bfloat16)
-    gate_up = dense(act3, wide_b[0:2].reshape(2 * FF, D))
-    gate_part = gate_up[:, :FF]
-    up_part = gate_up[:, FF:]
+    hidden2 = answers(hidden1) + dense(attended_b, square_b[6])
+    act3 = member_gather(rms_scale(hidden2, gains[2]).astype(jnp.bfloat16))
+    gate_up = dense(act3, wide_b[0:2].reshape(2 * hidden_units, D))
+    gate_part = gate_up[:, :hidden_units]
+    up_part = gate_up[:, hidden_units:]
     inner_b = (jax.nn.silu(gate_part) * up_part).astype(jnp.bfloat16)
-    hidden3 = hidden2 + jnp.dot(inner_b, wide_b[2], preferred_element_type=jnp.float32)
+    ffn_part = jnp.dot(inner_b, wide_b[2], preferred_element_type=jnp.float32)
+    hidden3 = hidden2 + member_return(ffn_part.astype(jnp.bfloat16).reshape(members, RESP, D))
     final_b = rms_scale(hidden3, gains[3]).astype(jnp.bfloat16)
-    answer_b = lax.dynamic_slice_in_dim(final_b, start, RESP, 0)
-    response_tokens = lax.all_gather(answer_b, ALL, axis=0, tiled=True)
+    response_tokens = lax.all_gather(final_b, ALL, axis=0, tiled=True)
     logit_scores = dense(response_tokens, table_b)
     local_target = jnp.where(targets // block_rows == device, targets % block_rows, -1)
     onehot = jnp.arange(block_rows)[None, :] == local_target[:, None]
     top = jnp.max(logit_scores, axis=-1)
     exp_total = jnp.sum(jnp.exp(logit_scores - top[:, None]), axis=-1)
     picked = jnp.sum(jnp.where(onehot, logit_scores, 0.0), axis=-1)
-    stats = lax.all_gather(jnp.stack([top, exp_total, picked]), ALL, axis=0)
+    stats = jnp.stack([top, exp_total, picked]).reshape(3, devices, RESP).transpose(1, 0, 2)
+    stats = exchanged(stats)
     top = jnp.max(stats[:, 0], axis=0)
     exp_total = jnp.sum(stats[:, 1] * jnp.exp(stats[:, 0] - top[None, :]), axis=0)
-    picked = jnp.sum(stats[:, 2], axis=0)
-    log_total = top + jnp.log(exp_total)
-    seq_logp = jnp.sum((picked - log_total).reshape(groups, members, RESP), axis=-1)
+    own_log_total = top + jnp.log(exp_total)
+    own_logp = jnp.sum(jnp.sum(stats[:, 2], axis=0) - own_log_total)
+    joined = spread(jnp.concatenate([own_log_total, own_logp[None]]))
+    log_total = joined[:, :RESP].reshape(-1)
+    seq_logp = joined[:, RESP].reshape(groups, members)
     slots = jnp.arange(members)
     chosen_mask = (orders[:, 0::2, None] == slots[None, None, :]).astype(jnp.float32)
     rejected_mask = (orders[:, 1::2, None] == slots[None, None, :]).astype(jnp.float32)
@@ -317,24 +374,27 @@
     )
     grad_answers = jnp.dot(grad_logits, table_b, preferred_element_type=jnp.float32)
     grad_table = outer(grad_logits, response_tokens)
-    grad_answer_own = scatter_sum(grad_answers.astype(jnp.bfloat16), 0).astype(jnp.float32)
-    grad_final = lax.dynamic_update_slice_in_dim(
-        jnp.zeros((SEQ, D), jnp.float32), grad_answer_own, start, 0
-    )
+    grad_answer_group = lax.psum_scatter(
+        grad_answers.astype(jnp.bfloat16), DP, scatter_dimension=0, tiled=True
+    )
+    grad_final = member_scatter(grad_answer_group.reshape(members, RESP, D), member)
     grad_hidden3, grad_gain3 = norm_back(hidden3, gains[3], grad_final)
-    grad_ffn_out = grad_hidden3.astype(jnp.bfloat16)
+    grad_ffn_out = member_gather(grad_hidden3.astype(jnp.bfloat16))
     grad_inner = dense(grad_ffn_out, wide_b[2])
     grad_down_w = outer(inner_b, grad_ffn_out)
     _, silu_pull = jax.vjp(lambda gate_in, up_in: jax.nn.silu(gate_in) * up_in, gate_part, up_part)
     grad_gate, grad_up = silu_pull(grad_inner)
     grad_gate_up = jnp.concatenate([grad_gate, grad_up], axis=1).astype(jnp.bfloat16)
-    grad_act3 = back_dense(grad_gate_up, wide_b[0:2].reshape(2 * FF, D))
+    grad_act3_part = back_dense(grad_gate_up, wide_b[0:2].reshape(2 * hidden_units, D))
+    grad_act3 = member_return(grad_act3_part.astype(jnp.bfloat16).reshape(members, RESP, D))
     grad_gate_up_w = outer(grad_gate_up, act3)
     grad_norm2, grad_gain2 = norm_back(hidden2, gains[2], grad_act3)
     grad_hidden2 = grad_hidden3 + grad_norm2
     grad_attn_out = grad_hidden2.astype(jnp.bfloat16)
     grad_attended = (
-        back_dense(grad_attn_out, square_b[6]).astype(jnp.bfloat16).reshape(SEQ, KV, groups_per, HD)
+        back_dense(grad_attn_out, square_b[6])
+        .astype(jnp.bfloat16)
+        .reshape(RESP, KV, groups_per, HD)
     )
     grad_out_w = outer(grad_attn_out, attended_b)
     scores = (
@@ -351,24 +411,24 @@
     grad_scores = (probs * (grad_probs - delta)).astype(jnp.bfloat16)
     grad_query = (
         jnp.einsum("grst,tgd->sgrd", grad_scores, key_b, preferred_element_type=jnp.float32) * scale
-    ).reshape(SEQ, HEADS, HD)
+    ).reshape(RESP, HEADS, HD)
     grad_keys = (
         jnp.einsum("grst,sgrd->tgd", grad_scores, query_b, preferred_element_type=jnp.float32)
         * scale
     )
     _, query_pull = jax.vjp(query_prep, query_raw, head_gains[0])
     grad_query_raw, grad_query_gain = query_pull(grad_query)
-    _, key_pull = jax.vjp(query_prep, key_raw, head_gains[1])
+    _, key_pull = jax.vjp(key_prep, key_raw, head_gains[1])
     grad_key_raw, grad_key_gain = key_pull(grad_keys)
-    grad_query_b = grad_query_raw.reshape(SEQ, D).astype(jnp.bfloat16)
+    grad_query_b = grad_query_raw.reshape(RESP, D).astype(jnp.bfloat16)
     grad_pair_b = jnp.concatenate(
         [grad_key_raw.reshape(SEQ, KV * HD), grad_values.reshape(SEQ, KV * HD)], axis=1
     ).astype(jnp.bfloat16)
-    grad_act2 = back_dense(grad_query_b, square_b[4]) + back_dense(grad_pair_b, square_b[5])
-    grad_query_w = outer(grad_query_b, act2)
+    grad_act2 = back_dense(grad_pair_b, square_b[5]) + placed(back_dense(grad_query_b, square_b[4]))
+    grad_query_w = outer(grad_query_b, answer_act2)
     grad_pair_w = outer(grad_pair_b, act2)
     grad_norm1, grad_gain1 = norm_back(hidden1, gains[1], grad_act2)
-    grad_hidden1 = grad_hidden2 + grad_norm1
+    grad_hidden1 = placed(grad_hidden2) + grad_norm1
     grad_mix_out = grad_hidden1.astype(jnp.bfloat16)
     grad_mixer = back_dense(grad_mix_out, square_b[3])
     grad_mixer_w = outer(grad_mix_out, mixer)
@@ -412,16 +472,37 @@
         [grad_gain0, grad_gain1, grad_gain2, grad_gain3, grad_tap0, grad_tap1, grad_tap2]
     )
     grad_head_gains = jnp.stack([grad_query_gain, grad_key_gain])
-    share_square = scatter_sum(grad_square, 1).astype(jnp.float32)
-    share_gate_up = scatter_sum(grad_gate_up_w.astype(jnp.bfloat16).reshape(2, FF, D), 1)
-    share_down = scatter_sum(grad_down_w.astype(jnp.bfloat16), 0)
-    share_wide = jnp.concatenate([share_gate_up, share_down[None]], axis=0).astype(jnp.float32)
-    vector_total, gains_total = lax.psum((grad_vector, grad_head_gains), ALL)
+    grad_wide = jnp.concatenate(
+        [
+            grad_gate_up_w.astype(jnp.bfloat16).reshape(2, hidden_units, D),
+            grad_down_w.astype(jnp.bfloat16)[None],
+        ],
+        axis=0,
+    )
+    share_wide_b = lax.psum_scatter(grad_wide, DP, scatter_dimension=1, tiled=True)
+    share_wide = share_wide_b.astype(jnp.float32)
+    squares, square_rows = square_master.shape[0], square_master.shape[1]
+    wides, wide_rows = wide_master.shape[0], wide_master.shape[1]
+    group_square = lax.psum_scatter(grad_square, DP, scatter_dimension=1, tiled=True)
+    share_square = member_scatter(
+        group_square.reshape(squares, members, square_rows, D).transpose(1, 0, 2, 3), member
+    )
     width = vector_master.shape[1]
-    share_vector = lax.dynamic_slice_in_dim(vector_total, device * width, width, 1)
+    vector_notes = grad_vector.reshape(-1, devices, width).transpose(1, 0, 2).reshape(devices, -1)
+    vector_notes = jnp.concatenate(
+        [
+            vector_notes,
+            jnp.broadcast_to(grad_head_gains.reshape(1, -1), (devices, grad_head_gains.size)),
+        ],
+        axis=1,
+    )
+    vector_notes = jnp.sum(exchanged(vector_notes), axis=0)
+    share_vector = vector_notes[: vector_master.size].reshape(vector_master.shape)
+    gains_total = vector_notes[vector_master.size :].reshape(grad_head_gains.shape)
     own_squares = (
         jnp.sum(share_square * share_square)
         + jnp.sum(share_wide * share_wide)
+        + jnp.sum(share_vector * share_vector)
         + jnp.sum(share_table * share_table)
     )
     moment_squares = jnp.concatenate(
@@ -443,10 +524,10 @@
         ]
     )
     moment_stats = jnp.stack([moment_squares, moment_cross, grad_squares])
-    stats_total, squares_total = lax.psum((moment_stats, own_squares), ALL)
-    grad_norm = jnp.sqrt(
-        squares_total + jnp.sum(vector_total * vector_total) + jnp.sum(gains_total * gains_total)
-    )
+    sums = jnp.concatenate([moment_stats.reshape(-1), own_squares[None]])
+    sums = jnp.sum(spread(sums), axis=0)
+    stats_total = sums[:-1].reshape(moment_stats.shape)
+    grad_norm = jnp.sqrt(sums[-1] + jnp.sum(gains_total * gains_total))
     factor = jnp.minimum(1.0, clip_limit / grad_norm)
     square_moment_new = muon_decay * square_moment + (1.0 - muon_decay) * (factor * share_square)
     wide_moment_new = muon_decay * wide_moment + (1.0 - muon_decay) * (factor * share_wide)
@@ -457,48 +538,55 @@
     )
     ortho_square = square_moment_new / (moment_norm[:7][:, None, None] + ortho_epsilon)
     ortho_wide = wide_moment_new / (moment_norm[7:][:, None, None] + ortho_epsilon)
-    squares, square_rows = square_master.shape[0], square_master.shape[1]
-    wides, wide_rows = wide_master.shape[0], wide_master.shape[1]
-    chunk = max(squares * square_rows, wide_rows)
-    wide_jobs = jnp.pad(ortho_wide.astype(jnp.bfloat16), ((0, 0), (0, chunk - wide_rows), (0, 0)))
-    square_jobs = ortho_square.astype(jnp.bfloat16).reshape(1, squares * square_rows, D)
-    square_jobs = jnp.pad(square_jobs, ((0, 0), (0, chunk - squares * square_rows), (0, 0)))
-    jobs = jnp.concatenate([wide_jobs, square_jobs], axis=0).reshape(members * chunk, D)
-    jobs = lax.all_to_all(jobs, "vocab", 0, 0, tiled=True).reshape(members, chunk, D)
-    on_square = member == wides
-    group_square = (
-        jobs[:, : squares * square_rows]
-        .reshape(members, squares, square_rows, D)
-        .transpose(1, 0, 2, 3)
-        .reshape(squares, members * square_rows, D)
-    )
-    group_square = jnp.pad(group_square, ((0, groups - squares), (0, 0), (0, 0)))
-    whole_square = lax.all_to_all(
-        group_square.reshape(groups * members * square_rows, D), DP, 0, 0, tiled=True
-    )
-    wide_part = jobs[:, :wide_rows].reshape(members * wide_rows, D)
-    wide_part = jnp.pad(wide_part, ((0, D - members * wide_rows), (0, 0)))
-    job = jnp.where(on_square, whole_square, wide_part)
-    gram = outer(job, job)
-    gram_sum = lax.psum(gram.astype(jnp.bfloat16), DP).astype(jnp.float32)
-    gram = jnp.where(on_square, gram, gram_sum)
+    core = lax.axis_index("core")
+    per_member = -(-squares // members)
+    wide_early = jnp.stack([wide_moment.astype(jnp.bfloat16), share_wide_b], axis=1)
+    wide_early = jnp.pad(wide_early, ((0, members - wides), (0, 0), (0, 0), (0, 0)))
+    wide_early = lax.all_to_all(wide_early, "vocab", 0, 0, tiled=True).astype(jnp.float32)
+    wide_inverse = 1.0 / (moment_norm[squares:] + ortho_epsilon)
+    wide_inverse = jnp.pad(wide_inverse, (0, members - wides))[member]
+    wide_job = (
+        (
+            (muon_decay * wide_inverse) * wide_early[:, 0]
+            + ((1.0 - muon_decay) * factor * wide_inverse) * wide_early[:, 1]
+        )
+        .reshape(members * wide_rows, D)
+        .astype(jnp.bfloat16)
+    )
+    wide_gram = lax.psum(outer(wide_job, wide_job).astype(jnp.bfloat16), DP)
+
+    def to_members(values):
+        values = jnp.pad(values, ((0, per_member * members - squares), (0, 0), (0, 0)))
+        values = values.reshape(per_member, members, square_rows, D).transpose(1, 0, 2, 3)
+        return lax.all_to_all(values, "vocab", 0, 0, tiled=True)
+
+    def from_members(values):
+        values = lax.all_to_all(values, "vocab", 0, 0, tiled=True).transpose(1, 0, 2, 3)
+        return values.reshape(per_member * members, square_rows, D)[:squares]
+
+    group_rows = members * square_rows
+    square_part = to_members(ortho_square.astype(jnp.bfloat16)).transpose(1, 0, 2, 3)
+    square_part = square_part.reshape(per_member, 1, group_rows, D)
+    square_part = jnp.pad(
+        square_part, ((0, groups // 2 - per_member), (1, 0), (0, 0), (0, 0))
+    ).reshape(groups * group_rows, D)
+    square_job = lax.all_to_all(square_part, DP, 0, 0, tiled=True)
+    square_gram = outer(square_job, square_job)
+    gram = jnp.where(core == 0, wide_gram.astype(jnp.float32), square_gram)
     power, rest = ortho_rest(gram)
-    product_rows = square_product(job, rest).astype(jnp.bfloat16)
-    back_square = lax.all_to_all(product_rows, DP, 0, 0, tiled=True)
-    back_square = (
-        back_square.reshape(groups, members, square_rows, D)[:squares]
-        .transpose(1, 0, 2, 3)
-        .reshape(members, squares * square_rows, D)
-    )
-    back_square = jnp.pad(back_square, ((0, 0), (0, chunk - squares * square_rows), (0, 0)))
-    back_wide = product_rows[: members * wide_rows].reshape(members, wide_rows, D)
-    back_wide = jnp.pad(back_wide, ((0, 0), (0, chunk - wide_rows), (0, 0)))
-    backs = jnp.where(on_square, back_square, back_wide).reshape(members * chunk, D)
-    backs = lax.all_to_all(backs, "vocab", 0, 0, tiled=True).reshape(members, chunk, D)
-    ortho_wide = power * ortho_wide + backs[:wides, :wide_rows].astype(jnp.float32)
-    ortho_square = power * ortho_square + backs[wides, : squares * square_rows].reshape(
-        squares, square_rows, D
-    ).astype(jnp.float32)
+    rest_b = rest.astype(jnp.bfloat16)
+    wide_rest = jnp.where(core == 0, rest_b, lax.ppermute(rest_b, "core", [(0, 1), (1, 0)]))
+    back_square = lax.all_to_all(
+        square_product(square_job, rest_b).astype(jnp.bfloat16), DP, 0, 0, tiled=True
+    )
+    back_square = back_square.reshape(groups // 2, 2, members, square_rows, D)[:per_member, 1]
+    back_square = from_members(back_square.transpose(1, 0, 2, 3))
+    back_wide = square_product(wide_job, wide_rest).astype(jnp.bfloat16)
+    back_wide = lax.all_to_all(
+        back_wide.reshape(members, wide_rows, D), "vocab", 0, 0, tiled=True
+    )[:wides]
+    ortho_wide = power * ortho_wide + back_wide.astype(jnp.float32)
+    ortho_square = power * ortho_square + back_square.astype(jnp.float32)
     wide_scale = jnp.array([math.sqrt(FF / D), math.sqrt(FF / D), 1.0], jnp.float32)
     square_new = square_master - muon_rate * ortho_square
     wide_new = wide_master - muon_rate * wide_scale[:, None, None] * ortho_wide

time: 1710 us -> 1140 us (0.67)
  waiting for transfers between devices: 1040 us -> 575 us
  matrix products: 318 us -> 229 us
  blocking collectives: 85.3 us -> 10.4 us
  starting transfers between devices: 27.3 us -> 74.5 us
    reduce_scatter x8 -> x3, waiting for transfers between devices: 456 us -> 135 us  [the longest x1 63 us: body(): lax.psum_scatter(grad_answers.astype(jnp.bfloat16), DP, scatter_dimension...]
    all_gather x3 -> x2, waiting for transfers between devices: 232 us -> 79.9 us  [the longest x1 66.1 us: body(): response_tokens = lax.all_gather(final_b, ALL, axis=0, tiled=True)]
    unnamed x15 -> x7, waiting for transfers between devices: 116 us -> 0.11 us
    ppermute x0 -> x19, waiting for transfers between devices: none -> 59.7 us  [the longest x18 59.7 us: turned(): lax.ppermute(values, 'vocab', [(i, (i + step) % count) for i in range(cou...]
    all_to_all x2 -> x4, waiting for transfers between devices: 69.1 us -> 125 us  [exchanged(): return lax.all_to_all(rows, ALL, 0, 0, tiled=True)]
    psum x1 -> x0, blocking collectives: 40.2 us -> none  [body(): stats_total, squares_total = lax.psum((moment_stats, own_squares), ALL)]
    all_to_all x1, blocking collectives: 45.1 us -> 10.4 us  [exchanged(): return lax.all_to_all(rows, ALL, 0, 0, tiled=True)]
    all_gather x1, waiting for transfers between devices: 43.4 us -> 13 us  [body(): lax.all_gather(square_master.astype(jnp.bfloat16), ALL, axis=1, tiled=True)]
  transfers between devices with their start and end apart: 19 -> 38, of which waited for: 18 -> 27; matrix products, arithmetic and copies ran while one was open for 11% -> 17% of each run, Pallas kernels for 0% -> 0%
where the time goes in v2:
time: 1140 us; the launch traced here: 1120 us
  waiting for transfers between devices  575 us (50%)
  matrix products  229 us (20%)
  other arithmetic  128 us (11%)
  local copies, waits for them, and re-layouts  76.6 us (7%)
  starting transfers between devices  74.5 us (7%)
  between operations  28.6 us (3%)
    all_to_all x4, waiting for transfers between devices, exchanged(): return lax.all_to_all(rows, ALL, 0, 0, tiled=True)  125 us
    psum x1, waiting for transfers between devices, body(): wide_gram = lax.psum(outer(wide_job, wide_job).astype(jnp.bfloat16), DP)  69.5 us
    all_gather x1, waiting for transfers between devices, body(): response_tokens = lax.all_gather(final_b, ALL, axis=0, tiled=True)  66.1 us
    reduce_scatter x1, waiting for transfers between devices, body(): lax.psum_scatter(grad_answers.astype(jnp.bfloat16), DP, scatter_dimension...  63 us
    dot_general x12, matrix products, outer(): lax.dot_general(grads, inputs, (((0,), (0,)), ((), ())), preferred_elemen...  62.4 us
    ppermute x18, waiting for transfers between devices, turned(): lax.ppermute(values, 'vocab', [(i, (i + step) % count) for i in range(cou...  59.7 us
    dot_general x11, matrix products, square_product(): jnp.dot(left.astype(jnp.bfloat16), right.astype(jnp.bfloat16), preferred_...  58.4 us
    reduce_scatter x1, waiting for transfers between devices, body(): lax.psum_scatter(grad_wide, DP, scatter_dimension=1, tiled=True)  56.2 us
  transfers between devices with their start and end apart: 38, of which 27 were waited for; matrix products, arithmetic and copies ran while one was open for 17% of the time, Pallas kernels for 0%

profile of v2, /device:TPU:0, one launch (start us, length us, event | category | flops | bytes accessed | tf_op | source)
XLA Modules:
  0.0 1122.8 jit_solution(13419764622790008843)
XLA Ops:
  19.0 7.3 all-to-all-start.4
  26.3 6.1 convert_element_type.338
  34.5 8.1 fusion.63
  52.4 82.3 %all-to-all-done.5 = bf16[32,32,1024]{2,1,0:T(8,128)(2,1)} async-done(((bf16[32,32,1024]{2,1,0:T(8,128)(2,1)}), bf16[32,32,1024]{2,1,0:T(8,128)(2,1)}, u32[]{:S(2)}, u32[]{:S(2)}) %all-to-all-start.5) | async-done | bytes 2097184 | tf_op jit(solution)/shard_map/all_to_all | solution.py:109
  140.9 13.0 %all-gather.4.cloned.1.call-done = bf16[7,1024,1024]{2,1,0:T(8,128)(2,1)} async-done(((bf16[7,32,1024]{2,1,0:T(8,128)(2,1)}), bf16[7,1024,1024]{2,1,0:T(8,128)(2,1)}) %all-gather.4.cloned.1.call-update) | async-done | bytes 14680080 | tf_op jit(solution)/shard_map/all_gather | solution.py:247
  153.9 6.2 slice.328
  160.2 6.0 fusion.166
  190.5 13.8 %all-gather.6.cloned.1.call-done = bf16[3,1152,1024]{2,1,0:T(8,128)(2,1)} async-done(((bf16[3,144,1024]{2,1,0:T(8,128)(2,1)}), bf16[3,1152,1024]{2,1,0:T(8,128)(2,1)}) %all-gather.6.cloned.1.call-update) | async-done | bytes 7077904 | tf_op jit(solution)/shard_map/all_gather | solution.py:248
  225.6 5.3 collective-permute-done.5
  230.9 6.7 collective-permute-done.4
  244.5 66.1 %all-gather.8.cloned.1.call-done = bf16[3072,1024]{1,0:T(8,128)(2,1)} async-done(((bf16[96,1024]{1,0:T(8,128)(2,1)}), bf16[3072,1024]{1,0:T(8,128)(2,1)}) %all-gather.8.cloned.1.call-update) | async-done | bytes 6291472 | tf_op jit(solution)/shard_map/all_gather | solution.py:345
  310.6 20.4 %fusion.182 = (f32[3072]{0:T(1024)}, f32[3072,2048]{0,1:T(8,128)}) fusion(bf16[3072,1024]{1,0:T(8,128)(2,1)} %all-gather.8.cloned.1.call-done, bf16[2048,1024]{1,0:T(8,128)(2,1)} %get-tuple-element.572), kind=kOutput, calls=%fused_computation.424 | convolution fusion | flops 12891190272 | bytes 35663872 | tf_op jit(solution)/shard_map/dot_general | solution.py:59
  332.5 12.4 %exponential_reduce_fusion = (f32[3072]{0:T(1024)}, f32[3072]{0:T(1024)}) fusion(f32[3072,2048]{0,1:T(8,128)} %get-tuple-element.374, f32[3072]{0:T(1024)} %get-tuple-element.373, s32[3072]{0:T(1024)} %fusion.124), kind=kLoop, calls=%fused_computation.31 | loop fusion | flops 31451136 | bytes 25214976 | tf_op jit(solution)/shard_map/reduce_sum | solution.py:350
  348.5 10.4 all_to_all.154
  388.5 22.9 %convolution_convert_fusion.2 = bf16[3072,1024]{1,0:T(8,128)(2,1)} fusion(bf16[2048,1024]{1,0:T(8,128)(2,1)} %get-tuple-element.572, f32[3072,2048]{0,1:T(8,128)} %get-tuple-element.374, f32[3072]{0:T(1024)} %sub.201, f32[3072]{0:T(1024)} %mul.1177, s32[3072]{0:T(1024)} %fusion.124), kind=kOutput, calls=%fused_computation.43 | convolution fusion | flops 12925796352 | bytes 35688448 | tf_op jit(solution)/shard_map/dot_general | solution.py:375
  411.6 63.0 %reduce-scatter.4.cloned.1.call-done = bf16[384,1024]{1,0:T(8,128)(2,1)} async-done(((bf16[3072,1024]{1,0:T(8,128)(2,1)}), bf16[384,1024]{1,0:T(8,128)(2,1)}) %reduce-scatter.4.cloned.1.call-update) | async-done | bytes 786448 | tf_op jit(solution)/shard_map/reduce_scatter | solution.py:377
  481.0 4.5 collective-permute-done.6
  485.5 5.3 collective-permute-done.8
  490.8 6.3 collective-permute-done.7
  504.1 4.8 collective-permute-done.11
  508.9 9.5 collective-permute-done.10
  518.4 4.5 fusion.72
  531.9 8.5 collective-permute-done.14
  540.4 5.2 collective-permute-done.13
  570.2 7.2 multiply_reduce_fusion.2
  580.6 5.2 convolution_convert_fusion.1
  599.9 10.8 multiply_reduce_fusion.1
  620.9 4.7 all-to-all-done.8
  639.8 35.7 %all-to-all-done.9 = bf16[32,32,1024]{2,1,0:T(8,128)(2,1)S(1)} async-done(((bf16[32,32,1024]{2,1,0:T(8,128)(2,1)}), bf16[32,32,1024]{2,1,0:T(8,128)(2,1)S(1)}, u32[]{:S(2)}, u32[]{:S(2)}) %all-to-all-start.9) | async-done | bytes 2097184 | tf_op jit(solution)/shard_map/all_to_all | solution.py:109
  675.5 7.0 fusion.15
  682.5 24.0 %convolution_add_fusion = f32[2048,1024]{1,0:T(8,128)} fusion(f32[2048,1024]{1,0:T(8,128)} %fusion.15, bf16[3072,1024]{1,0:T(8,128)(2,1)} %all-gather.8.cloned.1.call-done, f32[3072,2048]{0,1:T(8,128)} %get-tuple-element.374, f32[3072]{0:T(1024)S(1)} %copy-done.105, f32[3072]{0:T(1024)S(1)} %copy-done.106, s32[3072]{0:T(1024)S(1)} %copy-done.89), kind=kOutput, calls=%fused_computation.47 | convolution fusion | flops 12924747776 | bytes 48271360 | tf_op jit(solution)/shard_map/dot_general | solution.py:65
  706.5 15.6 %reduce-scatter.6.cloned.1.call-done = bf16[7,128,1024]{2,1,0:T(8,128)(2,1)} async-done(((bf16[7,1024,1024]{2,1,0:T(8,128)(2,1)}), bf16[7,128,1024]{2,1,0:T(8,128)(2,1)}) %reduce-scatter.6.cloned.1.call-update) | async-done | bytes 1835024 | tf_op jit(solution)/shard_map/reduce_scatter | solution.py:486
  729.0 6.8 multiply_reduce_fusion
  735.8 56.2 %reduce-scatter.8.cloned.1.call-done = bf16[3,144,1024]{2,1,0:T(8,128)(2,1)} async-done(((bf16[3,1152,1024]{2,1,0:T(8,128)(2,1)}), bf16[3,144,1024]{2,1,0:T(8,128)(2,1)}) %reduce-scatter.8.cloned.1.call-update) | async-done | bytes 884752 | tf_op jit(solution)/shard_map/reduce_scatter | solution.py:482
  802.8 4.6 all-to-all-start.10
  809.1 5.4 all-to-all-done.10
  824.5 47.6 %all-to-all-done.13 = bf16[4,2,144,1024]{3,2,1,0:T(8,128)(2,1)S(1)} async-done(((bf16[4,2,144,1024]{3,2,1,0:T(8,128)(2,1)}), bf16[4,2,144,1024]{3,2,1,0:T(8,128)(2,1)S(1)}, u32[]{:S(2)}, u32[]{:S(2)}) %all-to-all-start.13) | async-done | bytes 2359328 | tf_op jit(solution)/shard_map/all_to_all | solution.py:545
  880.9 9.4 all-to-all-done.11
  904.3 69.5 %all-reduce.14.cloned.1.call-done = bf16[1024,1024]{1,0:T(8,128)(2,1)} async-done(((bf16[1024,1024]{1,0:T(8,128)(2,1)}), bf16[1024,1024]{1,0:T(8,128)(2,1)}) %all-reduce.14.cloned.1.call-update) | async-done | bytes 2097168 | tf_op jit(solution)/shard_map/psum | solution.py:556
  990.6 4.5 fusion.157
  995.1 4.4 fusion.47
  999.5 17.4 %multiply_add_fusion.2 = f32[1024,1024]{1,0:T(8,128)} fusion(f32[1024,1024]{1,0:T(8,128)} %fusion.47, f32[1024,1024]{1,0:T(8,128)} %copy-done.141, f32[1024,1024]{1,0:T(8,128)} %copy-done.139), kind=kOutput, calls=%fused_computation.52 | convolution fusion | flops 2160066560 | bytes 16777216 | tf_op jit(solution)/shard_map/dot_general | solution.py:172
  1016.9 11.6 %add_convert_fusion = bf16[1024,1024]{1,0:T(8,128)(2,1)S(1)} fusion(f32[1024,1024]{1,0:T(8,128)} %multiply_add_fusion.2, f32[1024,1024]{1,0:T(8,128)} %fusion.157, f32[1024,1024]{1,0:T(8,128)S(1)} %multiply_add_fusion.4, f32[1024,1024]{1,0:T(8,128)} %copy-done.140), kind=kOutput, calls=%fused_computation.51 | convolution fusion | flops 2161115136 | bytes 18874368 | tf_op jit(solution)/shard_map/dot_general | solution.py:172
  1038.7 24.0 %all-to-all-done.14 = bf16[8,128,1024]{2,1,0:T(8,128)(2,1)S(1)} async-done(((bf16[8,128,1024]{2,1,0:T(8,128)(2,1)}), bf16[8,128,1024]{2,1,0:T(8,128)(2,1)S(1)}, u32[]{:S(2)}, u32[]{:S(2)}) %all-to-all-start.14) | async-done | bytes 2097184 | tf_op jit(solution)/shard_map/all_to_all | solution.py:579
  1063.6 4.6 all-to-all-start.15
  1073.0 6.9 all-to-all-done.15
  1084.2 22.7 %add_multiply_fusion = (f32[2048,1024]{1,0:T(8,128)}, f32[2048,1024]{1,0:T(8,128)}, f32[2048,1024]{1,0:T(8,128)}) fusion(f32[2048,1024]{1,0:T(8,128)} %param.25, f32[]{:T(128)S(6)} %sub.214, f32[]{:T(128)S(6)} %sub.213, f32[2048,1024]{1,0:T(8,128)} %get-tuple-element.227, f32[]{:T(128)S(6)} %min.3, f32[2048,1024]{1,0:T(8,128)} %param.27, f32[2048,1024]{1,0:T(8,128)} %param.26), kind=kLoop, calls=%fused_computation.34 | loop fusion | flops 31457280 | bytes 58720268 | tf_op jit(solution)/shard_map/mul | solution.py:98
  1110.0 4.6 fusion.171
  (605 shorter events, 285.2 us)
Async XLA Ops:
  7.2 146.7 %all-gather.4.cloned.1.call-start = ((), (), s32[]{:S(2)}) async-start(), calls=%async_computation.20 | async-start | bytes 15138816 | tf_op jit(solution)/shard_map/all_gather | solution.py:247
  16.1 118.5 %copy-start.123 = (s32[512]{0:T(512)}, s32[512]{0:T(512)S(1)}, u32[]{:S(2)}) copy-start(s32[512]{0:T(512)S(1)} %get-tuple-element.353) | copy-start | bytes 6148
  19.0 15.4 %all-to-all-start.4 = ((f32[32,1,357]{2,1,0:T(1,128)}), f32[32,1,357]{2,1,0:T(1,128)S(1)}, u32[]{:S(2)}, u32[]{:S(2)}) async-start(f32[32,1,357]{2,1,0:T(1,128)} %all_to_all.105), calls=%async_computation.4 | async-start | bytes 98304 | tf_op jit(solution)/shard_map/all_to_all | solution.py:109
  42.5 92.1 %all-to-all-start.5 = ((bf16[32,32,1024]{2,1,0:T(8,128)(2,1)}), bf16[32,32,1024]{2,1,0:T(8,128)(2,1)}, u32[]{:S(2)}, u32[]{:S(2)}) async-start(bf16[32,32,1024]{2,1,0:T(8,128)(2,1)} %bitcast.320), calls=%async_computation.5 | async-start | bytes 4194304 | tf_op jit(solution)/shard_map/all_to_all | solution.py:109
  46.6 157.7 %all-gather.6.cloned.1.call-start = ((), (), s32[]{:S(2)}) async-start(), calls=%async_computation.21 | async-start | bytes 7962624 | tf_op jit(solution)/shard_map/all_gather | solution.py:248
  47.7 263.0 %all-gather.8.cloned.1.call-start = ((), (), s32[]{:S(2)}) async-start(), calls=%async_computation.22 | async-start | bytes 6488064 | tf_op jit(solution)/shard_map/all_gather | solution.py:345
  49.4 130.7 %copy-start.48 = (f32[512,32]{0,1:T(8,128)}, f32[512,32]{0,1:T(8,128)S(1)}, u32[]{:S(2)}) copy-start(f32[512,32]{0,1:T(8,128)S(1)} %get-tuple-element.361) | copy-start | bytes 196612
  49.4 130.7 %copy-start.50 = (f32[512,32]{0,1:T(8,128)}, f32[512,32]{0,1:T(8,128)S(1)}, u32[]{:S(2)}) copy-start(f32[512,32]{0,1:T(8,128)S(1)} %get-tuple-element.362) | copy-start | bytes 196612
  49.5 130.1 %copy-start.69 = (f32[96,32]{0,1:T(8,128)}, f32[96,32]{0,1:T(8,128)S(1)}, u32[]{:S(2)}) copy-start(f32[96,32]{0,1:T(8,128)S(1)} %get-tuple-element.380) | copy-start | bytes 36868
  49.5 130.1 %copy-start.71 = (f32[96,32]{0,1:T(8,128)}, f32[96,32]{0,1:T(8,128)S(1)}, u32[]{:S(2)}) copy-start(f32[96,32]{0,1:T(8,128)S(1)} %get-tuple-element.381) | copy-start | bytes 36868
  49.5 130.0 %copy-start.107 = (f32[64]{0:T(128)}, f32[64]{0:T(128)S(1)}, u32[]{:S(2)}) copy-start(f32[64]{0:T(128)S(1)} %get-tuple-element.357) | copy-start | bytes 772
  49.5 130.2 %copy-start.109 = (f32[64]{0:T(128)}, f32[64]{0:T(128)S(1)}, u32[]{:S(2)}) copy-start(f32[64]{0:T(128)S(1)} %get-tuple-element.358) | copy-start | bytes 772
  52.1 135.2 %copy-start.87 = (f32[1024]{0:T(1024)}, f32[1024]{0:T(1024)S(1)}, u32[]{:S(2)}) copy-start(f32[1024]{0:T(1024)S(1)} %mul.1156) | copy-start | bytes 12292
  52.2 120.7 %copy-start.85 = (f32[1024]{0:T(1024)}, f32[1024]{0:T(1024)S(1)}, u32[]{:S(2)}) copy-start(f32[1024]{0:T(1024)S(1)} %mul.1121) | copy-start | bytes 12292
  52.3 114.4 %copy-start.90 = (f32[1024]{0:T(1024)}, f32[1024]{0:T(1024)S(1)}, u32[]{:S(2)}) copy-start(f32[1024]{0:T(1024)S(1)} %mul.1114) | copy-start | bytes 12292
  188.1 19.0 %collective-permute-start.2 = (bf16[96,1024]{1,0:T(8,128)(2,1)S(1)}, bf16[96,1024]{1,0:T(8,128)(2,1)S(1)}, u32[]{:S(2)}, u32[]{:S(2)}) collective-permute-start(bf16[96,1024]{1,0:T(8,128)(2,1)S(1)} %multiply_convert_fusion.10), channel_id=1, source_target_pairs={{0,3},{1,0},{2,1},{3,2},{4,7},{5,4},{6,5},{7,6},{8,11},{9,8},{10,9... | collective-permute-start | bytes 589832 | tf_op jit(solution)/shard_map/ppermute | solution.py:119
  189.1 18.1 %collective-permute-start.1 = (bf16[96,1024]{1,0:T(8,128)(2,1)S(1)}, bf16[96,1024]{1,0:T(8,128)(2,1)}, u32[]{:S(2)}, u32[]{:S(2)}) collective-permute-start(bf16[96,1024]{1,0:T(8,128)(2,1)S(1)} %multiply_convert_fusion.10), channel_id=1, source_target_pairs={{0,2},{1,3},{2,0},{3,1},{4,6},{5,7},{6,4},{7,5},{8,10},{9,11},{10,... | collective-permute-start | bytes 589832 | tf_op jit(solution)/shard_map/ppermute | solution.py:119
  189.1 18.1 %collective-permute-start = (bf16[96,1024]{1,0:T(8,128)(2,1)S(1)}, bf16[96,1024]{1,0:T(8,128)(2,1)}, u32[]{:S(2)}, u32[]{:S(2)}) collective-permute-start(bf16[96,1024]{1,0:T(8,128)(2,1)S(1)} %multiply_convert_fusion.10), channel_id=1, source_target_pairs={{0,1},{1,2},{2,3},{3,0},{4,5},{5,6},{6,7},{7,4},{8,9},{9,10},{10,1... | collective-permute-start | bytes 589832 | tf_op jit(solution)/shard_map/ppermute | solution.py:119
  216.7 8.9 collective-permute-start.3
  220.0 10.9 collective-permute-start.5
  220.0 17.6 %collective-permute-start.4 = (bf16[96,1024]{1,0:T(8,128)(2,1)S(1)}, bf16[96,1024]{1,0:T(8,128)(2,1)}, u32[]{:S(2)}, u32[]{:S(2)}) collective-permute-start(bf16[96,1024]{1,0:T(8,128)(2,1)S(1)} %get-tuple-element.343), channel_id=1, source_target_pairs={{0,2},{1,3},{2,0},{3,1},{4,6},{5,7},{6,4},{7,5},{8,10},{9,11},{10,... | collective-permute-start | bytes 589832 | tf_op jit(solution)/shard_map/ppermute | solution.py:119
  364.7 10.4 all-to-all-start.7
  367.9 106.7 %reduce-scatter.4.cloned.1.call-start = ((), (), s32[]{:S(2)}) async-start(), calls=%async_computation.23 | async-start | bytes 7077888 | tf_op jit(solution)/shard_map/reduce_scatter | solution.py:377
  411.5 310.6 %reduce-scatter.6.cloned.1.call-start = ((), (), s32[]{:S(2)}) async-start(), calls=%async_computation.24 | async-start | bytes 16515072 | tf_op jit(solution)/shard_map/reduce_scatter | solution.py:486
  476.5 8.9 collective-permute-start.6
  479.8 10.9 collective-permute-start.8
  479.8 17.2 %collective-permute-start.7 = (bf16[96,1024]{1,0:T(8,128)(2,1)}, bf16[96,1024]{1,0:T(8,128)(2,1)}, u32[]{:S(2)}, u32[]{:S(2)}) collective-permute-start(bf16[96,1024]{1,0:T(8,128)(2,1)} %get-tuple-element.340), channel_id=1, source_target_pairs={{0,2},{1,3},{2,0},{3,1},{4,6},{5,7},{6,4},{7,5},{8,10},{9,11},{10,... | collective-permute-start | bytes 589832 | tf_op jit(solution)/shard_map/ppermute | solution.py:119
  500.8 8.1 collective-permute-start.11
  503.4 14.9 %collective-permute-start.10 = (bf16[96,1024]{1,0:T(8,128)(2,1)S(1)}, bf16[96,1024]{1,0:T(8,128)(2,1)S(1)}, u32[]{:S(2)}, u32[]{:S(2)}) collective-permute-start(bf16[96,1024]{1,0:T(8,128)(2,1)S(1)} %fusion.165), channel_id=1, source_target_pairs={{0,2},{1,3},{2,0},{3,1},{4,6},{5,7},{6,4},{7,5},{8,10},{9,11},{10,... | collective-permute-start | bytes 589832 | tf_op jit(solution)/shard_map/ppermute | solution.py:119
  503.5 14.9 %collective-permute-start.9 = (bf16[96,1024]{1,0:T(8,128)(2,1)S(1)}, bf16[96,1024]{1,0:T(8,128)(2,1)S(1)}, u32[]{:S(2)}, u32[]{:S(2)}) collective-permute-start(bf16[96,1024]{1,0:T(8,128)(2,1)S(1)} %fusion.165), channel_id=1, source_target_pairs={{0,1},{1,2},{2,3},{3,0},{4,5},{5,6},{6,7},{7,4},{8,9},{9,10},{10,1... | collective-permute-start | bytes 589832 | tf_op jit(solution)/shard_map/ppermute | solution.py:119
  525.3 6.6 collective-permute-start.12
  526.5 13.9 %collective-permute-start.14 = (bf16[96,1024]{1,0:T(8,128)(2,1)S(1)}, bf16[96,1024]{1,0:T(8,128)(2,1)S(1)}, u32[]{:S(2)}, u32[]{:S(2)}) collective-permute-start(bf16[96,1024]{1,0:T(8,128)(2,1)S(1)} %get-tuple-element.336), channel_id=1, source_target_pairs={{0,1},{1,2},{2,3},{3,0},{4,5},{5,6},{6,7},{7,4},{8,9},{9,10},{10,1... | collective-permute-start | bytes 589832 | tf_op jit(solution)/shard_map/ppermute | solution.py:119
  527.5 18.1 %collective-permute-start.13 = (bf16[96,1024]{1,0:T(8,128)(2,1)S(1)}, bf16[96,1024]{1,0:T(8,128)(2,1)S(1)}, u32[]{:S(2)}, u32[]{:S(2)}) collective-permute-start(bf16[96,1024]{1,0:T(8,128)(2,1)S(1)} %get-tuple-element.337), channel_id=1, source_target_pairs={{0,2},{1,3},{2,0},{3,1},{4,6},{5,7},{6,4},{7,5},{8,10},{9,11},{10,... | collective-permute-start | bytes 589832 | tf_op jit(solution)/shard_map/ppermute | solution.py:119
  615.6 10.0 all-to-all-start.8
  625.6 49.9 %all-to-all-start.9 = ((bf16[32,32,1024]{2,1,0:T(8,128)(2,1)}), bf16[32,32,1024]{2,1,0:T(8,128)(2,1)S(1)}, u32[]{:S(2)}, u32[]{:S(2)}) async-start(bf16[32,32,1024]{2,1,0:T(8,128)(2,1)} %bitcast.91), calls=%async_computation.12 | async-start | bytes 4194304 | tf_op jit(solution)/shard_map/all_to_all | solution.py:109
  628.3 163.7 %reduce-scatter.8.cloned.1.call-start = ((), (), s32[]{:S(2)}) async-start(), calls=%async_computation.25 | async-start | bytes 7962624 | tf_op jit(solution)/shard_map/reduce_scatter | solution.py:482
  724.5 71.2 %collective-permute-start.15 = (bf16[7,32,1024]{2,1,0:T(8,128)(2,1)}, bf16[7,32,1024]{2,1,0:T(8,128)(2,1)}, u32[]{:S(2)}, u32[]{:S(2)}) collective-permute-start(bf16[7,32,1024]{2,1,0:T(8,128)(2,1)} %get-tuple-element.327), channel_id=1, source_target_pairs={{0,3},{1,0},{2,1},{3,2},{4,7},{5,4},{6,5},{7,6},{8,11},{9,8},{10,9... | collective-permute-start | bytes 1376264 | tf_op jit(solution)/shard_map/ppermute | solution.py:119
  727.8 67.8 %collective-permute-start.17 = (bf16[7,32,1024]{2,1,0:T(8,128)(2,1)}, bf16[7,32,1024]{2,1,0:T(8,128)(2,1)}, u32[]{:S(2)}, u32[]{:S(2)}) collective-permute-start(bf16[7,32,1024]{2,1,0:T(8,128)(2,1)} %get-tuple-element.328), channel_id=1, source_target_pairs={{0,1},{1,2},{2,3},{3,0},{4,5},{5,6},{6,7},{7,4},{8,9},{9,10},{10,1... | collective-permute-start | bytes 1376264 | tf_op jit(solution)/shard_map/ppermute | solution.py:119
  727.8 67.8 %collective-permute-start.16 = (bf16[7,32,1024]{2,1,0:T(8,128)(2,1)}, bf16[7,32,1024]{2,1,0:T(8,128)(2,1)}, u32[]{:S(2)}, u32[]{:S(2)}) collective-permute-start(bf16[7,32,1024]{2,1,0:T(8,128)(2,1)} %get-tuple-element.329), channel_id=1, source_target_pairs={{0,2},{1,3},{2,0},{3,1},{4,6},{5,7},{6,4},{7,5},{8,10},{9,11},{10,... | collective-permute-start | bytes 1376264 | tf_op jit(solution)/shard_map/ppermute | solution.py:119
  802.8 11.7 %all-to-all-start.10 = ((f32[32,1,31]{2,1,0:T(1,128)}), f32[32,1,31]{2,1,0:T(1,128)S(1)}, u32[]{:S(2)}, u32[]{:S(2)}) async-start(f32[32,1,31]{2,1,0:T(1,128)} %broadcast_in_dim.247), calls=%async_computation.13 | async-start | bytes 32768 | tf_op jit(solution)/shard_map/all_to_all | solution.py:114
  814.5 57.6 %all-to-all-start.13 = ((bf16[4,2,144,1024]{3,2,1,0:T(8,128)(2,1)}), bf16[4,2,144,1024]{3,2,1,0:T(8,128)(2,1)S(1)}, u32[]{:S(2)}, u32[]{:S(2)}) async-start(bf16[4,2,144,1024]{3,2,1,0:T(8,128)(2,1)} %fusion.26), calls=%async_computation.16 | async-start | bytes 4718592 | tf_op jit(solution)/shard_map/all_to_all | solution.py:545
  872.1 18.2 %all-to-all-start.11 = ((bf16[4,2,32,1024]{3,2,1,0:T(8,128)(2,1)}), bf16[4,2,32,1024]{3,2,1,0:T(8,128)(2,1)}, u32[]{:S(2)}, u32[]{:S(2)}) async-start(bf16[4,2,32,1024]{3,2,1,0:T(8,128)(2,1)} %bitcast.329), calls=%async_computation.14 | async-start | bytes 1048576 | tf_op jit(solution)/shard_map/all_to_all | solution.py:561
  893.0 80.8 %all-to-all-start.12 = ((bf16[8,128,1024]{2,1,0:T(8,128)(2,1)}), bf16[8,128,1024]{2,1,0:T(8,128)(2,1)S(1)}, u32[]{:S(2)}, u32[]{:S(2)}) async-start(bf16[8,128,1024]{2,1,0:T(8,128)(2,1)} %bitcast.99), calls=%async_computation.15 | async-start | bytes 4194304 | tf_op jit(solution)/shard_map/all_to_all | solution.py:573
  896.6 77.2 %all-reduce.14.cloned.1.call-start = ((), (), s32[]{:S(2)}) async-start(), calls=%async_computation.26 | async-start | bytes 4194304 | tf_op jit(solution)/shard_map/psum | solution.py:556
  1032.4 30.3 %all-to-all-start.14 = ((bf16[8,128,1024]{2,1,0:T(8,128)(2,1)}), bf16[8,128,1024]{2,1,0:T(8,128)(2,1)S(1)}, u32[]{:S(2)}, u32[]{:S(2)}) async-start(bf16[8,128,1024]{2,1,0:T(8,128)(2,1)} %bitcast.323), calls=%async_computation.17 | async-start | bytes 4194304 | tf_op jit(solution)/shard_map/all_to_all | solution.py:579
  1036.2 32.8 %collective-permute-start.18 = (bf16[1024,1024]{1,0:T(8,128)(2,1)}, bf16[1024,1024]{1,0:T(8,128)(2,1)}, u32[]{:S(2)}, u32[]{:S(2)}) collective-permute-start(bf16[1024,1024]{1,0:T(8,128)(2,1)} %copy-done.131), channel_id=1, source_target_pairs={{0,4},{4,0},{1,5},{5,1},{2,6},{6,2},{3,7},{7,3},{8,12},{12,8},{9,1... | collective-permute-start | bytes 6291464 | tf_op jit(solution)/shard_map/ppermute | solution.py:578
  1063.6 16.3 %all-to-all-start.15 = ((bf16[4,2,32,1024]{3,2,1,0:T(8,128)(2,1)}), bf16[4,2,32,1024]{3,2,1,0:T(8,128)(2,1)S(1)}, u32[]{:S(2)}, u32[]{:S(2)}) async-start(bf16[4,2,32,1024]{3,2,1,0:T(8,128)(2,1)} %copy.141), calls=%async_computation.18 | async-start | bytes 1048576 | tf_op jit(solution)/shard_map/all_to_all | solution.py:564
  1079.9 30.1 %all-to-all-start.16 = ((bf16[4,144,1024]{2,1,0:T(8,128)(2,1)}), bf16[4,144,1024]{2,1,0:T(8,128)(2,1)}, u32[]{:S(2)}, u32[]{:S(2)}) async-start(bf16[4,144,1024]{2,1,0:T(8,128)(2,1)} %bitcast.114), calls=%async_computation.19 | async-start | bytes 2359296 | tf_op jit(solution)/shard_map/all_to_all | solution.py:585
  (153 other events, 1609.7 us)
Sparse Core Ops, SparseCore 0:
  11.6 142.2 all-gather.3
  156.3 47.9 all-gather.5
  241.9 68.6 all-gather.7
  411.6 62.9 reduce-scatter.3
  598.6 123.4 reduce-scatter.5
  726.5 65.5 reduce-scatter.7
  904.4 69.3 all-reduce.13

commit v3 on v2

--- a/solution.py
+++ b/solution.py
@@ -3,6 +3,8 @@
 import jax
 import jax.numpy as jnp
 from jax import lax
+from jax.experimental import pallas as pl
+from jax.experimental.pallas import tpu as pltpu
 from jax.sharding import Mesh
 from jax.sharding import PartitionSpec as P
 
@@ -119,6 +121,36 @@
     return lax.ppermute(values, "vocab", [(i, (i + step) % count) for i in range(count)])
 
 
+def other_core(values):
+    return lax.ppermute(values, "core", [(0, 1), (1, 0)])
+
+
+def pair_sum(halves, core):
+    given = lax.dynamic_index_in_dim(halves, 1 - core, 0, keepdims=False)
+    kept = lax.dynamic_index_in_dim(halves, core, 0, keepdims=False)
+    total = kept.astype(jnp.float32) + other_core(given).astype(jnp.float32)
+    return total.astype(jnp.bfloat16)
+
+
+def chip_sum(blocks):
+    blocks = lax.all_to_all(blocks, "chip", 0, 0, tiled=True)
+    return jnp.sum(blocks.astype(jnp.float32), axis=0)
+
+
+def group_sum(values, core):
+    rows = values.shape[0] // 2
+    chips = lax.axis_size("chip")
+    half = pair_sum(values.reshape(2, rows, -1), core).reshape(chips, rows // chips, -1)
+    part = chip_sum(half).astype(jnp.bfloat16)
+    half = lax.all_to_all(
+        jnp.broadcast_to(part[None], (chips,) + part.shape), "chip", 0, 0, tiled=True
+    ).reshape(rows, -1)
+    other = other_core(half)
+    first = jnp.where(core == 0, half, other)
+    second = jnp.where(core == 0, other, half)
+    return jnp.concatenate([first, second], axis=0)
+
+
 def member_gather(values):
     return jnp.concatenate(
         [values] + [turned(values, step) for step in range(1, lax.axis_size("vocab"))], axis=0
@@ -174,20 +206,85 @@
     )
 
 
+def rest_kernel(
+    gram_ref, rest_ref, gram_scratch, change_scratch, rest_scratch, grams, change_b, rest_b
+):
+    lead = leading_coefficient
+    size = gram_ref.shape[0]
+    tile = 256
+
+    def dot(left, right):
+        return jnp.dot(left, right, preferred_element_type=jnp.float32)
+
+    @pl.loop(0, size // tile)
+    def _(step):
+        rows = pl.ds(pl.multiple_of(step * tile, tile), tile)
+        gram_scratch[rows, :] = gram_ref[rows, :]
+        grams[0, rows, :] = gram_ref[rows, :].astype(jnp.bfloat16)
+
+    power = 1.0
+    for turn in range(NS_ITERS):
+        now, later = turn % 2, (turn + 1) % 2
+
+        @pl.loop(0, size // tile)
+        def _(step):
+            rows = pl.ds(pl.multiple_of(step * tile, tile), tile)
+            change = coef_second * gram_scratch[rows, :] + coef_third * dot(
+                grams[now, rows, :], grams[now]
+            )
+            change_scratch[rows, :] = change
+            change_b[rows, :] = change.astype(jnp.bfloat16)
+
+        @pl.loop(0, size // tile)
+        def _(step):
+            rows = pl.ds(pl.multiple_of(step * tile, tile), tile)
+            if turn == 0:
+                rest = change_scratch[rows, :]
+            else:
+                rest = (
+                    lead * rest_scratch[rows, :]
+                    + power * change_scratch[rows, :]
+                    + dot(rest_b[rows, :], change_b[...])
+                )
+            if turn + 1 < NS_ITERS:
+                rest_scratch[rows, :] = rest
+                rest_b[rows, :] = rest.astype(jnp.bfloat16)
+                mixed = dot(change_b[rows, :], grams[now])
+                gram = (
+                    lead * lead * gram_scratch[rows, :]
+                    + 2.0 * lead * mixed
+                    + dot(mixed.astype(jnp.bfloat16), change_b[...])
+                )
+                gram_scratch[rows, :] = gram
+                grams[later, rows, :] = gram.astype(jnp.bfloat16)
+            else:
+                rest_ref[rows, :] = rest.astype(jnp.bfloat16)
+
+        power = power * lead
+
+
 def ortho_rest(gram):
-    lead = leading_coefficient
-    power, rest = 1.0, None
-    for turn in range(NS_ITERS):
-        change = coef_second * gram + coef_third * square_product(gram, gram)
-        if turn + 1 < NS_ITERS:
-            mixed = square_product(change, gram)
-            gram = lead * lead * gram + 2.0 * lead * mixed + square_product(mixed, change)
-        if rest is None:
-            rest = change
-        else:
-            rest = lead * rest + power * change + square_product(rest, change)
-        power = power * lead
-    return power, rest
+    size = gram.shape[0]
+    wide = pltpu.VMEM((size, size), jnp.float32)
+    narrow = pltpu.VMEM((size, size), jnp.bfloat16)
+    return pl.pallas_call(
+        rest_kernel,
+        out_shape=jax.ShapeDtypeStruct((size, size), jnp.bfloat16),
+        in_specs=[pl.BlockSpec(memory_space=pltpu.VMEM)],
+        out_specs=pl.BlockSpec(memory_space=pltpu.VMEM),
+        scratch_shapes=[
+            wide,
+            wide,
+            wide,
+            pltpu.VMEM((2, size, size), jnp.bfloat16),
+            narrow,
+            narrow,
+        ],
+        compiler_params=pltpu.CompilerParams(vmem_limit_bytes=44 * 1024 * 1024),
+        cost_estimate=pl.CostEstimate(
+            flops=18 * size**3, bytes_accessed=6 * size * size, transcendentals=0
+        ),
+    )(gram)
 
 
 def body(
@@ -217,6 +314,7 @@
     groups_per = HEADS // KV
     scale = HD ** (-0.5)
 
+    core = lax.axis_index("core")
     devices = lax.axis_size(ALL)
     device = lax.axis_index(ALL)
     groups = devices // members
@@ -374,9 +472,13 @@
     )
     grad_answers = jnp.dot(grad_logits, table_b, preferred_element_type=jnp.float32)
     grad_table = outer(grad_logits, response_tokens)
-    grad_answer_group = lax.psum_scatter(
-        grad_answers.astype(jnp.bfloat16), DP, scatter_dimension=0, tiled=True
-    )
+    grad_answer_pair = pair_sum(
+        grad_answers.astype(jnp.bfloat16)
+        .reshape(groups // 2, 2, members * RESP, D)
+        .transpose(1, 0, 2, 3),
+        core,
+    )
+    grad_answer_group = chip_sum(grad_answer_pair).astype(jnp.bfloat16)
     grad_final = member_scatter(grad_answer_group.reshape(members, RESP, D), member)
     grad_hidden3, grad_gain3 = norm_back(hidden3, gains[3], grad_final)
     grad_ffn_out = member_gather(grad_hidden3.astype(jnp.bfloat16))
@@ -483,10 +585,34 @@
     share_wide = share_wide_b.astype(jnp.float32)
     squares, square_rows = square_master.shape[0], square_master.shape[1]
     wides, wide_rows = wide_master.shape[0], wide_master.shape[1]
+    wide_early = jnp.stack([wide_moment.astype(jnp.bfloat16), share_wide_b], axis=1)
+    wide_early = jnp.pad(wide_early, ((0, members - wides), (0, 0), (0, 0), (0, 0)))
+    wide_early = lax.all_to_all(wide_early, "vocab", 0, 0, tiled=True)
+    per_member = -(-squares // members)
+    group_rows = members * square_rows
+
+    def by_member(values):
+        values = jnp.pad(values, ((0, per_member * members - squares), (0, 0), (0, 0)))
+        return values.reshape(per_member, members, -1, D).transpose(1, 0, 2, 3)
+
+    square_moment_job = lax.all_to_all(
+        by_member(square_moment.astype(jnp.bfloat16)), "vocab", 0, 0, tiled=True
+    )
+    square_moment_job = square_moment_job.transpose(1, 0, 2, 3).reshape(per_member, group_rows, D)
+    grad_square, share_wide_b = lax.optimization_barrier((grad_square, share_wide_b))
     group_square = lax.psum_scatter(grad_square, DP, scatter_dimension=1, tiled=True)
-    share_square = member_scatter(
-        group_square.reshape(squares, members, square_rows, D).transpose(1, 0, 2, 3), member
-    )
+    group_square, wide_early, square_moment_job = lax.optimization_barrier(
+        (group_square, wide_early, square_moment_job)
+    )
+    square_grad_job = member_scatter(by_member(group_square), member)
+
+    def from_members(values):
+        values = values.reshape(per_member, members, square_rows, D).transpose(1, 0, 2, 3)
+        values = lax.all_to_all(values.astype(jnp.bfloat16), "vocab", 0, 0, tiled=True)
+        values = values.transpose(1, 0, 2, 3).reshape(per_member * members, square_rows, D)
+        return values[:squares].astype(jnp.float32)
+
+    share_square = from_members(square_grad_job)
     width = vector_master.shape[1]
     vector_notes = grad_vector.reshape(-1, devices, width).transpose(1, 0, 2).reshape(devices, -1)
     vector_notes = jnp.concatenate(
@@ -499,12 +625,12 @@
     vector_notes = jnp.sum(exchanged(vector_notes), axis=0)
     share_vector = vector_notes[: vector_master.size].reshape(vector_master.shape)
     gains_total = vector_notes[vector_master.size :].reshape(grad_head_gains.shape)
-    own_squares = (
-        jnp.sum(share_square * share_square)
-        + jnp.sum(share_wide * share_wide)
-        + jnp.sum(share_vector * share_vector)
-        + jnp.sum(share_table * share_table)
-    )
+
+    def job_sums(values):
+        sums = jnp.sum(values, axis=(1, 2))[:, None]
+        sums = jnp.where(jnp.arange(members)[None, :] == member, sums, 0.0)
+        return sums.reshape(-1)[:squares]
+
     moment_squares = jnp.concatenate(
         [
             jnp.sum(square_moment * square_moment, axis=(1, 2)),
@@ -513,17 +639,22 @@
     )
     moment_cross = jnp.concatenate(
         [
-            jnp.sum(square_moment * share_square, axis=(1, 2)),
+            job_sums(square_moment_job.astype(jnp.float32) * square_grad_job),
             jnp.sum(wide_moment * share_wide, axis=(1, 2)),
         ]
     )
     grad_squares = jnp.concatenate(
         [
-            jnp.sum(share_square * share_square, axis=(1, 2)),
+            job_sums(square_grad_job * square_grad_job),
             jnp.sum(share_wide * share_wide, axis=(1, 2)),
         ]
     )
     moment_stats = jnp.stack([moment_squares, moment_cross, grad_squares])
+    own_squares = (
+        jnp.sum(grad_squares)
+        + jnp.sum(share_vector * share_vector)
+        + jnp.sum(share_table * share_table)
+    )
     sums = jnp.concatenate([moment_stats.reshape(-1), own_squares[None]])
     sums = jnp.sum(spread(sums), axis=0)
     stats_total = sums[:-1].reshape(moment_stats.shape)
@@ -538,13 +669,12 @@
     )
     ortho_square = square_moment_new / (moment_norm[:7][:, None, None] + ortho_epsilon)
     ortho_wide = wide_moment_new / (moment_norm[7:][:, None, None] + ortho_epsilon)
-    core = lax.axis_index("core")
-    per_member = -(-squares // members)
-    wide_early = jnp.stack([wide_moment.astype(jnp.bfloat16), share_wide_b], axis=1)
-    wide_early = jnp.pad(wide_early, ((0, members - wides), (0, 0), (0, 0), (0, 0)))
-    wide_early = lax.all_to_all(wide_early, "vocab", 0, 0, tiled=True).astype(jnp.float32)
+    table_step, table_first_new, table_second_new = adam_step(
+        table_master, table_first, table_second, share_table, factor, adam_count
+    )
     wide_inverse = 1.0 / (moment_norm[squares:] + ortho_epsilon)
     wide_inverse = jnp.pad(wide_inverse, (0, members - wides))[member]
+    wide_early = wide_early.astype(jnp.float32)
     wide_job = (
         (
             (muon_decay * wide_inverse) * wide_early[:, 0]
@@ -553,46 +683,40 @@
         .reshape(members * wide_rows, D)
         .astype(jnp.bfloat16)
     )
-    wide_gram = lax.psum(outer(wide_job, wide_job).astype(jnp.bfloat16), DP)
-
-    def to_members(values):
-        values = jnp.pad(values, ((0, per_member * members - squares), (0, 0), (0, 0)))
-        values = values.reshape(per_member, members, square_rows, D).transpose(1, 0, 2, 3)
-        return lax.all_to_all(values, "vocab", 0, 0, tiled=True)
-
-    def from_members(values):
-        values = lax.all_to_all(values, "vocab", 0, 0, tiled=True).transpose(1, 0, 2, 3)
-        return values.reshape(per_member * members, square_rows, D)[:squares]
-
-    group_rows = members * square_rows
-    square_part = to_members(ortho_square.astype(jnp.bfloat16)).transpose(1, 0, 2, 3)
-    square_part = square_part.reshape(per_member, 1, group_rows, D)
+    wide_gram = group_sum(outer(wide_job, wide_job).astype(jnp.bfloat16), core)
+    square_inverse = 1.0 / (moment_norm[:squares] + ortho_epsilon)
+    square_inverse = jnp.pad(square_inverse, (0, per_member * members - squares))
+    square_inverse = square_inverse.reshape(per_member, members)[:, member][:, None, None]
+    square_part = (muon_decay * square_inverse) * square_moment_job.astype(jnp.float32) + (
+        (1.0 - muon_decay) * factor * square_inverse
+    ) * square_grad_job
+    square_part = square_part.astype(jnp.bfloat16).reshape(per_member, 1, group_rows, D)
     square_part = jnp.pad(
         square_part, ((0, groups // 2 - per_member), (1, 0), (0, 0), (0, 0))
     ).reshape(groups * group_rows, D)
     square_job = lax.all_to_all(square_part, DP, 0, 0, tiled=True)
     square_gram = outer(square_job, square_job)
     gram = jnp.where(core == 0, wide_gram.astype(jnp.float32), square_gram)
-    power, rest = ortho_rest(gram)
-    rest_b = rest.astype(jnp.bfloat16)
-    wide_rest = jnp.where(core == 0, rest_b, lax.ppermute(rest_b, "core", [(0, 1), (1, 0)]))
+    gram, table_step, table_first_new, table_second_new = lax.optimization_barrier(
+        (gram, table_step, table_first_new, table_second_new)
+    )
+    rest_b = ortho_rest(gram)
+    power = leading_coefficient**NS_ITERS
+    wide_rest = jnp.where(core == 0, rest_b, other_core(rest_b))
     back_square = lax.all_to_all(
         square_product(square_job, rest_b).astype(jnp.bfloat16), DP, 0, 0, tiled=True
     )
-    back_square = back_square.reshape(groups // 2, 2, members, square_rows, D)[:per_member, 1]
-    back_square = from_members(back_square.transpose(1, 0, 2, 3))
+    back_square = back_square.reshape(groups // 2, 2, group_rows, D)[:per_member, 1]
+    back_square = from_members(back_square)
     back_wide = square_product(wide_job, wide_rest).astype(jnp.bfloat16)
     back_wide = lax.all_to_all(
         back_wide.reshape(members, wide_rows, D), "vocab", 0, 0, tiled=True
     )[:wides]
     ortho_wide = power * ortho_wide + back_wide.astype(jnp.float32)
-    ortho_square = power * ortho_square + back_square.astype(jnp.float32)
+    ortho_square = power * ortho_square + back_square
     wide_scale = jnp.array([math.sqrt(FF / D), math.sqrt(FF / D), 1.0], jnp.float32)
     square_new = square_master - muon_rate * ortho_square
     wide_new = wide_master - muon_rate * wide_scale[:, None, None] * ortho_wide
-    table_step, table_first_new, table_second_new = adam_step(
-        table_master, table_first, table_second, share_table, factor, adam_count
-    )
     vector_step, vector_first_new, vector_second_new = adam_step(
         vector_master, vector_first, vector_second, share_vector, factor, adam_count
     )

time: 1140 us -> 1080 us (0.947)
  waiting for transfers between devices: 575 us -> 482 us
  matrix products: 229 us -> 185 us
  Pallas kernels: 0 us -> 25.1 us
  starting transfers between devices: 74.5 us -> 92.7 us
  blocking collectives: 10.4 us -> 27.5 us
    psum x1 -> x0, waiting for transfers between devices: 69.5 us -> none  [body(): wide_gram = lax.psum(outer(wide_job, wide_job).astype(jnp.bfloat16), DP)]
    reduce_scatter x1 -> x0, waiting for transfers between devices: 63 us -> none  [body(): lax.psum_scatter(grad_answers.astype(jnp.bfloat16), DP, scatter_dimension...]
    reduce_scatter x1, waiting for transfers between devices: 56.2 us -> 0.01 us  [body(): lax.psum_scatter(grad_wide, DP, scatter_dimension=1, tiled=True)]
    dot_general x11 -> x2, matrix products: 58.4 us -> 8.97 us  [square_product(): jnp.dot(left.astype(jnp.bfloat16), right.astype(jnp.bfloat16), preferred_...]
    all_to_all x3 -> x6, waiting for transfers between devices: 63.9 us -> 104 us  [the longest x1 36.6 us: chip_sum(): blocks = lax.all_to_all(blocks, 'chip', 0, 0, tiled=True)]
    ppermute x18, waiting for transfers between devices: 59.7 us -> 93.4 us  [turned(): lax.ppermute(values, 'vocab', [(i, (i + step) % count) for i in range(cou...]
    pallas_call x0 -> x1, Pallas kernels: none -> 25.1 us  [ortho_rest(): pl.pallas_call(rest_kernel, out_shape=jax.ShapeDtypeStruct((size, size),...]
    all_to_all x1, waiting for transfers between devices: 0.01 us -> 20 us  [body(): lax.all_to_all(back_wide.reshape(members, wide_rows, D), 'vocab', 0, 0, t...]
  transfers between devices with their start and end apart: 38 -> 42, of which waited for: 27 -> 30; matrix products, arithmetic and copies ran while one was open for 17% -> 22% of each run, Pallas kernels for 0% -> 0%
where the time goes in v3:
time: 1080 us; the launch traced here: 1060 us
  waiting for transfers between devices  482 us (45%)
  matrix products  185 us (17%)
  other arithmetic  135 us (12%)
  starting transfers between devices  92.7 us (9%)
  local copies, waits for them, and re-layouts  85.1 us (8%)
  between operations  28.3 us (3%)
  blocking collectives  27.5 us (3%)
  Pallas kernels  25.1 us (2%)
    all_to_all x4, waiting for transfers between devices, exchanged(): return lax.all_to_all(rows, ALL, 0, 0, tiled=True)  133 us
    ppermute x18, waiting for transfers between devices, turned(): lax.ppermute(values, 'vocab', [(i, (i + step) % count) for i in range(cou...  93.4 us
    all_gather x1, waiting for transfers between devices, body(): response_tokens = lax.all_gather(final_b, ALL, axis=0, tiled=True)  66.1 us
    dot_general x12, matrix products, outer(): lax.dot_general(grads, inputs, (((0,), (0,)), ((), ())), preferred_elemen...  61.6 us
    dot_general x8, matrix products, dense(): lax.dot_general(inputs, weight, (((1,), (1,)), ((), ())), preferred_eleme...  41.3 us
    all_to_all x1, waiting for transfers between devices, chip_sum(): blocks = lax.all_to_all(blocks, 'chip', 0, 0, tiled=True)  36.6 us
    all_to_all x1, waiting for transfers between devices, body(): wide_early = lax.all_to_all(wide_early, 'vocab', 0, 0, tiled=True)  30.5 us
    dot_general x6, matrix products, back_dense(): return jnp.dot(grads, weight, preferred_element_type=jnp.float32)  29.1 us
  transfers between devices with their start and end apart: 42, of which 30 were waited for; matrix products, arithmetic and copies ran while one was open for 22% of the time, Pallas kernels for 0%

profile of v3, /device:TPU:0, one launch (start us, length us, event | category | flops | bytes accessed | tf_op | source)
XLA Modules:
  0.0 1061.1 jit_solution(1086083663240914059)
XLA Ops:
  19.0 7.3 all-to-all-start.4
  26.3 6.0 convert_element_type.350
  34.5 8.1 fusion.50
  52.4 82.3 %all-to-all-done.5 = bf16[32,32,1024]{2,1,0:T(8,128)(2,1)} async-done(((bf16[32,32,1024]{2,1,0:T(8,128)(2,1)}), bf16[32,32,1024]{2,1,0:T(8,128)(2,1)}, u32[]{:S(2)}, u32[]{:S(2)}) %all-to-all-start.5) | async-done | bytes 2097184 | tf_op jit(solution)/shard_map/all_to_all | solution.py:111
  141.2 12.7 %all-gather.4.cloned.1.call-done = bf16[7,1024,1024]{2,1,0:T(8,128)(2,1)} async-done(((bf16[7,32,1024]{2,1,0:T(8,128)(2,1)}), bf16[7,1024,1024]{2,1,0:T(8,128)(2,1)}) %all-gather.4.cloned.1.call-update) | async-done | bytes 14680080 | tf_op jit(solution)/shard_map/all_gather | solution.py:345
  153.9 6.2 slice.341
  160.2 6.0 fusion.140
  192.3 12.0 %all-gather.6.cloned.1.call-done = bf16[3,1152,1024]{2,1,0:T(8,128)(2,1)} async-done(((bf16[3,144,1024]{2,1,0:T(8,128)(2,1)}), bf16[3,1152,1024]{2,1,0:T(8,128)(2,1)}) %all-gather.6.cloned.1.call-update) | async-done | bytes 7077904 | tf_op jit(solution)/shard_map/all_gather | solution.py:346
  225.7 12.1 %collective-permute-done.4 = bf16[96,1024]{1,0:T(8,128)(2,1)} collective-permute-done((bf16[96,1024]{1,0:T(8,128)(2,1)S(1)}, bf16[96,1024]{1,0:T(8,128)(2,1)}, u32[]{:S(2)}, u32[]{:S(2)}) %collective-permute-start.4) | collective-permute-done | bytes 196640 | tf_op jit(solution)/shard_map/ppermute | solution.py:121
  244.6 66.1 %all-gather.8.cloned.1.call-done = bf16[3072,1024]{1,0:T(8,128)(2,1)} async-done(((bf16[96,1024]{1,0:T(8,128)(2,1)}), bf16[3072,1024]{1,0:T(8,128)(2,1)}) %all-gather.8.cloned.1.call-update) | async-done | bytes 6291472 | tf_op jit(solution)/shard_map/all_gather | solution.py:443
  310.7 20.4 %fusion.158 = (f32[3072]{0:T(1024)}, f32[3072,2048]{0,1:T(8,128)}) fusion(bf16[3072,1024]{1,0:T(8,128)(2,1)} %all-gather.8.cloned.1.call-done, bf16[2048,1024]{1,0:T(8,128)(2,1)} %get-tuple-element.597), kind=kOutput, calls=%fused_computation.408 | convolution fusion | flops 12891190272 | bytes 35663872 | tf_op jit(solution)/shard_map/dot_general | solution.py:61
  332.5 12.4 %exponential_reduce_fusion = (f32[3072]{0:T(1024)}, f32[3072]{0:T(1024)}) fusion(f32[3072,2048]{0,1:T(8,128)} %get-tuple-element.400, f32[3072]{0:T(1024)} %get-tuple-element.399, s32[3072]{0:T(1024)} %fusion.108), kind=kLoop, calls=%fused_computation.31 | loop fusion | flops 31451136 | bytes 25214976 | tf_op jit(solution)/shard_map/reduce_sum | solution.py:448
  348.5 10.4 all_to_all.174
  388.7 22.9 %convolution_convert_fusion.2 = bf16[3072,1024]{1,0:T(8,128)(2,1)} fusion(bf16[2048,1024]{1,0:T(8,128)(2,1)} %get-tuple-element.597, f32[3072,2048]{0,1:T(8,128)} %get-tuple-element.400, f32[3072]{0:T(1024)} %sub.205, f32[3072]{0:T(1024)} %mul.1175, s32[3072]{0:T(1024)} %fusion.108), kind=kOutput, calls=%fused_computation.45 | convolution fusion | flops 12925796352 | bytes 35688448 | tf_op jit(solution)/shard_map/dot_general | solution.py:473
  415.5 6.0 collective-permute-done.6
  421.5 6.1 fusion.17
  427.6 4.7 all-to-all-start.8
  432.4 36.6 %all-to-all-done.8 = bf16[4,384,1024]{2,1,0:T(8,128)(2,1)} async-done(((bf16[4,384,1024]{2,1,0:T(8,128)(2,1)}), bf16[4,384,1024]{2,1,0:T(8,128)(2,1)}, u32[]{:S(2)}, u32[]{:S(2)}) %all-to-all-start.8) | async-done | bytes 3145760 | tf_op jit(solution)/shard_map/all_to_all | solution.py:136
  479.0 4.7 collective-permute-done.7
  483.7 10.9 %collective-permute-done.8 = bf16[96,1024]{1,0:T(8,128)(2,1)} collective-permute-done((bf16[96,1024]{1,0:T(8,128)(2,1)}, bf16[96,1024]{1,0:T(8,128)(2,1)}, u32[]{:S(2)}, u32[]{:S(2)}) %collective-permute-start.8) | collective-permute-done | bytes 196640 | tf_op jit(solution)/shard_map/ppermute | solution.py:121
  507.9 6.5 collective-permute-done.11
  528.0 4.9 convolution_convert_fusion.5
  533.1 6.2 collective-permute-start.13
  544.7 11.7 %collective-permute-done.14 = bf16[96,1024]{1,0:T(8,128)(2,1)S(1)} collective-permute-done((bf16[96,1024]{1,0:T(8,128)(2,1)S(1)}, bf16[96,1024]{1,0:T(8,128)(2,1)S(1)}, u32[]{:S(2)}, u32[]{:S(2)}) %collective-permute-start.14) | collective-permute-done | bytes 196640 | tf_op jit(solution)/shard_map/ppermute | solution.py:121
  581.8 7.8 multiply_reduce_fusion.2
  592.9 5.0 convolution_convert_fusion.1
  613.0 11.8 %multiply_reduce_fusion.1 = (f32[512]{0:T(512)S(1)}, f32[1024]{0:T(1024)S(1)}, f32[512,1024]{1,0:T(8,128)}) fusion(f32[512,1024]{1,0:T(8,128)} %get-tuple-element.234, f32[1024]{0:T(1024)S(1)} %copy-done.109, f32[512]{0:T(512)S(1)} %copy-done.120, bf16[3072,1024]{1,0:T(8,128)(2,1)} %bitcast.330, bf16[512,1024]{1,0:T(8,128)(2,1)} %copy-done.43, ...), kind=kOutput, calls=%fused_computation.105 | convolution fusion | flops 3233806848 | bytes 13643776 | tf_op jit(solution)/shard_map/dot_general | solution.py:73
  634.0 8.4 all-to-all-done.10
  657.2 45.6 %all-to-all-done.12 = bf16[32,32,1024]{2,1,0:T(8,128)(2,1)S(1)} async-done(((bf16[32,32,1024]{2,1,0:T(8,128)(2,1)}), bf16[32,32,1024]{2,1,0:T(8,128)(2,1)S(1)}, u32[]{:S(2)}, u32[]{:S(2)}) %all-to-all-start.12) | async-done | bytes 2097184 | tf_op jit(solution)/shard_map/all_to_all | solution.py:111
  702.8 7.0 fusion.15
  713.1 4.9 all-to-all-start.9
  718.0 24.0 %convolution_add_fusion = f32[2048,1024]{1,0:T(8,128)} fusion(f32[2048,1024]{1,0:T(8,128)} %fusion.15, bf16[3072,1024]{1,0:T(8,128)(2,1)} %all-gather.8.cloned.1.call-done, f32[3072,2048]{0,1:T(8,128)} %get-tuple-element.400, f32[3072]{0:T(1024)S(1)} %copy-done.114, f32[3072]{0:T(1024)S(1)} %copy-done.113, s32[3072]{0:T(1024)S(1)} %copy-done.97), kind=kOutput, calls=%fused_computation.49 | convolution fusion | flops 12924747776 | bytes 48271360 | tf_op jit(solution)/shard_map/dot_general | solution.py:67
  742.0 30.5 %all-to-all-done.9 = bf16[4,2,144,1024]{3,2,1,0:T(8,128)(2,1)S(1)} async-done(((bf16[4,2,144,1024]{3,2,1,0:T(8,128)(2,1)}), bf16[4,2,144,1024]{3,2,1,0:T(8,128)(2,1)S(1)}, u32[]{:S(2)}, u32[]{:S(2)}) %all-to-all-start.9) | async-done | bytes 2359328 | tf_op jit(solution)/shard_map/all_to_all | solution.py:590
  779.1 6.1 multiply_reduce_fusion
  785.3 6.8 collective-permute-done.16
  792.1 29.9 %collective-permute-done.17 = bf16[2,128,1024]{2,1,0:T(8,128)(2,1)} collective-permute-done((bf16[2,128,1024]{2,1,0:T(8,128)(2,1)}, bf16[2,128,1024]{2,1,0:T(8,128)(2,1)}, u32[]{:S(2)}, u32[]{:S(2)}) %collective-permute-start.17) | collective-permute-done | bytes 524320 | tf_op jit(solution)/shard_map/ppermute | solution.py:121
  829.5 5.9 all-to-all-start.13
  854.7 17.1 %all_to_all.175 = bf16[4,128,1024]{2,1,0:T(8,128)(2,1)S(1)} all-to-all(bf16[4,128,1024]{2,1,0:T(8,128)(2,1)S(1)} %bitcast.342), channel_id=1, replica_groups=mesh['chip'=4,'core'=2,'vocab'=4] {'chip'}, dimensions={0} | all-to-all | bytes 2097152 | tf_op jit(solution)/shard_map/all_to_all | solution.py:136
  879.5 10.1 all-to-all-done.17
  894.7 22.7 %add_multiply_fusion = (f32[2048,1024]{1,0:T(8,128)}, f32[2048,1024]{1,0:T(8,128)}, f32[2048,1024]{1,0:T(8,128)}) fusion(f32[2048,1024]{1,0:T(8,128)} %param.25, f32[]{:T(128)S(6)} %sub.217, f32[]{:T(128)S(6)} %sub.216, f32[2048,1024]{1,0:T(8,128)} %get-tuple-element.238, f32[]{:T(128)S(6)} %min.3, f32[2048,1024]{1,0:T(8,128)} %param.27, f32[2048,1024]{1,0:T(8,128)} %param.26), kind=kLoop, calls=%fused_computation.34 | loop fusion | flops 31457280 | bytes 58720268 | tf_op jit(solution)/shard_map/mul | solution.py:100
  920.9 5.2 bitcast_select_fusion.gram_ref
  926.0 25.1 %shard_map.313 = bf16[1024,1024]{1,0:T(8,128)(2,1)S(1)} custom-call(f32[1024,1024]{1,0:T(8,128)S(1)} %bitcast_select_fusion.gram_ref), custom_call_target="tpu_custom_call" | custom-call | flops 19327352832 | bytes 6291456 | tf_op jit(solution)/shard_map/pallas_call | solution.py:270
  951.1 5.3 convolution_convert_fusion.4
  962.1 25.4 %all-to-all-done.18 = bf16[8,128,1024]{2,1,0:T(8,128)(2,1)} async-done(((bf16[8,128,1024]{2,1,0:T(8,128)(2,1)}), bf16[8,128,1024]{2,1,0:T(8,128)(2,1)}, u32[]{:S(2)}, u32[]{:S(2)}) %all-to-all-start.18) | async-done | bytes 2097184 | tf_op jit(solution)/shard_map/all_to_all | solution.py:706
  993.0 9.8 all-to-all-done.14
  1010.3 8.5 all-to-all-done.19
  1028.7 20.0 %all-to-all-done.20 = bf16[4,144,1024]{2,1,0:T(8,128)(2,1)} async-done(((bf16[4,144,1024]{2,1,0:T(8,128)(2,1)}), bf16[4,144,1024]{2,1,0:T(8,128)(2,1)}, u32[]{:S(2)}, u32[]{:S(2)}) %all-to-all-start.20) | async-done | bytes 1179680 | tf_op jit(solution)/shard_map/all_to_all | solution.py:712
  1048.6 4.6 fusion.144
  (613 shorter events, 302.2 us)
Async XLA Ops:
  7.2 146.7 %all-gather.4.cloned.1.call-start = ((), (), s32[]{:S(2)}) async-start(), calls=%async_computation.23 | async-start | bytes 15138816 | tf_op jit(solution)/shard_map/all_gather | solution.py:345
  19.0 15.4 %all-to-all-start.4 = ((f32[32,1,357]{2,1,0:T(1,128)}), f32[32,1,357]{2,1,0:T(1,128)S(1)}, u32[]{:S(2)}, u32[]{:S(2)}) async-start(f32[32,1,357]{2,1,0:T(1,128)} %all_to_all.117), calls=%async_computation.4 | async-start | bytes 98304 | tf_op jit(solution)/shard_map/all_to_all | solution.py:111
  42.5 92.1 %all-to-all-start.5 = ((bf16[32,32,1024]{2,1,0:T(8,128)(2,1)}), bf16[32,32,1024]{2,1,0:T(8,128)(2,1)}, u32[]{:S(2)}, u32[]{:S(2)}) async-start(bf16[32,32,1024]{2,1,0:T(8,128)(2,1)} %bitcast.353), calls=%async_computation.5 | async-start | bytes 4194304 | tf_op jit(solution)/shard_map/all_to_all | solution.py:111
  46.5 157.8 %all-gather.6.cloned.1.call-start = ((), (), s32[]{:S(2)}) async-start(), calls=%async_computation.24 | async-start | bytes 7962624 | tf_op jit(solution)/shard_map/all_gather | solution.py:346
  47.7 263.0 %all-gather.8.cloned.1.call-start = ((), (), s32[]{:S(2)}) async-start(), calls=%async_computation.25 | async-start | bytes 6488064 | tf_op jit(solution)/shard_map/all_gather | solution.py:443
  49.4 130.7 %copy-start.58 = (f32[512,32]{0,1:T(8,128)}, f32[512,32]{0,1:T(8,128)S(1)}, u32[]{:S(2)}) copy-start(f32[512,32]{0,1:T(8,128)S(1)} %get-tuple-element.387) | copy-start | bytes 196612
  49.4 130.7 %copy-start.60 = (f32[512,32]{0,1:T(8,128)}, f32[512,32]{0,1:T(8,128)S(1)}, u32[]{:S(2)}) copy-start(f32[512,32]{0,1:T(8,128)S(1)} %get-tuple-element.388) | copy-start | bytes 196612
  49.5 130.2 %copy-start.77 = (f32[96,32]{0,1:T(8,128)}, f32[96,32]{0,1:T(8,128)S(1)}, u32[]{:S(2)}) copy-start(f32[96,32]{0,1:T(8,128)S(1)} %get-tuple-element.406) | copy-start | bytes 36868
  49.5 130.2 %copy-start.79 = (f32[96,32]{0,1:T(8,128)}, f32[96,32]{0,1:T(8,128)S(1)}, u32[]{:S(2)}) copy-start(f32[96,32]{0,1:T(8,128)S(1)} %get-tuple-element.407) | copy-start | bytes 36868
  49.5 130.3 %copy-start.117 = (f32[64]{0:T(128)}, f32[64]{0:T(128)S(1)}, u32[]{:S(2)}) copy-start(f32[64]{0:T(128)S(1)} %get-tuple-element.378) | copy-start | bytes 772
  52.4 135.0 %copy-start.95 = (f32[1024]{0:T(1024)}, f32[1024]{0:T(1024)S(1)}, u32[]{:S(2)}) copy-start(f32[1024]{0:T(1024)S(1)} %mul.1154) | copy-start | bytes 12292
  188.2 19.0 %collective-permute-start = (bf16[96,1024]{1,0:T(8,128)(2,1)S(1)}, bf16[96,1024]{1,0:T(8,128)(2,1)S(1)}, u32[]{:S(2)}, u32[]{:S(2)}) collective-permute-start(bf16[96,1024]{1,0:T(8,128)(2,1)S(1)} %multiply_convert_fusion.10), channel_id=1, source_target_pairs={{0,1},{1,2},{2,3},{3,0},{4,5},{5,6},{6,7},{7,4},{8,9},{9,10},{10,1... | collective-permute-start | bytes 589832 | tf_op jit(solution)/shard_map/ppermute | solution.py:121
  188.3 18.9 %collective-permute-start.1 = (bf16[96,1024]{1,0:T(8,128)(2,1)S(1)}, bf16[96,1024]{1,0:T(8,128)(2,1)}, u32[]{:S(2)}, u32[]{:S(2)}) collective-permute-start(bf16[96,1024]{1,0:T(8,128)(2,1)S(1)} %multiply_convert_fusion.10), channel_id=1, source_target_pairs={{0,2},{1,3},{2,0},{3,1},{4,6},{5,7},{6,4},{7,5},{8,10},{9,11},{10,... | collective-permute-start | bytes 589832 | tf_op jit(solution)/shard_map/ppermute | solution.py:121
  189.7 17.5 %collective-permute-start.2 = (bf16[96,1024]{1,0:T(8,128)(2,1)S(1)}, bf16[96,1024]{1,0:T(8,128)(2,1)}, u32[]{:S(2)}, u32[]{:S(2)}) collective-permute-start(bf16[96,1024]{1,0:T(8,128)(2,1)S(1)} %multiply_convert_fusion.10), channel_id=1, source_target_pairs={{0,3},{1,0},{2,1},{3,2},{4,7},{5,4},{6,5},{7,6},{8,11},{9,8},{10,9... | collective-permute-start | bytes 589832 | tf_op jit(solution)/shard_map/ppermute | solution.py:121
  216.7 9.0 collective-permute-start.3
  220.0 17.7 %collective-permute-start.4 = (bf16[96,1024]{1,0:T(8,128)(2,1)S(1)}, bf16[96,1024]{1,0:T(8,128)(2,1)}, u32[]{:S(2)}, u32[]{:S(2)}) collective-permute-start(bf16[96,1024]{1,0:T(8,128)(2,1)S(1)} %get-tuple-element.363), channel_id=1, source_target_pairs={{0,2},{1,3},{2,0},{3,1},{4,6},{5,7},{6,4},{7,5},{8,10},{9,11},{10,... | collective-permute-start | bytes 589832 | tf_op jit(solution)/shard_map/ppermute | solution.py:121
  220.6 17.2 %collective-permute-start.5 = (bf16[96,1024]{1,0:T(8,128)(2,1)S(1)}, bf16[96,1024]{1,0:T(8,128)(2,1)}, u32[]{:S(2)}, u32[]{:S(2)}) collective-permute-start(bf16[96,1024]{1,0:T(8,128)(2,1)S(1)} %get-tuple-element.362), channel_id=1, source_target_pairs={{0,1},{1,2},{2,3},{3,0},{4,5},{5,6},{6,7},{7,4},{8,9},{9,10},{10,1... | collective-permute-start | bytes 589832 | tf_op jit(solution)/shard_map/ppermute | solution.py:121
  364.7 10.5 all-to-all-start.7
  415.5 6.0 collective-permute-start.6
  427.6 41.4 %all-to-all-start.8 = ((bf16[4,384,1024]{2,1,0:T(8,128)(2,1)}), bf16[4,384,1024]{2,1,0:T(8,128)(2,1)}, u32[]{:S(2)}, u32[]{:S(2)}) async-start(bf16[4,384,1024]{2,1,0:T(8,128)(2,1)} %fusion.17), calls=%async_computation.8 | async-start | bytes 6291456 | tf_op jit(solution)/shard_map/all_to_all | solution.py:136
  432.3 178.4 %reduce-scatter.3.cloned.1.call-start = ((), (), s32[]{:S(2)}) async-start(), calls=%async_computation.26 | async-start | bytes 7962624 | tf_op jit(solution)/shard_map/reduce_scatter | solution.py:584
  474.6 9.1 collective-permute-start.7
  478.0 16.6 %collective-permute-start.8 = (bf16[96,1024]{1,0:T(8,128)(2,1)}, bf16[96,1024]{1,0:T(8,128)(2,1)}, u32[]{:S(2)}, u32[]{:S(2)}) collective-permute-start(bf16[96,1024]{1,0:T(8,128)(2,1)} %get-tuple-element.360), channel_id=1, source_target_pairs={{0,2},{1,3},{2,0},{3,1},{4,6},{5,7},{6,4},{7,5},{8,10},{9,11},{10,... | collective-permute-start | bytes 589832 | tf_op jit(solution)/shard_map/ppermute | solution.py:121
  478.0 16.6 %collective-permute-start.9 = (bf16[96,1024]{1,0:T(8,128)(2,1)}, bf16[96,1024]{1,0:T(8,128)(2,1)}, u32[]{:S(2)}, u32[]{:S(2)}) collective-permute-start(bf16[96,1024]{1,0:T(8,128)(2,1)} %get-tuple-element.359), channel_id=1, source_target_pairs={{0,1},{1,2},{2,3},{3,0},{4,5},{5,6},{6,7},{7,4},{8,9},{9,10},{10,1... | collective-permute-start | bytes 589832 | tf_op jit(solution)/shard_map/ppermute | solution.py:121
  498.2 9.7 collective-permute-start.10
  499.1 15.4 %collective-permute-start.11 = (bf16[96,1024]{1,0:T(8,128)(2,1)S(1)}, bf16[96,1024]{1,0:T(8,128)(2,1)S(1)}, u32[]{:S(2)}, u32[]{:S(2)}) collective-permute-start(bf16[96,1024]{1,0:T(8,128)(2,1)S(1)} %fusion.139), channel_id=1, source_target_pairs={{0,2},{1,3},{2,0},{3,1},{4,6},{5,7},{6,4},{7,5},{8,10},{9,11},{10,... | collective-permute-start | bytes 589832 | tf_op jit(solution)/shard_map/ppermute | solution.py:121
  501.1 13.4 %collective-permute-start.12 = (bf16[96,1024]{1,0:T(8,128)(2,1)S(1)}, bf16[96,1024]{1,0:T(8,128)(2,1)S(1)}, u32[]{:S(2)}, u32[]{:S(2)}) collective-permute-start(bf16[96,1024]{1,0:T(8,128)(2,1)S(1)} %fusion.139), channel_id=1, source_target_pairs={{0,3},{1,0},{2,1},{3,2},{4,7},{5,4},{6,5},{7,6},{8,11},{9,8},{10,9... | collective-permute-start | bytes 589832 | tf_op jit(solution)/shard_map/ppermute | solution.py:121
  527.9 244.5 %reduce-scatter.5.cloned.1.call-start = ((), (), s32[]{:S(2)}) async-start(), calls=%async_computation.27 | async-start | bytes 16515072 | tf_op jit(solution)/shard_map/reduce_scatter | solution.py:603
  533.1 11.6 %collective-permute-start.13 = (bf16[96,1024]{1,0:T(8,128)(2,1)S(1)}, bf16[96,1024]{1,0:T(8,128)(2,1)S(1)}, u32[]{:S(2)}, u32[]{:S(2)}) collective-permute-start(bf16[96,1024]{1,0:T(8,128)(2,1)S(1)} %get-tuple-element.355), channel_id=1, source_target_pairs={{0,3},{1,0},{2,1},{3,2},{4,7},{5,4},{6,5},{7,6},{8,11},{9,8},{10,9... | collective-permute-start | bytes 589832 | tf_op jit(solution)/shard_map/ppermute | solution.py:121
  539.3 17.1 %collective-permute-start.14 = (bf16[96,1024]{1,0:T(8,128)(2,1)S(1)}, bf16[96,1024]{1,0:T(8,128)(2,1)S(1)}, u32[]{:S(2)}, u32[]{:S(2)}) collective-permute-start(bf16[96,1024]{1,0:T(8,128)(2,1)S(1)} %get-tuple-element.357), channel_id=1, source_target_pairs={{0,2},{1,3},{2,0},{3,1},{4,6},{5,7},{6,4},{7,5},{8,10},{9,11},{10,... | collective-permute-start | bytes 589832 | tf_op jit(solution)/shard_map/ppermute | solution.py:121
  539.3 17.1 %collective-permute-start.15 = (bf16[96,1024]{1,0:T(8,128)(2,1)S(1)}, bf16[96,1024]{1,0:T(8,128)(2,1)S(1)}, u32[]{:S(2)}, u32[]{:S(2)}) collective-permute-start(bf16[96,1024]{1,0:T(8,128)(2,1)S(1)} %get-tuple-element.356), channel_id=1, source_target_pairs={{0,1},{1,2},{2,3},{3,0},{4,5},{5,6},{6,7},{7,4},{8,9},{9,10},{10,1... | collective-permute-start | bytes 589832 | tf_op jit(solution)/shard_map/ppermute | solution.py:121
  625.8 16.6 %all-to-all-start.10 = ((bf16[4,2,32,1024]{3,2,1,0:T(8,128)(2,1)}), bf16[4,2,32,1024]{3,2,1,0:T(8,128)(2,1)S(1)}, u32[]{:S(2)}, u32[]{:S(2)}) async-start(bf16[4,2,32,1024]{3,2,1,0:T(8,128)(2,1)} %copy.161), calls=%async_computation.12 | async-start | bytes 1048576 | tf_op jit(solution)/shard_map/all_to_all | solution.py:598
  642.4 10.0 all-to-all-start.11
  652.4 50.4 %all-to-all-start.12 = ((bf16[32,32,1024]{2,1,0:T(8,128)(2,1)}), bf16[32,32,1024]{2,1,0:T(8,128)(2,1)S(1)}, u32[]{:S(2)}, u32[]{:S(2)}) async-start(bf16[32,32,1024]{2,1,0:T(8,128)(2,1)} %bitcast.100), calls=%async_computation.14 | async-start | bytes 4194304 | tf_op jit(solution)/shard_map/all_to_all | solution.py:111
  713.1 59.3 %all-to-all-start.9 = ((bf16[4,2,144,1024]{3,2,1,0:T(8,128)(2,1)}), bf16[4,2,144,1024]{3,2,1,0:T(8,128)(2,1)S(1)}, u32[]{:S(2)}, u32[]{:S(2)}) async-start(bf16[4,2,144,1024]{3,2,1,0:T(8,128)(2,1)} %fusion.27), calls=%async_computation.11 | async-start | bytes 4718592 | tf_op jit(solution)/shard_map/all_to_all | solution.py:590
  776.9 15.3 %collective-permute-start.16 = (bf16[2,128,1024]{2,1,0:T(8,128)(2,1)}, bf16[2,128,1024]{2,1,0:T(8,128)(2,1)}, u32[]{:S(2)}, u32[]{:S(2)}) collective-permute-start(bf16[2,128,1024]{2,1,0:T(8,128)(2,1)} %get-tuple-element.344), channel_id=1, source_target_pairs={{0,3},{1,0},{2,1},{3,2},{4,7},{5,4},{6,5},{7,6},{8,11},{9,8},{10,9... | collective-permute-start | bytes 1572872 | tf_op jit(solution)/shard_map/ppermute | solution.py:121
  778.3 43.7 %collective-permute-start.17 = (bf16[2,128,1024]{2,1,0:T(8,128)(2,1)}, bf16[2,128,1024]{2,1,0:T(8,128)(2,1)}, u32[]{:S(2)}, u32[]{:S(2)}) collective-permute-start(bf16[2,128,1024]{2,1,0:T(8,128)(2,1)} %get-tuple-element.346), channel_id=1, source_target_pairs={{0,2},{1,3},{2,0},{3,1},{4,6},{5,7},{6,4},{7,5},{8,10},{9,11},{10,... | collective-permute-start | bytes 1572872 | tf_op jit(solution)/shard_map/ppermute | solution.py:121
  778.3 43.7 %collective-permute-start.18 = (bf16[2,128,1024]{2,1,0:T(8,128)(2,1)}, bf16[2,128,1024]{2,1,0:T(8,128)(2,1)}, u32[]{:S(2)}, u32[]{:S(2)}) collective-permute-start(bf16[2,128,1024]{2,1,0:T(8,128)(2,1)} %get-tuple-element.345), channel_id=1, source_target_pairs={{0,1},{1,2},{2,3},{3,0},{4,5},{5,6},{6,7},{7,4},{8,9},{9,10},{10,1... | collective-permute-start | bytes 1572872 | tf_op jit(solution)/shard_map/ppermute | solution.py:121
  829.5 13.0 %all-to-all-start.13 = ((f32[32,1,31]{2,1,0:T(1,128)}), f32[32,1,31]{2,1,0:T(1,128)S(1)}, u32[]{:S(2)}, u32[]{:S(2)}) async-start(f32[32,1,31]{2,1,0:T(1,128)} %broadcast_in_dim.290), calls=%async_computation.15 | async-start | bytes 32768 | tf_op jit(solution)/shard_map/all_to_all | solution.py:116
  851.5 2.7 collective-permute-start.19
  873.1 16.5 %all-to-all-start.17 = ((bf16[4,128,1024]{2,1,0:T(8,128)(2,1)}), bf16[4,128,1024]{2,1,0:T(8,128)(2,1)S(1)}, u32[]{:S(2)}, u32[]{:S(2)}) async-start(bf16[4,128,1024]{2,1,0:T(8,128)(2,1)} %broadcast_in_dim.291), calls=%async_computation.19 | async-start | bytes 2097152 | tf_op jit(solution)/shard_map/all_to_all | solution.py:145
  889.6 31.2 %all-to-all-start.15 = ((bf16[8,128,1024]{2,1,0:T(8,128)(2,1)}), bf16[8,128,1024]{2,1,0:T(8,128)(2,1)}, u32[]{:S(2)}, u32[]{:S(2)}) async-start(bf16[8,128,1024]{2,1,0:T(8,128)(2,1)} %bitcast.109), calls=%async_computation.17 | async-start | bytes 4194304 | tf_op jit(solution)/shard_map/all_to_all | solution.py:697
  894.2 23.2 %collective-permute-start.20 = (bf16[512,1024]{1,0:T(8,128)(2,1)S(1)}, bf16[512,1024]{1,0:T(8,128)(2,1)S(1)}, u32[]{:S(2)}, u32[]{:S(2)}) collective-permute-start(bf16[512,1024]{1,0:T(8,128)(2,1)S(1)} %bitcast.341), channel_id=1, source_target_pairs={{0,4},{4,0},{1,5},{5,1},{2,6},{6,2},{3,7},{7,3},{8,12},{12,8},{9,1... | collective-permute-start | bytes 3145736 | tf_op jit(solution)/shard_map/ppermute | solution.py:125
  956.4 31.1 %all-to-all-start.18 = ((bf16[8,128,1024]{2,1,0:T(8,128)(2,1)}), bf16[8,128,1024]{2,1,0:T(8,128)(2,1)}, u32[]{:S(2)}, u32[]{:S(2)}) async-start(bf16[8,128,1024]{2,1,0:T(8,128)(2,1)} %bitcast.355), calls=%async_computation.20 | async-start | bytes 4194304 | tf_op jit(solution)/shard_map/all_to_all | solution.py:706
  960.9 45.6 %collective-permute-start.21 = (bf16[1024,1024]{1,0:T(8,128)(2,1)S(1)}, bf16[1024,1024]{1,0:T(8,128)(2,1)}, u32[]{:S(2)}, u32[]{:S(2)}) collective-permute-start(bf16[1024,1024]{1,0:T(8,128)(2,1)S(1)} %shard_map.313), channel_id=1, source_target_pairs={{0,4},{4,0},{1,5},{5,1},{2,6},{6,2},{3,7},{7,3},{8,12},{12,8},{9,1... | collective-permute-start | bytes 6291464 | tf_op jit(solution)/shard_map/ppermute | solution.py:125
  987.5 15.2 %all-to-all-start.14 = ((bf16[4,2,32,1024]{3,2,1,0:T(8,128)(2,1)}), bf16[4,2,32,1024]{3,2,1,0:T(8,128)(2,1)S(1)}, u32[]{:S(2)}, u32[]{:S(2)}) async-start(bf16[4,2,32,1024]{3,2,1,0:T(8,128)(2,1)} %copy.166), calls=%async_computation.16 | async-start | bytes 1048576 | tf_op jit(solution)/shard_map/all_to_all | solution.py:611
  1002.8 16.0 %all-to-all-start.19 = ((bf16[4,2,32,1024]{3,2,1,0:T(8,128)(2,1)}), bf16[4,2,32,1024]{3,2,1,0:T(8,128)(2,1)S(1)}, u32[]{:S(2)}, u32[]{:S(2)}) async-start(bf16[4,2,32,1024]{3,2,1,0:T(8,128)(2,1)} %copy.170), calls=%async_computation.21 | async-start | bytes 1048576 | tf_op jit(solution)/shard_map/all_to_all | solution.py:611
  1018.7 29.9 %all-to-all-start.20 = ((bf16[4,144,1024]{2,1,0:T(8,128)(2,1)}), bf16[4,144,1024]{2,1,0:T(8,128)(2,1)}, u32[]{:S(2)}, u32[]{:S(2)}) async-start(bf16[4,144,1024]{2,1,0:T(8,128)(2,1)} %bitcast.365), calls=%async_computation.22 | async-start | bytes 2359296 | tf_op jit(solution)/shard_map/all_to_all | solution.py:712
  (152 other events, 2007.9 us)
Sparse Core Ops, SparseCore 0:
  11.6 142.2 all-gather.3
  156.3 47.9 all-gather.5
  242.0 68.6 all-gather.7
  528.1 68.3 reduce-scatter.2
  610.8 124.3 reduce-scatter.4

commit v4 on v3

--- a/solution.py
+++ b/solution.py
@@ -116,9 +116,45 @@
     return lax.all_to_all(jnp.broadcast_to(values[None], (count,) + values.shape), ALL, 0, 0)
 
 
-def turned(values, step):
-    count = lax.axis_size("vocab")
-    return lax.ppermute(values, "vocab", [(i, (i + step) % count) for i in range(count)])
+def turned(values, axis, step):
+    count = lax.axis_size(axis)
+    return lax.ppermute(values, axis, [(i, (i + step) % count) for i in range(count)])
+
+
+def block_at(blocks, index):
+    return lax.dynamic_index_in_dim(blocks, index % blocks.shape[0], 0, keepdims=False)
+
+
+def handed_out(blocks, axis):
+    place, count = lax.axis_index(axis), lax.axis_size(axis)
+    return [block_at(blocks, place)] + [
+        turned(block_at(blocks, place + step), axis, step) for step in range(1, count)
+    ]
+
+
+def handed_back(pieces, axis):
+    return [pieces[0]] + [turned(pieces[step], axis, -step) for step in range(1, len(pieces))]
+
+
+def gathered(values, axis):
+    return [values] + [turned(values, axis, step) for step in range(1, lax.axis_size(axis))]
+
+
+def placed_before(pieces, axis):
+    pieces, place = jnp.stack(pieces), lax.axis_index(axis)
+    return jnp.stack([block_at(pieces, place - j) for j in range(pieces.shape[0])])
+
+
+def placed_after(pieces, axis):
+    pieces, place = jnp.stack(pieces), lax.axis_index(axis)
+    return jnp.stack([block_at(pieces, j - place) for j in range(pieces.shape[0])])
+
+
+def added(pieces):
+    total = pieces[0].astype(jnp.float32)
+    for piece in pieces[1:]:
+        total = total + piece.astype(jnp.float32)
+    return total
 
 
 def other_core(values):
@@ -133,8 +169,7 @@
 
 
 def chip_sum(blocks):
-    blocks = lax.all_to_all(blocks, "chip", 0, 0, tiled=True)
-    return jnp.sum(blocks.astype(jnp.float32), axis=0)
+    return added(handed_out(blocks, "chip"))
 
 
 def group_sum(values, core):
@@ -142,9 +177,7 @@
     chips = lax.axis_size("chip")
     half = pair_sum(values.reshape(2, rows, -1), core).reshape(chips, rows // chips, -1)
     part = chip_sum(half).astype(jnp.bfloat16)
-    half = lax.all_to_all(
-        jnp.broadcast_to(part[None], (chips,) + part.shape), "chip", 0, 0, tiled=True
-    ).reshape(rows, -1)
+    half = placed_before(gathered(part, "chip"), "chip").reshape(rows, -1)
     other = other_core(half)
     first = jnp.where(core == 0, half, other)
     second = jnp.where(core == 0, other, half)
@@ -152,26 +185,15 @@
 
 
 def member_gather(values):
-    return jnp.concatenate(
-        [values] + [turned(values, step) for step in range(1, lax.axis_size("vocab"))], axis=0
-    )
-
-
-def member_return(blocks):
-    total = blocks[0].astype(jnp.float32)
-    for step in range(1, len(blocks)):
-        total = total + turned(blocks[step], -step).astype(jnp.float32)
-    return total
-
-
-def member_scatter(blocks, member):
-    count = blocks.shape[0]
-    return member_return(
-        [
-            lax.dynamic_index_in_dim(blocks, (member - step) % count, 0, keepdims=False)
-            for step in range(count)
-        ]
-    )
+    return jnp.concatenate(gathered(values, "vocab"), axis=0)
+
+
+def member_return(pieces):
+    return added(handed_back(pieces, "vocab"))
+
+
+def member_scatter(blocks):
+    return added(handed_out(blocks, "vocab"))
 
 
 def onehot_rows(index, count):
@@ -356,6 +378,17 @@
     targets = numbers[:, :RESP].reshape(-1)
     orders = numbers[:, RESP : RESP + members].reshape(groups, members, members)[:, 0]
     turns = (jnp.max(numbers[:, RESP + members]) + SLOTS - 1) // SLOTS
+    slots = jnp.arange(members)
+    chosen_mask = (orders[:, 0::2, None] == slots[None, None, :]).astype(jnp.float32)
+    rejected_mask = (orders[:, 1::2, None] == slots[None, None, :]).astype(jnp.float32)
+    pair_rows = jnp.sum(
+        (chosen_mask + rejected_mask)[:, :, :, None] * (chosen_mask - rejected_mask)[:, :, None, :],
+        axis=1,
+    )
+    same_group = jnp.arange(groups)[:, None] == jnp.arange(groups)[None, :]
+    pair_rows = jnp.where(same_group[:, None, :, None], pair_rows[:, :, None, :], 0.0)
+    pair_rows = pair_rows.reshape(devices, devices) * (pref_beta / RESP)
+    chosen_sign = jnp.sum(chosen_mask - rejected_mask, axis=1).reshape(devices, 1)
     table_b = table_master.astype(jnp.bfloat16)
     head_gains = low_copy(norm_gains)
     cosine, sine = rope_tables(SEQ, HD // 2)
@@ -455,17 +488,10 @@
     own_logp = jnp.sum(jnp.sum(stats[:, 2], axis=0) - own_log_total)
     joined = spread(jnp.concatenate([own_log_total, own_logp[None]]))
     log_total = joined[:, :RESP].reshape(-1)
-    seq_logp = joined[:, RESP].reshape(groups, members)
-    slots = jnp.arange(members)
-    chosen_mask = (orders[:, 0::2, None] == slots[None, None, :]).astype(jnp.float32)
-    rejected_mask = (orders[:, 1::2, None] == slots[None, None, :]).astype(jnp.float32)
-    margin = (
-        pref_beta * jnp.sum((chosen_mask - rejected_mask) * seq_logp[:, None, :], axis=2) / RESP
-    )
-    pair_loss = jnp.sum(jax.nn.softplus(-margin))
-    pull = jax.nn.sigmoid(-margin) * pref_beta / RESP
-    grad_logp = jnp.sum((rejected_mask - chosen_mask) * pull[:, :, None], axis=1)
-    row_weight = jnp.repeat(grad_logp.reshape(-1), RESP)
+    margin = jnp.sum(pair_rows * joined[:, RESP][None, :], axis=1, keepdims=True)
+    pair_loss = 0.5 * jnp.sum(jax.nn.softplus(-margin))
+    grad_logp = chosen_sign * jax.nn.sigmoid(-margin) * (-pref_beta / RESP)
+    row_weight = jnp.broadcast_to(grad_logp, (devices, RESP)).reshape(-1)
     softmax_rows = jnp.exp(logit_scores - log_total[:, None])
     grad_logits = (row_weight[:, None] * (onehot.astype(jnp.float32) - softmax_rows)).astype(
         jnp.bfloat16
@@ -479,7 +505,7 @@
         core,
     )
     grad_answer_group = chip_sum(grad_answer_pair).astype(jnp.bfloat16)
-    grad_final = member_scatter(grad_answer_group.reshape(members, RESP, D), member)
+    grad_final = member_scatter(grad_answer_group.reshape(members, RESP, D))
     grad_hidden3, grad_gain3 = norm_back(hidden3, gains[3], grad_final)
     grad_ffn_out = member_gather(grad_hidden3.astype(jnp.bfloat16))
     grad_inner = dense(grad_ffn_out, wide_b[2])
@@ -550,16 +576,6 @@
     grad_norm0, grad_gain0 = norm_back(hidden0, gains[0], grad_act1)
     grad_embed_b = (grad_hidden1 + grad_norm0).astype(jnp.bfloat16)
 
-    def returned(wanted, row_keys):
-        rows = outer(onehot_rows(row_keys, devices * SLOTS), grad_embed_b)
-        rows = exchanged(rows.astype(jnp.bfloat16))
-        return outer(onehot_rows(wanted, block_rows), rows)
-
-    def return_more(turn, total):
-        later_keys, later_asked = later_round(turn)
-        return total + returned(later_asked, later_keys)
-
-    share_table = lax.fori_loop(1, turns, return_more, grad_table + returned(asked, keys))
     grad_square = jnp.concatenate(
         [
             grad_inner_w.astype(jnp.bfloat16).reshape(3, D, D),
@@ -585,9 +601,6 @@
     share_wide = share_wide_b.astype(jnp.float32)
     squares, square_rows = square_master.shape[0], square_master.shape[1]
     wides, wide_rows = wide_master.shape[0], wide_master.shape[1]
-    wide_early = jnp.stack([wide_moment.astype(jnp.bfloat16), share_wide_b], axis=1)
-    wide_early = jnp.pad(wide_early, ((0, members - wides), (0, 0), (0, 0), (0, 0)))
-    wide_early = lax.all_to_all(wide_early, "vocab", 0, 0, tiled=True)
     per_member = -(-squares // members)
     group_rows = members * square_rows
 
@@ -595,24 +608,47 @@
         values = jnp.pad(values, ((0, per_member * members - squares), (0, 0), (0, 0)))
         return values.reshape(per_member, members, -1, D).transpose(1, 0, 2, 3)
 
-    square_moment_job = lax.all_to_all(
-        by_member(square_moment.astype(jnp.bfloat16)), "vocab", 0, 0, tiled=True
-    )
+    def wide_by_member(values):
+        return jnp.pad(values, ((0, members - wides), (0, 0), (0, 0)))
+
+    moment_jobs = jnp.concatenate(
+        [
+            wide_by_member(wide_moment.astype(jnp.bfloat16)),
+            by_member(square_moment.astype(jnp.bfloat16)).reshape(members, -1, D),
+        ],
+        axis=1,
+    )
+    moment_jobs = jnp.stack(handed_out(moment_jobs, "vocab"))
+    grad_square, share_wide_b, moment_jobs = lax.optimization_barrier(
+        (grad_square, share_wide_b, moment_jobs)
+    )
+    wide_moment_job = moment_jobs[:, :wide_rows]
+    square_moment_job = placed_before(list(moment_jobs[:, wide_rows:]), "vocab")
+    square_moment_job = square_moment_job.reshape(members, per_member, square_rows, D)
     square_moment_job = square_moment_job.transpose(1, 0, 2, 3).reshape(per_member, group_rows, D)
-    grad_square, share_wide_b = lax.optimization_barrier((grad_square, share_wide_b))
+    wide_grad_job = jnp.stack(handed_out(wide_by_member(share_wide_b), "vocab"))
+    grad_embed_b, wide_grad_job = lax.optimization_barrier((grad_embed_b, wide_grad_job))
     group_square = lax.psum_scatter(grad_square, DP, scatter_dimension=1, tiled=True)
-    group_square, wide_early, square_moment_job = lax.optimization_barrier(
-        (group_square, wide_early, square_moment_job)
-    )
-    square_grad_job = member_scatter(by_member(group_square), member)
+    square_grad_job = member_scatter(by_member(group_square))
 
     def from_members(values):
         values = values.reshape(per_member, members, square_rows, D).transpose(1, 0, 2, 3)
-        values = lax.all_to_all(values.astype(jnp.bfloat16), "vocab", 0, 0, tiled=True)
+        values = placed_before(handed_out(values.astype(jnp.bfloat16), "vocab"), "vocab")
         values = values.transpose(1, 0, 2, 3).reshape(per_member * members, square_rows, D)
         return values[:squares].astype(jnp.float32)
 
     share_square = from_members(square_grad_job)
+
+    def returned(wanted, row_keys):
+        rows = outer(onehot_rows(row_keys, devices * SLOTS), grad_embed_b)
+        rows = exchanged(rows.astype(jnp.bfloat16))
+        return outer(onehot_rows(wanted, block_rows), rows)
+
+    def return_more(turn, total):
+        later_keys, later_asked = later_round(turn)
+        return total + returned(later_asked, later_keys)
+
+    share_table = lax.fori_loop(1, turns, return_more, grad_table + returned(asked, keys))
     width = vector_master.shape[1]
     vector_notes = grad_vector.reshape(-1, devices, width).transpose(1, 0, 2).reshape(devices, -1)
     vector_notes = jnp.concatenate(
@@ -674,44 +710,44 @@
     )
     wide_inverse = 1.0 / (moment_norm[squares:] + ortho_epsilon)
     wide_inverse = jnp.pad(wide_inverse, (0, members - wides))[member]
-    wide_early = wide_early.astype(jnp.float32)
-    wide_job = (
-        (
-            (muon_decay * wide_inverse) * wide_early[:, 0]
-            + ((1.0 - muon_decay) * factor * wide_inverse) * wide_early[:, 1]
-        )
-        .reshape(members * wide_rows, D)
-        .astype(jnp.bfloat16)
-    )
-    wide_gram = group_sum(outer(wide_job, wide_job).astype(jnp.bfloat16), core)
     square_inverse = 1.0 / (moment_norm[:squares] + ortho_epsilon)
     square_inverse = jnp.pad(square_inverse, (0, per_member * members - squares))
     square_inverse = square_inverse.reshape(per_member, members)[:, member][:, None, None]
     square_part = (muon_decay * square_inverse) * square_moment_job.astype(jnp.float32) + (
         (1.0 - muon_decay) * factor * square_inverse
     ) * square_grad_job
-    square_part = square_part.astype(jnp.bfloat16).reshape(per_member, 1, group_rows, D)
-    square_part = jnp.pad(
-        square_part, ((0, groups // 2 - per_member), (1, 0), (0, 0), (0, 0))
-    ).reshape(groups * group_rows, D)
-    square_job = lax.all_to_all(square_part, DP, 0, 0, tiled=True)
+    square_part, wide_grad_job = lax.optimization_barrier(
+        (square_part.astype(jnp.bfloat16), wide_grad_job)
+    )
+    square_part = jnp.pad(square_part, ((0, groups // 2 - per_member), (0, 0), (0, 0)))
+    square_half = jnp.concatenate(handed_out(square_part, "chip"), axis=0)
+    square_job = jnp.concatenate([square_half, other_core(square_half)], axis=0)
+    wide_job = (
+        (muon_decay * wide_inverse) * wide_moment_job.astype(jnp.float32)
+        + ((1.0 - muon_decay) * factor * wide_inverse) * wide_grad_job.astype(jnp.float32)
+    )
+    wide_job = wide_job.reshape(members * wide_rows, D).astype(jnp.bfloat16)
+    wide_gram = group_sum(outer(wide_job, wide_job).astype(jnp.bfloat16), core)
     square_gram = outer(square_job, square_job)
     gram = jnp.where(core == 0, wide_gram.astype(jnp.float32), square_gram)
-    gram, table_step, table_first_new, table_second_new = lax.optimization_barrier(
-        (gram, table_step, table_first_new, table_second_new)
+    gram, share_square, table_step, table_first_new, table_second_new = lax.optimization_barrier(
+        (gram, share_square, table_step, table_first_new, table_second_new)
     )
     rest_b = ortho_rest(gram)
     power = leading_coefficient**NS_ITERS
     wide_rest = jnp.where(core == 0, rest_b, other_core(rest_b))
-    back_square = lax.all_to_all(
-        square_product(square_job, rest_b).astype(jnp.bfloat16), DP, 0, 0, tiled=True
-    )
-    back_square = back_square.reshape(groups // 2, 2, group_rows, D)[:per_member, 1]
+    back_square = square_product(square_job, rest_b).astype(jnp.bfloat16)
+    half_rows = square_half.shape[0]
+    back_square = jnp.where(
+        core == 0, other_core(back_square[half_rows:]), back_square[:half_rows]
+    )
+    back_square = handed_back(list(back_square.reshape(-1, group_rows, D)), "chip")
+    back_square = placed_after(back_square, "chip")[:per_member]
+    back_wide = square_product(wide_job, wide_rest).astype(jnp.bfloat16)
+    back_wide = handed_back(list(back_wide.reshape(members, wide_rows, D)), "vocab")
+    back_wide = placed_after(back_wide, "vocab")[:wides]
+    back_square, back_wide = lax.optimization_barrier((back_square, back_wide))
     back_square = from_members(back_square)
-    back_wide = square_product(wide_job, wide_rest).astype(jnp.bfloat16)
-    back_wide = lax.all_to_all(
-        back_wide.reshape(members, wide_rows, D), "vocab", 0, 0, tiled=True
-    )[:wides]
     ortho_wide = power * ortho_wide + back_wide.astype(jnp.float32)
     ortho_square = power * ortho_square + back_square
     wide_scale = jnp.array([math.sqrt(FF / D), math.sqrt(FF / D), 1.0], jnp.float32)

time: 1080 us -> 1040 us (0.963)
  waiting for transfers between devices: 482 us -> 444 us
  blocking collectives: 27.5 us -> 0 us
  starting transfers between devices: 92.7 us -> 118 us
    all_to_all x9 -> x0, waiting for transfers between devices: 151 us -> none  [the longest x1 36.6 us: chip_sum(): blocks = lax.all_to_all(blocks, 'chip', 0, 0, tiled=True)]
    ppermute x18 -> x48, waiting for transfers between devices: 93.4 us -> 201 us  [turned(): lax.ppermute(values, axis, [(i, (i + step) % count) for i in range(count)])]
    ppermute x18 -> x48, starting transfers between devices: 28 us -> 72.7 us  [turned(): lax.ppermute(values, axis, [(i, (i + step) % count) for i in range(count)])]
    all_to_all x9 -> x0, starting transfers between devices: 37 us -> none  [the longest x2 7.2 us: from_members(): lax.all_to_all(values.astype(jnp.bfloat16), 'vocab', 0, 0, tiled=True)]
    all_to_all x2 -> x0, blocking collectives: 27.5 us -> none  [the longest x1 17.1 us: chip_sum(): blocks = lax.all_to_all(blocks, 'chip', 0, 0, tiled=True)]
    all_to_all x4 -> x5, starting transfers between devices: 17.1 us -> 27.2 us  [exchanged(): return lax.all_to_all(rows, ALL, 0, 0, tiled=True)]
    unnamed x318 -> x340, local copies, waits for them, and re-layouts: 21.9 us -> 31.4 us
    all_to_all x4 -> x5, waiting for transfers between devices: 133 us -> 139 us  [exchanged(): return lax.all_to_all(rows, ALL, 0, 0, tiled=True)]
  transfers between devices with their start and end apart: 42 -> 66, of which waited for: 30 -> 39; matrix products, arithmetic and copies ran while one was open for 22% -> 23% of each run, Pallas kernels for 0% -> 2%
where the time goes in v4:
time: 1040 us; the launch traced here: 1030 us
  waiting for transfers between devices  444 us (43%)
  matrix products  176 us (17%)
  other arithmetic  143 us (14%)
  starting transfers between devices  118 us (11%)
  local copies, waits for them, and re-layouts  94.5 us (9%)
  between operations  30.2 us (3%)
  Pallas kernels  25.2 us (2%)
    ppermute x48, waiting for transfers between devices, turned(): lax.ppermute(values, axis, [(i, (i + step) % count) for i in range(count)])  201 us
    all_to_all x5, waiting for transfers between devices, exchanged(): return lax.all_to_all(rows, ALL, 0, 0, tiled=True)  139 us
    ppermute x48, starting transfers between devices, turned(): lax.ppermute(values, axis, [(i, (i + step) % count) for i in range(count)])  72.7 us
    dot_general x12, matrix products, outer(): lax.dot_general(grads, inputs, (((0,), (0,)), ((), ())), preferred_elemen...  61.8 us
    all_gather x1, waiting for transfers between devices, body(): response_tokens = lax.all_gather(final_b, ALL, axis=0, tiled=True)  58.7 us
    dot_general x8, matrix products, dense(): lax.dot_general(inputs, weight, (((1,), (1,)), ((), ())), preferred_eleme...  41.4 us
    unnamed x340, local copies, waits for them, and re-layouts  31.4 us
    all_to_all x5, starting transfers between devices, exchanged(): return lax.all_to_all(rows, ALL, 0, 0, tiled=True)  27.2 us
  transfers between devices with their start and end apart: 66, of which 39 were waited for; matrix products, arithmetic and copies ran while one was open for 23% of the time, Pallas kernels for 2%

profile of v4, /device:TPU:0, one launch (start us, length us, event | category | flops | bytes accessed | tf_op | source)
XLA Modules:
  0.0 1031.8 jit_solution(14628449568700322265)
XLA Ops:
  19.0 7.3 all-to-all-start.4
  26.3 6.1 convert_element_type.409
  34.5 8.1 fusion.46
  52.5 82.2 %all-to-all-done.5 = bf16[32,32,1024]{2,1,0:T(8,128)(2,1)} async-done(((bf16[32,32,1024]{2,1,0:T(8,128)(2,1)}), bf16[32,32,1024]{2,1,0:T(8,128)(2,1)}, u32[]{:S(2)}, u32[]{:S(2)}) %all-to-all-start.5) | async-done | bytes 2097184 | tf_op jit(solution)/shard_map/all_to_all | solution.py:111
  141.2 12.6 %all-gather.4.cloned.1.call-done = bf16[7,1024,1024]{2,1,0:T(8,128)(2,1)} async-done(((bf16[7,32,1024]{2,1,0:T(8,128)(2,1)}), bf16[7,1024,1024]{2,1,0:T(8,128)(2,1)}) %all-gather.4.cloned.1.call-update) | async-done | bytes 14680080 | tf_op jit(solution)/shard_map/all_gather | solution.py:367
  153.9 6.2 slice.351
  160.2 6.0 fusion.147
  192.3 12.0 %all-gather.6.cloned.1.call-done = bf16[3,1152,1024]{2,1,0:T(8,128)(2,1)} async-done(((bf16[3,144,1024]{2,1,0:T(8,128)(2,1)}), bf16[3,1152,1024]{2,1,0:T(8,128)(2,1)}) %all-gather.6.cloned.1.call-update) | async-done | bytes 7077904 | tf_op jit(solution)/shard_map/all_gather | solution.py:368
  225.7 12.1 %collective-permute-done.4 = bf16[96,1024]{1,0:T(8,128)(2,1)} collective-permute-done((bf16[96,1024]{1,0:T(8,128)(2,1)S(1)}, bf16[96,1024]{1,0:T(8,128)(2,1)}, u32[]{:S(2)}, u32[]{:S(2)}) %collective-permute-start.4) | collective-permute-done | bytes 196640 | tf_op jit(solution)/shard_map/ppermute | solution.py:121
  251.9 58.7 %all-gather.8.cloned.1.call-done = bf16[3072,1024]{1,0:T(8,128)(2,1)} async-done(((bf16[96,1024]{1,0:T(8,128)(2,1)}), bf16[3072,1024]{1,0:T(8,128)(2,1)}) %all-gather.8.cloned.1.call-update) | async-done | bytes 6291472 | tf_op jit(solution)/shard_map/all_gather | solution.py:476
  310.7 20.5 %fusion.166 = (f32[3072]{0:T(1024)}, f32[3072,2048]{0,1:T(8,128)}) fusion(bf16[3072,1024]{1,0:T(8,128)(2,1)} %all-gather.8.cloned.1.call-done, bf16[2048,1024]{1,0:T(8,128)(2,1)} %get-tuple-element.661), kind=kOutput, calls=%fused_computation.488 | convolution fusion | flops 12891190272 | bytes 35663872 | tf_op jit(solution)/shard_map/dot_general | solution.py:61
  332.6 12.4 %exponential_reduce_fusion = (f32[3072]{0:T(1024)}, f32[3072]{0:T(1024)}) fusion(f32[3072,2048]{0,1:T(8,128)} %get-tuple-element.469, f32[3072]{0:T(1024)} %get-tuple-element.468, s32[3072]{0:T(1024)} %fusion.119), kind=kLoop, calls=%fused_computation.31 | loop fusion | flops 31451136 | bytes 25214976 | tf_op jit(solution)/shard_map/reduce_sum | solution.py:481
  354.4 5.6 all-to-all-done.6
  371.6 5.3 all-to-all-done.7
  390.5 22.9 %convolution_convert_fusion.2 = bf16[3072,1024]{1,0:T(8,128)(2,1)} fusion(bf16[2048,1024]{1,0:T(8,128)(2,1)} %get-tuple-element.661, f32[3072,2048]{0,1:T(8,128)} %get-tuple-element.469, f32[3072]{0:T(1024)} %sub.236, f32[3072]{0:T(1024)} %mul.1208, s32[3072]{0:T(1024)} %fusion.119), kind=kOutput, calls=%fused_computation.45 | convolution fusion | flops 12925796352 | bytes 35688448 | tf_op jit(solution)/shard_map/dot_general | solution.py:499
  417.2 6.0 collective-permute-done.6
  423.2 4.4 fusion.17
  433.6 18.0 %collective-permute-done.7 = bf16[384,1024]{1,0:T(8,128)(2,1)} collective-permute-done((bf16[384,1024]{1,0:T(8,128)(2,1)}, bf16[384,1024]{1,0:T(8,128)(2,1)}, u32[]{:S(2)}, u32[]{:S(2)}) %collective-permute-start.7) | collective-permute-done | bytes 786464 | tf_op jit(solution)/shard_map/ppermute | solution.py:121
  451.7 15.4 %collective-permute-done.8 = bf16[384,1024]{1,0:T(8,128)(2,1)} collective-permute-done((bf16[384,1024]{1,0:T(8,128)(2,1)}, bf16[384,1024]{1,0:T(8,128)(2,1)}, u32[]{:S(2)}, u32[]{:S(2)}) %collective-permute-start.8) | collective-permute-done | bytes 786464 | tf_op jit(solution)/shard_map/ppermute | solution.py:121
  475.1 6.2 collective-permute-done.10
  481.3 6.9 collective-permute-done.11
  491.8 4.4 collective-permute-start.13
  501.6 6.9 collective-permute-done.14
  508.5 4.4 fusion.55
  525.3 4.4 convolution_convert_fusion.5
  529.8 7.3 collective-permute-start.16
  542.4 11.0 %collective-permute-done.17 = bf16[96,1024]{1,0:T(8,128)(2,1)S(1)} collective-permute-done((bf16[96,1024]{1,0:T(8,128)(2,1)S(1)}, bf16[96,1024]{1,0:T(8,128)(2,1)S(1)}, u32[]{:S(2)}, u32[]{:S(2)}) %collective-permute-start.17) | collective-permute-done | bytes 196640 | tf_op jit(solution)/shard_map/ppermute | solution.py:121
  579.1 7.3 multiply_reduce_fusion.2
  589.6 5.2 convolution_convert_fusion.1
  618.1 5.9 collective-permute-done.19
  623.9 16.4 %collective-permute-done.20 = bf16[208,1024]{1,0:T(8,128)(2,1)} collective-permute-done((bf16[208,1024]{1,0:T(8,128)(2,1)}, bf16[208,1024]{1,0:T(8,128)(2,1)}, u32[]{:S(2)}, u32[]{:S(2)}) %collective-permute-start.20) | collective-permute-done | bytes 426016 | tf_op jit(solution)/shard_map/ppermute | solution.py:121
  643.8 9.3 multiply_reduce_fusion.1
  655.2 8.7 collective-permute-start.25
  673.5 10.6 %collective-permute-done.26 = bf16[144,1024]{1,0:T(8,128)(2,1)S(1)} collective-permute-done((bf16[144,1024]{1,0:T(8,128)(2,1)S(1)}, bf16[144,1024]{1,0:T(8,128)(2,1)S(1)}, u32[]{:S(2)}, u32[]{:S(2)}) %collective-permute-start.26) | collective-permute-done | bytes 294944 | tf_op jit(solution)/shard_map/ppermute | solution.py:121
  685.3 9.0 all-to-all-start.8
  706.3 46.1 %all-to-all-done.9 = bf16[32,32,1024]{2,1,0:T(8,128)(2,1)} async-done(((bf16[32,32,1024]{2,1,0:T(8,128)(2,1)}), bf16[32,32,1024]{2,1,0:T(8,128)(2,1)}, u32[]{:S(2)}, u32[]{:S(2)}) %all-to-all-start.9) | async-done | bytes 2097184 | tf_op jit(solution)/shard_map/all_to_all | solution.py:111
  752.4 8.6 fusion.15
  761.0 23.9 %convolution_add_fusion = f32[2048,1024]{1,0:T(8,128)} fusion(f32[2048,1024]{1,0:T(8,128)} %fusion.15, bf16[3072,1024]{1,0:T(8,128)(2,1)} %all-gather.8.cloned.1.call-done, f32[3072,2048]{0,1:T(8,128)} %get-tuple-element.469, f32[3072]{0:T(1024)S(1)} %copy-done.118, f32[3072]{0:T(1024)S(1)} %copy-done.117, s32[3072]{0:T(1024)S(1)} %copy-done.100), kind=kOutput, calls=%fused_computation.46 | convolution fusion | flops 12924747776 | bytes 48271360 | tf_op jit(solution)/shard_map/dot_general | solution.py:67
  795.4 6.1 multiply_reduce_fusion
  805.8 22.9 %collective-permute-done.23 = bf16[2,128,1024]{2,1,0:T(8,128)(2,1)} collective-permute-done((bf16[2,128,1024]{2,1,0:T(8,128)(2,1)}, bf16[2,128,1024]{2,1,0:T(8,128)(2,1)}, u32[]{:S(2)}, u32[]{:S(2)}) %collective-permute-start.23) | collective-permute-done | bytes 524320 | tf_op jit(solution)/shard_map/ppermute | solution.py:121
  835.3 13.6 %all-to-all-start.10 = ((f32[32,1,31]{2,1,0:T(1,128)}), f32[32,1,31]{2,1,0:T(1,128)S(1)}, u32[]{:S(2)}, u32[]{:S(2)}) async-start(f32[32,1,31]{2,1,0:T(1,128)} %broadcast_in_dim.315), calls=%async_computation.12 | async-start | bytes 32768 | tf_op jit(solution)/shard_map/all_to_all | solution.py:116
  849.5 6.4 all-to-all-done.10
  879.7 5.2 collective-permute-done.37
  891.1 4.9 collective-permute-done.32
  906.6 22.7 %add_multiply_fusion = (f32[2048,1024]{1,0:T(8,128)}, f32[2048,1024]{1,0:T(8,128)}, f32[2048,1024]{1,0:T(8,128)}) fusion(f32[2048,1024]{1,0:T(8,128)} %param.25, f32[]{:T(128)S(6)} %sub.251, f32[]{:T(128)S(6)} %sub.250, f32[2048,1024]{1,0:T(8,128)} %get-tuple-element.244, f32[]{:T(128)S(6)} %min.3, f32[2048,1024]{1,0:T(8,128)} %param.27, f32[2048,1024]{1,0:T(8,128)} %param.26), kind=kLoop, calls=%fused_computation.34 | loop fusion | flops 31457280 | bytes 58720268 | tf_op jit(solution)/shard_map/mul | solution.py:100
  941.0 25.2 %shard_map.313 = bf16[1024,1024]{1,0:T(8,128)(2,1)S(1)} custom-call(f32[1024,1024]{1,0:T(8,128)S(1)} %convert_select_fusion.gram_ref), custom_call_target="tpu_custom_call" | custom-call | flops 19327352832 | bytes 6291456 | tf_op jit(solution)/shard_map/pallas_call | solution.py:292
  985.4 5.3 collective-permute-done.45
  991.0 17.2 %collective-permute-done.49 = bf16[144,1024]{1,0:T(8,128)(2,1)S(1)} collective-permute-done((bf16[144,1024]{1,0:T(8,128)(2,1)S(1)}, bf16[144,1024]{1,0:T(8,128)(2,1)S(1)}, u32[]{:S(2)}, u32[]{:S(2)}) %collective-permute-start.49) | collective-permute-done | bytes 294944 | tf_op jit(solution)/shard_map/ppermute | solution.py:121
  (709 shorter events, 347.6 us)
Async XLA Ops:
  7.2 146.7 %all-gather.4.cloned.1.call-start = ((), (), s32[]{:S(2)}) async-start(), calls=%async_computation.13 | async-start | bytes 15138816 | tf_op jit(solution)/shard_map/all_gather | solution.py:367
  19.0 15.4 %all-to-all-start.4 = ((f32[32,1,357]{2,1,0:T(1,128)}), f32[32,1,357]{2,1,0:T(1,128)S(1)}, u32[]{:S(2)}, u32[]{:S(2)}) async-start(f32[32,1,357]{2,1,0:T(1,128)} %all_to_all.79), calls=%async_computation.4 | async-start | bytes 98304 | tf_op jit(solution)/shard_map/all_to_all | solution.py:111
  42.5 92.1 %all-to-all-start.5 = ((bf16[32,32,1024]{2,1,0:T(8,128)(2,1)}), bf16[32,32,1024]{2,1,0:T(8,128)(2,1)}, u32[]{:S(2)}, u32[]{:S(2)}) async-start(bf16[32,32,1024]{2,1,0:T(8,128)(2,1)} %bitcast.427), calls=%async_computation.5 | async-start | bytes 4194304 | tf_op jit(solution)/shard_map/all_to_all | solution.py:111
  46.6 157.7 %all-gather.6.cloned.1.call-start = ((), (), s32[]{:S(2)}) async-start(), calls=%async_computation.14 | async-start | bytes 7962624 | tf_op jit(solution)/shard_map/all_gather | solution.py:368
  47.8 262.9 %all-gather.8.cloned.1.call-start = ((), (), s32[]{:S(2)}) async-start(), calls=%async_computation.15 | async-start | bytes 6488064 | tf_op jit(solution)/shard_map/all_gather | solution.py:476
  188.2 19.0 %collective-permute-start = (bf16[96,1024]{1,0:T(8,128)(2,1)S(1)}, bf16[96,1024]{1,0:T(8,128)(2,1)S(1)}, u32[]{:S(2)}, u32[]{:S(2)}) collective-permute-start(bf16[96,1024]{1,0:T(8,128)(2,1)S(1)} %multiply_convert_fusion.10), channel_id=1, source_target_pairs={{0,1},{1,2},{2,3},{3,0},{4,5},{5,6},{6,7},{7,4},{8,9},{9,10},{10,1... | collective-permute-start | bytes 589832 | tf_op jit(solution)/shard_map/ppermute | solution.py:121
  188.3 18.9 %collective-permute-start.1 = (bf16[96,1024]{1,0:T(8,128)(2,1)S(1)}, bf16[96,1024]{1,0:T(8,128)(2,1)}, u32[]{:S(2)}, u32[]{:S(2)}) collective-permute-start(bf16[96,1024]{1,0:T(8,128)(2,1)S(1)} %multiply_convert_fusion.10), channel_id=1, source_target_pairs={{0,2},{1,3},{2,0},{3,1},{4,6},{5,7},{6,4},{7,5},{8,10},{9,11},{10,... | collective-permute-start | bytes 589832 | tf_op jit(solution)/shard_map/ppermute | solution.py:121
  189.7 17.4 %collective-permute-start.2 = (bf16[96,1024]{1,0:T(8,128)(2,1)S(1)}, bf16[96,1024]{1,0:T(8,128)(2,1)}, u32[]{:S(2)}, u32[]{:S(2)}) collective-permute-start(bf16[96,1024]{1,0:T(8,128)(2,1)S(1)} %multiply_convert_fusion.10), channel_id=1, source_target_pairs={{0,3},{1,0},{2,1},{3,2},{4,7},{5,4},{6,5},{7,6},{8,11},{9,8},{10,9... | collective-permute-start | bytes 589832 | tf_op jit(solution)/shard_map/ppermute | solution.py:121
  220.0 17.7 %collective-permute-start.4 = (bf16[96,1024]{1,0:T(8,128)(2,1)S(1)}, bf16[96,1024]{1,0:T(8,128)(2,1)}, u32[]{:S(2)}, u32[]{:S(2)}) collective-permute-start(bf16[96,1024]{1,0:T(8,128)(2,1)S(1)} %get-tuple-element.406), channel_id=1, source_target_pairs={{0,2},{1,3},{2,0},{3,1},{4,6},{5,7},{6,4},{7,5},{8,10},{9,11},{10,... | collective-permute-start | bytes 589832 | tf_op jit(solution)/shard_map/ppermute | solution.py:121
  220.6 17.2 %collective-permute-start.5 = (bf16[96,1024]{1,0:T(8,128)(2,1)S(1)}, bf16[96,1024]{1,0:T(8,128)(2,1)}, u32[]{:S(2)}, u32[]{:S(2)}) collective-permute-start(bf16[96,1024]{1,0:T(8,128)(2,1)S(1)} %get-tuple-element.405), channel_id=1, source_target_pairs={{0,1},{1,2},{2,3},{3,0},{4,5},{5,6},{6,7},{7,4},{8,9},{9,10},{10,1... | collective-permute-start | bytes 589832 | tf_op jit(solution)/shard_map/ppermute | solution.py:121
  370.0 233.8 %reduce-scatter.3.cloned.1.call-start = ((), (), s32[]{:S(2)}) async-start(), calls=%async_computation.16 | async-start | bytes 7962624 | tf_op jit(solution)/shard_map/reduce_scatter | solution.py:600
  430.0 21.6 %collective-permute-start.7 = (bf16[384,1024]{1,0:T(8,128)(2,1)}, bf16[384,1024]{1,0:T(8,128)(2,1)}, u32[]{:S(2)}, u32[]{:S(2)}) collective-permute-start(bf16[384,1024]{1,0:T(8,128)(2,1)} %get-tuple-element.354), channel_id=1, source_target_pairs={{0,8},{8,16},{16,24},{24,0},{1,9},{9,17},{17,25},{25,1},{2,10},{10... | collective-permute-start | bytes 2359304 | tf_op jit(solution)/shard_map/ppermute | solution.py:121
  430.6 36.5 %collective-permute-start.8 = (bf16[384,1024]{1,0:T(8,128)(2,1)}, bf16[384,1024]{1,0:T(8,128)(2,1)}, u32[]{:S(2)}, u32[]{:S(2)}) collective-permute-start(bf16[384,1024]{1,0:T(8,128)(2,1)} %get-tuple-element.356), channel_id=1, source_target_pairs={{0,16},{8,24},{16,0},{24,8},{1,17},{9,25},{17,1},{25,9},{2,18},{10... | collective-permute-start | bytes 2359304 | tf_op jit(solution)/shard_map/ppermute | solution.py:121
  431.3 35.8 %collective-permute-start.9 = (bf16[384,1024]{1,0:T(8,128)(2,1)}, bf16[384,1024]{1,0:T(8,128)(2,1)}, u32[]{:S(2)}, u32[]{:S(2)}) collective-permute-start(bf16[384,1024]{1,0:T(8,128)(2,1)} %get-tuple-element.355), channel_id=1, source_target_pairs={{0,24},{8,0},{16,8},{24,16},{1,25},{9,1},{17,9},{25,17},{2,26},{10... | collective-permute-start | bytes 2359304 | tf_op jit(solution)/shard_map/ppermute | solution.py:121
  471.7 16.5 %collective-permute-start.11 = (bf16[96,1024]{1,0:T(8,128)(2,1)}, bf16[96,1024]{1,0:T(8,128)(2,1)}, u32[]{:S(2)}, u32[]{:S(2)}) collective-permute-start(bf16[96,1024]{1,0:T(8,128)(2,1)} %get-tuple-element.403), channel_id=1, source_target_pairs={{0,2},{1,3},{2,0},{3,1},{4,6},{5,7},{6,4},{7,5},{8,10},{9,11},{10,... | collective-permute-start | bytes 589832 | tf_op jit(solution)/shard_map/ppermute | solution.py:121
  472.4 15.8 %collective-permute-start.12 = (bf16[96,1024]{1,0:T(8,128)(2,1)}, bf16[96,1024]{1,0:T(8,128)(2,1)}, u32[]{:S(2)}, u32[]{:S(2)}) collective-permute-start(bf16[96,1024]{1,0:T(8,128)(2,1)} %get-tuple-element.402), channel_id=1, source_target_pairs={{0,3},{1,0},{2,1},{3,2},{4,7},{5,4},{6,5},{7,6},{8,11},{9,8},{10,9... | collective-permute-start | bytes 589832 | tf_op jit(solution)/shard_map/ppermute | solution.py:121
  522.0 263.0 %reduce-scatter.5.cloned.1.call-start = ((), (), s32[]{:S(2)}) async-start(), calls=%async_computation.17 | async-start | bytes 16515072 | tf_op jit(solution)/shard_map/reduce_scatter | solution.py:631
  529.8 12.7 %collective-permute-start.16 = (bf16[96,1024]{1,0:T(8,128)(2,1)S(1)}, bf16[96,1024]{1,0:T(8,128)(2,1)S(1)}, u32[]{:S(2)}, u32[]{:S(2)}) collective-permute-start(bf16[96,1024]{1,0:T(8,128)(2,1)S(1)} %get-tuple-element.398), channel_id=1, source_target_pairs={{0,3},{1,0},{2,1},{3,2},{4,7},{5,4},{6,5},{7,6},{8,11},{9,8},{10,9... | collective-permute-start | bytes 589832 | tf_op jit(solution)/shard_map/ppermute | solution.py:121
  537.0 16.4 %collective-permute-start.17 = (bf16[96,1024]{1,0:T(8,128)(2,1)S(1)}, bf16[96,1024]{1,0:T(8,128)(2,1)S(1)}, u32[]{:S(2)}, u32[]{:S(2)}) collective-permute-start(bf16[96,1024]{1,0:T(8,128)(2,1)S(1)} %get-tuple-element.400), channel_id=1, source_target_pairs={{0,2},{1,3},{2,0},{3,1},{4,6},{5,7},{6,4},{7,5},{8,10},{9,11},{10,... | collective-permute-start | bytes 589832 | tf_op jit(solution)/shard_map/ppermute | solution.py:121
  537.0 16.4 %collective-permute-start.18 = (bf16[96,1024]{1,0:T(8,128)(2,1)S(1)}, bf16[96,1024]{1,0:T(8,128)(2,1)S(1)}, u32[]{:S(2)}, u32[]{:S(2)}) collective-permute-start(bf16[96,1024]{1,0:T(8,128)(2,1)S(1)} %get-tuple-element.399), channel_id=1, source_target_pairs={{0,1},{1,2},{2,3},{3,0},{4,5},{5,6},{6,7},{7,4},{8,9},{9,10},{10,1... | collective-permute-start | bytes 589832 | tf_op jit(solution)/shard_map/ppermute | solution.py:121
  609.0 15.0 %collective-permute-start.19 = (bf16[208,1024]{1,0:T(8,128)(2,1)}, bf16[208,1024]{1,0:T(8,128)(2,1)}, u32[]{:S(2)}, u32[]{:S(2)}) collective-permute-start(bf16[208,1024]{1,0:T(8,128)(2,1)} %get-tuple-element.367), channel_id=1, source_target_pairs={{0,1},{1,2},{2,3},{3,0},{4,5},{5,6},{6,7},{7,4},{8,9},{9,10},{10,1... | collective-permute-start | bytes 1277960 | tf_op jit(solution)/shard_map/ppermute | solution.py:121
  609.1 31.2 %collective-permute-start.20 = (bf16[208,1024]{1,0:T(8,128)(2,1)}, bf16[208,1024]{1,0:T(8,128)(2,1)}, u32[]{:S(2)}, u32[]{:S(2)}) collective-permute-start(bf16[208,1024]{1,0:T(8,128)(2,1)} %get-tuple-element.366), channel_id=1, source_target_pairs={{0,2},{1,3},{2,0},{3,1},{4,6},{5,7},{6,4},{7,5},{8,10},{9,11},{10,... | collective-permute-start | bytes 1277960 | tf_op jit(solution)/shard_map/ppermute | solution.py:121
  610.5 29.8 %collective-permute-start.21 = (bf16[208,1024]{1,0:T(8,128)(2,1)S(1)}, bf16[208,1024]{1,0:T(8,128)(2,1)}, u32[]{:S(2)}, u32[]{:S(2)}) collective-permute-start(bf16[208,1024]{1,0:T(8,128)(2,1)S(1)} %get-tuple-element.365), channel_id=1, source_target_pairs={{0,3},{1,0},{2,1},{3,2},{4,7},{5,4},{6,5},{7,6},{8,11},{9,8},{10,9... | collective-permute-start | bytes 1277960 | tf_op jit(solution)/shard_map/ppermute | solution.py:121
  655.2 18.3 %collective-permute-start.25 = (bf16[144,1024]{1,0:T(8,128)(2,1)S(1)}, bf16[144,1024]{1,0:T(8,128)(2,1)S(1)}, u32[]{:S(2)}, u32[]{:S(2)}) collective-permute-start(bf16[144,1024]{1,0:T(8,128)(2,1)S(1)} %get-tuple-element.395), channel_id=1, source_target_pairs={{0,1},{1,2},{2,3},{3,0},{4,5},{5,6},{6,7},{7,4},{8,9},{9,10},{10,1... | collective-permute-start | bytes 884744 | tf_op jit(solution)/shard_map/ppermute | solution.py:121
  663.9 20.2 %collective-permute-start.26 = (bf16[144,1024]{1,0:T(8,128)(2,1)S(1)}, bf16[144,1024]{1,0:T(8,128)(2,1)S(1)}, u32[]{:S(2)}, u32[]{:S(2)}) collective-permute-start(bf16[144,1024]{1,0:T(8,128)(2,1)S(1)} %get-tuple-element.396), channel_id=1, source_target_pairs={{0,2},{1,3},{2,0},{3,1},{4,6},{5,7},{6,4},{7,5},{8,10},{9,11},{10,... | collective-permute-start | bytes 884744 | tf_op jit(solution)/shard_map/ppermute | solution.py:121
  666.0 18.1 %collective-permute-start.27 = (bf16[144,1024]{1,0:T(8,128)(2,1)S(1)}, bf16[144,1024]{1,0:T(8,128)(2,1)S(1)}, u32[]{:S(2)}, u32[]{:S(2)}) collective-permute-start(bf16[144,1024]{1,0:T(8,128)(2,1)S(1)} %get-tuple-element.397), channel_id=1, source_target_pairs={{0,3},{1,0},{2,1},{3,2},{4,7},{5,4},{6,5},{7,6},{8,11},{9,8},{10,9... | collective-permute-start | bytes 884744 | tf_op jit(solution)/shard_map/ppermute | solution.py:121
  685.3 16.4 %all-to-all-start.8 = ((f32[32,1,352]{2,1,0:T(1,128)}), f32[32,1,352]{2,1,0:T(1,128)S(1)}, u32[]{:S(2)}, u32[]{:S(2)}) async-start(f32[32,1,352]{2,1,0:T(1,128)} %copy.127), calls=%async_computation.10 | async-start | bytes 98304 | tf_op jit(solution)/shard_map/all_to_all | solution.py:111
  701.6 50.8 %all-to-all-start.9 = ((bf16[32,32,1024]{2,1,0:T(8,128)(2,1)}), bf16[32,32,1024]{2,1,0:T(8,128)(2,1)}, u32[]{:S(2)}, u32[]{:S(2)}) async-start(bf16[32,32,1024]{2,1,0:T(8,128)(2,1)} %bitcast.116), calls=%async_computation.11 | async-start | bytes 4194304 | tf_op jit(solution)/shard_map/all_to_all | solution.py:111
  789.1 16.6 %collective-permute-start.22 = (bf16[2,128,1024]{2,1,0:T(8,128)(2,1)}, bf16[2,128,1024]{2,1,0:T(8,128)(2,1)}, u32[]{:S(2)}, u32[]{:S(2)}) collective-permute-start(bf16[2,128,1024]{2,1,0:T(8,128)(2,1)} %get-tuple-element.359), channel_id=1, source_target_pairs={{0,1},{1,2},{2,3},{3,0},{4,5},{5,6},{6,7},{7,4},{8,9},{9,10},{10,1... | collective-permute-start | bytes 1572872 | tf_op jit(solution)/shard_map/ppermute | solution.py:121
  792.8 35.9 %collective-permute-start.23 = (bf16[2,128,1024]{2,1,0:T(8,128)(2,1)}, bf16[2,128,1024]{2,1,0:T(8,128)(2,1)}, u32[]{:S(2)}, u32[]{:S(2)}) collective-permute-start(bf16[2,128,1024]{2,1,0:T(8,128)(2,1)} %get-tuple-element.361), channel_id=1, source_target_pairs={{0,2},{1,3},{2,0},{3,1},{4,6},{5,7},{6,4},{7,5},{8,10},{9,11},{10,... | collective-permute-start | bytes 1572872 | tf_op jit(solution)/shard_map/ppermute | solution.py:121
  792.8 35.9 %collective-permute-start.24 = (bf16[2,128,1024]{2,1,0:T(8,128)(2,1)}, bf16[2,128,1024]{2,1,0:T(8,128)(2,1)}, u32[]{:S(2)}, u32[]{:S(2)}) collective-permute-start(bf16[2,128,1024]{2,1,0:T(8,128)(2,1)} %get-tuple-element.360), channel_id=1, source_target_pairs={{0,3},{1,0},{2,1},{3,2},{4,7},{5,4},{6,5},{7,6},{8,11},{9,8},{10,9... | collective-permute-start | bytes 1572872 | tf_op jit(solution)/shard_map/ppermute | solution.py:121
  835.3 20.7 %all-to-all-start.10 = ((f32[32,1,31]{2,1,0:T(1,128)}), f32[32,1,31]{2,1,0:T(1,128)S(1)}, u32[]{:S(2)}, u32[]{:S(2)}) async-start(f32[32,1,31]{2,1,0:T(1,128)} %broadcast_in_dim.315), calls=%async_computation.12 | async-start | bytes 32768 | tf_op jit(solution)/shard_map/all_to_all | solution.py:116
  869.3 15.5 %collective-permute-start.37 = (bf16[128,1024]{1,0:T(8,128)(2,1)}, bf16[128,1024]{1,0:T(8,128)(2,1)}, u32[]{:S(2)}, u32[]{:S(2)}) collective-permute-start(bf16[128,1024]{1,0:T(8,128)(2,1)} %get-tuple-element.391), channel_id=1, source_target_pairs={{0,16},{8,24},{16,0},{24,8},{1,17},{9,25},{17,1},{25,9},{2,18},{10... | collective-permute-start | bytes 786440 | tf_op jit(solution)/shard_map/ppermute | solution.py:121
  869.8 15.0 %collective-permute-start.38 = (bf16[128,1024]{1,0:T(8,128)(2,1)}, bf16[128,1024]{1,0:T(8,128)(2,1)}, u32[]{:S(2)}, u32[]{:S(2)}) collective-permute-start(bf16[128,1024]{1,0:T(8,128)(2,1)} %get-tuple-element.390), channel_id=1, source_target_pairs={{0,24},{8,0},{16,8},{24,16},{1,25},{9,1},{17,9},{25,17},{2,26},{10... | collective-permute-start | bytes 786440 | tf_op jit(solution)/shard_map/ppermute | solution.py:121
  874.4 15.9 %collective-permute-start.31 = (bf16[128,1024]{1,0:T(8,128)(2,1)S(1)}, bf16[128,1024]{1,0:T(8,128)(2,1)S(1)}, u32[]{:S(2)}, u32[]{:S(2)}) collective-permute-start(bf16[128,1024]{1,0:T(8,128)(2,1)S(1)} %get-tuple-element.428), channel_id=1, source_target_pairs={{0,8},{8,16},{16,24},{24,0},{1,9},{9,17},{17,25},{25,1},{2,10},{10... | collective-permute-start | bytes 786440 | tf_op jit(solution)/shard_map/ppermute | solution.py:121
  875.3 20.6 %collective-permute-start.32 = (bf16[128,1024]{1,0:T(8,128)(2,1)S(1)}, bf16[128,1024]{1,0:T(8,128)(2,1)S(1)}, u32[]{:S(2)}, u32[]{:S(2)}) collective-permute-start(bf16[128,1024]{1,0:T(8,128)(2,1)S(1)} %get-tuple-element.429), channel_id=1, source_target_pairs={{0,16},{8,24},{16,0},{24,8},{1,17},{9,25},{17,1},{25,9},{2,18},{10... | collective-permute-start | bytes 786440 | tf_op jit(solution)/shard_map/ppermute | solution.py:121
  879.1 17.3 %collective-permute-start.33 = (bf16[128,1024]{1,0:T(8,128)(2,1)S(1)}, bf16[128,1024]{1,0:T(8,128)(2,1)S(1)}, u32[]{:S(2)}, u32[]{:S(2)}) collective-permute-start(bf16[128,1024]{1,0:T(8,128)(2,1)S(1)} %get-tuple-element.427), channel_id=1, source_target_pairs={{0,24},{8,0},{16,8},{24,16},{1,25},{9,1},{17,9},{25,17},{2,26},{10... | collective-permute-start | bytes 786440 | tf_op jit(solution)/shard_map/ppermute | solution.py:121
  886.1 15.5 %collective-permute-start.39 = (bf16[128,1024]{1,0:T(8,128)(2,1)S(1)}, bf16[128,1024]{1,0:T(8,128)(2,1)S(1)}, u32[]{:S(2)}, u32[]{:S(2)}) collective-permute-start(bf16[128,1024]{1,0:T(8,128)(2,1)S(1)} %fusion.92), channel_id=1, source_target_pairs={{0,8},{8,16},{16,24},{24,0},{1,9},{9,17},{17,25},{25,1},{2,10},{10... | collective-permute-start | bytes 786440 | tf_op jit(solution)/shard_map/ppermute | solution.py:121
  887.2 18.5 %collective-permute-start.40 = (bf16[128,1024]{1,0:T(8,128)(2,1)S(1)}, bf16[128,1024]{1,0:T(8,128)(2,1)S(1)}, u32[]{:S(2)}, u32[]{:S(2)}) collective-permute-start(bf16[128,1024]{1,0:T(8,128)(2,1)S(1)} %fusion.92), channel_id=1, source_target_pairs={{0,16},{8,24},{16,0},{24,8},{1,17},{9,25},{17,1},{25,9},{2,18},{10... | collective-permute-start | bytes 786440 | tf_op jit(solution)/shard_map/ppermute | solution.py:121
  890.3 15.4 %collective-permute-start.41 = (bf16[128,1024]{1,0:T(8,128)(2,1)S(1)}, bf16[128,1024]{1,0:T(8,128)(2,1)S(1)}, u32[]{:S(2)}, u32[]{:S(2)}) collective-permute-start(bf16[128,1024]{1,0:T(8,128)(2,1)S(1)} %fusion.92), channel_id=1, source_target_pairs={{0,24},{8,0},{16,8},{24,16},{1,25},{9,1},{17,9},{25,17},{2,26},{10... | collective-permute-start | bytes 786440 | tf_op jit(solution)/shard_map/ppermute | solution.py:121
  895.9 76.9 %collective-permute-start.28 = (bf16[2,32,1024]{2,1,0:T(8,128)(2,1)}, bf16[2,32,1024]{2,1,0:T(8,128)(2,1)}, u32[]{:S(2)}, u32[]{:S(2)}) collective-permute-start(bf16[2,32,1024]{2,1,0:T(8,128)(2,1)} %get-tuple-element.418), channel_id=1, source_target_pairs={{0,1},{1,2},{2,3},{3,0},{4,5},{5,6},{6,7},{7,4},{8,9},{9,10},{10,1... | collective-permute-start | bytes 393224 | tf_op jit(solution)/shard_map/ppermute | solution.py:121
  896.4 76.5 %collective-permute-start.29 = (bf16[2,32,1024]{2,1,0:T(8,128)(2,1)}, bf16[2,32,1024]{2,1,0:T(8,128)(2,1)}, u32[]{:S(2)}, u32[]{:S(2)}) collective-permute-start(bf16[2,32,1024]{2,1,0:T(8,128)(2,1)} %get-tuple-element.417), channel_id=1, source_target_pairs={{0,2},{1,3},{2,0},{3,1},{4,6},{5,7},{6,4},{7,5},{8,10},{9,11},{10,... | collective-permute-start | bytes 393224 | tf_op jit(solution)/shard_map/ppermute | solution.py:121
  901.6 71.3 %collective-permute-start.30 = (bf16[2,32,1024]{2,1,0:T(8,128)(2,1)}, bf16[2,32,1024]{2,1,0:T(8,128)(2,1)}, u32[]{:S(2)}, u32[]{:S(2)}) collective-permute-start(bf16[2,32,1024]{2,1,0:T(8,128)(2,1)} %get-tuple-element.416), channel_id=1, source_target_pairs={{0,3},{1,0},{2,1},{3,2},{4,7},{5,4},{6,5},{7,6},{8,11},{9,8},{10,9... | collective-permute-start | bytes 393224 | tf_op jit(solution)/shard_map/ppermute | solution.py:121
  905.7 29.1 %collective-permute-start.34 = (bf16[512,1024]{1,0:T(8,128)(2,1)}, bf16[512,1024]{1,0:T(8,128)(2,1)}, u32[]{:S(2)}, u32[]{:S(2)}) collective-permute-start(bf16[512,1024]{1,0:T(8,128)(2,1)} %pad_maximum_fusion.11), channel_id=1, source_target_pairs={{0,4},{4,0},{1,5},{5,1},{2,6},{6,2},{3,7},{7,3},{8,12},{12,8},{9,1... | collective-permute-start | bytes 3145736 | tf_op jit(solution)/shard_map/ppermute | solution.py:161
  906.0 31.0 %collective-permute-start.42 = (bf16[512,1024]{1,0:T(8,128)(2,1)S(1)}, bf16[512,1024]{1,0:T(8,128)(2,1)S(1)}, u32[]{:S(2)}, u32[]{:S(2)}) collective-permute-start(bf16[512,1024]{1,0:T(8,128)(2,1)S(1)} %bitcast.413), channel_id=1, source_target_pairs={{0,4},{4,0},{1,5},{5,1},{2,6},{6,2},{3,7},{7,3},{8,12},{12,8},{9,1... | collective-permute-start | bytes 3145736 | tf_op jit(solution)/shard_map/ppermute | solution.py:161
  978.0 12.7 %collective-permute-start.45 = (bf16[128,1024]{1,0:T(8,128)(2,1)S(1)}, bf16[128,1024]{1,0:T(8,128)(2,1)S(1)}, u32[]{:S(2)}, u32[]{:S(2)}) collective-permute-start(bf16[128,1024]{1,0:T(8,128)(2,1)S(1)} %get-tuple-element.383), channel_id=1, source_target_pairs={{0,16},{8,24},{16,0},{24,8},{1,17},{9,25},{17,1},{25,9},{2,18},{10... | collective-permute-start | bytes 786440 | tf_op jit(solution)/shard_map/ppermute | solution.py:121
  981.0 27.2 %collective-permute-start.49 = (bf16[144,1024]{1,0:T(8,128)(2,1)S(1)}, bf16[144,1024]{1,0:T(8,128)(2,1)S(1)}, u32[]{:S(2)}, u32[]{:S(2)}) collective-permute-start(bf16[144,1024]{1,0:T(8,128)(2,1)S(1)} %get-tuple-element.373), channel_id=1, source_target_pairs={{0,2},{1,3},{2,0},{3,1},{4,6},{5,7},{6,4},{7,5},{8,10},{9,11},{10,... | collective-permute-start | bytes 884744 | tf_op jit(solution)/shard_map/ppermute | solution.py:121
  984.9 23.3 %collective-permute-start.50 = (bf16[144,1024]{1,0:T(8,128)(2,1)S(1)}, bf16[144,1024]{1,0:T(8,128)(2,1)S(1)}, u32[]{:S(2)}, u32[]{:S(2)}) collective-permute-start(bf16[144,1024]{1,0:T(8,128)(2,1)S(1)} %get-tuple-element.372), channel_id=1, source_target_pairs={{0,1},{1,2},{2,3},{3,0},{4,5},{5,6},{6,7},{7,4},{8,9},{9,10},{10,1... | collective-permute-start | bytes 884744 | tf_op jit(solution)/shard_map/ppermute | solution.py:121
  (186 other events, 2899.4 us)
Sparse Core Ops, SparseCore 0:
  11.6 142.2 all-gather.3
  156.3 47.8 all-gather.5
  242.0 68.5 all-gather.7
  522.1 68.9 reduce-scatter.2
  643.1 130.8 reduce-scatter.4

commit v5 on v4

--- a/solution.py
+++ b/solution.py
@@ -307,6 +307,106 @@
             flops=18 * size**3, bytes_accessed=6 * size * size, transcendentals=0
         ),
     )(gram)
+
+
+def logits_kernel(target_ref, answers_ref, table_ref, shares_ref, stats_ref, logits):
+    rows, width = logits.shape
+    piece = 256
+    target = target_ref[...]
+    top = jnp.full((8, width), -jnp.inf, jnp.float32)
+    total = jnp.zeros((8, width), jnp.float32)
+    picked = jnp.zeros((8, width), jnp.float32)
+    for first in range(0, rows, piece):
+        scores = lax.dot_general(
+            table_ref[first : first + piece, :],
+            answers_ref[...],
+            (((1,), (1,)), ((), ())),
+            preferred_element_type=jnp.float32,
+        )
+        logits[first : first + piece, :] = scores
+        top = jnp.maximum(top, jnp.max(scores.reshape(-1, 8, width), axis=0))
+    top = jnp.max(top, axis=0, keepdims=True)
+    for first in range(0, rows, piece):
+        scores = logits[first : first + piece, :]
+        share = jnp.exp(scores - top)
+        shares_ref[first : first + piece, :] = share.astype(jnp.bfloat16)
+        total = total + jnp.sum(share.reshape(-1, 8, width), axis=0)
+        place = lax.broadcasted_iota(jnp.int32, (piece, width), 0)
+        hit = jnp.where(place == target - first, scores, 0.0)
+        picked = picked + jnp.sum(hit.reshape(-1, 8, width), axis=0)
+    stats_ref[0:1, :] = top
+    stats_ref[1:2, :] = jnp.sum(total, axis=0, keepdims=True)
+    stats_ref[2:3, :] = jnp.sum(picked, axis=0, keepdims=True)
+    stats_ref[3:8, :] = jnp.zeros((5, width), jnp.float32)
+
+
+def answer_shares(target, answers, table):
+    count, rows = answers.shape[0], table.shape[0]
+    tile = 256
+    return pl.pallas_call(
+        logits_kernel,
+        grid=(count // tile,),
+        in_specs=[
+            pl.BlockSpec((1, tile), lambda i: (0, i)),
+            pl.BlockSpec((tile, D), lambda i: (i, 0)),
+            pl.BlockSpec((rows, D), lambda i: (0, 0)),
+        ],
+        out_specs=[
+            pl.BlockSpec((rows, tile), lambda i: (0, i)),
+            pl.BlockSpec((8, tile), lambda i: (0, i)),
+        ],
+        out_shape=[
+            jax.ShapeDtypeStruct((rows, count), jnp.bfloat16),
+            jax.ShapeDtypeStruct((8, count), jnp.float32),
+        ],
+        scratch_shapes=[pltpu.VMEM((rows, tile), jnp.float32)],
+        compiler_params=pltpu.CompilerParams(vmem_limit_bytes=40 * 1024 * 1024),
+        cost_estimate=pl.CostEstimate(
+            flops=2 * count * rows * D,
+            bytes_accessed=2 * count * (rows + D),
+            transcendentals=count * rows,
+        ),
+    )(target, answers, table)
+
+
+def logit_grads(place, target, scale, value, shares):
+    return jnp.where(place == target, value, shares.astype(jnp.float32) * scale).astype(jnp.bfloat16)
+
+
+def grads_kernel(core_ref, target_ref, scale_ref, value_ref, shares_ref, table_ref, grads_ref):
+    place = lax.broadcasted_iota(jnp.int32, shares_ref.shape, 0)
+    grads = logit_grads(place, target_ref[...], scale_ref[...], value_ref[...], shares_ref[...])
+    grads_ref[...] = lax.dot_general(
+        grads, table_ref[...], (((0,), (0,)), ((), ())), preferred_element_type=jnp.float32
+    ).astype(jnp.bfloat16)
+
+
+def answer_grads(core, target, scale, value, shares, table, width):
+    rows, count = shares.shape
+    steps = count // (2 * width)
+    row = pl.BlockSpec((1, width), lambda i, core_ref: (0, 2 * i + core_ref[0]))
+    return pl.pallas_call(
+        grads_kernel,
+        grid_spec=pltpu.PrefetchScalarGridSpec(
+            num_scalar_prefetch=1,
+            grid=(steps,),
+            in_specs=[
+                row,
+                row,
+                row,
+                pl.BlockSpec((rows, width), lambda i, core_ref: (0, 2 * i + core_ref[0])),
+                pl.BlockSpec((rows, D), lambda i, core_ref: (0, 0)),
+            ],
+            out_specs=pl.BlockSpec((width, D), lambda i, core_ref: (i, 0)),
+        ),
+        out_shape=jax.ShapeDtypeStruct((steps * width, D), jnp.bfloat16),
+        compiler_params=pltpu.CompilerParams(vmem_limit_bytes=40 * 1024 * 1024),
+        cost_estimate=pl.CostEstimate(
+            flops=2 * steps * width * rows * D,
+            bytes_accessed=2 * steps * width * (rows + D),
+            transcendentals=0,
+        ),
+    )(core.reshape(1), target, scale, value, shares, table)
 
 
 def body(
@@ -474,37 +574,42 @@
     hidden3 = hidden2 + member_return(ffn_part.astype(jnp.bfloat16).reshape(members, RESP, D))
     final_b = rms_scale(hidden3, gains[3]).astype(jnp.bfloat16)
     response_tokens = lax.all_gather(final_b, ALL, axis=0, tiled=True)
-    logit_scores = dense(response_tokens, table_b)
-    local_target = jnp.where(targets // block_rows == device, targets % block_rows, -1)
-    onehot = jnp.arange(block_rows)[None, :] == local_target[:, None]
-    top = jnp.max(logit_scores, axis=-1)
-    exp_total = jnp.sum(jnp.exp(logit_scores - top[:, None]), axis=-1)
-    picked = jnp.sum(jnp.where(onehot, logit_scores, 0.0), axis=-1)
-    stats = jnp.stack([top, exp_total, picked]).reshape(3, devices, RESP).transpose(1, 0, 2)
+    local_target = jnp.where(targets // block_rows == device, targets % block_rows, -1)[None, :]
+    shares, own_stats = answer_shares(local_target, response_tokens, table_b)
+    stats = own_stats[:3].reshape(3, devices, RESP).transpose(1, 0, 2)
     stats = exchanged(stats)
     top = jnp.max(stats[:, 0], axis=0)
     exp_total = jnp.sum(stats[:, 1] * jnp.exp(stats[:, 0] - top[None, :]), axis=0)
     own_log_total = top + jnp.log(exp_total)
     own_logp = jnp.sum(jnp.sum(stats[:, 2], axis=0) - own_log_total)
     joined = spread(jnp.concatenate([own_log_total, own_logp[None]]))
-    log_total = joined[:, :RESP].reshape(-1)
+    log_total = joined[:, :RESP].reshape(1, -1)
     margin = jnp.sum(pair_rows * joined[:, RESP][None, :], axis=1, keepdims=True)
     pair_loss = 0.5 * jnp.sum(jax.nn.softplus(-margin))
     grad_logp = chosen_sign * jax.nn.sigmoid(-margin) * (-pref_beta / RESP)
-    row_weight = jnp.broadcast_to(grad_logp, (devices, RESP)).reshape(-1)
-    softmax_rows = jnp.exp(logit_scores - log_total[:, None])
-    grad_logits = (row_weight[:, None] * (onehot.astype(jnp.float32) - softmax_rows)).astype(
+    row_weight = jnp.broadcast_to(grad_logp, (devices, RESP)).reshape(1, -1)
+    share_scale = -row_weight * jnp.exp(own_stats[0:1] - log_total)
+    target_value = row_weight * (1.0 - jnp.exp(own_stats[2:3] - log_total))
+    given, kept = (
+        answer_grads(
+            which, local_target, share_scale, target_value, shares, table_b, members * RESP
+        )
+        for which in (1 - core, core)
+    )
+    grad_answer_pair = (kept.astype(jnp.float32) + other_core(given).astype(jnp.float32)).astype(
         jnp.bfloat16
     )
-    grad_answers = jnp.dot(grad_logits, table_b, preferred_element_type=jnp.float32)
-    grad_table = outer(grad_logits, response_tokens)
-    grad_answer_pair = pair_sum(
-        grad_answers.astype(jnp.bfloat16)
-        .reshape(groups // 2, 2, members * RESP, D)
-        .transpose(1, 0, 2, 3),
-        core,
-    )
-    grad_answer_group = chip_sum(grad_answer_pair).astype(jnp.bfloat16)
+    grad_answer_group = chip_sum(grad_answer_pair.reshape(groups // 2, members * RESP, D))
+    grad_table = jnp.dot(
+        logit_grads(
+            jnp.arange(block_rows)[:, None], local_target, share_scale, target_value, shares
+        ),
+        response_tokens,
+        preferred_element_type=jnp.float32,
+    )
+    grad_answer_group, grad_table = lax.optimization_barrier(
+        (grad_answer_group.astype(jnp.bfloat16), grad_table)
+    )
     grad_final = member_scatter(grad_answer_group.reshape(members, RESP, D))
     grad_hidden3, grad_gain3 = norm_back(hidden3, gains[3], grad_final)
     grad_ffn_out = member_gather(grad_hidden3.astype(jnp.bfloat16))
@@ -557,6 +662,31 @@
     grad_pair_w = outer(grad_pair_b, act2)
     grad_norm1, grad_gain1 = norm_back(hidden1, gains[1], grad_act2)
     grad_hidden1 = placed(grad_hidden2) + grad_norm1
+    squares, square_rows = square_master.shape[0], square_master.shape[1]
+    wides, wide_rows = wide_master.shape[0], wide_master.shape[1]
+    per_member = -(-squares // members)
+    group_rows = members * square_rows
+
+    def by_member(values):
+        values = jnp.pad(values, ((0, per_member * members - squares), (0, 0), (0, 0)))
+        return values.reshape(per_member, members, -1, D).transpose(1, 0, 2, 3)
+
+    def wide_by_member(values):
+        return jnp.pad(values, ((0, members - wides), (0, 0), (0, 0)))
+
+    moment_jobs = jnp.concatenate(
+        [
+            wide_by_member(wide_moment.astype(jnp.bfloat16)),
+            by_member(square_moment.astype(jnp.bfloat16)).reshape(members, -1, D),
+        ],
+        axis=1,
+    )
+    moment_jobs = jnp.stack(handed_out(moment_jobs, "vocab"))
+    grad_hidden1, moment_jobs = lax.optimization_barrier((grad_hidden1, moment_jobs))
+    wide_moment_job = moment_jobs[:, :wide_rows]
+    square_moment_job = placed_before(list(moment_jobs[:, wide_rows:]), "vocab")
+    square_moment_job = square_moment_job.reshape(members, per_member, square_rows, D)
+    square_moment_job = square_moment_job.transpose(1, 0, 2, 3).reshape(per_member, group_rows, D)
     grad_mix_out = grad_hidden1.astype(jnp.bfloat16)
     grad_mixer = back_dense(grad_mix_out, square_b[3])
     grad_mixer_w = outer(grad_mix_out, mixer)
@@ -599,35 +729,8 @@
     )
     share_wide_b = lax.psum_scatter(grad_wide, DP, scatter_dimension=1, tiled=True)
     share_wide = share_wide_b.astype(jnp.float32)
-    squares, square_rows = square_master.shape[0], square_master.shape[1]
-    wides, wide_rows = wide_master.shape[0], wide_master.shape[1]
-    per_member = -(-squares // members)
-    group_rows = members * square_rows
-
-    def by_member(values):
-        values = jnp.pad(values, ((0, per_member * members - squares), (0, 0), (0, 0)))
-        return values.reshape(per_member, members, -1, D).transpose(1, 0, 2, 3)
-
-    def wide_by_member(values):
-        return jnp.pad(values, ((0, members - wides), (0, 0), (0, 0)))
-
-    moment_jobs = jnp.concatenate(
-        [
-            wide_by_member(wide_moment.astype(jnp.bfloat16)),
-            by_member(square_moment.astype(jnp.bfloat16)).reshape(members, -1, D),
-        ],
-        axis=1,
-    )
-    moment_jobs = jnp.stack(handed_out(moment_jobs, "vocab"))
-    grad_square, share_wide_b, moment_jobs = lax.optimization_barrier(
-        (grad_square, share_wide_b, moment_jobs)
-    )
-    wide_moment_job = moment_jobs[:, :wide_rows]
-    square_moment_job = placed_before(list(moment_jobs[:, wide_rows:]), "vocab")
-    square_moment_job = square_moment_job.reshape(members, per_member, square_rows, D)
-    square_moment_job = square_moment_job.transpose(1, 0, 2, 3).reshape(per_member, group_rows, D)
+    grad_square, share_wide_b = lax.optimization_barrier((grad_square, share_wide_b))
     wide_grad_job = jnp.stack(handed_out(wide_by_member(share_wide_b), "vocab"))
-    grad_embed_b, wide_grad_job = lax.optimization_barrier((grad_embed_b, wide_grad_job))
     group_square = lax.psum_scatter(grad_square, DP, scatter_dimension=1, tiled=True)
     square_grad_job = member_scatter(by_member(group_square))
 
@@ -639,16 +742,19 @@
 
     share_square = from_members(square_grad_job)
 
-    def returned(wanted, row_keys):
+    def returned(row_keys):
         rows = outer(onehot_rows(row_keys, devices * SLOTS), grad_embed_b)
-        rows = exchanged(rows.astype(jnp.bfloat16))
+        return exchanged(rows.astype(jnp.bfloat16))
+
+    def put(wanted, rows):
         return outer(onehot_rows(wanted, block_rows), rows)
 
     def return_more(turn, total):
         later_keys, later_asked = later_round(turn)
-        return total + returned(later_asked, later_keys)
-
-    share_table = lax.fori_loop(1, turns, return_more, grad_table + returned(asked, keys))
+        return total + put(later_asked, returned(later_keys))
+
+    returned_rows, wide_grad_job = lax.optimization_barrier((returned(keys), wide_grad_job))
+    share_table = lax.fori_loop(1, turns, return_more, grad_table + put(asked, returned_rows))
     width = vector_master.shape[1]
     vector_notes = grad_vector.reshape(-1, devices, width).transpose(1, 0, 2).reshape(devices, -1)
     vector_notes = jnp.concatenate(
@@ -730,9 +836,6 @@
     wide_gram = group_sum(outer(wide_job, wide_job).astype(jnp.bfloat16), core)
     square_gram = outer(square_job, square_job)
     gram = jnp.where(core == 0, wide_gram.astype(jnp.float32), square_gram)
-    gram, share_square, table_step, table_first_new, table_second_new = lax.optimization_barrier(
-        (gram, share_square, table_step, table_first_new, table_second_new)
-    )
     rest_b = ortho_rest(gram)
     power = leading_coefficient**NS_ITERS
     wide_rest = jnp.where(core == 0, rest_b, other_core(rest_b))

time: 1040 us -> 1000 us (0.962)
  matrix products: 176 us -> 126 us
  Pallas kernels: 25.2 us -> 71.3 us
  waiting for transfers between devices: 444 us -> 489 us
  other arithmetic: 143 us -> 110 us
  starting transfers between devices: 118 us -> 93.5 us
  local copies, waits for them, and re-layouts: 94.5 us -> 73.2 us
    ppermute x48, waiting for transfers between devices: 201 us -> 255 us  [turned(): lax.ppermute(values, axis, [(i, (i + step) % count) for i in range(count)])]
    pallas_call x0 -> x3, Pallas kernels: none -> 46.1 us  [the longest x1 25.4 us: answer_shares(): pl.pallas_call(logits_kernel, grid=(count // tile,), in_specs=[pl.BlockSp...]
    all_to_all x5, waiting for transfers between devices: 139 us -> 95.6 us  [exchanged(): return lax.all_to_all(rows, ALL, 0, 0, tiled=True)]
    dot_general x12 -> x11, matrix products: 61.8 us -> 37.1 us  [outer(): lax.dot_general(grads, inputs, (((0,), (0,)), ((), ())), preferred_elemen...]
    dot_general x8 -> x7, matrix products: 41.4 us -> 19.5 us  [dense(): lax.dot_general(inputs, weight, (((1,), (1,)), ((), ())), preferred_eleme...]
    reduce_scatter x1, waiting for transfers between devices: 0.01 us -> 16.8 us  [body(): lax.psum_scatter(grad_wide, DP, scatter_dimension=1, tiled=True)]
    all_gather x1, waiting for transfers between devices: 58.7 us -> 74.5 us  [body(): response_tokens = lax.all_gather(final_b, ALL, axis=0, tiled=True)]
    reduce_sum x1 -> x0, other arithmetic: 12.4 us -> none  [body(): exp_total = jnp.sum(jnp.exp(logit_scores - top[:, None]), axis=-1)]
  transfers between devices with their start and end apart: 66 -> 66, of which waited for: 39 -> 39; matrix products, arithmetic and copies ran while one was open for 23% -> 20% of each run, Pallas kernels for 2% -> 4%
where the time goes in v5:
time: 1000 us; the launch traced here: 994 us
  waiting for transfers between devices  489 us (49%)
  matrix products  126 us (13%)
  other arithmetic  110 us (11%)
  starting transfers between devices  93.5 us (9%)
  local copies, waits for them, and re-layouts  73.2 us (7%)
  Pallas kernels  71.3 us (7%)
  between operations  30.3 us (3%)
    ppermute x48, waiting for transfers between devices, turned(): lax.ppermute(values, axis, [(i, (i + step) % count) for i in range(count)])  255 us
    all_to_all x5, waiting for transfers between devices, exchanged(): return lax.all_to_all(rows, ALL, 0, 0, tiled=True)  95.6 us
    all_gather x1, waiting for transfers between devices, body(): response_tokens = lax.all_gather(final_b, ALL, axis=0, tiled=True)  74.5 us
    ppermute x48, starting transfers between devices, turned(): lax.ppermute(values, axis, [(i, (i + step) % count) for i in range(count)])  63.8 us
    dot_general x11, matrix products, outer(): lax.dot_general(grads, inputs, (((0,), (0,)), ((), ())), preferred_elemen...  37.1 us
    unnamed x342, local copies, waits for them, and re-layouts  31.8 us
    dot_general x6, matrix products, back_dense(): return jnp.dot(grads, weight, preferred_element_type=jnp.float32)  26.9 us
    pallas_call x1, Pallas kernels, answer_shares(): pl.pallas_call(logits_kernel, grid=(count // tile,), in_specs=[pl.BlockSp...  25.4 us
  transfers between devices with their start and end apart: 66, of which 39 were waited for; matrix products, arithmetic and copies ran while one was open for 20% of the time, Pallas kernels for 4%

profile of v5, /device:TPU:0, one launch (start us, length us, event | category | flops | bytes accessed | tf_op | source)
XLA Modules:
  0.0 993.9 jit_solution(16744882315420549258)
XLA Ops:
  19.0 7.3 all-to-all-start.4
  26.3 6.1 convert_element_type.403.table_ref
  34.5 8.1 fusion.50
  42.5 4.0 all-to-all-start.5
  52.0 82.7 %all-to-all-done.5 = bf16[32,32,1024]{2,1,0:T(8,128)(2,1)} async-done(((bf16[32,32,1024]{2,1,0:T(8,128)(2,1)}), bf16[32,32,1024]{2,1,0:T(8,128)(2,1)}, u32[]{:S(2)}, u32[]{:S(2)}) %all-to-all-start.5) | async-done | bytes 2097184 | tf_op jit(solution)/shard_map/all_to_all | solution.py:111
  134.7 4.2 fusion.44
  141.0 12.9 %all-gather.4.cloned.1.call-done = bf16[7,1024,1024]{2,1,0:T(8,128)(2,1)} async-done(((bf16[7,32,1024]{2,1,0:T(8,128)(2,1)}), bf16[7,1024,1024]{2,1,0:T(8,128)(2,1)}) %all-gather.4.cloned.1.call-update) | async-done | bytes 14680080 | tf_op jit(solution)/shard_map/all_gather | solution.py:467
  153.9 6.2 slice.364
  160.2 6.0 fusion.151
  193.9 10.4 %all-gather.6.cloned.1.call-done = bf16[3,1152,1024]{2,1,0:T(8,128)(2,1)} async-done(((bf16[3,144,1024]{2,1,0:T(8,128)(2,1)}), bf16[3,1152,1024]{2,1,0:T(8,128)(2,1)}) %all-gather.6.cloned.1.call-update) | async-done | bytes 7077904 | tf_op jit(solution)/shard_map/all_gather | solution.py:468
  224.1 7.8 collective-permute-done.4
  234.3 74.5 %all-gather.8.cloned.1.call-done.answers_ref = bf16[3072,1024]{1,0:T(8,128)(2,1)} async-done(((bf16[96,1024]{1,0:T(8,128)(2,1)}), bf16[3072,1024]{1,0:T(8,128)(2,1)}) %all-gather.8.cloned.1.call-update) | async-done | bytes 6291472 | tf_op jit(solution)/shard_map/all_gather | solution.py:576
  311.7 25.4 %shard_map.313 = (bf16[2048,3072]{1,0:T(8,128)(2,1)}, f32[8,3072]{1,0:T(8,128)S(1)}) custom-call(s32[1,3072]{1,0:T(1,128)S(1)} %compare_select_fusion.target_ref, bf16[3072,1024]{1,0:T(8,128)(2,1)S(1)} %copy-done, bf16[2048,1024]{1,0:T(8,128)(2,1)} %get-tuple-element.663), custom_call_target="tpu_custom_call" | custom-call | flops 12884901888 | bytes 18874368 | tf_op jit(solution)/shard_map/pallas_call | solution.py:346
  340.9 7.5 all-to-all-done.6
  353.1 7.1 all-to-all-done.7
  361.8 10.3 %shard_map.315 = bf16[1536,1024]{1,0:T(8,128)(2,1)S(1)} custom-call(s32[1]{0:T(128)} %bitcast.52.core_ref, s32[1,3072]{1,0:T(1,128)S(1)} %compare_select_fusion.target_ref, f32[1,3072]{1,0:T(1,128)S(1)} %get-tuple-element.435.scale_ref, f32[1,3072]{1,0:T(1,128)S(1)} %get-tuple-element.434.value_ref, bf16[2048,3072]{1,0:T(8,128)(2,1)} %get-tuple-element.242.shares_ref, ...), custom_call_target="tpu_custom_call" | custom-call | flops 6442450944 | bytes 9437184 | tf_op jit(solution)/shard_map/pallas_call | solution.py:388
  372.4 10.4 %shard_map.314 = bf16[1536,1024]{1,0:T(8,128)(2,1)S(1)} custom-call(s32[1]{0:T(128)} %bitcast.51.core_ref, s32[1,3072]{1,0:T(1,128)S(1)} %compare_select_fusion.target_ref, f32[1,3072]{1,0:T(1,128)S(1)} %get-tuple-element.435.scale_ref, f32[1,3072]{1,0:T(1,128)S(1)} %get-tuple-element.434.value_ref, bf16[2048,3072]{1,0:T(8,128)(2,1)} %get-tuple-element.242.shares_ref, ...), custom_call_target="tpu_custom_call" | custom-call | flops 6442450944 | bytes 9437184 | tf_op jit(solution)/shard_map/pallas_call | solution.py:388
  389.5 17.5 %fusion.14 = f32[2048,1024]{1,0:T(8,128)} fusion(bf16[3072,1024]{1,0:T(8,128)(2,1)} %all-gather.8.cloned.1.call-done.answers_ref, bf16[2048,3072]{1,0:T(8,128)(2,1)S(1)} %bitcast.489, f32[3072]{0:T(1024)S(1)} %bitcast.386, f32[3072]{0:T(1024)S(1)} %bitcast.385, s32[3072]{0:T(1024)S(1)} %fusion.123), kind=kOutput, calls=%fused_computation.30 | convolution fusion | flops 12910067712 | bytes 27299840 | tf_op jit(solution)/shard_map/dot_general | solution.py:603
  407.1 16.6 %collective-permute-done.8 = bf16[384,1024]{1,0:T(8,128)(2,1)S(1)} collective-permute-done((bf16[384,1024]{1,0:T(8,128)(2,1)S(1)}, bf16[384,1024]{1,0:T(8,128)(2,1)S(1)}, u32[]{:S(2)}, u32[]{:S(2)}) %collective-permute-start.8) | collective-permute-done | bytes 786464 | tf_op jit(solution)/shard_map/ppermute | solution.py:121
  427.0 4.2 collective-permute-done.12
  431.3 12.0 %collective-permute-done.11 = bf16[96,1024]{1,0:T(8,128)(2,1)S(1)} collective-permute-done((bf16[96,1024]{1,0:T(8,128)(2,1)S(1)}, bf16[96,1024]{1,0:T(8,128)(2,1)S(1)}, u32[]{:S(2)}, u32[]{:S(2)}) %collective-permute-start.11) | collective-permute-done | bytes 196640 | tf_op jit(solution)/shard_map/ppermute | solution.py:121
  449.9 13.5 %collective-permute-done.14 = bf16[96,1024]{1,0:T(8,128)(2,1)S(1)} collective-permute-done((bf16[96,1024]{1,0:T(8,128)(2,1)S(1)}, bf16[96,1024]{1,0:T(8,128)(2,1)S(1)}, u32[]{:S(2)}, u32[]{:S(2)}) %collective-permute-start.14) | collective-permute-done | bytes 196640 | tf_op jit(solution)/shard_map/ppermute | solution.py:121
  463.4 4.3 fusion.59
  479.0 4.6 convolution_convert_fusion.4
  488.3 5.0 collective-permute-done.18
  493.4 7.4 collective-permute-done.17
  522.8 16.8 %reduce-scatter.3.cloned.1.call-done = bf16[3,144,1024]{2,1,0:T(8,128)(2,1)} async-done(((bf16[3,1152,1024]{2,1,0:T(8,128)(2,1)}), bf16[3,144,1024]{2,1,0:T(8,128)(2,1)}) %reduce-scatter.3.cloned.1.call-update) | async-done | bytes 884752 | tf_op jit(solution)/shard_map/reduce_scatter | solution.py:730
  554.3 4.5 collective-permute-done.21
  558.8 26.3 %collective-permute-done.20 = bf16[208,1024]{1,0:T(8,128)(2,1)} collective-permute-done((bf16[208,1024]{1,0:T(8,128)(2,1)}, bf16[208,1024]{1,0:T(8,128)(2,1)}, u32[]{:S(2)}, u32[]{:S(2)}) %collective-permute-start.20) | collective-permute-done | bytes 426016 | tf_op jit(solution)/shard_map/ppermute | solution.py:121
  587.9 7.3 multiply_reduce_fusion.2
  598.3 5.0 convolution_convert_fusion.1
  617.4 9.7 multiply_reduce_fusion.1
  628.4 4.8 fusion.37
  654.7 34.3 %collective-permute-done.27 = bf16[144,1024]{1,0:T(8,128)(2,1)S(1)} collective-permute-done((bf16[144,1024]{1,0:T(8,128)(2,1)}, bf16[144,1024]{1,0:T(8,128)(2,1)S(1)}, u32[]{:S(2)}, u32[]{:S(2)}) %collective-permute-start.27) | collective-permute-done | bytes 294944 | tf_op jit(solution)/shard_map/ppermute | solution.py:121
  689.1 33.0 %collective-permute-done.26 = bf16[144,1024]{1,0:T(8,128)(2,1)S(1)} collective-permute-done((bf16[144,1024]{1,0:T(8,128)(2,1)}, bf16[144,1024]{1,0:T(8,128)(2,1)S(1)}, u32[]{:S(2)}, u32[]{:S(2)}) %collective-permute-start.26) | collective-permute-done | bytes 294944 | tf_op jit(solution)/shard_map/ppermute | solution.py:121
  723.3 10.2 %fusion.23 = f32[2048,1024]{1,0:T(8,128)} fusion(f32[2048,1024]{1,0:T(8,128)} %fusion.14, bf16[1024,1024]{1,0:T(8,128)(2,1)} %bitcast.113, s32[1024]{0:T(1024)S(1)} %copy-done.125), kind=kOutput, calls=%fused_computation.50 | convolution fusion | flops 4299161600 | bytes 18878464 | tf_op jit(solution)/shard_map/dot_general | solution.py:67
  733.5 8.2 reduce-scatter.5.cloned.1.call-done
  750.3 6.1 multiply_reduce_fusion
  756.5 5.4 collective-permute-done.24
  761.9 32.6 %collective-permute-done.23 = bf16[2,128,1024]{2,1,0:T(8,128)(2,1)} collective-permute-done((bf16[2,128,1024]{2,1,0:T(8,128)(2,1)}, bf16[2,128,1024]{2,1,0:T(8,128)(2,1)}, u32[]{:S(2)}, u32[]{:S(2)}) %collective-permute-start.23) | collective-permute-done | bytes 524320 | tf_op jit(solution)/shard_map/ppermute | solution.py:121
  805.6 6.4 all-to-all-done.10
  839.3 9.7 collective-permute-done.37
  860.7 4.6 collective-permute-done.40
  866.2 22.9 %add_multiply_fusion = (f32[2048,1024]{1,0:T(8,128)}, f32[2048,1024]{1,0:T(8,128)}, f32[2048,1024]{1,0:T(8,128)}) fusion(f32[2048,1024]{1,0:T(8,128)} %param.25, f32[]{:T(128)S(6)} %sub.250, f32[]{:T(128)S(6)} %sub.249, f32[2048,1024]{1,0:T(8,128)} %get-tuple-element.250, f32[]{:T(128)S(6)} %min.3, f32[2048,1024]{1,0:T(8,128)} %param.27, f32[2048,1024]{1,0:T(8,128)} %param.26), kind=kLoop, calls=%fused_computation.36 | loop fusion | flops 31457280 | bytes 58720268 | tf_op jit(solution)/shard_map/mul | solution.py:100
  899.6 25.3 %shard_map.316 = bf16[1024,1024]{1,0:T(8,128)(2,1)S(1)} custom-call(f32[1024,1024]{1,0:T(8,128)S(1)} %convert_select_fusion.gram_ref), custom_call_target="tpu_custom_call" | custom-call | flops 19327352832 | bytes 6291456 | tf_op jit(solution)/shard_map/pallas_call | solution.py:292
  952.2 11.6 %collective-permute-done.49 = bf16[144,1024]{1,0:T(8,128)(2,1)S(1)} collective-permute-done((bf16[144,1024]{1,0:T(8,128)(2,1)S(1)}, bf16[144,1024]{1,0:T(8,128)(2,1)S(1)}, u32[]{:S(2)}, u32[]{:S(2)}) %collective-permute-start.49) | collective-permute-done | bytes 294944 | tf_op jit(solution)/shard_map/ppermute | solution.py:121
  964.2 5.8 collective-permute-start.53
  974.7 8.2 collective-permute-done.52
  (713 shorter events, 289.0 us)
Async XLA Ops:
  7.2 146.7 %all-gather.4.cloned.1.call-start = ((), (), s32[]{:S(2)}) async-start(), calls=%async_computation.13 | async-start | bytes 15138816 | tf_op jit(solution)/shard_map/all_gather | solution.py:467
  19.0 15.4 %all-to-all-start.4 = ((f32[32,1,357]{2,1,0:T(1,128)}), f32[32,1,357]{2,1,0:T(1,128)S(1)}, u32[]{:S(2)}, u32[]{:S(2)}) async-start(f32[32,1,357]{2,1,0:T(1,128)} %all_to_all.79), calls=%async_computation.4 | async-start | bytes 98304 | tf_op jit(solution)/shard_map/all_to_all | solution.py:111
  42.5 92.1 %all-to-all-start.5 = ((bf16[32,32,1024]{2,1,0:T(8,128)(2,1)}), bf16[32,32,1024]{2,1,0:T(8,128)(2,1)}, u32[]{:S(2)}, u32[]{:S(2)}) async-start(bf16[32,32,1024]{2,1,0:T(8,128)(2,1)} %bitcast.424), calls=%async_computation.5 | async-start | bytes 4194304 | tf_op jit(solution)/shard_map/all_to_all | solution.py:111
  46.6 157.7 %all-gather.6.cloned.1.call-start = ((), (), s32[]{:S(2)}) async-start(), calls=%async_computation.14 | async-start | bytes 7962624 | tf_op jit(solution)/shard_map/all_gather | solution.py:468
  47.7 261.2 %all-gather.8.cloned.1.call-start = ((), (), s32[]{:S(2)}) async-start(), calls=%async_computation.15 | async-start | bytes 6488064 | tf_op jit(solution)/shard_map/all_gather | solution.py:576
  191.5 15.7 %collective-permute-start.2 = (bf16[96,1024]{1,0:T(8,128)(2,1)S(1)}, bf16[96,1024]{1,0:T(8,128)(2,1)S(1)}, u32[]{:S(2)}, u32[]{:S(2)}) collective-permute-start(bf16[96,1024]{1,0:T(8,128)(2,1)S(1)} %multiply_convert_fusion.9), channel_id=1, source_target_pairs={{0,3},{1,0},{2,1},{3,2},{4,7},{5,4},{6,5},{7,6},{8,11},{9,8},{10,9... | collective-permute-start | bytes 589832 | tf_op jit(solution)/shard_map/ppermute | solution.py:121
  192.3 16.1 %collective-permute-start.1 = (bf16[96,1024]{1,0:T(8,128)(2,1)S(1)}, bf16[96,1024]{1,0:T(8,128)(2,1)S(1)}, u32[]{:S(2)}, u32[]{:S(2)}) collective-permute-start(bf16[96,1024]{1,0:T(8,128)(2,1)S(1)} %multiply_convert_fusion.9), channel_id=1, source_target_pairs={{0,2},{1,3},{2,0},{3,1},{4,6},{5,7},{6,4},{7,5},{8,10},{9,11},{10,... | collective-permute-start | bytes 589832 | tf_op jit(solution)/shard_map/ppermute | solution.py:121
  192.3 16.1 %collective-permute-start = (bf16[96,1024]{1,0:T(8,128)(2,1)S(1)}, bf16[96,1024]{1,0:T(8,128)(2,1)S(1)}, u32[]{:S(2)}, u32[]{:S(2)}) collective-permute-start(bf16[96,1024]{1,0:T(8,128)(2,1)S(1)} %multiply_convert_fusion.9), channel_id=1, source_target_pairs={{0,1},{1,2},{2,3},{3,0},{4,5},{5,6},{6,7},{7,4},{8,9},{9,10},{10,1... | collective-permute-start | bytes 589832 | tf_op jit(solution)/shard_map/ppermute | solution.py:121
  217.9 14.0 %collective-permute-start.4 = (bf16[96,1024]{1,0:T(8,128)(2,1)S(1)}, bf16[96,1024]{1,0:T(8,128)(2,1)S(1)}, u32[]{:S(2)}, u32[]{:S(2)}) collective-permute-start(bf16[96,1024]{1,0:T(8,128)(2,1)S(1)} %get-tuple-element.406), channel_id=1, source_target_pairs={{0,2},{1,3},{2,0},{3,1},{4,6},{5,7},{6,4},{7,5},{8,10},{9,11},{10,... | collective-permute-start | bytes 589832 | tf_op jit(solution)/shard_map/ppermute | solution.py:121
  353.0 186.5 %reduce-scatter.3.cloned.1.call-start = ((), (), s32[]{:S(2)}) async-start(), calls=%async_computation.16 | async-start | bytes 7962624 | tf_op jit(solution)/shard_map/reduce_scatter | solution.py:730
  386.7 20.4 %collective-permute-start.9 = (bf16[384,1024]{1,0:T(8,128)(2,1)S(1)}, bf16[384,1024]{1,0:T(8,128)(2,1)S(1)}, u32[]{:S(2)}, u32[]{:S(2)}) collective-permute-start(bf16[384,1024]{1,0:T(8,128)(2,1)S(1)} %get-tuple-element.355), channel_id=1, source_target_pairs={{0,24},{8,0},{16,8},{24,16},{1,25},{9,1},{17,9},{25,17},{2,26},{10... | collective-permute-start | bytes 2359304 | tf_op jit(solution)/shard_map/ppermute | solution.py:121
  387.3 36.4 %collective-permute-start.8 = (bf16[384,1024]{1,0:T(8,128)(2,1)S(1)}, bf16[384,1024]{1,0:T(8,128)(2,1)S(1)}, u32[]{:S(2)}, u32[]{:S(2)}) collective-permute-start(bf16[384,1024]{1,0:T(8,128)(2,1)S(1)} %get-tuple-element.356), channel_id=1, source_target_pairs={{0,16},{8,24},{16,0},{24,8},{1,17},{9,25},{17,1},{25,9},{2,18},{10... | collective-permute-start | bytes 2359304 | tf_op jit(solution)/shard_map/ppermute | solution.py:121
  388.8 34.9 %collective-permute-start.7 = (bf16[384,1024]{1,0:T(8,128)(2,1)S(1)}, bf16[384,1024]{1,0:T(8,128)(2,1)S(1)}, u32[]{:S(2)}, u32[]{:S(2)}) collective-permute-start(bf16[384,1024]{1,0:T(8,128)(2,1)S(1)} %get-tuple-element.354), channel_id=1, source_target_pairs={{0,8},{8,16},{16,24},{24,0},{1,9},{9,17},{17,25},{25,1},{2,10},{10... | collective-permute-start | bytes 2359304 | tf_op jit(solution)/shard_map/ppermute | solution.py:121
  425.0 18.2 %collective-permute-start.11 = (bf16[96,1024]{1,0:T(8,128)(2,1)S(1)}, bf16[96,1024]{1,0:T(8,128)(2,1)S(1)}, u32[]{:S(2)}, u32[]{:S(2)}) collective-permute-start(bf16[96,1024]{1,0:T(8,128)(2,1)S(1)} %get-tuple-element.403), channel_id=1, source_target_pairs={{0,2},{1,3},{2,0},{3,1},{4,6},{5,7},{6,4},{7,5},{8,10},{9,11},{10,... | collective-permute-start | bytes 589832 | tf_op jit(solution)/shard_map/ppermute | solution.py:121
  426.4 16.8 %collective-permute-start.10 = (bf16[96,1024]{1,0:T(8,128)(2,1)S(1)}, bf16[96,1024]{1,0:T(8,128)(2,1)S(1)}, u32[]{:S(2)}, u32[]{:S(2)}) collective-permute-start(bf16[96,1024]{1,0:T(8,128)(2,1)S(1)} %get-tuple-element.401), channel_id=1, source_target_pairs={{0,1},{1,2},{2,3},{3,0},{4,5},{5,6},{6,7},{7,4},{8,9},{9,10},{10,1... | collective-permute-start | bytes 589832 | tf_op jit(solution)/shard_map/ppermute | solution.py:121
  444.3 19.2 %collective-permute-start.14 = (bf16[96,1024]{1,0:T(8,128)(2,1)S(1)}, bf16[96,1024]{1,0:T(8,128)(2,1)S(1)}, u32[]{:S(2)}, u32[]{:S(2)}) collective-permute-start(bf16[96,1024]{1,0:T(8,128)(2,1)S(1)} %fusion.150), channel_id=1, source_target_pairs={{0,2},{1,3},{2,0},{3,1},{4,6},{5,7},{6,4},{7,5},{8,10},{9,11},{10,... | collective-permute-start | bytes 589832 | tf_op jit(solution)/shard_map/ppermute | solution.py:121
  445.8 17.6 %collective-permute-start.13 = (bf16[96,1024]{1,0:T(8,128)(2,1)S(1)}, bf16[96,1024]{1,0:T(8,128)(2,1)S(1)}, u32[]{:S(2)}, u32[]{:S(2)}) collective-permute-start(bf16[96,1024]{1,0:T(8,128)(2,1)S(1)} %fusion.150), channel_id=1, source_target_pairs={{0,1},{1,2},{2,3},{3,0},{4,5},{5,6},{6,7},{7,4},{8,9},{9,10},{10,1... | collective-permute-start | bytes 589832 | tf_op jit(solution)/shard_map/ppermute | solution.py:121
  476.2 265.4 %reduce-scatter.5.cloned.1.call-start = ((), (), s32[]{:S(2)}) async-start(), calls=%async_computation.17 | async-start | bytes 16515072 | tf_op jit(solution)/shard_map/reduce_scatter | solution.py:734
  483.7 17.1 %collective-permute-start.17 = (bf16[96,1024]{1,0:T(8,128)(2,1)S(1)}, bf16[96,1024]{1,0:T(8,128)(2,1)S(1)}, u32[]{:S(2)}, u32[]{:S(2)}) collective-permute-start(bf16[96,1024]{1,0:T(8,128)(2,1)S(1)} %get-tuple-element.400), channel_id=1, source_target_pairs={{0,2},{1,3},{2,0},{3,1},{4,6},{5,7},{6,4},{7,5},{8,10},{9,11},{10,... | collective-permute-start | bytes 589832 | tf_op jit(solution)/shard_map/ppermute | solution.py:121
  483.8 17.0 %collective-permute-start.16 = (bf16[96,1024]{1,0:T(8,128)(2,1)S(1)}, bf16[96,1024]{1,0:T(8,128)(2,1)S(1)}, u32[]{:S(2)}, u32[]{:S(2)}) collective-permute-start(bf16[96,1024]{1,0:T(8,128)(2,1)S(1)} %get-tuple-element.398), channel_id=1, source_target_pairs={{0,3},{1,0},{2,1},{3,2},{4,7},{5,4},{6,5},{7,6},{8,11},{9,8},{10,9... | collective-permute-start | bytes 589832 | tf_op jit(solution)/shard_map/ppermute | solution.py:121
  544.9 13.9 %collective-permute-start.21 = (bf16[208,1024]{1,0:T(8,128)(2,1)}, bf16[208,1024]{1,0:T(8,128)(2,1)}, u32[]{:S(2)}, u32[]{:S(2)}) collective-permute-start(bf16[208,1024]{1,0:T(8,128)(2,1)} %get-tuple-element.365), channel_id=1, source_target_pairs={{0,3},{1,0},{2,1},{3,2},{4,7},{5,4},{6,5},{7,6},{8,11},{9,8},{10,9... | collective-permute-start | bytes 1277960 | tf_op jit(solution)/shard_map/ppermute | solution.py:121
  548.2 36.9 %collective-permute-start.20 = (bf16[208,1024]{1,0:T(8,128)(2,1)}, bf16[208,1024]{1,0:T(8,128)(2,1)}, u32[]{:S(2)}, u32[]{:S(2)}) collective-permute-start(bf16[208,1024]{1,0:T(8,128)(2,1)} %get-tuple-element.366), channel_id=1, source_target_pairs={{0,2},{1,3},{2,0},{3,1},{4,6},{5,7},{6,4},{7,5},{8,10},{9,11},{10,... | collective-permute-start | bytes 1277960 | tf_op jit(solution)/shard_map/ppermute | solution.py:121
  548.2 36.9 %collective-permute-start.19 = (bf16[208,1024]{1,0:T(8,128)(2,1)}, bf16[208,1024]{1,0:T(8,128)(2,1)}, u32[]{:S(2)}, u32[]{:S(2)}) collective-permute-start(bf16[208,1024]{1,0:T(8,128)(2,1)} %get-tuple-element.367), channel_id=1, source_target_pairs={{0,1},{1,2},{2,3},{3,0},{4,5},{5,6},{6,7},{7,4},{8,9},{9,10},{10,1... | collective-permute-start | bytes 1277960 | tf_op jit(solution)/shard_map/ppermute | solution.py:121
  644.2 79.0 %all-to-all-start.9 = ((bf16[32,32,1024]{2,1,0:T(8,128)(2,1)}), bf16[32,32,1024]{2,1,0:T(8,128)(2,1)}, u32[]{:S(2)}, u32[]{:S(2)}) async-start(bf16[32,32,1024]{2,1,0:T(8,128)(2,1)} %bitcast.112), calls=%async_computation.11 | async-start | bytes 4194304 | tf_op jit(solution)/shard_map/all_to_all | solution.py:111
  649.2 39.9 %collective-permute-start.27 = (bf16[144,1024]{1,0:T(8,128)(2,1)}, bf16[144,1024]{1,0:T(8,128)(2,1)S(1)}, u32[]{:S(2)}, u32[]{:S(2)}) collective-permute-start(bf16[144,1024]{1,0:T(8,128)(2,1)} %get-tuple-element.397), channel_id=1, source_target_pairs={{0,3},{1,0},{2,1},{3,2},{4,7},{5,4},{6,5},{7,6},{8,11},{9,8},{10,9... | collective-permute-start | bytes 884744 | tf_op jit(solution)/shard_map/ppermute | solution.py:121
  652.8 69.3 %collective-permute-start.26 = (bf16[144,1024]{1,0:T(8,128)(2,1)}, bf16[144,1024]{1,0:T(8,128)(2,1)S(1)}, u32[]{:S(2)}, u32[]{:S(2)}) collective-permute-start(bf16[144,1024]{1,0:T(8,128)(2,1)} %get-tuple-element.396), channel_id=1, source_target_pairs={{0,2},{1,3},{2,0},{3,1},{4,6},{5,7},{6,4},{7,5},{8,10},{9,11},{10,... | collective-permute-start | bytes 884744 | tf_op jit(solution)/shard_map/ppermute | solution.py:121
  652.8 69.3 %collective-permute-start.25 = (bf16[144,1024]{1,0:T(8,128)(2,1)S(1)}, bf16[144,1024]{1,0:T(8,128)(2,1)S(1)}, u32[]{:S(2)}, u32[]{:S(2)}) collective-permute-start(bf16[144,1024]{1,0:T(8,128)(2,1)S(1)} %get-tuple-element.395), channel_id=1, source_target_pairs={{0,1},{1,2},{2,3},{3,0},{4,5},{5,6},{6,7},{7,4},{8,9},{9,10},{10,1... | collective-permute-start | bytes 884744 | tf_op jit(solution)/shard_map/ppermute | solution.py:121
  745.9 16.0 %collective-permute-start.24 = (bf16[2,128,1024]{2,1,0:T(8,128)(2,1)}, bf16[2,128,1024]{2,1,0:T(8,128)(2,1)}, u32[]{:S(2)}, u32[]{:S(2)}) collective-permute-start(bf16[2,128,1024]{2,1,0:T(8,128)(2,1)} %get-tuple-element.360), channel_id=1, source_target_pairs={{0,3},{1,0},{2,1},{3,2},{4,7},{5,4},{6,5},{7,6},{8,11},{9,8},{10,9... | collective-permute-start | bytes 1572872 | tf_op jit(solution)/shard_map/ppermute | solution.py:121
  749.2 45.3 %collective-permute-start.23 = (bf16[2,128,1024]{2,1,0:T(8,128)(2,1)}, bf16[2,128,1024]{2,1,0:T(8,128)(2,1)}, u32[]{:S(2)}, u32[]{:S(2)}) collective-permute-start(bf16[2,128,1024]{2,1,0:T(8,128)(2,1)} %get-tuple-element.361), channel_id=1, source_target_pairs={{0,2},{1,3},{2,0},{3,1},{4,6},{5,7},{6,4},{7,5},{8,10},{9,11},{10,... | collective-permute-start | bytes 1572872 | tf_op jit(solution)/shard_map/ppermute | solution.py:121
  749.2 45.3 %collective-permute-start.22 = (bf16[2,128,1024]{2,1,0:T(8,128)(2,1)}, bf16[2,128,1024]{2,1,0:T(8,128)(2,1)}, u32[]{:S(2)}, u32[]{:S(2)}) collective-permute-start(bf16[2,128,1024]{2,1,0:T(8,128)(2,1)} %get-tuple-element.359), channel_id=1, source_target_pairs={{0,1},{1,2},{2,3},{3,0},{4,5},{5,6},{6,7},{7,4},{8,9},{9,10},{10,1... | collective-permute-start | bytes 1572872 | tf_op jit(solution)/shard_map/ppermute | solution.py:121
  828.9 20.1 %collective-permute-start.37 = (bf16[128,1024]{1,0:T(8,128)(2,1)}, bf16[128,1024]{1,0:T(8,128)(2,1)}, u32[]{:S(2)}, u32[]{:S(2)}) collective-permute-start(bf16[128,1024]{1,0:T(8,128)(2,1)} %get-tuple-element.391), channel_id=1, source_target_pairs={{0,16},{8,24},{16,0},{24,8},{1,17},{9,25},{17,1},{25,9},{2,18},{10... | collective-permute-start | bytes 786440 | tf_op jit(solution)/shard_map/ppermute | solution.py:121
  830.4 18.6 %collective-permute-start.36 = (bf16[128,1024]{1,0:T(8,128)(2,1)}, bf16[128,1024]{1,0:T(8,128)(2,1)}, u32[]{:S(2)}, u32[]{:S(2)}) collective-permute-start(bf16[128,1024]{1,0:T(8,128)(2,1)} %get-tuple-element.389), channel_id=1, source_target_pairs={{0,8},{8,16},{16,24},{24,0},{1,9},{9,17},{17,25},{25,1},{2,10},{10... | collective-permute-start | bytes 786440 | tf_op jit(solution)/shard_map/ppermute | solution.py:121
  833.2 18.8 %collective-permute-start.31 = (bf16[128,1024]{1,0:T(8,128)(2,1)S(1)}, bf16[128,1024]{1,0:T(8,128)(2,1)S(1)}, u32[]{:S(2)}, u32[]{:S(2)}) collective-permute-start(bf16[128,1024]{1,0:T(8,128)(2,1)S(1)} %get-tuple-element.428), channel_id=1, source_target_pairs={{0,8},{8,16},{16,24},{24,0},{1,9},{9,17},{17,25},{25,1},{2,10},{10... | collective-permute-start | bytes 786440 | tf_op jit(solution)/shard_map/ppermute | solution.py:121
  835.4 19.3 %collective-permute-start.32 = (bf16[128,1024]{1,0:T(8,128)(2,1)S(1)}, bf16[128,1024]{1,0:T(8,128)(2,1)S(1)}, u32[]{:S(2)}, u32[]{:S(2)}) collective-permute-start(bf16[128,1024]{1,0:T(8,128)(2,1)S(1)} %get-tuple-element.429), channel_id=1, source_target_pairs={{0,16},{8,24},{16,0},{24,8},{1,17},{9,25},{17,1},{25,9},{2,18},{10... | collective-permute-start | bytes 786440 | tf_op jit(solution)/shard_map/ppermute | solution.py:121
  837.8 17.5 %collective-permute-start.33 = (bf16[128,1024]{1,0:T(8,128)(2,1)S(1)}, bf16[128,1024]{1,0:T(8,128)(2,1)S(1)}, u32[]{:S(2)}, u32[]{:S(2)}) collective-permute-start(bf16[128,1024]{1,0:T(8,128)(2,1)S(1)} %get-tuple-element.427), channel_id=1, source_target_pairs={{0,24},{8,0},{16,8},{24,16},{1,25},{9,1},{17,9},{25,17},{2,26},{10... | collective-permute-start | bytes 786440 | tf_op jit(solution)/shard_map/ppermute | solution.py:121
  850.3 15.0 %collective-permute-start.40 = (bf16[128,1024]{1,0:T(8,128)(2,1)S(1)}, bf16[128,1024]{1,0:T(8,128)(2,1)S(1)}, u32[]{:S(2)}, u32[]{:S(2)}) collective-permute-start(bf16[128,1024]{1,0:T(8,128)(2,1)S(1)} %fusion.96), channel_id=1, source_target_pairs={{0,16},{8,24},{16,0},{24,8},{1,17},{9,25},{17,1},{25,9},{2,18},{10... | collective-permute-start | bytes 786440 | tf_op jit(solution)/shard_map/ppermute | solution.py:121
  852.0 13.3 %collective-permute-start.39 = (bf16[128,1024]{1,0:T(8,128)(2,1)S(1)}, bf16[128,1024]{1,0:T(8,128)(2,1)S(1)}, u32[]{:S(2)}, u32[]{:S(2)}) collective-permute-start(bf16[128,1024]{1,0:T(8,128)(2,1)S(1)} %fusion.96), channel_id=1, source_target_pairs={{0,8},{8,16},{16,24},{24,0},{1,9},{9,17},{17,25},{25,1},{2,10},{10... | collective-permute-start | bytes 786440 | tf_op jit(solution)/shard_map/ppermute | solution.py:121
  854.7 76.9 %collective-permute-start.30 = (bf16[2,32,1024]{2,1,0:T(8,128)(2,1)}, bf16[2,32,1024]{2,1,0:T(8,128)(2,1)}, u32[]{:S(2)}, u32[]{:S(2)}) collective-permute-start(bf16[2,32,1024]{2,1,0:T(8,128)(2,1)} %get-tuple-element.416), channel_id=1, source_target_pairs={{0,3},{1,0},{2,1},{3,2},{4,7},{5,4},{6,5},{7,6},{8,11},{9,8},{10,9... | collective-permute-start | bytes 393224 | tf_op jit(solution)/shard_map/ppermute | solution.py:121
  855.3 76.3 %collective-permute-start.29 = (bf16[2,32,1024]{2,1,0:T(8,128)(2,1)}, bf16[2,32,1024]{2,1,0:T(8,128)(2,1)}, u32[]{:S(2)}, u32[]{:S(2)}) collective-permute-start(bf16[2,32,1024]{2,1,0:T(8,128)(2,1)} %get-tuple-element.417), channel_id=1, source_target_pairs={{0,2},{1,3},{2,0},{3,1},{4,6},{5,7},{6,4},{7,5},{8,10},{9,11},{10,... | collective-permute-start | bytes 393224 | tf_op jit(solution)/shard_map/ppermute | solution.py:121
  860.2 71.4 %collective-permute-start.28 = (bf16[2,32,1024]{2,1,0:T(8,128)(2,1)}, bf16[2,32,1024]{2,1,0:T(8,128)(2,1)}, u32[]{:S(2)}, u32[]{:S(2)}) collective-permute-start(bf16[2,32,1024]{2,1,0:T(8,128)(2,1)} %get-tuple-element.418), channel_id=1, source_target_pairs={{0,1},{1,2},{2,3},{3,0},{4,5},{5,6},{6,7},{7,4},{8,9},{9,10},{10,1... | collective-permute-start | bytes 393224 | tf_op jit(solution)/shard_map/ppermute | solution.py:121
  865.3 28.0 %collective-permute-start.34 = (bf16[512,1024]{1,0:T(8,128)(2,1)}, bf16[512,1024]{1,0:T(8,128)(2,1)}, u32[]{:S(2)}, u32[]{:S(2)}) collective-permute-start(bf16[512,1024]{1,0:T(8,128)(2,1)} %pad_maximum_fusion.11), channel_id=1, source_target_pairs={{0,4},{4,0},{1,5},{5,1},{2,6},{6,2},{3,7},{7,3},{8,12},{12,8},{9,1... | collective-permute-start | bytes 3145736 | tf_op jit(solution)/shard_map/ppermute | solution.py:161
  865.7 29.9 %collective-permute-start.42 = (bf16[512,1024]{1,0:T(8,128)(2,1)S(1)}, bf16[512,1024]{1,0:T(8,128)(2,1)S(1)}, u32[]{:S(2)}, u32[]{:S(2)}) collective-permute-start(bf16[512,1024]{1,0:T(8,128)(2,1)S(1)} %bitcast.410), channel_id=1, source_target_pairs={{0,4},{4,0},{1,5},{5,1},{2,6},{6,2},{3,7},{7,3},{8,12},{12,8},{9,1... | collective-permute-start | bytes 3145736 | tf_op jit(solution)/shard_map/ppermute | solution.py:161
  924.9 14.0 %collective-permute-start.47 = (bf16[1024,1024]{1,0:T(8,128)(2,1)S(1)}, bf16[1024,1024]{1,0:T(8,128)(2,1)}, u32[]{:S(2)}, u32[]{:S(2)}) collective-permute-start(bf16[1024,1024]{1,0:T(8,128)(2,1)S(1)} %shard_map.316), channel_id=1, source_target_pairs={{0,4},{4,0},{1,5},{5,1},{2,6},{6,2},{3,7},{7,3},{8,12},{12,8},{9,1... | collective-permute-start | bytes 6291464 | tf_op jit(solution)/shard_map/ppermute | solution.py:161
  935.6 12.6 %collective-permute-start.45 = (bf16[128,1024]{1,0:T(8,128)(2,1)S(1)}, bf16[128,1024]{1,0:T(8,128)(2,1)S(1)}, u32[]{:S(2)}, u32[]{:S(2)}) collective-permute-start(bf16[128,1024]{1,0:T(8,128)(2,1)S(1)} %get-tuple-element.383), channel_id=1, source_target_pairs={{0,16},{8,24},{16,0},{24,8},{1,17},{9,25},{17,1},{25,9},{2,18},{10... | collective-permute-start | bytes 786440 | tf_op jit(solution)/shard_map/ppermute | solution.py:121
  936.2 12.1 %collective-permute-start.44 = (bf16[128,1024]{1,0:T(8,128)(2,1)S(1)}, bf16[128,1024]{1,0:T(8,128)(2,1)S(1)}, u32[]{:S(2)}, u32[]{:S(2)}) collective-permute-start(bf16[128,1024]{1,0:T(8,128)(2,1)S(1)} %get-tuple-element.384), channel_id=1, source_target_pairs={{0,24},{8,0},{16,8},{24,16},{1,25},{9,1},{17,9},{25,17},{2,26},{10... | collective-permute-start | bytes 786440 | tf_op jit(solution)/shard_map/ppermute | solution.py:121
  940.9 22.9 %collective-permute-start.49 = (bf16[144,1024]{1,0:T(8,128)(2,1)S(1)}, bf16[144,1024]{1,0:T(8,128)(2,1)S(1)}, u32[]{:S(2)}, u32[]{:S(2)}) collective-permute-start(bf16[144,1024]{1,0:T(8,128)(2,1)S(1)} %get-tuple-element.373), channel_id=1, source_target_pairs={{0,2},{1,3},{2,0},{3,1},{4,6},{5,7},{6,4},{7,5},{8,10},{9,11},{10,... | collective-permute-start | bytes 884744 | tf_op jit(solution)/shard_map/ppermute | solution.py:121
  944.5 19.2 %collective-permute-start.48 = (bf16[144,1024]{1,0:T(8,128)(2,1)S(1)}, bf16[144,1024]{1,0:T(8,128)(2,1)S(1)}, u32[]{:S(2)}, u32[]{:S(2)}) collective-permute-start(bf16[144,1024]{1,0:T(8,128)(2,1)S(1)} %get-tuple-element.374), channel_id=1, source_target_pairs={{0,3},{1,0},{2,1},{3,2},{4,7},{5,4},{6,5},{7,6},{8,11},{9,8},{10,9... | collective-permute-start | bytes 884744 | tf_op jit(solution)/shard_map/ppermute | solution.py:121
  970.1 12.8 %collective-permute-start.52 = (bf16[2,32,1024]{2,1,0:T(8,128)(2,1)S(1)}, bf16[2,32,1024]{2,1,0:T(8,128)(2,1)S(1)}, u32[]{:S(2)}, u32[]{:S(2)}) collective-permute-start(bf16[2,32,1024]{2,1,0:T(8,128)(2,1)S(1)} %get-tuple-element.425), channel_id=1, source_target_pairs={{0,2},{1,3},{2,0},{3,1},{4,6},{5,7},{6,4},{7,5},{8,10},{9,11},{10,... | collective-permute-start | bytes 393224 | tf_op jit(solution)/shard_map/ppermute | solution.py:121
  (187 other events, 3960.8 us)
Sparse Core Ops, SparseCore 0:
  11.6 142.2 all-gather.3
  156.3 47.9 all-gather.5
  233.9 74.9 all-gather.7
  476.3 63.1 reduce-scatter.2
  616.3 125.3 reduce-scatter.4

commit v6 on v5

--- a/solution.py
+++ b/solution.py
@@ -104,7 +104,8 @@
 
 DP = ("chip", "core")
 ALL = ("chip", "core", "vocab")
-SLOTS = 32
+SLOTS = 24
+LATER_SLOTS = 8
 
 
 def exchanged(rows):
@@ -212,13 +213,13 @@
     return owner, first, slot
 
 
-def round_keys(owner, slot, turn):
-    within = slot - turn * SLOTS
-    return jnp.where((within >= 0) & (within < SLOTS), owner * SLOTS + within, -1)
-
-
-def round_asks(keys, first, local, count):
-    hits = (keys[None, :] == jnp.arange(count)[:, None]) & first[None, :]
+def round_keys(owner, slot, first, count):
+    within = slot - first
+    return jnp.where((within >= 0) & (within < count), owner * count + within, -1)
+
+
+def round_asks(keys, first_seen, local, count):
+    hits = (keys[None, :] == jnp.arange(count)[:, None]) & first_seen[None, :]
     return jnp.sum(jnp.where(hits, local[None, :] + 1, 0), axis=1) - 1
 
 
@@ -446,7 +447,7 @@
     start = own_length - 1 - RESP
     owner, first_seen, slot = token_slots(own_ids, block_rows)
     local_ids = own_ids % block_rows
-    keys = round_keys(owner, slot, 0)
+    keys = round_keys(owner, slot, 0, SLOTS)
     asks = round_asks(keys, first_seen, local_ids, devices * SLOTS)
     own_targets = lax.dynamic_slice_in_dim(own_ids, start + 1, RESP, 0)
     vector_low = vector_master.astype(jnp.bfloat16).astype(jnp.float32)
@@ -477,7 +478,8 @@
     numbers = notes[:, SLOTS + vector_low.size :].astype(jnp.int32)
     targets = numbers[:, :RESP].reshape(-1)
     orders = numbers[:, RESP : RESP + members].reshape(groups, members, members)[:, 0]
-    turns = (jnp.max(numbers[:, RESP + members]) + SLOTS - 1) // SLOTS
+    later = jnp.maximum(jnp.max(numbers[:, RESP + members]) - SLOTS, 0)
+    later_turns = (later + LATER_SLOTS - 1) // LATER_SLOTS
     slots = jnp.arange(members)
     chosen_mask = (orders[:, 0::2, None] == slots[None, None, :]).astype(jnp.float32)
     rejected_mask = (orders[:, 1::2, None] == slots[None, None, :]).astype(jnp.float32)
@@ -498,21 +500,21 @@
             onehot_rows(wanted, block_rows), table_b, preferred_element_type=jnp.float32
         ).astype(jnp.bfloat16)
         return jnp.dot(
-            onehot_rows(row_keys, devices * SLOTS),
+            onehot_rows(row_keys, wanted.shape[0]),
             exchanged(rows),
             preferred_element_type=jnp.float32,
         )
 
     def later_round(turn):
-        later_keys = round_keys(owner, slot, turn)
-        later_asks = round_asks(later_keys, first_seen, local_ids, devices * SLOTS)
-        return later_keys, exchanged(later_asks)
+        count = devices * LATER_SLOTS
+        later_keys = round_keys(owner, slot, SLOTS + turn * LATER_SLOTS, LATER_SLOTS)
+        return later_keys, exchanged(round_asks(later_keys, first_seen, local_ids, count))
 
     def fetch_more(turn, rows):
         later_keys, later_asked = later_round(turn)
         return rows + fetched(later_asked, later_keys)
 
-    hidden0 = lax.fori_loop(1, turns, fetch_more, fetched(asked, keys))
+    hidden0 = lax.fori_loop(0, later_turns, fetch_more, fetched(asked, keys))
     act1 = rms_scale(hidden0, gains[0]).astype(jnp.bfloat16)
     inner = dense(act1, square_b[0:3].reshape(3 * D, D))
     entry = inner[:, :D]
@@ -574,6 +576,43 @@
     hidden3 = hidden2 + member_return(ffn_part.astype(jnp.bfloat16).reshape(members, RESP, D))
     final_b = rms_scale(hidden3, gains[3]).astype(jnp.bfloat16)
     response_tokens = lax.all_gather(final_b, ALL, axis=0, tiled=True)
+    squares, square_rows = square_master.shape[0], square_master.shape[1]
+    wides, wide_rows = wide_master.shape[0], wide_master.shape[1]
+    per_member = -(-squares // members)
+    group_rows = members * square_rows
+
+    def by_member(values):
+        values = jnp.pad(values, ((0, per_member * members - squares), (0, 0), (0, 0)))
+        return values.reshape(per_member, members, -1, D).transpose(1, 0, 2, 3)
+
+    def wide_by_member(values):
+        return jnp.pad(values, ((0, members - wides), (0, 0), (0, 0)))
+
+    moment_rows = jnp.concatenate(
+        [
+            wide_by_member(wide_moment.astype(jnp.bfloat16)).reshape(-1, D),
+            square_moment.astype(jnp.bfloat16).reshape(-1, D),
+        ],
+        axis=0,
+    )
+    moment_rows, response_tokens = lax.optimization_barrier((moment_rows, response_tokens))
+    moment_rows = lax.all_gather(moment_rows, "vocab", axis=0)
+    wide_moment_job = jnp.stack(
+        [
+            lax.dynamic_slice_in_dim(
+                block_at(moment_rows, member - step), member * wide_rows, wide_rows, 0
+            )
+            for step in range(members)
+        ]
+    )
+    square_moment_job = moment_rows[:, members * wide_rows :].reshape(
+        members, squares, square_rows, D
+    )
+    square_moment_job = jnp.pad(
+        square_moment_job, ((0, 0), (0, per_member * members - squares), (0, 0), (0, 0))
+    ).reshape(members, per_member, members, square_rows, D)
+    square_moment_job = lax.dynamic_index_in_dim(square_moment_job, member, 2, keepdims=False)
+    square_moment_job = square_moment_job.transpose(1, 0, 2, 3).reshape(per_member, group_rows, D)
     local_target = jnp.where(targets // block_rows == device, targets % block_rows, -1)[None, :]
     shares, own_stats = answer_shares(local_target, response_tokens, table_b)
     stats = own_stats[:3].reshape(3, devices, RESP).transpose(1, 0, 2)
@@ -607,8 +646,8 @@
         response_tokens,
         preferred_element_type=jnp.float32,
     )
-    grad_answer_group, grad_table = lax.optimization_barrier(
-        (grad_answer_group.astype(jnp.bfloat16), grad_table)
+    grad_answer_group, grad_table, wide_moment_job, square_moment_job = lax.optimization_barrier(
+        (grad_answer_group.astype(jnp.bfloat16), grad_table, wide_moment_job, square_moment_job)
     )
     grad_final = member_scatter(grad_answer_group.reshape(members, RESP, D))
     grad_hidden3, grad_gain3 = norm_back(hidden3, gains[3], grad_final)
@@ -662,31 +701,6 @@
     grad_pair_w = outer(grad_pair_b, act2)
     grad_norm1, grad_gain1 = norm_back(hidden1, gains[1], grad_act2)
     grad_hidden1 = placed(grad_hidden2) + grad_norm1
-    squares, square_rows = square_master.shape[0], square_master.shape[1]
-    wides, wide_rows = wide_master.shape[0], wide_master.shape[1]
-    per_member = -(-squares // members)
-    group_rows = members * square_rows
-
-    def by_member(values):
-        values = jnp.pad(values, ((0, per_member * members - squares), (0, 0), (0, 0)))
-        return values.reshape(per_member, members, -1, D).transpose(1, 0, 2, 3)
-
-    def wide_by_member(values):
-        return jnp.pad(values, ((0, members - wides), (0, 0), (0, 0)))
-
-    moment_jobs = jnp.concatenate(
-        [
-            wide_by_member(wide_moment.astype(jnp.bfloat16)),
-            by_member(square_moment.astype(jnp.bfloat16)).reshape(members, -1, D),
-        ],
-        axis=1,
-    )
-    moment_jobs = jnp.stack(handed_out(moment_jobs, "vocab"))
-    grad_hidden1, moment_jobs = lax.optimization_barrier((grad_hidden1, moment_jobs))
-    wide_moment_job = moment_jobs[:, :wide_rows]
-    square_moment_job = placed_before(list(moment_jobs[:, wide_rows:]), "vocab")
-    square_moment_job = square_moment_job.reshape(members, per_member, square_rows, D)
-    square_moment_job = square_moment_job.transpose(1, 0, 2, 3).reshape(per_member, group_rows, D)
     grad_mix_out = grad_hidden1.astype(jnp.bfloat16)
     grad_mixer = back_dense(grad_mix_out, square_b[3])
     grad_mixer_w = outer(grad_mix_out, mixer)
@@ -728,8 +742,9 @@
         axis=0,
     )
     share_wide_b = lax.psum_scatter(grad_wide, DP, scatter_dimension=1, tiled=True)
+    grad_square, share_wide_b = lax.optimization_barrier((grad_square, share_wide_b))
+    share_wide_b, grad_embed_b = lax.optimization_barrier((share_wide_b, grad_embed_b))
     share_wide = share_wide_b.astype(jnp.float32)
-    grad_square, share_wide_b = lax.optimization_barrier((grad_square, share_wide_b))
     wide_grad_job = jnp.stack(handed_out(wide_by_member(share_wide_b), "vocab"))
     group_square = lax.psum_scatter(grad_square, DP, scatter_dimension=1, tiled=True)
     square_grad_job = member_scatter(by_member(group_square))
@@ -742,8 +757,8 @@
 
     share_square = from_members(square_grad_job)
 
-    def returned(row_keys):
-        rows = outer(onehot_rows(row_keys, devices * SLOTS), grad_embed_b)
+    def returned(row_keys, count):
+        rows = outer(onehot_rows(row_keys, count), grad_embed_b)
         return exchanged(rows.astype(jnp.bfloat16))
 
     def put(wanted, rows):
@@ -751,10 +766,13 @@
 
     def return_more(turn, total):
         later_keys, later_asked = later_round(turn)
-        return total + put(later_asked, returned(later_keys))
-
-    returned_rows, wide_grad_job = lax.optimization_barrier((returned(keys), wide_grad_job))
-    share_table = lax.fori_loop(1, turns, return_more, grad_table + put(asked, returned_rows))
+        return total + put(later_asked, returned(later_keys, later_asked.shape[0]))
+
+    returned_rows, wide_grad_job = lax.optimization_barrier(
+        (returned(keys, devices * SLOTS), wide_grad_job)
+    )
+    share_table = lax.fori_loop(
+        0, later_turns, return_more, grad_table + put(asked, returned_rows))
     width = vector_master.shape[1]
     vector_notes = grad_vector.reshape(-1, devices, width).transpose(1, 0, 2).reshape(devices, -1)
     vector_notes = jnp.concatenate(
@@ -811,9 +829,6 @@
     )
     ortho_square = square_moment_new / (moment_norm[:7][:, None, None] + ortho_epsilon)
     ortho_wide = wide_moment_new / (moment_norm[7:][:, None, None] + ortho_epsilon)
-    table_step, table_first_new, table_second_new = adam_step(
-        table_master, table_first, table_second, share_table, factor, adam_count
-    )
     wide_inverse = 1.0 / (moment_norm[squares:] + ortho_epsilon)
     wide_inverse = jnp.pad(wide_inverse, (0, members - wides))[member]
     square_inverse = 1.0 / (moment_norm[:squares] + ortho_epsilon)
@@ -838,6 +853,10 @@
     gram = jnp.where(core == 0, wide_gram.astype(jnp.float32), square_gram)
     rest_b = ortho_rest(gram)
     power = leading_coefficient**NS_ITERS
+    share_table, rest_b = lax.optimization_barrier((share_table, rest_b))
+    table_step, table_first_new, table_second_new = adam_step(
+        table_master, table_first, table_second, share_table, factor, adam_count
+    )
     wide_rest = jnp.where(core == 0, rest_b, other_core(rest_b))
     back_square = square_product(square_job, rest_b).astype(jnp.bfloat16)
     half_rows = square_half.shape[0]

time: 1000 us -> 966 us (0.966)
  waiting for transfers between devices: 489 us -> 469 us
    all_gather x0 -> x1, waiting for transfers between devices: none -> 40.2 us  [body(): moment_rows = lax.all_gather(moment_rows, 'vocab', axis=0)]
    all_to_all x5, waiting for transfers between devices: 95.6 us -> 58.7 us  [exchanged(): return lax.all_to_all(rows, ALL, 0, 0, tiled=True)]
    ppermute x48 -> x45, waiting for transfers between devices: 255 us -> 220 us  [turned(): lax.ppermute(values, axis, [(i, (i + step) % count) for i in range(count)])]
    all_gather x1, waiting for transfers between devices: 12.9 us -> 38 us  [body(): lax.all_gather(square_master.astype(jnp.bfloat16), ALL, axis=1, tiled=True)]
    reduce_scatter x1, waiting for transfers between devices: 16.8 us -> 0.01 us  [body(): lax.psum_scatter(grad_wide, DP, scatter_dimension=1, tiled=True)]
    ppermute x48 -> x45, starting transfers between devices: 63.8 us -> 57.1 us  [turned(): lax.ppermute(values, axis, [(i, (i + step) % count) for i in range(count)])]
  transfers between devices with their start and end apart: 66 -> 64, of which waited for: 39 -> 36; matrix products, arithmetic and copies ran while one was open for 20% -> 23% of each run, Pallas kernels for 4% -> 2%
where the time goes in v6:
time: 966 us; the launch traced here: 958 us
  waiting for transfers between devices  469 us (49%)
  matrix products  118 us (12%)
  other arithmetic  110 us (11%)
  starting transfers between devices  89 us (9%)
  Pallas kernels  71.3 us (7%)
  local copies, waits for them, and re-layouts  69.5 us (7%)
  between operations  31 us (3%)
    ppermute x45, waiting for transfers between devices, turned(): lax.ppermute(values, axis, [(i, (i + step) % count) for i in range(count)])  220 us
    all_gather x1, waiting for transfers between devices, body(): response_tokens = lax.all_gather(final_b, ALL, axis=0, tiled=True)  67.2 us
    all_to_all x5, waiting for transfers between devices, exchanged(): return lax.all_to_all(rows, ALL, 0, 0, tiled=True)  58.7 us
    ppermute x45, starting transfers between devices, turned(): lax.ppermute(values, axis, [(i, (i + step) % count) for i in range(count)])  57.1 us
    all_gather x1, waiting for transfers between devices, body(): moment_rows = lax.all_gather(moment_rows, 'vocab', axis=0)  40.2 us
    all_gather x1, waiting for transfers between devices, body(): lax.all_gather(square_master.astype(jnp.bfloat16), ALL, axis=1, tiled=True)  38 us
    dot_general x11, matrix products, outer(): lax.dot_general(grads, inputs, (((0,), (0,)), ((), ())), preferred_elemen...  34.2 us
    dot_general x6, matrix products, back_dense(): return jnp.dot(grads, weight, preferred_element_type=jnp.float32)  26 us
  transfers between devices with their start and end apart: 64, of which 36 were waited for; matrix products, arithmetic and copies ran while one was open for 23% of the time, Pallas kernels for 2%

profile of v6, /device:TPU:0, one launch (start us, length us, event | category | flops | bytes accessed | tf_op | source)
XLA Modules:
  0.0 957.5 jit_solution(2530393168274831109)
XLA Ops:
  19.5 7.3 all-to-all-start.4
  26.8 6.1 convert_element_type.396.table_ref
  35.3 6.8 fusion.56
  42.2 4.1 all-to-all-start.5
  56.3 44.9 %all-to-all-done.5 = bf16[32,24,1024]{2,1,0:T(8,128)(2,1)S(1)} async-done(((bf16[32,24,1024]{2,1,0:T(8,128)(2,1)}), bf16[32,24,1024]{2,1,0:T(8,128)(2,1)S(1)}, u32[]{:S(2)}, u32[]{:S(2)}) %all-to-all-start.5) | async-done | bytes 1572896 | tf_op jit(solution)/shard_map/all_to_all | solution.py:112
  105.3 38.0 %all-gather.6.cloned.1.call-done = bf16[7,1024,1024]{2,1,0:T(8,128)(2,1)} async-done(((bf16[7,32,1024]{2,1,0:T(8,128)(2,1)}), bf16[7,1024,1024]{2,1,0:T(8,128)(2,1)}) %all-gather.6.cloned.1.call-update) | async-done | bytes 14680080 | tf_op jit(solution)/shard_map/all_gather | solution.py:468
  143.3 6.2 slice.358
  149.6 6.1 fusion.145
  181.3 12.1 %all-gather.8.cloned.1.call-done = bf16[3,1152,1024]{2,1,0:T(8,128)(2,1)} async-done(((bf16[3,144,1024]{2,1,0:T(8,128)(2,1)}), bf16[3,1152,1024]{2,1,0:T(8,128)(2,1)}) %all-gather.8.cloned.1.call-update) | async-done | bytes 7077904 | tf_op jit(solution)/shard_map/all_gather | solution.py:469
  210.1 5.1 collective-permute-done.5
  215.2 6.9 collective-permute-done.4
  230.0 67.2 %all-gather.10.cloned.1.call-done.answers_ref = bf16[3072,1024]{1,0:T(8,128)(2,1)} async-done(((bf16[96,1024]{1,0:T(8,128)(2,1)}), bf16[3072,1024]{1,0:T(8,128)(2,1)}) %all-gather.10.cloned.1.call-update) | async-done | bytes 6291472 | tf_op jit(solution)/shard_map/all_gather | solution.py:578
  300.1 25.4 %shard_map.313 = (bf16[2048,3072]{1,0:T(8,128)(2,1)}, f32[8,3072]{1,0:T(8,128)S(1)}) custom-call(s32[1,3072]{1,0:T(1,128)S(1)} %compare_select_fusion.target_ref, bf16[3072,1024]{1,0:T(8,128)(2,1)S(1)} %copy-done, bf16[2048,1024]{1,0:T(8,128)(2,1)} %get-tuple-element.677), custom_call_target="tpu_custom_call" | custom-call | flops 12884901888 | bytes 18874368 | tf_op jit(solution)/shard_map/pallas_call | solution.py:347
  329.9 6.9 all-to-all-done.6
  341.5 7.0 all-to-all-done.7
  350.2 10.3 %shard_map.315 = bf16[1536,1024]{1,0:T(8,128)(2,1)S(1)} custom-call(s32[1]{0:T(128)} %bitcast.52.core_ref, s32[1,3072]{1,0:T(1,128)S(1)} %compare_select_fusion.target_ref, f32[1,3072]{1,0:T(1,128)S(1)} %get-tuple-element.442.scale_ref, f32[1,3072]{1,0:T(1,128)S(1)} %get-tuple-element.441.value_ref, bf16[2048,3072]{1,0:T(8,128)(2,1)} %get-tuple-element.249.shares_ref, ...), custom_call_target="tpu_custom_call" | custom-call | flops 6442450944 | bytes 9437184 | tf_op jit(solution)/shard_map/pallas_call | solution.py:389
  360.9 10.4 %shard_map.314 = bf16[1536,1024]{1,0:T(8,128)(2,1)S(1)} custom-call(s32[1]{0:T(128)} %bitcast.51.core_ref, s32[1,3072]{1,0:T(1,128)S(1)} %compare_select_fusion.target_ref, f32[1,3072]{1,0:T(1,128)S(1)} %get-tuple-element.442.scale_ref, f32[1,3072]{1,0:T(1,128)S(1)} %get-tuple-element.441.value_ref, bf16[2048,3072]{1,0:T(8,128)(2,1)} %get-tuple-element.249.shares_ref, ...), custom_call_target="tpu_custom_call" | custom-call | flops 6442450944 | bytes 9437184 | tf_op jit(solution)/shard_map/pallas_call | solution.py:389
  378.1 17.5 %fusion.12 = f32[2048,1024]{1,0:T(8,128)} fusion(bf16[3072,1024]{1,0:T(8,128)(2,1)} %all-gather.10.cloned.1.call-done.answers_ref, bf16[2048,3072]{1,0:T(8,128)(2,1)S(1)} %bitcast.478, f32[3072]{0:T(1024)S(1)} %bitcast.370, f32[3072]{0:T(1024)S(1)} %bitcast.369, s32[3072]{0:T(1024)S(1)} %fusion.117), kind=kOutput, calls=%fused_computation.31 | convolution fusion | flops 12910067712 | bytes 27299840 | tf_op jit(solution)/shard_map/dot_general | solution.py:642
  395.6 16.5 %collective-permute-done.8 = bf16[384,1024]{1,0:T(8,128)(2,1)S(1)} collective-permute-done((bf16[384,1024]{1,0:T(8,128)(2,1)S(1)}, bf16[384,1024]{1,0:T(8,128)(2,1)S(1)}, u32[]{:S(2)}, u32[]{:S(2)}) %collective-permute-start.8) | collective-permute-done | bytes 786464 | tf_op jit(solution)/shard_map/ppermute | solution.py:122
  412.7 40.2 %all-gather.12.cloned.1.call-done = bf16[3200,1024]{1,0:T(8,128)(2,1)} async-done(((bf16[800,1024]{1,0:T(8,128)(2,1)}), bf16[3200,1024]{1,0:T(8,128)(2,1)}) %all-gather.12.cloned.1.call-update) | async-done | bytes 6553616 | tf_op jit(solution)/shard_map/all_gather | solution.py:599
  461.3 5.5 collective-permute-done.12
  466.8 10.0 %collective-permute-done.11 = bf16[96,1024]{1,0:T(8,128)(2,1)S(1)} collective-permute-done((bf16[96,1024]{1,0:T(8,128)(2,1)S(1)}, bf16[96,1024]{1,0:T(8,128)(2,1)S(1)}, u32[]{:S(2)}, u32[]{:S(2)}) %collective-permute-start.11) | collective-permute-done | bytes 196640 | tf_op jit(solution)/shard_map/ppermute | solution.py:122
  483.8 14.3 %collective-permute-done.14 = bf16[96,1024]{1,0:T(8,128)(2,1)S(1)} collective-permute-done((bf16[96,1024]{1,0:T(8,128)(2,1)S(1)}, bf16[96,1024]{1,0:T(8,128)(2,1)S(1)}, u32[]{:S(2)}, u32[]{:S(2)}) %collective-permute-start.14) | collective-permute-done | bytes 196640 | tf_op jit(solution)/shard_map/ppermute | solution.py:122
  509.7 4.6 convolution_convert_fusion.6
  518.9 5.3 collective-permute-done.18
  524.2 7.0 collective-permute-done.17
  556.1 8.3 multiply_reduce_fusion.1
  569.9 5.0 convolution_convert_fusion.2
  588.4 8.3 multiply_reduce_fusion.5
  602.2 5.9 all-to-all-start.8
  610.4 5.1 all-to-all-done.8
  627.8 23.8 %collective-permute-done.24 = bf16[144,1024]{1,0:T(8,128)(2,1)S(1)} collective-permute-done((bf16[144,1024]{1,0:T(8,128)(2,1)S(1)}, bf16[144,1024]{1,0:T(8,128)(2,1)S(1)}, u32[]{:S(2)}, u32[]{:S(2)}) %collective-permute-start.24) | collective-permute-done | bytes 294944 | tf_op jit(solution)/shard_map/ppermute | solution.py:122
  651.6 30.1 %collective-permute-done.23 = bf16[144,1024]{1,0:T(8,128)(2,1)S(1)} collective-permute-done((bf16[144,1024]{1,0:T(8,128)(2,1)S(1)}, bf16[144,1024]{1,0:T(8,128)(2,1)S(1)}, u32[]{:S(2)}, u32[]{:S(2)}) %collective-permute-start.23) | collective-permute-done | bytes 294944 | tf_op jit(solution)/shard_map/ppermute | solution.py:122
  681.9 9.1 fusion.19
  691.0 18.1 %reduce-scatter.5.cloned.1.call-done = bf16[7,128,1024]{2,1,0:T(8,128)(2,1)} async-done(((bf16[7,1024,1024]{2,1,0:T(8,128)(2,1)}), bf16[7,128,1024]{2,1,0:T(8,128)(2,1)}) %reduce-scatter.5.cloned.1.call-update) | async-done | bytes 1835024 | tf_op jit(solution)/shard_map/reduce_scatter | solution.py:749
  717.7 6.1 multiply_reduce_fusion
  723.8 5.4 collective-permute-done.21
  729.2 32.6 %collective-permute-done.20 = bf16[2,128,1024]{2,1,0:T(8,128)(2,1)} collective-permute-done((bf16[2,128,1024]{2,1,0:T(8,128)(2,1)}, bf16[2,128,1024]{2,1,0:T(8,128)(2,1)}, u32[]{:S(2)}, u32[]{:S(2)}) %collective-permute-start.20) | collective-permute-done | bytes 524320 | tf_op jit(solution)/shard_map/ppermute | solution.py:122
  769.3 4.0 all-to-all-start.10
  773.9 6.4 all-to-all-done.10
  803.3 6.2 collective-permute-done.35
  811.0 9.4 collective-permute-done.34
  830.4 5.4 collective-permute-done.37
  842.5 25.2 %shard_map.316 = bf16[1024,1024]{1,0:T(8,128)(2,1)S(1)} custom-call(f32[1024,1024]{1,0:T(8,128)S(1)} %convert_select_fusion.gram_ref), custom_call_target="tpu_custom_call" | custom-call | flops 19327352832 | bytes 6291456 | tf_op jit(solution)/shard_map/pallas_call | solution.py:293
  872.6 22.7 %add_multiply_fusion = (f32[2048,1024]{1,0:T(8,128)}, f32[2048,1024]{1,0:T(8,128)}, f32[2048,1024]{1,0:T(8,128)}) fusion(f32[2048,1024]{1,0:T(8,128)} %param.25, f32[]{:T(128)S(6)} %sub.255, f32[]{:T(128)S(6)} %sub.254, f32[2048,1024]{1,0:T(8,128)} %get-tuple-element.267, f32[]{:T(128)S(6)} %min.3, f32[2048,1024]{1,0:T(8,128)} %param.27, f32[2048,1024]{1,0:T(8,128)} %param.26), kind=kLoop, calls=%fused_computation.37 | loop fusion | flops 31457280 | bytes 58720268 | tf_op jit(solution)/shard_map/mul | solution.py:100
  914.2 12.0 %collective-permute-done.46 = bf16[144,1024]{1,0:T(8,128)(2,1)S(1)} collective-permute-done((bf16[144,1024]{1,0:T(8,128)(2,1)S(1)}, bf16[144,1024]{1,0:T(8,128)(2,1)S(1)}, u32[]{:S(2)}, u32[]{:S(2)}) %collective-permute-start.46) | collective-permute-done | bytes 294944 | tf_op jit(solution)/shard_map/ppermute | solution.py:122
  926.7 6.3 collective-permute-start.50
  937.6 8.7 collective-permute-done.49
  (708 shorter events, 270.3 us)
Async XLA Ops:
  7.2 136.2 %all-gather.6.cloned.1.call-start = ((), (), s32[]{:S(2)}) async-start(), calls=%async_computation.13 | async-start | bytes 15138816 | tf_op jit(solution)/shard_map/all_gather | solution.py:468
  19.5 15.1 %all-to-all-start.4 = ((f32[32,1,349]{2,1,0:T(1,128)}), f32[32,1,349]{2,1,0:T(1,128)S(1)}, u32[]{:S(2)}, u32[]{:S(2)}) async-start(f32[32,1,349]{2,1,0:T(1,128)} %all_to_all.79), calls=%async_computation.4 | async-start | bytes 98304 | tf_op jit(solution)/shard_map/all_to_all | solution.py:112
  42.2 59.0 %all-to-all-start.5 = ((bf16[32,24,1024]{2,1,0:T(8,128)(2,1)}), bf16[32,24,1024]{2,1,0:T(8,128)(2,1)S(1)}, u32[]{:S(2)}, u32[]{:S(2)}) async-start(bf16[32,24,1024]{2,1,0:T(8,128)(2,1)} %bitcast.417), calls=%async_computation.5 | async-start | bytes 3145728 | tf_op jit(solution)/shard_map/all_to_all | solution.py:112
  46.3 147.1 %all-gather.8.cloned.1.call-start = ((), (), s32[]{:S(2)}) async-start(), calls=%async_computation.14 | async-start | bytes 7962624 | tf_op jit(solution)/shard_map/all_gather | solution.py:469
  47.4 249.8 %all-gather.10.cloned.1.call-start = ((), (), s32[]{:S(2)}) async-start(), calls=%async_computation.15 | async-start | bytes 6488064 | tf_op jit(solution)/shard_map/all_gather | solution.py:578
  177.8 18.5 %collective-permute-start.2 = (bf16[96,1024]{1,0:T(8,128)(2,1)S(1)}, bf16[96,1024]{1,0:T(8,128)(2,1)S(1)}, u32[]{:S(2)}, u32[]{:S(2)}) collective-permute-start(bf16[96,1024]{1,0:T(8,128)(2,1)S(1)} %multiply_convert_fusion.9), channel_id=1, source_target_pairs={{0,3},{1,0},{2,1},{3,2},{4,7},{5,4},{6,5},{7,6},{8,11},{9,8},{10,9... | collective-permute-start | bytes 589832 | tf_op jit(solution)/shard_map/ppermute | solution.py:122
  178.6 18.7 %collective-permute-start.1 = (bf16[96,1024]{1,0:T(8,128)(2,1)S(1)}, bf16[96,1024]{1,0:T(8,128)(2,1)S(1)}, u32[]{:S(2)}, u32[]{:S(2)}) collective-permute-start(bf16[96,1024]{1,0:T(8,128)(2,1)S(1)} %multiply_convert_fusion.9), channel_id=1, source_target_pairs={{0,2},{1,3},{2,0},{3,1},{4,6},{5,7},{6,4},{7,5},{8,10},{9,11},{10,... | collective-permute-start | bytes 589832 | tf_op jit(solution)/shard_map/ppermute | solution.py:122
  179.6 17.7 %collective-permute-start = (bf16[96,1024]{1,0:T(8,128)(2,1)S(1)}, bf16[96,1024]{1,0:T(8,128)(2,1)S(1)}, u32[]{:S(2)}, u32[]{:S(2)}) collective-permute-start(bf16[96,1024]{1,0:T(8,128)(2,1)S(1)} %multiply_convert_fusion.9), channel_id=1, source_target_pairs={{0,1},{1,2},{2,3},{3,0},{4,5},{5,6},{6,7},{7,4},{8,9},{9,10},{10,1... | collective-permute-start | bytes 589832 | tf_op jit(solution)/shard_map/ppermute | solution.py:122
  205.9 16.2 %collective-permute-start.4 = (bf16[96,1024]{1,0:T(8,128)(2,1)S(1)}, bf16[96,1024]{1,0:T(8,128)(2,1)}, u32[]{:S(2)}, u32[]{:S(2)}) collective-permute-start(bf16[96,1024]{1,0:T(8,128)(2,1)S(1)} %get-tuple-element.417), channel_id=1, source_target_pairs={{0,2},{1,3},{2,0},{3,1},{4,6},{5,7},{6,4},{7,5},{8,10},{9,11},{10,... | collective-permute-start | bytes 589832 | tf_op jit(solution)/shard_map/ppermute | solution.py:122
  208.3 13.8 %collective-permute-start.3 = (bf16[96,1024]{1,0:T(8,128)(2,1)S(1)}, bf16[96,1024]{1,0:T(8,128)(2,1)}, u32[]{:S(2)}, u32[]{:S(2)}) collective-permute-start(bf16[96,1024]{1,0:T(8,128)(2,1)S(1)} %get-tuple-element.415), channel_id=1, source_target_pairs={{0,3},{1,0},{2,1},{3,2},{4,7},{5,4},{6,5},{7,6},{8,11},{9,8},{10,9... | collective-permute-start | bytes 589832 | tf_op jit(solution)/shard_map/ppermute | solution.py:122
  329.3 123.6 %all-gather.12.cloned.1.call-start = ((), (), s32[]{:S(2)}) async-start(), calls=%async_computation.18 | async-start | bytes 8192000 | tf_op jit(solution)/shard_map/all_gather | solution.py:599
  341.5 246.1 %reduce-scatter.3.cloned.1.call-start = ((), (), s32[]{:S(2)}) async-start(), calls=%async_computation.16 | async-start | bytes 7962624 | tf_op jit(solution)/shard_map/reduce_scatter | solution.py:744
  375.2 20.4 %collective-permute-start.9 = (bf16[384,1024]{1,0:T(8,128)(2,1)S(1)}, bf16[384,1024]{1,0:T(8,128)(2,1)S(1)}, u32[]{:S(2)}, u32[]{:S(2)}) collective-permute-start(bf16[384,1024]{1,0:T(8,128)(2,1)S(1)} %get-tuple-element.371), channel_id=1, source_target_pairs={{0,24},{8,0},{16,8},{24,16},{1,25},{9,1},{17,9},{25,17},{2,26},{10... | collective-permute-start | bytes 2359304 | tf_op jit(solution)/shard_map/ppermute | solution.py:122
  375.8 36.3 %collective-permute-start.8 = (bf16[384,1024]{1,0:T(8,128)(2,1)S(1)}, bf16[384,1024]{1,0:T(8,128)(2,1)S(1)}, u32[]{:S(2)}, u32[]{:S(2)}) collective-permute-start(bf16[384,1024]{1,0:T(8,128)(2,1)S(1)} %get-tuple-element.372), channel_id=1, source_target_pairs={{0,16},{8,24},{16,0},{24,8},{1,17},{9,25},{17,1},{25,9},{2,18},{10... | collective-permute-start | bytes 2359304 | tf_op jit(solution)/shard_map/ppermute | solution.py:122
  377.3 34.8 %collective-permute-start.7 = (bf16[384,1024]{1,0:T(8,128)(2,1)S(1)}, bf16[384,1024]{1,0:T(8,128)(2,1)S(1)}, u32[]{:S(2)}, u32[]{:S(2)}) collective-permute-start(bf16[384,1024]{1,0:T(8,128)(2,1)S(1)} %get-tuple-element.370), channel_id=1, source_target_pairs={{0,8},{8,16},{16,24},{24,0},{1,9},{9,17},{17,25},{25,1},{2,10},{10... | collective-permute-start | bytes 2359304 | tf_op jit(solution)/shard_map/ppermute | solution.py:122
  459.0 17.8 %collective-permute-start.11 = (bf16[96,1024]{1,0:T(8,128)(2,1)S(1)}, bf16[96,1024]{1,0:T(8,128)(2,1)S(1)}, u32[]{:S(2)}, u32[]{:S(2)}) collective-permute-start(bf16[96,1024]{1,0:T(8,128)(2,1)S(1)} %get-tuple-element.414), channel_id=1, source_target_pairs={{0,2},{1,3},{2,0},{3,1},{4,6},{5,7},{6,4},{7,5},{8,10},{9,11},{10,... | collective-permute-start | bytes 589832 | tf_op jit(solution)/shard_map/ppermute | solution.py:122
  459.3 17.4 %collective-permute-start.10 = (bf16[96,1024]{1,0:T(8,128)(2,1)S(1)}, bf16[96,1024]{1,0:T(8,128)(2,1)S(1)}, u32[]{:S(2)}, u32[]{:S(2)}) collective-permute-start(bf16[96,1024]{1,0:T(8,128)(2,1)S(1)} %get-tuple-element.412), channel_id=1, source_target_pairs={{0,1},{1,2},{2,3},{3,0},{4,5},{5,6},{6,7},{7,4},{8,9},{9,10},{10,1... | collective-permute-start | bytes 589832 | tf_op jit(solution)/shard_map/ppermute | solution.py:122
  477.8 20.4 %collective-permute-start.14 = (bf16[96,1024]{1,0:T(8,128)(2,1)S(1)}, bf16[96,1024]{1,0:T(8,128)(2,1)S(1)}, u32[]{:S(2)}, u32[]{:S(2)}) collective-permute-start(bf16[96,1024]{1,0:T(8,128)(2,1)S(1)} %fusion.144), channel_id=1, source_target_pairs={{0,2},{1,3},{2,0},{3,1},{4,6},{5,7},{6,4},{7,5},{8,10},{9,11},{10,... | collective-permute-start | bytes 589832 | tf_op jit(solution)/shard_map/ppermute | solution.py:122
  480.5 17.6 %collective-permute-start.13 = (bf16[96,1024]{1,0:T(8,128)(2,1)S(1)}, bf16[96,1024]{1,0:T(8,128)(2,1)S(1)}, u32[]{:S(2)}, u32[]{:S(2)}) collective-permute-start(bf16[96,1024]{1,0:T(8,128)(2,1)S(1)} %fusion.144), channel_id=1, source_target_pairs={{0,1},{1,2},{2,3},{3,0},{4,5},{5,6},{6,7},{7,4},{8,9},{9,10},{10,1... | collective-permute-start | bytes 589832 | tf_op jit(solution)/shard_map/ppermute | solution.py:122
  509.6 199.5 %reduce-scatter.5.cloned.1.call-start = ((), (), s32[]{:S(2)}) async-start(), calls=%async_computation.17 | async-start | bytes 16515072 | tf_op jit(solution)/shard_map/reduce_scatter | solution.py:749
  514.5 16.7 %collective-permute-start.17 = (bf16[96,1024]{1,0:T(8,128)(2,1)S(1)}, bf16[96,1024]{1,0:T(8,128)(2,1)S(1)}, u32[]{:S(2)}, u32[]{:S(2)}) collective-permute-start(bf16[96,1024]{1,0:T(8,128)(2,1)S(1)} %get-tuple-element.411), channel_id=1, source_target_pairs={{0,2},{1,3},{2,0},{3,1},{4,6},{5,7},{6,4},{7,5},{8,10},{9,11},{10,... | collective-permute-start | bytes 589832 | tf_op jit(solution)/shard_map/ppermute | solution.py:122
  514.5 16.6 %collective-permute-start.16 = (bf16[96,1024]{1,0:T(8,128)(2,1)S(1)}, bf16[96,1024]{1,0:T(8,128)(2,1)S(1)}, u32[]{:S(2)}, u32[]{:S(2)}) collective-permute-start(bf16[96,1024]{1,0:T(8,128)(2,1)S(1)} %get-tuple-element.409), channel_id=1, source_target_pairs={{0,3},{1,0},{2,1},{3,2},{4,7},{5,4},{6,5},{7,6},{8,11},{9,8},{10,9... | collective-permute-start | bytes 589832 | tf_op jit(solution)/shard_map/ppermute | solution.py:122
  602.2 13.3 %all-to-all-start.8 = ((f32[32,1,352]{2,1,0:T(1,128)}), f32[32,1,352]{2,1,0:T(1,128)S(1)}, u32[]{:S(2)}, u32[]{:S(2)}) async-start(f32[32,1,352]{2,1,0:T(1,128)} %copy.132), calls=%async_computation.10 | async-start | bytes 98304 | tf_op jit(solution)/shard_map/all_to_all | solution.py:112
  615.5 66.3 %all-to-all-start.9 = ((bf16[32,24,1024]{2,1,0:T(8,128)(2,1)}), bf16[32,24,1024]{2,1,0:T(8,128)(2,1)}, u32[]{:S(2)}, u32[]{:S(2)}) async-start(bf16[32,24,1024]{2,1,0:T(8,128)(2,1)} %bitcast.418), calls=%async_computation.11 | async-start | bytes 3145728 | tf_op jit(solution)/shard_map/all_to_all | solution.py:112
  621.4 30.2 %collective-permute-start.24 = (bf16[144,1024]{1,0:T(8,128)(2,1)S(1)}, bf16[144,1024]{1,0:T(8,128)(2,1)S(1)}, u32[]{:S(2)}, u32[]{:S(2)}) collective-permute-start(bf16[144,1024]{1,0:T(8,128)(2,1)S(1)} %get-tuple-element.406), channel_id=1, source_target_pairs={{0,3},{1,0},{2,1},{3,2},{4,7},{5,4},{6,5},{7,6},{8,11},{9,8},{10,9... | collective-permute-start | bytes 884744 | tf_op jit(solution)/shard_map/ppermute | solution.py:122
  625.0 56.7 %collective-permute-start.23 = (bf16[144,1024]{1,0:T(8,128)(2,1)S(1)}, bf16[144,1024]{1,0:T(8,128)(2,1)S(1)}, u32[]{:S(2)}, u32[]{:S(2)}) collective-permute-start(bf16[144,1024]{1,0:T(8,128)(2,1)S(1)} %get-tuple-element.408), channel_id=1, source_target_pairs={{0,2},{1,3},{2,0},{3,1},{4,6},{5,7},{6,4},{7,5},{8,10},{9,11},{10,... | collective-permute-start | bytes 884744 | tf_op jit(solution)/shard_map/ppermute | solution.py:122
  625.0 56.7 %collective-permute-start.22 = (bf16[144,1024]{1,0:T(8,128)(2,1)S(1)}, bf16[144,1024]{1,0:T(8,128)(2,1)S(1)}, u32[]{:S(2)}, u32[]{:S(2)}) collective-permute-start(bf16[144,1024]{1,0:T(8,128)(2,1)S(1)} %get-tuple-element.407), channel_id=1, source_target_pairs={{0,1},{1,2},{2,3},{3,0},{4,5},{5,6},{6,7},{7,4},{8,9},{9,10},{10,1... | collective-permute-start | bytes 884744 | tf_op jit(solution)/shard_map/ppermute | solution.py:122
  713.2 16.0 %collective-permute-start.21 = (bf16[2,128,1024]{2,1,0:T(8,128)(2,1)}, bf16[2,128,1024]{2,1,0:T(8,128)(2,1)}, u32[]{:S(2)}, u32[]{:S(2)}) collective-permute-start(bf16[2,128,1024]{2,1,0:T(8,128)(2,1)} %get-tuple-element.376), channel_id=1, source_target_pairs={{0,3},{1,0},{2,1},{3,2},{4,7},{5,4},{6,5},{7,6},{8,11},{9,8},{10,9... | collective-permute-start | bytes 1572872 | tf_op jit(solution)/shard_map/ppermute | solution.py:122
  716.5 45.3 %collective-permute-start.20 = (bf16[2,128,1024]{2,1,0:T(8,128)(2,1)}, bf16[2,128,1024]{2,1,0:T(8,128)(2,1)}, u32[]{:S(2)}, u32[]{:S(2)}) collective-permute-start(bf16[2,128,1024]{2,1,0:T(8,128)(2,1)} %get-tuple-element.377), channel_id=1, source_target_pairs={{0,2},{1,3},{2,0},{3,1},{4,6},{5,7},{6,4},{7,5},{8,10},{9,11},{10,... | collective-permute-start | bytes 1572872 | tf_op jit(solution)/shard_map/ppermute | solution.py:122
  716.5 45.3 %collective-permute-start.19 = (bf16[2,128,1024]{2,1,0:T(8,128)(2,1)S(1)}, bf16[2,128,1024]{2,1,0:T(8,128)(2,1)}, u32[]{:S(2)}, u32[]{:S(2)}) collective-permute-start(bf16[2,128,1024]{2,1,0:T(8,128)(2,1)S(1)} %get-tuple-element.375), channel_id=1, source_target_pairs={{0,1},{1,2},{2,3},{3,0},{4,5},{5,6},{6,7},{7,4},{8,9},{9,10},{10,1... | collective-permute-start | bytes 1572872 | tf_op jit(solution)/shard_map/ppermute | solution.py:122
  794.5 29.1 %collective-permute-start.28 = (bf16[128,1024]{1,0:T(8,128)(2,1)}, bf16[128,1024]{1,0:T(8,128)(2,1)S(1)}, u32[]{:S(2)}, u32[]{:S(2)}) collective-permute-start(bf16[128,1024]{1,0:T(8,128)(2,1)} %get-tuple-element.439), channel_id=1, source_target_pairs={{0,8},{8,16},{16,24},{24,0},{1,9},{9,17},{17,25},{25,1},{2,10},{10... | collective-permute-start | bytes 786440 | tf_op jit(solution)/shard_map/ppermute | solution.py:122
  795.1 28.7 %collective-permute-start.29 = (bf16[128,1024]{1,0:T(8,128)(2,1)}, bf16[128,1024]{1,0:T(8,128)(2,1)}, u32[]{:S(2)}, u32[]{:S(2)}) collective-permute-start(bf16[128,1024]{1,0:T(8,128)(2,1)} %get-tuple-element.440), channel_id=1, source_target_pairs={{0,16},{8,24},{16,0},{24,8},{1,17},{9,25},{17,1},{25,9},{2,18},{10... | collective-permute-start | bytes 786440 | tf_op jit(solution)/shard_map/ppermute | solution.py:122
  797.5 12.1 %collective-permute-start.35 = (bf16[128,1024]{1,0:T(8,128)(2,1)S(1)}, bf16[128,1024]{1,0:T(8,128)(2,1)S(1)}, u32[]{:S(2)}, u32[]{:S(2)}) collective-permute-start(bf16[128,1024]{1,0:T(8,128)(2,1)S(1)} %get-tuple-element.401), channel_id=1, source_target_pairs={{0,24},{8,0},{16,8},{24,16},{1,25},{9,1},{17,9},{25,17},{2,26},{10... | collective-permute-start | bytes 786440 | tf_op jit(solution)/shard_map/ppermute | solution.py:122
  799.9 20.5 %collective-permute-start.34 = (bf16[128,1024]{1,0:T(8,128)(2,1)S(1)}, bf16[128,1024]{1,0:T(8,128)(2,1)S(1)}, u32[]{:S(2)}, u32[]{:S(2)}) collective-permute-start(bf16[128,1024]{1,0:T(8,128)(2,1)S(1)} %get-tuple-element.402), channel_id=1, source_target_pairs={{0,16},{8,24},{16,0},{24,8},{1,17},{9,25},{17,1},{25,9},{2,18},{10... | collective-permute-start | bytes 786440 | tf_op jit(solution)/shard_map/ppermute | solution.py:122
  801.3 19.1 %collective-permute-start.33 = (bf16[128,1024]{1,0:T(8,128)(2,1)S(1)}, bf16[128,1024]{1,0:T(8,128)(2,1)S(1)}, u32[]{:S(2)}, u32[]{:S(2)}) collective-permute-start(bf16[128,1024]{1,0:T(8,128)(2,1)S(1)} %get-tuple-element.400), channel_id=1, source_target_pairs={{0,8},{8,16},{16,24},{24,0},{1,9},{9,17},{17,25},{25,1},{2,10},{10... | collective-permute-start | bytes 786440 | tf_op jit(solution)/shard_map/ppermute | solution.py:122
  809.5 14.8 %collective-permute-start.30 = (bf16[128,1024]{1,0:T(8,128)(2,1)}, bf16[128,1024]{1,0:T(8,128)(2,1)S(1)}, u32[]{:S(2)}, u32[]{:S(2)}) collective-permute-start(bf16[128,1024]{1,0:T(8,128)(2,1)} %get-tuple-element.438), channel_id=1, source_target_pairs={{0,24},{8,0},{16,8},{24,16},{1,25},{9,1},{17,9},{25,17},{2,26},{10... | collective-permute-start | bytes 786440 | tf_op jit(solution)/shard_map/ppermute | solution.py:122
  823.0 12.8 %collective-permute-start.37 = (bf16[128,1024]{1,0:T(8,128)(2,1)S(1)}, bf16[128,1024]{1,0:T(8,128)(2,1)S(1)}, u32[]{:S(2)}, u32[]{:S(2)}) collective-permute-start(bf16[128,1024]{1,0:T(8,128)(2,1)S(1)} %fusion.90), channel_id=1, source_target_pairs={{0,16},{8,24},{16,0},{24,8},{1,17},{9,25},{17,1},{25,9},{2,18},{10... | collective-permute-start | bytes 786440 | tf_op jit(solution)/shard_map/ppermute | solution.py:122
  823.6 12.2 %collective-permute-start.36 = (bf16[128,1024]{1,0:T(8,128)(2,1)S(1)}, bf16[128,1024]{1,0:T(8,128)(2,1)S(1)}, u32[]{:S(2)}, u32[]{:S(2)}) collective-permute-start(bf16[128,1024]{1,0:T(8,128)(2,1)S(1)} %fusion.90), channel_id=1, source_target_pairs={{0,8},{8,16},{16,24},{24,0},{1,9},{9,17},{17,25},{25,1},{2,10},{10... | collective-permute-start | bytes 786440 | tf_op jit(solution)/shard_map/ppermute | solution.py:122
  823.8 13.6 %collective-permute-start.27 = (bf16[2,32,1024]{2,1,0:T(8,128)(2,1)S(1)}, bf16[2,32,1024]{2,1,0:T(8,128)(2,1)S(1)}, u32[]{:S(2)}, u32[]{:S(2)}) collective-permute-start(bf16[2,32,1024]{2,1,0:T(8,128)(2,1)S(1)} %copy-done.92), channel_id=1, source_target_pairs={{0,3},{1,0},{2,1},{3,2},{4,7},{5,4},{6,5},{7,6},{8,11},{9,8},{10,9... | collective-permute-start | bytes 393224 | tf_op jit(solution)/shard_map/ppermute | solution.py:122
  824.4 13.0 %collective-permute-start.26 = (bf16[2,32,1024]{2,1,0:T(8,128)(2,1)S(1)}, bf16[2,32,1024]{2,1,0:T(8,128)(2,1)S(1)}, u32[]{:S(2)}, u32[]{:S(2)}) collective-permute-start(bf16[2,32,1024]{2,1,0:T(8,128)(2,1)S(1)} %copy-done.91), channel_id=1, source_target_pairs={{0,2},{1,3},{2,0},{3,1},{4,6},{5,7},{6,4},{7,5},{8,10},{9,11},{10,... | collective-permute-start | bytes 393224 | tf_op jit(solution)/shard_map/ppermute | solution.py:122
  870.1 30.6 %collective-permute-start.44 = (bf16[1024,1024]{1,0:T(8,128)(2,1)S(1)}, bf16[1024,1024]{1,0:T(8,128)(2,1)}, u32[]{:S(2)}, u32[]{:S(2)}) collective-permute-start(bf16[1024,1024]{1,0:T(8,128)(2,1)S(1)} %shard_map.316), channel_id=1, source_target_pairs={{0,4},{4,0},{1,5},{5,1},{2,6},{6,2},{3,7},{7,3},{8,12},{12,8},{9,1... | collective-permute-start | bytes 6291464 | tf_op jit(solution)/shard_map/ppermute | solution.py:162
  872.5 22.9 %collective-permute-start.40 = (bf16[512,1024]{1,0:T(8,128)(2,1)}, bf16[512,1024]{1,0:T(8,128)(2,1)}, u32[]{:S(2)}, u32[]{:S(2)}) collective-permute-start(bf16[512,1024]{1,0:T(8,128)(2,1)} %slice.397), channel_id=1, source_target_pairs={{0,4},{4,0},{1,5},{5,1},{2,6},{6,2},{3,7},{7,3},{8,12},{12,8},{9,1... | collective-permute-start | bytes 3145736 | tf_op jit(solution)/shard_map/ppermute | solution.py:162
  897.6 13.7 %collective-permute-start.42 = (bf16[128,1024]{1,0:T(8,128)(2,1)S(1)}, bf16[128,1024]{1,0:T(8,128)(2,1)S(1)}, u32[]{:S(2)}, u32[]{:S(2)}) collective-permute-start(bf16[128,1024]{1,0:T(8,128)(2,1)S(1)} %get-tuple-element.394), channel_id=1, source_target_pairs={{0,16},{8,24},{16,0},{24,8},{1,17},{9,25},{17,1},{25,9},{2,18},{10... | collective-permute-start | bytes 786440 | tf_op jit(solution)/shard_map/ppermute | solution.py:122
  899.0 12.3 %collective-permute-start.41 = (bf16[128,1024]{1,0:T(8,128)(2,1)S(1)}, bf16[128,1024]{1,0:T(8,128)(2,1)S(1)}, u32[]{:S(2)}, u32[]{:S(2)}) collective-permute-start(bf16[128,1024]{1,0:T(8,128)(2,1)S(1)} %get-tuple-element.395), channel_id=1, source_target_pairs={{0,24},{8,0},{16,8},{24,16},{1,25},{9,1},{17,9},{25,17},{2,26},{10... | collective-permute-start | bytes 786440 | tf_op jit(solution)/shard_map/ppermute | solution.py:122
  902.3 11.9 %collective-permute-start.47 = (bf16[144,1024]{1,0:T(8,128)(2,1)S(1)}, bf16[144,1024]{1,0:T(8,128)(2,1)S(1)}, u32[]{:S(2)}, u32[]{:S(2)}) collective-permute-start(bf16[144,1024]{1,0:T(8,128)(2,1)S(1)} %get-tuple-element.383), channel_id=1, source_target_pairs={{0,1},{1,2},{2,3},{3,0},{4,5},{5,6},{6,7},{7,4},{8,9},{9,10},{10,1... | collective-permute-start | bytes 884744 | tf_op jit(solution)/shard_map/ppermute | solution.py:122
  902.8 23.4 %collective-permute-start.46 = (bf16[144,1024]{1,0:T(8,128)(2,1)S(1)}, bf16[144,1024]{1,0:T(8,128)(2,1)S(1)}, u32[]{:S(2)}, u32[]{:S(2)}) collective-permute-start(bf16[144,1024]{1,0:T(8,128)(2,1)S(1)} %get-tuple-element.384), channel_id=1, source_target_pairs={{0,2},{1,3},{2,0},{3,1},{4,6},{5,7},{6,4},{7,5},{8,10},{9,11},{10,... | collective-permute-start | bytes 884744 | tf_op jit(solution)/shard_map/ppermute | solution.py:122
  907.4 18.8 %collective-permute-start.45 = (bf16[144,1024]{1,0:T(8,128)(2,1)S(1)}, bf16[144,1024]{1,0:T(8,128)(2,1)S(1)}, u32[]{:S(2)}, u32[]{:S(2)}) collective-permute-start(bf16[144,1024]{1,0:T(8,128)(2,1)S(1)} %get-tuple-element.385), channel_id=1, source_target_pairs={{0,3},{1,0},{2,1},{3,2},{4,7},{5,4},{6,5},{7,6},{8,11},{9,8},{10,9... | collective-permute-start | bytes 884744 | tf_op jit(solution)/shard_map/ppermute | solution.py:122
  933.0 13.3 %collective-permute-start.49 = (bf16[2,32,1024]{2,1,0:T(8,128)(2,1)S(1)}, bf16[2,32,1024]{2,1,0:T(8,128)(2,1)S(1)}, u32[]{:S(2)}, u32[]{:S(2)}) collective-permute-start(bf16[2,32,1024]{2,1,0:T(8,128)(2,1)S(1)} %get-tuple-element.436), channel_id=1, source_target_pairs={{0,2},{1,3},{2,0},{3,1},{4,6},{5,7},{6,4},{7,5},{8,10},{9,11},{10,... | collective-permute-start | bytes 393224 | tf_op jit(solution)/shard_map/ppermute | solution.py:122
  (184 other events, 2825.0 us)
Sparse Core Ops, SparseCore 0:
  11.6 131.7 all-gather.5
  145.8 47.5 all-gather.7
  225.1 72.1 all-gather.9
  332.0 120.8 all-gather.11
  509.7 63.7 reduce-scatter.2
  587.7 121.3 reduce-scatter.4

commit v7 on v6

--- a/solution.py
+++ b/solution.py
@@ -516,10 +516,7 @@
 
     hidden0 = lax.fori_loop(0, later_turns, fetch_more, fetched(asked, keys))
     act1 = rms_scale(hidden0, gains[0]).astype(jnp.bfloat16)
-    inner = dense(act1, square_b[0:3].reshape(3 * D, D))
-    entry = inner[:, :D]
-    leave = inner[:, D : 2 * D]
-    conv_in = inner[:, 2 * D :]
+    entry, leave, conv_in = (dense(act1, square_b[place]) for place in range(3))
     product = entry * conv_in
     convolved = gains[4] * product + gains[5] * delayed(product, 1) + gains[6] * delayed(product, 2)
     mixer = (leave * convolved).astype(jnp.bfloat16)
@@ -568,9 +565,7 @@
     attended_b = attended.astype(jnp.bfloat16)
     hidden2 = answers(hidden1) + dense(attended_b, square_b[6])
     act3 = member_gather(rms_scale(hidden2, gains[2]).astype(jnp.bfloat16))
-    gate_up = dense(act3, wide_b[0:2].reshape(2 * hidden_units, D))
-    gate_part = gate_up[:, :hidden_units]
-    up_part = gate_up[:, hidden_units:]
+    gate_part, up_part = dense(act3, wide_b[0]), dense(act3, wide_b[1])
     inner_b = (jax.nn.silu(gate_part) * up_part).astype(jnp.bfloat16)
     ffn_part = jnp.dot(inner_b, wide_b[2], preferred_element_type=jnp.float32)
     hidden3 = hidden2 + member_return(ffn_part.astype(jnp.bfloat16).reshape(members, RESP, D))
@@ -590,29 +585,13 @@
 
     moment_rows = jnp.concatenate(
         [
-            wide_by_member(wide_moment.astype(jnp.bfloat16)).reshape(-1, D),
+            wide_moment.astype(jnp.bfloat16).reshape(-1, D),
             square_moment.astype(jnp.bfloat16).reshape(-1, D),
         ],
         axis=0,
     )
     moment_rows, response_tokens = lax.optimization_barrier((moment_rows, response_tokens))
     moment_rows = lax.all_gather(moment_rows, "vocab", axis=0)
-    wide_moment_job = jnp.stack(
-        [
-            lax.dynamic_slice_in_dim(
-                block_at(moment_rows, member - step), member * wide_rows, wide_rows, 0
-            )
-            for step in range(members)
-        ]
-    )
-    square_moment_job = moment_rows[:, members * wide_rows :].reshape(
-        members, squares, square_rows, D
-    )
-    square_moment_job = jnp.pad(
-        square_moment_job, ((0, 0), (0, per_member * members - squares), (0, 0), (0, 0))
-    ).reshape(members, per_member, members, square_rows, D)
-    square_moment_job = lax.dynamic_index_in_dim(square_moment_job, member, 2, keepdims=False)
-    square_moment_job = square_moment_job.transpose(1, 0, 2, 3).reshape(per_member, group_rows, D)
     local_target = jnp.where(targets // block_rows == device, targets % block_rows, -1)[None, :]
     shares, own_stats = answer_shares(local_target, response_tokens, table_b)
     stats = own_stats[:3].reshape(3, devices, RESP).transpose(1, 0, 2)
@@ -646,8 +625,8 @@
         response_tokens,
         preferred_element_type=jnp.float32,
     )
-    grad_answer_group, grad_table, wide_moment_job, square_moment_job = lax.optimization_barrier(
-        (grad_answer_group.astype(jnp.bfloat16), grad_table, wide_moment_job, square_moment_job)
+    grad_answer_group, grad_table = lax.optimization_barrier(
+        (grad_answer_group.astype(jnp.bfloat16), grad_table)
     )
     grad_final = member_scatter(grad_answer_group.reshape(members, RESP, D))
     grad_hidden3, grad_gain3 = norm_back(hidden3, gains[3], grad_final)
@@ -656,10 +635,10 @@
     grad_down_w = outer(inner_b, grad_ffn_out)
     _, silu_pull = jax.vjp(lambda gate_in, up_in: jax.nn.silu(gate_in) * up_in, gate_part, up_part)
     grad_gate, grad_up = silu_pull(grad_inner)
-    grad_gate_up = jnp.concatenate([grad_gate, grad_up], axis=1).astype(jnp.bfloat16)
-    grad_act3_part = back_dense(grad_gate_up, wide_b[0:2].reshape(2 * hidden_units, D))
+    grad_gate_b, grad_up_b = grad_gate.astype(jnp.bfloat16), grad_up.astype(jnp.bfloat16)
+    grad_act3_part = back_dense(grad_gate_b, wide_b[0]) + back_dense(grad_up_b, wide_b[1])
     grad_act3 = member_return(grad_act3_part.astype(jnp.bfloat16).reshape(members, RESP, D))
-    grad_gate_up_w = outer(grad_gate_up, act3)
+    grad_gate_w, grad_up_w = outer(grad_gate_b, act3), outer(grad_up_b, act3)
     grad_norm2, grad_gain2 = norm_back(hidden2, gains[2], grad_act3)
     grad_hidden2 = grad_hidden3 + grad_norm2
     grad_attn_out = grad_hidden2.astype(jnp.bfloat16)
@@ -712,35 +691,48 @@
     grad_product = (
         gains[4] * grad_conv + gains[5] * advanced(grad_conv, 1) + gains[6] * advanced(grad_conv, 2)
     )
-    grad_inner_b = jnp.concatenate(
-        [grad_product * conv_in, grad_leave, grad_product * entry], axis=1
-    ).astype(jnp.bfloat16)
-    grad_act1 = back_dense(grad_inner_b, square_b[0:3].reshape(3 * D, D))
-    grad_inner_w = outer(grad_inner_b, act1)
+    grad_inner = [
+        part.astype(jnp.bfloat16)
+        for part in (grad_product * conv_in, grad_leave, grad_product * entry)
+    ]
+    grad_act1 = sum(back_dense(grad_inner[place], square_b[place]) for place in range(3))
+    grad_inner_w = [outer(part, act1) for part in grad_inner]
     grad_norm0, grad_gain0 = norm_back(hidden0, gains[0], grad_act1)
     grad_embed_b = (grad_hidden1 + grad_norm0).astype(jnp.bfloat16)
 
-    grad_square = jnp.concatenate(
+    grad_square = jnp.stack(
         [
-            grad_inner_w.astype(jnp.bfloat16).reshape(3, D, D),
-            grad_mixer_w.astype(jnp.bfloat16)[None],
-            grad_query_w.astype(jnp.bfloat16)[None],
-            grad_pair_w.astype(jnp.bfloat16)[None],
-            grad_out_w.astype(jnp.bfloat16)[None],
-        ],
-        axis=0,
+            part.astype(jnp.bfloat16)
+            for part in (*grad_inner_w, grad_mixer_w, grad_query_w, grad_pair_w, grad_out_w)
+        ]
     )
     grad_vector = jnp.stack(
         [grad_gain0, grad_gain1, grad_gain2, grad_gain3, grad_tap0, grad_tap1, grad_tap2]
     )
     grad_head_gains = jnp.stack([grad_query_gain, grad_key_gain])
-    grad_wide = jnp.concatenate(
+    grad_wide = jnp.stack(
+        [part.astype(jnp.bfloat16) for part in (grad_gate_w, grad_up_w, grad_down_w)]
+    )
+    grad_wide, moment_rows = lax.optimization_barrier((grad_wide, moment_rows))
+    wide_moment_job = jnp.stack(
         [
-            grad_gate_up_w.astype(jnp.bfloat16).reshape(2, hidden_units, D),
-            grad_down_w.astype(jnp.bfloat16)[None],
-        ],
-        axis=0,
-    )
+            lax.dynamic_slice_in_dim(
+                block_at(moment_rows, member - step),
+                jnp.minimum(member, wides - 1) * wide_rows,
+                wide_rows,
+                0,
+            )
+            for step in range(members)
+        ]
+    )
+    square_moment_job = moment_rows[:, wides * wide_rows :].reshape(
+        members, squares, square_rows, D
+    )
+    square_moment_job = jnp.pad(
+        square_moment_job, ((0, 0), (0, per_member * members - squares), (0, 0), (0, 0))
+    ).reshape(members, per_member, members, square_rows, D)
+    square_moment_job = lax.dynamic_index_in_dim(square_moment_job, member, 2, keepdims=False)
+    square_moment_job = square_moment_job.transpose(1, 0, 2, 3).reshape(per_member, group_rows, D)
     share_wide_b = lax.psum_scatter(grad_wide, DP, scatter_dimension=1, tiled=True)
     grad_square, share_wide_b = lax.optimization_barrier((grad_square, share_wide_b))
     share_wide_b, grad_embed_b = lax.optimization_barrier((share_wide_b, grad_embed_b))
@@ -853,22 +845,23 @@
     gram = jnp.where(core == 0, wide_gram.astype(jnp.float32), square_gram)
     rest_b = ortho_rest(gram)
     power = leading_coefficient**NS_ITERS
-    share_table, rest_b = lax.optimization_barrier((share_table, rest_b))
-    table_step, table_first_new, table_second_new = adam_step(
-        table_master, table_first, table_second, share_table, factor, adam_count
-    )
     wide_rest = jnp.where(core == 0, rest_b, other_core(rest_b))
     back_square = square_product(square_job, rest_b).astype(jnp.bfloat16)
     half_rows = square_half.shape[0]
     back_square = jnp.where(
         core == 0, other_core(back_square[half_rows:]), back_square[:half_rows]
     )
+    back_wide = square_product(wide_job, wide_rest).astype(jnp.bfloat16)
+    share_table, back_square, back_wide = lax.optimization_barrier(
+        (share_table, back_square, back_wide)
+    )
+    table_step, table_first_new, table_second_new = adam_step(
+        table_master, table_first, table_second, share_table, factor, adam_count
+    )
     back_square = handed_back(list(back_square.reshape(-1, group_rows, D)), "chip")
     back_square = placed_after(back_square, "chip")[:per_member]
-    back_wide = square_product(wide_job, wide_rest).astype(jnp.bfloat16)
     back_wide = handed_back(list(back_wide.reshape(members, wide_rows, D)), "vocab")
     back_wide = placed_after(back_wide, "vocab")[:wides]
-    back_square, back_wide = lax.optimization_barrier((back_square, back_wide))
     back_square = from_members(back_square)
     ortho_wide = power * ortho_wide + back_wide.astype(jnp.float32)
     ortho_square = power * ortho_square + back_square

time: 966 us -> 950 us (0.983)
  waiting for transfers between devices: 469 us -> 442 us
  matrix products: 118 us -> 138 us
    all_gather x1, waiting for transfers between devices: 40.2 us -> 0.01 us  [body(): moment_rows = lax.all_gather(moment_rows, 'vocab', axis=0)]
    ppermute x45, waiting for transfers between devices: 220 us -> 232 us  [turned(): lax.ppermute(values, axis, [(i, (i + step) % count) for i in range(count)])]
    dot_general x7 -> x10, matrix products: 18.3 us -> 29 us  [dense(): lax.dot_general(inputs, weight, (((1,), (1,)), ((), ())), preferred_eleme...]
    dot_general x6 -> x9, matrix products: 26 us -> 33.8 us  [back_dense(): return jnp.dot(grads, weight, preferred_element_type=jnp.float32)]
    dot_general x11 -> x14, matrix products: 34.2 us -> 36.6 us  [outer(): lax.dot_general(grads, inputs, (((0,), (0,)), ((), ())), preferred_elemen...]
    unnamed x342 -> x347, local copies, waits for them, and re-layouts: 25.1 us -> 27.3 us
  transfers between devices with their start and end apart: 64 -> 64, of which waited for: 36 -> 31; matrix products, arithmetic and copies ran while one was open for 23% -> 26% of each run, Pallas kernels for 2% -> 4%
where the time goes in v7:
time: 950 us; the launch traced here: 941 us
  waiting for transfers between devices  442 us (47%)
  matrix products  138 us (15%)
  other arithmetic  107 us (11%)
  starting transfers between devices  86.2 us (9%)
  Pallas kernels  71.6 us (8%)
  local copies, waits for them, and re-layouts  64.9 us (7%)
  between operations  30.9 us (3%)
    ppermute x45, waiting for transfers between devices, turned(): lax.ppermute(values, axis, [(i, (i + step) % count) for i in range(count)])  232 us
    all_gather x1, waiting for transfers between devices, body(): response_tokens = lax.all_gather(final_b, ALL, axis=0, tiled=True)  67.2 us
    all_to_all x5, waiting for transfers between devices, exchanged(): return lax.all_to_all(rows, ALL, 0, 0, tiled=True)  59.3 us
    ppermute x45, starting transfers between devices, turned(): lax.ppermute(values, axis, [(i, (i + step) % count) for i in range(count)])  54.5 us
    all_gather x1, waiting for transfers between devices, body(): lax.all_gather(square_master.astype(jnp.bfloat16), ALL, axis=1, tiled=True)  37.7 us
    dot_general x14, matrix products, outer(): lax.dot_general(grads, inputs, (((0,), (0,)), ((), ())), preferred_elemen...  36.6 us
    dot_general x9, matrix products, back_dense(): return jnp.dot(grads, weight, preferred_element_type=jnp.float32)  33.8 us
    dot_general x10, matrix products, dense(): lax.dot_general(inputs, weight, (((1,), (1,)), ((), ())), preferred_eleme...  29 us
  transfers between devices with their start and end apart: 64, of which 31 were waited for; matrix products, arithmetic and copies ran while one was open for 26% of the time, Pallas kernels for 4%

profile of v7, /device:TPU:0, one launch (start us, length us, event | category | flops | bytes accessed | tf_op | source)
XLA Modules:
  0.0 941.2 jit_solution(908518943522007389)
XLA Ops:
  19.5 7.3 all-to-all-start.4
  26.8 6.1 convert_element_type.426.table_ref
  35.3 6.8 fusion.68
  42.1 4.1 all-to-all-start.5
  56.3 45.0 %all-to-all-done.5 = bf16[32,24,1024]{2,1,0:T(8,128)(2,1)S(1)} async-done(((bf16[32,24,1024]{2,1,0:T(8,128)(2,1)}), bf16[32,24,1024]{2,1,0:T(8,128)(2,1)S(1)}, u32[]{:S(2)}, u32[]{:S(2)}) %all-to-all-start.5) | async-done | bytes 1572896 | tf_op jit(solution)/shard_map/all_to_all | solution.py:112
  105.6 37.7 %all-gather.6.cloned.1.call-done = bf16[7,1024,1024]{2,1,0:T(8,128)(2,1)} async-done(((bf16[7,32,1024]{2,1,0:T(8,128)(2,1)}), bf16[7,1024,1024]{2,1,0:T(8,128)(2,1)}) %all-gather.6.cloned.1.call-update) | async-done | bytes 14680080 | tf_op jit(solution)/shard_map/all_gather | solution.py:468
  146.5 5.7 fusion.167
  152.2 3.6 multiply_convert_fusion.4
  176.5 16.9 %all-gather.8.cloned.1.call-done = bf16[3,1152,1024]{2,1,0:T(8,128)(2,1)} async-done(((bf16[3,144,1024]{2,1,0:T(8,128)(2,1)}), bf16[3,1152,1024]{2,1,0:T(8,128)(2,1)}) %all-gather.8.cloned.1.call-update) | async-done | bytes 7077904 | tf_op jit(solution)/shard_map/all_gather | solution.py:469
  207.2 4.6 collective-permute-done.5
  211.8 7.8 collective-permute-done.4
  227.2 67.2 %all-gather.10.cloned.1.call-done.answers_ref = bf16[3072,1024]{1,0:T(8,128)(2,1)} async-done(((bf16[96,1024]{1,0:T(8,128)(2,1)}), bf16[3072,1024]{1,0:T(8,128)(2,1)}) %all-gather.10.cloned.1.call-update) | async-done | bytes 6291472 | tf_op jit(solution)/shard_map/all_gather | solution.py:573
  297.3 25.3 %shard_map.313 = (bf16[2048,3072]{1,0:T(8,128)(2,1)}, f32[8,3072]{1,0:T(8,128)S(1)}) custom-call(s32[1,3072]{1,0:T(1,128)S(1)} %compare_select_fusion.target_ref, bf16[3072,1024]{1,0:T(8,128)(2,1)S(1)} %copy-done, bf16[2048,1024]{1,0:T(8,128)(2,1)} %get-tuple-element.680), custom_call_target="tpu_custom_call" | custom-call | flops 12884901888 | bytes 18874368 | tf_op jit(solution)/shard_map/pallas_call | solution.py:347
  326.5 7.5 all-to-all-done.6
  338.7 7.0 all-to-all-done.7
  347.3 10.3 %shard_map.315 = bf16[1536,1024]{1,0:T(8,128)(2,1)S(1)} custom-call(s32[1]{0:T(128)} %bitcast.55.core_ref, s32[1,3072]{1,0:T(1,128)S(1)} %compare_select_fusion.target_ref, f32[1,3072]{1,0:T(1,128)S(1)} %get-tuple-element.440.scale_ref, f32[1,3072]{1,0:T(1,128)S(1)} %get-tuple-element.439.value_ref, bf16[2048,3072]{1,0:T(8,128)(2,1)} %get-tuple-element.248.shares_ref, ...), custom_call_target="tpu_custom_call" | custom-call | flops 6442450944 | bytes 9437184 | tf_op jit(solution)/shard_map/pallas_call | solution.py:389
  358.2 10.9 %shard_map.314 = bf16[1536,1024]{1,0:T(8,128)(2,1)S(1)} custom-call(s32[1]{0:T(128)} %bitcast.54.core_ref, s32[1,3072]{1,0:T(1,128)S(1)} %compare_select_fusion.target_ref, f32[1,3072]{1,0:T(1,128)S(1)} %get-tuple-element.440.scale_ref, f32[1,3072]{1,0:T(1,128)S(1)} %get-tuple-element.439.value_ref, bf16[2048,3072]{1,0:T(8,128)(2,1)} %get-tuple-element.248.shares_ref, ...), custom_call_target="tpu_custom_call" | custom-call | flops 6442450944 | bytes 9437184 | tf_op jit(solution)/shard_map/pallas_call | solution.py:389
  375.3 17.5 %fusion.12 = f32[2048,1024]{1,0:T(8,128)} fusion(bf16[3072,1024]{1,0:T(8,128)(2,1)} %all-gather.10.cloned.1.call-done.answers_ref, bf16[2048,3072]{1,0:T(8,128)(2,1)S(1)} %bitcast.518, f32[3072]{0:T(1024)S(1)} %bitcast.427, f32[3072]{0:T(1024)S(1)} %bitcast.426, s32[3072]{0:T(1024)S(1)} %fusion.127), kind=kOutput, calls=%fused_computation.31 | convolution fusion | flops 12910067712 | bytes 27299840 | tf_op jit(solution)/shard_map/dot_general | solution.py:621
  393.4 16.5 %collective-permute-done.8 = bf16[384,1024]{1,0:T(8,128)(2,1)S(1)} collective-permute-done((bf16[384,1024]{1,0:T(8,128)(2,1)S(1)}, bf16[384,1024]{1,0:T(8,128)(2,1)S(1)}, u32[]{:S(2)}, u32[]{:S(2)}) %collective-permute-start.8) | collective-permute-done | bytes 786464 | tf_op jit(solution)/shard_map/ppermute | solution.py:122
  412.9 12.7 %collective-permute-done.12 = bf16[96,1024]{1,0:T(8,128)(2,1)S(1)} collective-permute-done((bf16[96,1024]{1,0:T(8,128)(2,1)S(1)}, bf16[96,1024]{1,0:T(8,128)(2,1)S(1)}, u32[]{:S(2)}, u32[]{:S(2)}) %collective-permute-start.12) | collective-permute-done | bytes 196640 | tf_op jit(solution)/shard_map/ppermute | solution.py:122
  425.7 25.6 %collective-permute-done.11 = bf16[96,1024]{1,0:T(8,128)(2,1)S(1)} collective-permute-done((bf16[96,1024]{1,0:T(8,128)(2,1)S(1)}, bf16[96,1024]{1,0:T(8,128)(2,1)S(1)}, u32[]{:S(2)}, u32[]{:S(2)}) %collective-permute-start.11) | collective-permute-done | bytes 196640 | tf_op jit(solution)/shard_map/ppermute | solution.py:122
  454.7 7.4 collective-permute-done.15
  462.1 22.9 %collective-permute-done.14 = bf16[96,1024]{1,0:T(8,128)(2,1)S(1)} collective-permute-done((bf16[96,1024]{1,0:T(8,128)(2,1)S(1)}, bf16[96,1024]{1,0:T(8,128)(2,1)S(1)}, u32[]{:S(2)}, u32[]{:S(2)}) %collective-permute-start.14) | collective-permute-done | bytes 196640 | tf_op jit(solution)/shard_map/ppermute | solution.py:122
  492.8 4.0 fusion.43
  508.2 5.3 collective-permute-done.18
  513.4 7.5 collective-permute-done.17
  549.5 7.8 multiply_reduce_fusion.1
  585.1 5.0 multiply_reduce_fusion.5
  591.8 3.9 fusion.36
  595.7 6.0 all-to-all-start.8
  604.0 5.1 all-to-all-done.8
  624.9 20.2 %collective-permute-done.24 = bf16[144,1024]{1,0:T(8,128)(2,1)S(1)} collective-permute-done((bf16[144,1024]{1,0:T(8,128)(2,1)S(1)}, bf16[144,1024]{1,0:T(8,128)(2,1)S(1)}, u32[]{:S(2)}, u32[]{:S(2)}) %collective-permute-start.24) | collective-permute-done | bytes 294944 | tf_op jit(solution)/shard_map/ppermute | solution.py:122
  645.1 30.1 %collective-permute-done.23 = bf16[144,1024]{1,0:T(8,128)(2,1)S(1)} collective-permute-done((bf16[144,1024]{1,0:T(8,128)(2,1)S(1)}, bf16[144,1024]{1,0:T(8,128)(2,1)S(1)}, u32[]{:S(2)}, u32[]{:S(2)}) %collective-permute-start.23) | collective-permute-done | bytes 294944 | tf_op jit(solution)/shard_map/ppermute | solution.py:122
  676.4 8.7 fusion.19
  685.0 14.5 %reduce-scatter.5.cloned.1.call-done = bf16[7,128,1024]{2,1,0:T(8,128)(2,1)} async-done(((bf16[7,1024,1024]{2,1,0:T(8,128)(2,1)}), bf16[7,128,1024]{2,1,0:T(8,128)(2,1)}) %reduce-scatter.5.cloned.1.call-update) | async-done | bytes 1835024 | tf_op jit(solution)/shard_map/reduce_scatter | solution.py:741
  708.5 6.1 multiply_reduce_fusion
  714.7 5.0 collective-permute-done.21
  719.7 32.6 %collective-permute-done.20 = bf16[2,128,1024]{2,1,0:T(8,128)(2,1)} collective-permute-done((bf16[2,128,1024]{2,1,0:T(8,128)(2,1)}, bf16[2,128,1024]{2,1,0:T(8,128)(2,1)}, u32[]{:S(2)}, u32[]{:S(2)}) %collective-permute-start.20) | collective-permute-done | bytes 524320 | tf_op jit(solution)/shard_map/ppermute | solution.py:122
  759.7 4.0 all-to-all-start.10
  766.1 4.6 all-to-all-done.10
  796.6 10.6 %collective-permute-done.34 = bf16[128,1024]{1,0:T(8,128)(2,1)} collective-permute-done((bf16[128,1024]{1,0:T(8,128)(2,1)}, bf16[128,1024]{1,0:T(8,128)(2,1)}, u32[]{:S(2)}, u32[]{:S(2)}) %collective-permute-start.34) | collective-permute-done | bytes 262176 | tf_op jit(solution)/shard_map/ppermute | solution.py:122
  814.1 3.8 collective-permute-done.38
  817.9 5.0 collective-permute-done.37
  839.4 25.1 %shard_map.316 = bf16[1024,1024]{1,0:T(8,128)(2,1)S(1)} custom-call(f32[1024,1024]{1,0:T(8,128)S(1)} %convert_select_fusion.gram_ref), custom_call_target="tpu_custom_call" | custom-call | flops 19327352832 | bytes 6291456 | tf_op jit(solution)/shard_map/pallas_call | solution.py:293
  864.6 3.9 convolution_convert_fusion.4
  887.0 22.7 %add_multiply_fusion = (f32[2048,1024]{1,0:T(8,128)}, f32[2048,1024]{1,0:T(8,128)}, f32[2048,1024]{1,0:T(8,128)}) fusion(f32[2048,1024]{1,0:T(8,128)} %param.25, f32[]{:T(128)S(6)} %sub.255, f32[]{:T(128)S(6)} %sub.254, f32[2048,1024]{1,0:T(8,128)} %get-tuple-element.265, f32[]{:T(128)S(6)} %min.4, f32[2048,1024]{1,0:T(8,128)} %param.27, f32[2048,1024]{1,0:T(8,128)} %param.26), kind=kLoop, calls=%fused_computation.37 | loop fusion | flops 31457280 | bytes 58720268 | tf_op jit(solution)/shard_map/mul | solution.py:100
  915.4 4.3 collective-permute-done.48
  922.9 7.0 collective-permute-done.46
  (714 shorter events, 281.0 us)
Async XLA Ops:
  7.2 136.2 %all-gather.6.cloned.1.call-start = ((), (), s32[]{:S(2)}) async-start(), calls=%async_computation.13 | async-start | bytes 15138816 | tf_op jit(solution)/shard_map/all_gather | solution.py:468
  19.5 15.1 %all-to-all-start.4 = ((f32[32,1,349]{2,1,0:T(1,128)}), f32[32,1,349]{2,1,0:T(1,128)S(1)}, u32[]{:S(2)}, u32[]{:S(2)}) async-start(f32[32,1,349]{2,1,0:T(1,128)} %all_to_all.79), calls=%async_computation.4 | async-start | bytes 98304 | tf_op jit(solution)/shard_map/all_to_all | solution.py:112
  42.1 59.1 %all-to-all-start.5 = ((bf16[32,24,1024]{2,1,0:T(8,128)(2,1)}), bf16[32,24,1024]{2,1,0:T(8,128)(2,1)S(1)}, u32[]{:S(2)}, u32[]{:S(2)}) async-start(bf16[32,24,1024]{2,1,0:T(8,128)(2,1)} %bitcast.466), calls=%async_computation.5 | async-start | bytes 3145728 | tf_op jit(solution)/shard_map/all_to_all | solution.py:112
  46.3 147.1 %all-gather.8.cloned.1.call-start = ((), (), s32[]{:S(2)}) async-start(), calls=%async_computation.14 | async-start | bytes 7962624 | tf_op jit(solution)/shard_map/all_gather | solution.py:469
  47.4 247.0 %all-gather.10.cloned.1.call-start = ((), (), s32[]{:S(2)}) async-start(), calls=%async_computation.15 | async-start | bytes 6488064 | tf_op jit(solution)/shard_map/all_gather | solution.py:573
  173.5 20.0 %collective-permute-start.2 = (bf16[96,1024]{1,0:T(8,128)(2,1)S(1)}, bf16[96,1024]{1,0:T(8,128)(2,1)S(1)}, u32[]{:S(2)}, u32[]{:S(2)}) collective-permute-start(bf16[96,1024]{1,0:T(8,128)(2,1)S(1)} %multiply_convert_fusion.9), channel_id=1, source_target_pairs={{0,3},{1,0},{2,1},{3,2},{4,7},{5,4},{6,5},{7,6},{8,11},{9,8},{10,9... | collective-permute-start | bytes 589832 | tf_op jit(solution)/shard_map/ppermute | solution.py:122
  173.8 19.6 %collective-permute-start.1 = (bf16[96,1024]{1,0:T(8,128)(2,1)S(1)}, bf16[96,1024]{1,0:T(8,128)(2,1)S(1)}, u32[]{:S(2)}, u32[]{:S(2)}) collective-permute-start(bf16[96,1024]{1,0:T(8,128)(2,1)S(1)} %multiply_convert_fusion.9), channel_id=1, source_target_pairs={{0,2},{1,3},{2,0},{3,1},{4,6},{5,7},{6,4},{7,5},{8,10},{9,11},{10,... | collective-permute-start | bytes 589832 | tf_op jit(solution)/shard_map/ppermute | solution.py:122
  174.7 18.7 %collective-permute-start = (bf16[96,1024]{1,0:T(8,128)(2,1)S(1)}, bf16[96,1024]{1,0:T(8,128)(2,1)S(1)}, u32[]{:S(2)}, u32[]{:S(2)}) collective-permute-start(bf16[96,1024]{1,0:T(8,128)(2,1)S(1)} %multiply_convert_fusion.9), channel_id=1, source_target_pairs={{0,1},{1,2},{2,3},{3,0},{4,5},{5,6},{6,7},{7,4},{8,9},{9,10},{10,1... | collective-permute-start | bytes 589832 | tf_op jit(solution)/shard_map/ppermute | solution.py:122
  203.3 16.3 %collective-permute-start.4 = (bf16[96,1024]{1,0:T(8,128)(2,1)S(1)}, bf16[96,1024]{1,0:T(8,128)(2,1)}, u32[]{:S(2)}, u32[]{:S(2)}) collective-permute-start(bf16[96,1024]{1,0:T(8,128)(2,1)S(1)} %get-tuple-element.415), channel_id=1, source_target_pairs={{0,2},{1,3},{2,0},{3,1},{4,6},{5,7},{6,4},{7,5},{8,10},{9,11},{10,... | collective-permute-start | bytes 589832 | tf_op jit(solution)/shard_map/ppermute | solution.py:122
  205.7 13.8 %collective-permute-start.3 = (bf16[96,1024]{1,0:T(8,128)(2,1)S(1)}, bf16[96,1024]{1,0:T(8,128)(2,1)}, u32[]{:S(2)}, u32[]{:S(2)}) collective-permute-start(bf16[96,1024]{1,0:T(8,128)(2,1)S(1)} %get-tuple-element.413), channel_id=1, source_target_pairs={{0,3},{1,0},{2,1},{3,2},{4,7},{5,4},{6,5},{7,6},{8,11},{9,8},{10,9... | collective-permute-start | bytes 589832 | tf_op jit(solution)/shard_map/ppermute | solution.py:122
  338.6 161.6 %all-gather.12.cloned.1.call-start = ((), (), s32[]{:S(2)}) async-start(), calls=%async_computation.18 | async-start | bytes 6717440 | tf_op jit(solution)/shard_map/all_gather | solution.py:594
  357.9 219.9 %reduce-scatter.3.cloned.1.call-start = ((), (), s32[]{:S(2)}) async-start(), calls=%async_computation.16 | async-start | bytes 7962624 | tf_op jit(solution)/shard_map/reduce_scatter | solution.py:736
  373.0 20.4 %collective-permute-start.9 = (bf16[384,1024]{1,0:T(8,128)(2,1)S(1)}, bf16[384,1024]{1,0:T(8,128)(2,1)S(1)}, u32[]{:S(2)}, u32[]{:S(2)}) collective-permute-start(bf16[384,1024]{1,0:T(8,128)(2,1)S(1)} %get-tuple-element.369), channel_id=1, source_target_pairs={{0,24},{8,0},{16,8},{24,16},{1,25},{9,1},{17,9},{25,17},{2,26},{10... | collective-permute-start | bytes 2359304 | tf_op jit(solution)/shard_map/ppermute | solution.py:122
  373.0 36.8 %collective-permute-start.8 = (bf16[384,1024]{1,0:T(8,128)(2,1)S(1)}, bf16[384,1024]{1,0:T(8,128)(2,1)S(1)}, u32[]{:S(2)}, u32[]{:S(2)}) collective-permute-start(bf16[384,1024]{1,0:T(8,128)(2,1)S(1)} %get-tuple-element.370), channel_id=1, source_target_pairs={{0,16},{8,24},{16,0},{24,8},{1,17},{9,25},{17,1},{25,9},{2,18},{10... | collective-permute-start | bytes 2359304 | tf_op jit(solution)/shard_map/ppermute | solution.py:122
  374.7 35.1 %collective-permute-start.7 = (bf16[384,1024]{1,0:T(8,128)(2,1)S(1)}, bf16[384,1024]{1,0:T(8,128)(2,1)S(1)}, u32[]{:S(2)}, u32[]{:S(2)}) collective-permute-start(bf16[384,1024]{1,0:T(8,128)(2,1)S(1)} %get-tuple-element.368), channel_id=1, source_target_pairs={{0,8},{8,16},{16,24},{24,0},{1,9},{9,17},{17,25},{25,1},{2,10},{10... | collective-permute-start | bytes 2359304 | tf_op jit(solution)/shard_map/ppermute | solution.py:122
  410.5 15.2 %collective-permute-start.12 = (bf16[96,1024]{1,0:T(8,128)(2,1)S(1)}, bf16[96,1024]{1,0:T(8,128)(2,1)S(1)}, u32[]{:S(2)}, u32[]{:S(2)}) collective-permute-start(bf16[96,1024]{1,0:T(8,128)(2,1)S(1)} %get-tuple-element.411), channel_id=1, source_target_pairs={{0,3},{1,0},{2,1},{3,2},{4,7},{5,4},{6,5},{7,6},{8,11},{9,8},{10,9... | collective-permute-start | bytes 589832 | tf_op jit(solution)/shard_map/ppermute | solution.py:122
  411.1 40.2 %collective-permute-start.11 = (bf16[96,1024]{1,0:T(8,128)(2,1)S(1)}, bf16[96,1024]{1,0:T(8,128)(2,1)S(1)}, u32[]{:S(2)}, u32[]{:S(2)}) collective-permute-start(bf16[96,1024]{1,0:T(8,128)(2,1)S(1)} %get-tuple-element.412), channel_id=1, source_target_pairs={{0,2},{1,3},{2,0},{3,1},{4,6},{5,7},{6,4},{7,5},{8,10},{9,11},{10,... | collective-permute-start | bytes 589832 | tf_op jit(solution)/shard_map/ppermute | solution.py:122
  412.2 39.0 %collective-permute-start.10 = (bf16[96,1024]{1,0:T(8,128)(2,1)S(1)}, bf16[96,1024]{1,0:T(8,128)(2,1)S(1)}, u32[]{:S(2)}, u32[]{:S(2)}) collective-permute-start(bf16[96,1024]{1,0:T(8,128)(2,1)S(1)} %get-tuple-element.410), channel_id=1, source_target_pairs={{0,1},{1,2},{2,3},{3,0},{4,5},{5,6},{6,7},{7,4},{8,9},{9,10},{10,1... | collective-permute-start | bytes 589832 | tf_op jit(solution)/shard_map/ppermute | solution.py:122
  452.7 32.4 %collective-permute-start.14 = (bf16[96,1024]{1,0:T(8,128)(2,1)S(1)}, bf16[96,1024]{1,0:T(8,128)(2,1)S(1)}, u32[]{:S(2)}, u32[]{:S(2)}) collective-permute-start(bf16[96,1024]{1,0:T(8,128)(2,1)S(1)} %fusion.149), channel_id=1, source_target_pairs={{0,2},{1,3},{2,0},{3,1},{4,6},{5,7},{6,4},{7,5},{8,10},{9,11},{10,... | collective-permute-start | bytes 589832 | tf_op jit(solution)/shard_map/ppermute | solution.py:122
  452.8 32.3 %collective-permute-start.13 = (bf16[96,1024]{1,0:T(8,128)(2,1)S(1)}, bf16[96,1024]{1,0:T(8,128)(2,1)S(1)}, u32[]{:S(2)}, u32[]{:S(2)}) collective-permute-start(bf16[96,1024]{1,0:T(8,128)(2,1)S(1)} %fusion.149), channel_id=1, source_target_pairs={{0,1},{1,2},{2,3},{3,0},{4,5},{5,6},{6,7},{7,4},{8,9},{9,10},{10,1... | collective-permute-start | bytes 589832 | tf_op jit(solution)/shard_map/ppermute | solution.py:122
  500.2 199.3 %reduce-scatter.5.cloned.1.call-start = ((), (), s32[]{:S(2)}) async-start(), calls=%async_computation.17 | async-start | bytes 16515072 | tf_op jit(solution)/shard_map/reduce_scatter | solution.py:741
  503.7 17.2 %collective-permute-start.17 = (bf16[96,1024]{1,0:T(8,128)(2,1)S(1)}, bf16[96,1024]{1,0:T(8,128)(2,1)S(1)}, u32[]{:S(2)}, u32[]{:S(2)}) collective-permute-start(bf16[96,1024]{1,0:T(8,128)(2,1)S(1)} %get-tuple-element.409), channel_id=1, source_target_pairs={{0,2},{1,3},{2,0},{3,1},{4,6},{5,7},{6,4},{7,5},{8,10},{9,11},{10,... | collective-permute-start | bytes 589832 | tf_op jit(solution)/shard_map/ppermute | solution.py:122
  504.5 16.4 %collective-permute-start.16 = (bf16[96,1024]{1,0:T(8,128)(2,1)S(1)}, bf16[96,1024]{1,0:T(8,128)(2,1)S(1)}, u32[]{:S(2)}, u32[]{:S(2)}) collective-permute-start(bf16[96,1024]{1,0:T(8,128)(2,1)S(1)} %get-tuple-element.407), channel_id=1, source_target_pairs={{0,3},{1,0},{2,1},{3,2},{4,7},{5,4},{6,5},{7,6},{8,11},{9,8},{10,9... | collective-permute-start | bytes 589832 | tf_op jit(solution)/shard_map/ppermute | solution.py:122
  595.7 13.4 %all-to-all-start.8 = ((f32[32,1,352]{2,1,0:T(1,128)}), f32[32,1,352]{2,1,0:T(1,128)S(1)}, u32[]{:S(2)}, u32[]{:S(2)}) async-start(f32[32,1,352]{2,1,0:T(1,128)} %copy.113), calls=%async_computation.10 | async-start | bytes 98304 | tf_op jit(solution)/shard_map/all_to_all | solution.py:112
  609.1 67.2 %all-to-all-start.9 = ((bf16[32,24,1024]{2,1,0:T(8,128)(2,1)}), bf16[32,24,1024]{2,1,0:T(8,128)(2,1)}, u32[]{:S(2)}, u32[]{:S(2)}) async-start(bf16[32,24,1024]{2,1,0:T(8,128)(2,1)} %bitcast.114), calls=%async_computation.11 | async-start | bytes 3145728 | tf_op jit(solution)/shard_map/all_to_all | solution.py:112
  618.0 27.1 %collective-permute-start.24 = (bf16[144,1024]{1,0:T(8,128)(2,1)S(1)}, bf16[144,1024]{1,0:T(8,128)(2,1)S(1)}, u32[]{:S(2)}, u32[]{:S(2)}) collective-permute-start(bf16[144,1024]{1,0:T(8,128)(2,1)S(1)} %get-tuple-element.404), channel_id=1, source_target_pairs={{0,3},{1,0},{2,1},{3,2},{4,7},{5,4},{6,5},{7,6},{8,11},{9,8},{10,9... | collective-permute-start | bytes 884744 | tf_op jit(solution)/shard_map/ppermute | solution.py:122
  621.6 53.6 %collective-permute-start.23 = (bf16[144,1024]{1,0:T(8,128)(2,1)S(1)}, bf16[144,1024]{1,0:T(8,128)(2,1)S(1)}, u32[]{:S(2)}, u32[]{:S(2)}) collective-permute-start(bf16[144,1024]{1,0:T(8,128)(2,1)S(1)} %get-tuple-element.406), channel_id=1, source_target_pairs={{0,2},{1,3},{2,0},{3,1},{4,6},{5,7},{6,4},{7,5},{8,10},{9,11},{10,... | collective-permute-start | bytes 884744 | tf_op jit(solution)/shard_map/ppermute | solution.py:122
  621.6 53.6 %collective-permute-start.22 = (bf16[144,1024]{1,0:T(8,128)(2,1)S(1)}, bf16[144,1024]{1,0:T(8,128)(2,1)S(1)}, u32[]{:S(2)}, u32[]{:S(2)}) collective-permute-start(bf16[144,1024]{1,0:T(8,128)(2,1)S(1)} %get-tuple-element.405), channel_id=1, source_target_pairs={{0,1},{1,2},{2,3},{3,0},{4,5},{5,6},{6,7},{7,4},{8,9},{9,10},{10,1... | collective-permute-start | bytes 884744 | tf_op jit(solution)/shard_map/ppermute | solution.py:122
  703.7 16.0 %collective-permute-start.21 = (bf16[2,128,1024]{2,1,0:T(8,128)(2,1)}, bf16[2,128,1024]{2,1,0:T(8,128)(2,1)}, u32[]{:S(2)}, u32[]{:S(2)}) collective-permute-start(bf16[2,128,1024]{2,1,0:T(8,128)(2,1)} %get-tuple-element.374), channel_id=1, source_target_pairs={{0,3},{1,0},{2,1},{3,2},{4,7},{5,4},{6,5},{7,6},{8,11},{9,8},{10,9... | collective-permute-start | bytes 1572872 | tf_op jit(solution)/shard_map/ppermute | solution.py:122
  707.0 45.3 %collective-permute-start.20 = (bf16[2,128,1024]{2,1,0:T(8,128)(2,1)}, bf16[2,128,1024]{2,1,0:T(8,128)(2,1)}, u32[]{:S(2)}, u32[]{:S(2)}) collective-permute-start(bf16[2,128,1024]{2,1,0:T(8,128)(2,1)} %get-tuple-element.375), channel_id=1, source_target_pairs={{0,2},{1,3},{2,0},{3,1},{4,6},{5,7},{6,4},{7,5},{8,10},{9,11},{10,... | collective-permute-start | bytes 1572872 | tf_op jit(solution)/shard_map/ppermute | solution.py:122
  707.0 45.3 %collective-permute-start.19 = (bf16[2,128,1024]{2,1,0:T(8,128)(2,1)}, bf16[2,128,1024]{2,1,0:T(8,128)(2,1)}, u32[]{:S(2)}, u32[]{:S(2)}) collective-permute-start(bf16[2,128,1024]{2,1,0:T(8,128)(2,1)} %get-tuple-element.373), channel_id=1, source_target_pairs={{0,1},{1,2},{2,3},{3,0},{4,5},{5,6},{6,7},{7,4},{8,9},{9,10},{10,1... | collective-permute-start | bytes 1572872 | tf_op jit(solution)/shard_map/ppermute | solution.py:122
  786.5 20.7 %collective-permute-start.34 = (bf16[128,1024]{1,0:T(8,128)(2,1)}, bf16[128,1024]{1,0:T(8,128)(2,1)}, u32[]{:S(2)}, u32[]{:S(2)}) collective-permute-start(bf16[128,1024]{1,0:T(8,128)(2,1)} %get-tuple-element.400), channel_id=1, source_target_pairs={{0,16},{8,24},{16,0},{24,8},{1,17},{9,25},{17,1},{25,9},{2,18},{10... | collective-permute-start | bytes 786440 | tf_op jit(solution)/shard_map/ppermute | solution.py:122
  788.0 19.3 %collective-permute-start.33 = (bf16[128,1024]{1,0:T(8,128)(2,1)}, bf16[128,1024]{1,0:T(8,128)(2,1)}, u32[]{:S(2)}, u32[]{:S(2)}) collective-permute-start(bf16[128,1024]{1,0:T(8,128)(2,1)} %get-tuple-element.398), channel_id=1, source_target_pairs={{0,8},{8,16},{16,24},{24,0},{1,9},{9,17},{17,25},{25,1},{2,10},{10... | collective-permute-start | bytes 786440 | tf_op jit(solution)/shard_map/ppermute | solution.py:122
  789.6 20.6 %collective-permute-start.28 = (bf16[128,1024]{1,0:T(8,128)(2,1)}, bf16[128,1024]{1,0:T(8,128)(2,1)S(1)}, u32[]{:S(2)}, u32[]{:S(2)}) collective-permute-start(bf16[128,1024]{1,0:T(8,128)(2,1)} %get-tuple-element.437), channel_id=1, source_target_pairs={{0,8},{8,16},{16,24},{24,0},{1,9},{9,17},{17,25},{25,1},{2,10},{10... | collective-permute-start | bytes 786440 | tf_op jit(solution)/shard_map/ppermute | solution.py:122
  791.0 21.9 %collective-permute-start.29 = (bf16[128,1024]{1,0:T(8,128)(2,1)}, bf16[128,1024]{1,0:T(8,128)(2,1)S(1)}, u32[]{:S(2)}, u32[]{:S(2)}) collective-permute-start(bf16[128,1024]{1,0:T(8,128)(2,1)} %get-tuple-element.438), channel_id=1, source_target_pairs={{0,16},{8,24},{16,0},{24,8},{1,17},{9,25},{17,1},{25,9},{2,18},{10... | collective-permute-start | bytes 786440 | tf_op jit(solution)/shard_map/ppermute | solution.py:122
  795.1 17.8 %collective-permute-start.30 = (bf16[128,1024]{1,0:T(8,128)(2,1)}, bf16[128,1024]{1,0:T(8,128)(2,1)S(1)}, u32[]{:S(2)}, u32[]{:S(2)}) collective-permute-start(bf16[128,1024]{1,0:T(8,128)(2,1)} %get-tuple-element.436), channel_id=1, source_target_pairs={{0,24},{8,0},{16,8},{24,16},{1,25},{9,1},{17,9},{25,17},{2,26},{10... | collective-permute-start | bytes 786440 | tf_op jit(solution)/shard_map/ppermute | solution.py:122
  808.6 14.3 %collective-permute-start.37 = (bf16[128,1024]{1,0:T(8,128)(2,1)S(1)}, bf16[128,1024]{1,0:T(8,128)(2,1)S(1)}, u32[]{:S(2)}, u32[]{:S(2)}) collective-permute-start(bf16[128,1024]{1,0:T(8,128)(2,1)S(1)} %fusion.101), channel_id=1, source_target_pairs={{0,16},{8,24},{16,0},{24,8},{1,17},{9,25},{17,1},{25,9},{2,18},{10... | collective-permute-start | bytes 786440 | tf_op jit(solution)/shard_map/ppermute | solution.py:122
  814.1 19.1 %collective-permute-start.31 = (bf16[512,1024]{1,0:T(8,128)(2,1)}, bf16[512,1024]{1,0:T(8,128)(2,1)}, u32[]{:S(2)}, u32[]{:S(2)}) collective-permute-start(bf16[512,1024]{1,0:T(8,128)(2,1)} %pad_maximum_fusion.5), channel_id=1, source_target_pairs={{0,4},{4,0},{1,5},{5,1},{2,6},{6,2},{3,7},{7,3},{8,12},{12,8},{9,1... | collective-permute-start | bytes 3145736 | tf_op jit(solution)/shard_map/ppermute | solution.py:162
  826.3 46.5 %collective-permute-start.27 = (bf16[2,32,1024]{2,1,0:T(8,128)(2,1)}, bf16[2,32,1024]{2,1,0:T(8,128)(2,1)}, u32[]{:S(2)}, u32[]{:S(2)}) collective-permute-start(bf16[2,32,1024]{2,1,0:T(8,128)(2,1)} %get-tuple-element.425), channel_id=1, source_target_pairs={{0,3},{1,0},{2,1},{3,2},{4,7},{5,4},{6,5},{7,6},{8,11},{9,8},{10,9... | collective-permute-start | bytes 393224 | tf_op jit(solution)/shard_map/ppermute | solution.py:122
  827.2 45.7 %collective-permute-start.26 = (bf16[2,32,1024]{2,1,0:T(8,128)(2,1)}, bf16[2,32,1024]{2,1,0:T(8,128)(2,1)}, u32[]{:S(2)}, u32[]{:S(2)}) collective-permute-start(bf16[2,32,1024]{2,1,0:T(8,128)(2,1)} %get-tuple-element.426), channel_id=1, source_target_pairs={{0,2},{1,3},{2,0},{3,1},{4,6},{5,7},{6,4},{7,5},{8,10},{9,11},{10,... | collective-permute-start | bytes 393224 | tf_op jit(solution)/shard_map/ppermute | solution.py:122
  828.3 44.5 %collective-permute-start.25 = (bf16[2,32,1024]{2,1,0:T(8,128)(2,1)}, bf16[2,32,1024]{2,1,0:T(8,128)(2,1)}, u32[]{:S(2)}, u32[]{:S(2)}) collective-permute-start(bf16[2,32,1024]{2,1,0:T(8,128)(2,1)} %get-tuple-element.427), channel_id=1, source_target_pairs={{0,1},{1,2},{2,3},{3,0},{4,5},{5,6},{6,7},{7,4},{8,9},{9,10},{10,1... | collective-permute-start | bytes 393224 | tf_op jit(solution)/shard_map/ppermute | solution.py:122
  877.9 31.9 %collective-permute-start.44 = (bf16[128,1024]{1,0:T(8,128)(2,1)}, bf16[128,1024]{1,0:T(8,128)(2,1)}, u32[]{:S(2)}, u32[]{:S(2)}) collective-permute-start(bf16[128,1024]{1,0:T(8,128)(2,1)} %get-tuple-element.391), channel_id=1, source_target_pairs={{0,8},{8,16},{16,24},{24,0},{1,9},{9,17},{17,25},{25,1},{2,10},{10... | collective-permute-start | bytes 786440 | tf_op jit(solution)/shard_map/ppermute | solution.py:122
  878.9 32.5 %collective-permute-start.43 = (bf16[128,1024]{1,0:T(8,128)(2,1)}, bf16[128,1024]{1,0:T(8,128)(2,1)}, u32[]{:S(2)}, u32[]{:S(2)}) collective-permute-start(bf16[128,1024]{1,0:T(8,128)(2,1)} %get-tuple-element.392), channel_id=1, source_target_pairs={{0,16},{8,24},{16,0},{24,8},{1,17},{9,25},{17,1},{25,9},{2,18},{10... | collective-permute-start | bytes 786440 | tf_op jit(solution)/shard_map/ppermute | solution.py:122
  879.5 31.9 %collective-permute-start.42 = (bf16[128,1024]{1,0:T(8,128)(2,1)S(1)}, bf16[128,1024]{1,0:T(8,128)(2,1)}, u32[]{:S(2)}, u32[]{:S(2)}) collective-permute-start(bf16[128,1024]{1,0:T(8,128)(2,1)S(1)} %get-tuple-element.393), channel_id=1, source_target_pairs={{0,24},{8,0},{16,8},{24,16},{1,25},{9,1},{17,9},{25,17},{2,26},{10... | collective-permute-start | bytes 786440 | tf_op jit(solution)/shard_map/ppermute | solution.py:122
  883.1 31.7 %collective-permute-start.50 = (bf16[144,1024]{1,0:T(8,128)(2,1)}, bf16[144,1024]{1,0:T(8,128)(2,1)S(1)}, u32[]{:S(2)}, u32[]{:S(2)}) collective-permute-start(bf16[144,1024]{1,0:T(8,128)(2,1)} %get-tuple-element.381), channel_id=1, source_target_pairs={{0,1},{1,2},{2,3},{3,0},{4,5},{5,6},{6,7},{7,4},{8,9},{9,10},{10,1... | collective-permute-start | bytes 884744 | tf_op jit(solution)/shard_map/ppermute | solution.py:122
  884.8 30.7 %collective-permute-start.49 = (bf16[144,1024]{1,0:T(8,128)(2,1)S(1)}, bf16[144,1024]{1,0:T(8,128)(2,1)S(1)}, u32[]{:S(2)}, u32[]{:S(2)}) collective-permute-start(bf16[144,1024]{1,0:T(8,128)(2,1)S(1)} %get-tuple-element.382), channel_id=1, source_target_pairs={{0,2},{1,3},{2,0},{3,1},{4,6},{5,7},{6,4},{7,5},{8,10},{9,11},{10,... | collective-permute-start | bytes 884744 | tf_op jit(solution)/shard_map/ppermute | solution.py:122
  913.4 16.5 %collective-permute-start.46 = (bf16[2,32,1024]{2,1,0:T(8,128)(2,1)S(1)}, bf16[2,32,1024]{2,1,0:T(8,128)(2,1)S(1)}, u32[]{:S(2)}, u32[]{:S(2)}) collective-permute-start(bf16[2,32,1024]{2,1,0:T(8,128)(2,1)S(1)} %get-tuple-element.434), channel_id=1, source_target_pairs={{0,2},{1,3},{2,0},{3,1},{4,6},{5,7},{6,4},{7,5},{8,10},{9,11},{10,... | collective-permute-start | bytes 393224 | tf_op jit(solution)/shard_map/ppermute | solution.py:122
  914.8 15.1 %collective-permute-start.45 = (bf16[2,32,1024]{2,1,0:T(8,128)(2,1)S(1)}, bf16[2,32,1024]{2,1,0:T(8,128)(2,1)S(1)}, u32[]{:S(2)}, u32[]{:S(2)}) collective-permute-start(bf16[2,32,1024]{2,1,0:T(8,128)(2,1)S(1)} %get-tuple-element.435), channel_id=1, source_target_pairs={{0,1},{1,2},{2,3},{3,0},{4,5},{5,6},{6,7},{7,4},{8,9},{9,10},{10,1... | collective-permute-start | bytes 393224 | tf_op jit(solution)/shard_map/ppermute | solution.py:122
  (187 other events, 2715.3 us)
Sparse Core Ops, SparseCore 0:
  11.6 131.7 all-gather.5
  145.8 47.5 all-gather.7
  222.6 71.8 all-gather.9
  358.0 130.1 all-gather.11
  500.3 63.7 reduce-scatter.2
  578.0 121.4 reduce-scatter.4

commit v8 on v7

--- a/solution.py
+++ b/solution.py
@@ -179,10 +179,7 @@
     half = pair_sum(values.reshape(2, rows, -1), core).reshape(chips, rows // chips, -1)
     part = chip_sum(half).astype(jnp.bfloat16)
     half = placed_before(gathered(part, "chip"), "chip").reshape(rows, -1)
-    other = other_core(half)
-    first = jnp.where(core == 0, half, other)
-    second = jnp.where(core == 0, other, half)
-    return jnp.concatenate([first, second], axis=0)
+    return half, other_core(half)
 
 
 def member_gather(values):
@@ -230,20 +227,36 @@
 
 
 def rest_kernel(
-    gram_ref, rest_ref, gram_scratch, change_scratch, rest_scratch, grams, change_b, rest_b
+    core_ref,
+    first_ref,
+    second_ref,
+    square_ref,
+    rest_ref,
+    gram_scratch,
+    change_scratch,
+    rest_scratch,
+    grams,
+    change_b,
+    rest_b,
 ):
     lead = leading_coefficient
-    size = gram_ref.shape[0]
+    size = square_ref.shape[0]
+    half = size // 2
     tile = 256
 
     def dot(left, right):
         return jnp.dot(left, right, preferred_element_type=jnp.float32)
 
-    @pl.loop(0, size // tile)
-    def _(step):
-        rows = pl.ds(pl.multiple_of(step * tile, tile), tile)
-        gram_scratch[rows, :] = gram_ref[rows, :]
-        grams[0, rows, :] = gram_ref[rows, :].astype(jnp.bfloat16)
+    on_wide = core_ref[0] == 0
+    for part, wide_ref in enumerate((first_ref, second_ref)):
+
+        @pl.loop(0, half // tile)
+        def _(step):
+            rows = pl.ds(pl.multiple_of(step * tile, tile), tile)
+            place = pl.ds(pl.multiple_of(part * half + step * tile, tile), tile)
+            gram = jnp.where(on_wide, wide_ref[rows, :].astype(jnp.float32), square_ref[place, :])
+            gram_scratch[place, :] = gram
+            grams[0, place, :] = gram.astype(jnp.bfloat16)
 
     power = 1.0
     for turn in range(NS_ITERS):
@@ -286,14 +299,15 @@
         power = power * lead
 
 
-def ortho_rest(gram):
-    size = gram.shape[0]
+def ortho_rest(core, first, second, square):
+    size = square.shape[0]
     wide = pltpu.VMEM((size, size), jnp.float32)
     narrow = pltpu.VMEM((size, size), jnp.bfloat16)
     return pl.pallas_call(
         rest_kernel,
         out_shape=jax.ShapeDtypeStruct((size, size), jnp.bfloat16),
-        in_specs=[pl.BlockSpec(memory_space=pltpu.VMEM)],
+        in_specs=[pl.BlockSpec(memory_space=pltpu.SMEM)]
+        + [pl.BlockSpec(memory_space=pltpu.VMEM)] * 3,
         out_specs=pl.BlockSpec(memory_space=pltpu.VMEM),
         scratch_shapes=[
             wide,
@@ -307,7 +321,7 @@
         cost_estimate=pl.CostEstimate(
             flops=18 * size**3, bytes_accessed=6 * size * size, transcendentals=0
         ),
-    )(gram)
+    )(core.reshape(1), first, second, square)
 
 
 def logits_kernel(target_ref, answers_ref, table_ref, shares_ref, stats_ref, logits):
@@ -570,7 +584,6 @@
     ffn_part = jnp.dot(inner_b, wide_b[2], preferred_element_type=jnp.float32)
     hidden3 = hidden2 + member_return(ffn_part.astype(jnp.bfloat16).reshape(members, RESP, D))
     final_b = rms_scale(hidden3, gains[3]).astype(jnp.bfloat16)
-    response_tokens = lax.all_gather(final_b, ALL, axis=0, tiled=True)
     squares, square_rows = square_master.shape[0], square_master.shape[1]
     wides, wide_rows = wide_master.shape[0], wide_master.shape[1]
     per_member = -(-squares // members)
@@ -583,15 +596,22 @@
     def wide_by_member(values):
         return jnp.pad(values, ((0, members - wides), (0, 0), (0, 0)))
 
-    moment_rows = jnp.concatenate(
+    moment_blocks = jnp.concatenate(
         [
-            wide_moment.astype(jnp.bfloat16).reshape(-1, D),
-            square_moment.astype(jnp.bfloat16).reshape(-1, D),
+            wide_by_member(wide_moment.astype(jnp.bfloat16)),
+            by_member(square_moment.astype(jnp.bfloat16)).reshape(members, -1, D),
         ],
-        axis=0,
-    )
-    moment_rows, response_tokens = lax.optimization_barrier((moment_rows, response_tokens))
-    moment_rows = lax.all_gather(moment_rows, "vocab", axis=0)
+        axis=1,
+    )
+    final_b, moment_blocks = lax.optimization_barrier((final_b, moment_blocks))
+    response_tokens = lax.all_gather(final_b, ALL, axis=0, tiled=True)
+    response_tokens, moment_jobs = lax.optimization_barrier(
+        (response_tokens, handed_out(moment_blocks, "vocab"))
+    )
+    wide_moment_job = jnp.stack([piece[:wide_rows] for piece in moment_jobs])
+    square_moment_job = placed_before([piece[wide_rows:] for piece in moment_jobs], "vocab")
+    square_moment_job = square_moment_job.reshape(members, per_member, square_rows, D)
+    square_moment_job = square_moment_job.transpose(1, 0, 2, 3).reshape(per_member, group_rows, D)
     local_target = jnp.where(targets // block_rows == device, targets % block_rows, -1)[None, :]
     shares, own_stats = answer_shares(local_target, response_tokens, table_b)
     stats = own_stats[:3].reshape(3, devices, RESP).transpose(1, 0, 2)
@@ -713,26 +733,6 @@
     grad_wide = jnp.stack(
         [part.astype(jnp.bfloat16) for part in (grad_gate_w, grad_up_w, grad_down_w)]
     )
-    grad_wide, moment_rows = lax.optimization_barrier((grad_wide, moment_rows))
-    wide_moment_job = jnp.stack(
-        [
-            lax.dynamic_slice_in_dim(
-                block_at(moment_rows, member - step),
-                jnp.minimum(member, wides - 1) * wide_rows,
-                wide_rows,
-                0,
-            )
-            for step in range(members)
-        ]
-    )
-    square_moment_job = moment_rows[:, wides * wide_rows :].reshape(
-        members, squares, square_rows, D
-    )
-    square_moment_job = jnp.pad(
-        square_moment_job, ((0, 0), (0, per_member * members - squares), (0, 0), (0, 0))
-    ).reshape(members, per_member, members, square_rows, D)
-    square_moment_job = lax.dynamic_index_in_dim(square_moment_job, member, 2, keepdims=False)
-    square_moment_job = square_moment_job.transpose(1, 0, 2, 3).reshape(per_member, group_rows, D)
     share_wide_b = lax.psum_scatter(grad_wide, DP, scatter_dimension=1, tiled=True)
     grad_square, share_wide_b = lax.optimization_barrier((grad_square, share_wide_b))
     share_wide_b, grad_embed_b = lax.optimization_barrier((share_wide_b, grad_embed_b))
@@ -840,10 +840,9 @@
         + ((1.0 - muon_decay) * factor * wide_inverse) * wide_grad_job.astype(jnp.float32)
     )
     wide_job = wide_job.reshape(members * wide_rows, D).astype(jnp.bfloat16)
-    wide_gram = group_sum(outer(wide_job, wide_job).astype(jnp.bfloat16), core)
+    wide_first, wide_second = group_sum(outer(wide_job, wide_job).astype(jnp.bfloat16), core)
     square_gram = outer(square_job, square_job)
-    gram = jnp.where(core == 0, wide_gram.astype(jnp.float32), square_gram)
-    rest_b = ortho_rest(gram)
+    rest_b = ortho_rest(core, wide_first, wide_second, square_gram)
     power = leading_coefficient**NS_ITERS
     wide_rest = jnp.where(core == 0, rest_b, other_core(rest_b))
     back_square = square_product(square_job, rest_b).astype(jnp.bfloat16)

time: 950 us -> 914 us (0.962)
  waiting for transfers between devices: 442 us -> 414 us
    all_gather x1, waiting for transfers between devices: 67.2 us -> 50.6 us  [body(): response_tokens = lax.all_gather(final_b, ALL, axis=0, tiled=True)]
    ppermute x45 -> x48, waiting for transfers between devices: 232 us -> 221 us  [turned(): lax.ppermute(values, axis, [(i, (i + step) % count) for i in range(count)])]
    unnamed x347 -> x355, local copies, waits for them, and re-layouts: 27.3 us -> 22.2 us
    ppermute x45 -> x48, starting transfers between devices: 54.5 us -> 59.3 us  [turned(): lax.ppermute(values, axis, [(i, (i + step) % count) for i in range(count)])]
  transfers between devices with their start and end apart: 64 -> 66, of which waited for: 31 -> 35; matrix products, arithmetic and copies ran while one was open for 26% -> 25% of each run, Pallas kernels for 4% -> 4%
where the time goes in v8:
time: 914 us; the launch traced here: 906 us
  waiting for transfers between devices  414 us (45%)
  matrix products  136 us (15%)
  other arithmetic  99.9 us (11%)
  starting transfers between devices  91.1 us (10%)
  Pallas kernels  71.2 us (8%)
  local copies, waits for them, and re-layouts  61.6 us (7%)
  between operations  30.9 us (3%)
    ppermute x48, waiting for transfers between devices, turned(): lax.ppermute(values, axis, [(i, (i + step) % count) for i in range(count)])  221 us
    ppermute x48, starting transfers between devices, turned(): lax.ppermute(values, axis, [(i, (i + step) % count) for i in range(count)])  59.3 us
    all_to_all x5, waiting for transfers between devices, exchanged(): return lax.all_to_all(rows, ALL, 0, 0, tiled=True)  59.3 us
    all_gather x1, waiting for transfers between devices, body(): response_tokens = lax.all_gather(final_b, ALL, axis=0, tiled=True)  50.6 us
    all_gather x1, waiting for transfers between devices, body(): lax.all_gather(square_master.astype(jnp.bfloat16), ALL, axis=1, tiled=True)  37.7 us
    dot_general x14, matrix products, outer(): lax.dot_general(grads, inputs, (((0,), (0,)), ((), ())), preferred_elemen...  36.7 us
    dot_general x9, matrix products, back_dense(): return jnp.dot(grads, weight, preferred_element_type=jnp.float32)  31.8 us
    dot_general x10, matrix products, dense(): lax.dot_general(inputs, weight, (((1,), (1,)), ((), ())), preferred_eleme...  29 us
  transfers between devices with their start and end apart: 66, of which 35 were waited for; matrix products, arithmetic and copies ran while one was open for 25% of the time, Pallas kernels for 4%

profile of v8, /device:TPU:0, one launch (start us, length us, event | category | flops | bytes accessed | tf_op | source)
XLA Modules:
  0.0 905.7 jit_solution(11286359172619959256)
XLA Ops:
  19.5 7.3 all-to-all-start.4
  26.8 6.1 convert_element_type.422.table_ref
  35.3 6.8 fusion.70
  42.1 4.1 all-to-all-start.5
  56.2 45.0 %all-to-all-done.5 = bf16[32,24,1024]{2,1,0:T(8,128)(2,1)S(1)} async-done(((bf16[32,24,1024]{2,1,0:T(8,128)(2,1)}), bf16[32,24,1024]{2,1,0:T(8,128)(2,1)S(1)}, u32[]{:S(2)}, u32[]{:S(2)}) %all-to-all-start.5) | async-done | bytes 1572896 | tf_op jit(solution)/shard_map/all_to_all | solution.py:112
  105.7 37.7 %all-gather.4.cloned.1.call-done = bf16[7,1024,1024]{2,1,0:T(8,128)(2,1)} async-done(((bf16[7,32,1024]{2,1,0:T(8,128)(2,1)}), bf16[7,1024,1024]{2,1,0:T(8,128)(2,1)}) %all-gather.4.cloned.1.call-update) | async-done | bytes 14680080 | tf_op jit(solution)/shard_map/all_gather | solution.py:482
  146.5 5.7 fusion.169
  176.5 17.0 %all-gather.6.cloned.1.call-done = bf16[3,1152,1024]{2,1,0:T(8,128)(2,1)} async-done(((bf16[3,144,1024]{2,1,0:T(8,128)(2,1)}), bf16[3,1152,1024]{2,1,0:T(8,128)(2,1)}) %all-gather.6.cloned.1.call-update) | async-done | bytes 7077904 | tf_op jit(solution)/shard_map/all_gather | solution.py:483
  211.0 7.8 collective-permute-done.4
  223.2 4.7 collective-permute-start.6
  230.3 11.2 %collective-permute-done.6 = bf16[208,1024]{1,0:T(8,128)(2,1)} collective-permute-done((bf16[208,1024]{1,0:T(8,128)(2,1)S(1)}, bf16[208,1024]{1,0:T(8,128)(2,1)}, u32[]{:S(2)}, u32[]{:S(2)}) %collective-permute-start.6) | collective-permute-done | bytes 426016 | tf_op jit(solution)/shard_map/ppermute | solution.py:122
  241.5 19.4 %collective-permute-done.7 = bf16[208,1024]{1,0:T(8,128)(2,1)} collective-permute-done((bf16[208,1024]{1,0:T(8,128)(2,1)S(1)}, bf16[208,1024]{1,0:T(8,128)(2,1)}, u32[]{:S(2)}, u32[]{:S(2)}) %collective-permute-start.7) | collective-permute-done | bytes 426016 | tf_op jit(solution)/shard_map/ppermute | solution.py:122
  260.9 50.6 %all-gather.8.cloned.1.call-done.answers_ref = bf16[3072,1024]{1,0:T(8,128)(2,1)} async-done(((bf16[96,1024]{1,0:T(8,128)(2,1)}), bf16[3072,1024]{1,0:T(8,128)(2,1)}) %all-gather.8.cloned.1.call-update) | async-done | bytes 6291472 | tf_op jit(solution)/shard_map/all_gather | solution.py:607
  314.3 25.3 %shard_map.313 = (bf16[2048,3072]{1,0:T(8,128)(2,1)}, f32[8,3072]{1,0:T(8,128)S(1)}) custom-call(s32[1,3072]{1,0:T(1,128)S(1)} %compare_select_fusion.target_ref, bf16[3072,1024]{1,0:T(8,128)(2,1)S(1)} %copy-done, bf16[2048,1024]{1,0:T(8,128)(2,1)} %get-tuple-element.687), custom_call_target="tpu_custom_call" | custom-call | flops 12884901888 | bytes 18874368 | tf_op jit(solution)/shard_map/pallas_call | solution.py:361
  343.5 7.5 all-to-all-done.6
  355.7 7.1 all-to-all-done.7
  364.4 10.3 %shard_map.315 = bf16[1536,1024]{1,0:T(8,128)(2,1)S(1)} custom-call(s32[1]{0:T(128)} %bitcast.69.core_ref, s32[1,3072]{1,0:T(1,128)S(1)} %compare_select_fusion.target_ref, f32[1,3072]{1,0:T(1,128)S(1)} %get-tuple-element.448.scale_ref, f32[1,3072]{1,0:T(1,128)S(1)} %get-tuple-element.447.value_ref, bf16[2048,3072]{1,0:T(8,128)(2,1)} %get-tuple-element.257.shares_ref, ...), custom_call_target="tpu_custom_call" | custom-call | flops 6442450944 | bytes 9437184 | tf_op jit(solution)/shard_map/pallas_call | solution.py:403
  374.9 10.4 %shard_map.314 = bf16[1536,1024]{1,0:T(8,128)(2,1)S(1)} custom-call(s32[1]{0:T(128)} %bitcast.68.core_ref, s32[1,3072]{1,0:T(1,128)S(1)} %compare_select_fusion.target_ref, f32[1,3072]{1,0:T(1,128)S(1)} %get-tuple-element.448.scale_ref, f32[1,3072]{1,0:T(1,128)S(1)} %get-tuple-element.447.value_ref, bf16[2048,3072]{1,0:T(8,128)(2,1)} %get-tuple-element.257.shares_ref, ...), custom_call_target="tpu_custom_call" | custom-call | flops 6442450944 | bytes 9437184 | tf_op jit(solution)/shard_map/pallas_call | solution.py:403
  392.0 17.5 %fusion.12 = f32[2048,1024]{1,0:T(8,128)} fusion(bf16[3072,1024]{1,0:T(8,128)(2,1)} %all-gather.8.cloned.1.call-done.answers_ref, bf16[2048,3072]{1,0:T(8,128)(2,1)S(1)} %bitcast.538, f32[3072]{0:T(1024)S(1)} %bitcast.449, f32[3072]{0:T(1024)S(1)} %bitcast.448, s32[3072]{0:T(1024)S(1)} %fusion.129), kind=kOutput, calls=%fused_computation.31 | convolution fusion | flops 12910067712 | bytes 27299840 | tf_op jit(solution)/shard_map/dot_general | solution.py:641
  409.6 16.7 %collective-permute-done.11 = bf16[384,1024]{1,0:T(8,128)(2,1)S(1)} collective-permute-done((bf16[384,1024]{1,0:T(8,128)(2,1)S(1)}, bf16[384,1024]{1,0:T(8,128)(2,1)S(1)}, u32[]{:S(2)}, u32[]{:S(2)}) %collective-permute-start.11) | collective-permute-done | bytes 786464 | tf_op jit(solution)/shard_map/ppermute | solution.py:122
  429.6 4.2 collective-permute-done.15
  433.9 12.0 %collective-permute-done.14 = bf16[96,1024]{1,0:T(8,128)(2,1)S(1)} collective-permute-done((bf16[96,1024]{1,0:T(8,128)(2,1)S(1)}, bf16[96,1024]{1,0:T(8,128)(2,1)S(1)}, u32[]{:S(2)}, u32[]{:S(2)}) %collective-permute-start.14) | collective-permute-done | bytes 196640 | tf_op jit(solution)/shard_map/ppermute | solution.py:122
  452.6 13.5 %collective-permute-done.17 = bf16[96,1024]{1,0:T(8,128)(2,1)S(1)} collective-permute-done((bf16[96,1024]{1,0:T(8,128)(2,1)S(1)}, bf16[96,1024]{1,0:T(8,128)(2,1)S(1)}, u32[]{:S(2)}, u32[]{:S(2)}) %collective-permute-start.17) | collective-permute-done | bytes 196640 | tf_op jit(solution)/shard_map/ppermute | solution.py:122
  484.7 4.0 collective-permute-start.19
  489.3 5.1 collective-permute-done.21
  494.4 6.8 collective-permute-done.20
  528.9 7.3 multiply_reduce_fusion.1
  564.1 5.3 multiply_reduce_fusion.5
  574.8 6.3 all-to-all-start.8
  583.3 5.1 all-to-all-done.8
  611.2 13.8 %collective-permute-done.27 = bf16[144,1024]{1,0:T(8,128)(2,1)S(1)} collective-permute-done((bf16[144,1024]{1,0:T(8,128)(2,1)S(1)}, bf16[144,1024]{1,0:T(8,128)(2,1)S(1)}, u32[]{:S(2)}, u32[]{:S(2)}) %collective-permute-start.27) | collective-permute-done | bytes 294944 | tf_op jit(solution)/shard_map/ppermute | solution.py:122
  625.0 30.1 %collective-permute-done.26 = bf16[144,1024]{1,0:T(8,128)(2,1)S(1)} collective-permute-done((bf16[144,1024]{1,0:T(8,128)(2,1)S(1)}, bf16[144,1024]{1,0:T(8,128)(2,1)S(1)}, u32[]{:S(2)}, u32[]{:S(2)}) %collective-permute-start.26) | collective-permute-done | bytes 294944 | tf_op jit(solution)/shard_map/ppermute | solution.py:122
  656.3 8.6 fusion.19
  664.9 14.4 %reduce-scatter.5.cloned.1.call-done = bf16[7,128,1024]{2,1,0:T(8,128)(2,1)} async-done(((bf16[7,1024,1024]{2,1,0:T(8,128)(2,1)}), bf16[7,128,1024]{2,1,0:T(8,128)(2,1)}) %reduce-scatter.5.cloned.1.call-update) | async-done | bytes 1835024 | tf_op jit(solution)/shard_map/reduce_scatter | solution.py:741
  687.2 6.1 multiply_reduce_fusion
  693.3 4.9 collective-permute-done.24
  698.2 32.7 %collective-permute-done.23 = bf16[2,128,1024]{2,1,0:T(8,128)(2,1)} collective-permute-done((bf16[2,128,1024]{2,1,0:T(8,128)(2,1)S(1)}, bf16[2,128,1024]{2,1,0:T(8,128)(2,1)}, u32[]{:S(2)}, u32[]{:S(2)}) %collective-permute-start.23) | collective-permute-done | bytes 524320 | tf_op jit(solution)/shard_map/ppermute | solution.py:122
  737.5 4.0 all-to-all-start.10
  742.1 6.4 all-to-all-done.10
  769.2 4.4 collective-permute-done.32
  773.8 5.0 collective-permute-done.38
  778.8 6.1 collective-permute-done.36
  794.9 5.0 collective-permute-done.40
  806.0 25.1 %shard_map.316 = bf16[1024,1024]{1,0:T(8,128)(2,1)S(1)} custom-call(s32[1]{0:T(128)} %bitcast.68.core_ref, bf16[512,1024]{1,0:T(8,128)(2,1)S(1)} %bitcast.447, bf16[512,1024]{1,0:T(8,128)(2,1)S(1)} %collective-permute-done.42.second_ref, f32[1024,1024]{1,0:T(8,128)S(1)} %fusion.171.square_ref), custom_call_target="tpu_custom_call" | custom-call | flops 19327352832 | bytes 6291456 | tf_op jit(solution)/shard_map/pallas_call | solution.py:306
  831.3 3.9 convolution_convert_fusion.4
  852.2 22.7 %add_multiply_fusion = (f32[2048,1024]{1,0:T(8,128)}, f32[2048,1024]{1,0:T(8,128)}, f32[2048,1024]{1,0:T(8,128)}) fusion(f32[2048,1024]{1,0:T(8,128)} %param.25, f32[]{:T(128)S(6)} %sub.255, f32[]{:T(128)S(6)} %sub.254, f32[2048,1024]{1,0:T(8,128)} %get-tuple-element.271, f32[]{:T(128)S(6)} %min.3, f32[2048,1024]{1,0:T(8,128)} %param.27, f32[2048,1024]{1,0:T(8,128)} %param.26), kind=kLoop, calls=%fused_computation.37 | loop fusion | flops 31457280 | bytes 58720268 | tf_op jit(solution)/shard_map/mul | solution.py:100
  880.4 4.4 collective-permute-done.51
  888.0 6.4 collective-permute-done.49
  (735 shorter events, 283.0 us)
Async XLA Ops:
  7.2 136.2 %all-gather.4.cloned.1.call-start = ((), (), s32[]{:S(2)}) async-start(), calls=%async_computation.13 | async-start | bytes 15138816 | tf_op jit(solution)/shard_map/all_gather | solution.py:482
  19.5 15.1 %all-to-all-start.4 = ((f32[32,1,349]{2,1,0:T(1,128)}), f32[32,1,349]{2,1,0:T(1,128)S(1)}, u32[]{:S(2)}, u32[]{:S(2)}) async-start(f32[32,1,349]{2,1,0:T(1,128)} %all_to_all.79), calls=%async_computation.4 | async-start | bytes 98304 | tf_op jit(solution)/shard_map/all_to_all | solution.py:112
  42.1 59.1 %all-to-all-start.5 = ((bf16[32,24,1024]{2,1,0:T(8,128)(2,1)}), bf16[32,24,1024]{2,1,0:T(8,128)(2,1)S(1)}, u32[]{:S(2)}, u32[]{:S(2)}) async-start(bf16[32,24,1024]{2,1,0:T(8,128)(2,1)} %bitcast.484), calls=%async_computation.5 | async-start | bytes 3145728 | tf_op jit(solution)/shard_map/all_to_all | solution.py:112
  46.3 147.2 %all-gather.6.cloned.1.call-start = ((), (), s32[]{:S(2)}) async-start(), calls=%async_computation.14 | async-start | bytes 7962624 | tf_op jit(solution)/shard_map/all_gather | solution.py:483
  47.4 264.1 %all-gather.8.cloned.1.call-start = ((), (), s32[]{:S(2)}) async-start(), calls=%async_computation.15 | async-start | bytes 6488064 | tf_op jit(solution)/shard_map/all_gather | solution.py:607
  173.4 20.0 %collective-permute-start.2 = (bf16[96,1024]{1,0:T(8,128)(2,1)S(1)}, bf16[96,1024]{1,0:T(8,128)(2,1)S(1)}, u32[]{:S(2)}, u32[]{:S(2)}) collective-permute-start(bf16[96,1024]{1,0:T(8,128)(2,1)S(1)} %multiply_convert_fusion.9), channel_id=1, source_target_pairs={{0,3},{1,0},{2,1},{3,2},{4,7},{5,4},{6,5},{7,6},{8,11},{9,8},{10,9... | collective-permute-start | bytes 589832 | tf_op jit(solution)/shard_map/ppermute | solution.py:122
  173.8 19.7 %collective-permute-start.1 = (bf16[96,1024]{1,0:T(8,128)(2,1)S(1)}, bf16[96,1024]{1,0:T(8,128)(2,1)S(1)}, u32[]{:S(2)}, u32[]{:S(2)}) collective-permute-start(bf16[96,1024]{1,0:T(8,128)(2,1)S(1)} %multiply_convert_fusion.9), channel_id=1, source_target_pairs={{0,2},{1,3},{2,0},{3,1},{4,6},{5,7},{6,4},{7,5},{8,10},{9,11},{10,... | collective-permute-start | bytes 589832 | tf_op jit(solution)/shard_map/ppermute | solution.py:122
  174.7 18.8 %collective-permute-start = (bf16[96,1024]{1,0:T(8,128)(2,1)S(1)}, bf16[96,1024]{1,0:T(8,128)(2,1)S(1)}, u32[]{:S(2)}, u32[]{:S(2)}) collective-permute-start(bf16[96,1024]{1,0:T(8,128)(2,1)S(1)} %multiply_convert_fusion.9), channel_id=1, source_target_pairs={{0,1},{1,2},{2,3},{3,0},{4,5},{5,6},{6,7},{7,4},{8,9},{9,10},{10,1... | collective-permute-start | bytes 589832 | tf_op jit(solution)/shard_map/ppermute | solution.py:122
  202.7 16.0 %collective-permute-start.4 = (bf16[96,1024]{1,0:T(8,128)(2,1)S(1)}, bf16[96,1024]{1,0:T(8,128)(2,1)}, u32[]{:S(2)}, u32[]{:S(2)}) collective-permute-start(bf16[96,1024]{1,0:T(8,128)(2,1)S(1)} %get-tuple-element.419), channel_id=1, source_target_pairs={{0,2},{1,3},{2,0},{3,1},{4,6},{5,7},{6,4},{7,5},{8,10},{9,11},{10,... | collective-permute-start | bytes 589832 | tf_op jit(solution)/shard_map/ppermute | solution.py:122
  205.1 13.6 %collective-permute-start.3 = (bf16[96,1024]{1,0:T(8,128)(2,1)S(1)}, bf16[96,1024]{1,0:T(8,128)(2,1)}, u32[]{:S(2)}, u32[]{:S(2)}) collective-permute-start(bf16[96,1024]{1,0:T(8,128)(2,1)S(1)} %get-tuple-element.417), channel_id=1, source_target_pairs={{0,3},{1,0},{2,1},{3,2},{4,7},{5,4},{6,5},{7,6},{8,11},{9,8},{10,9... | collective-permute-start | bytes 589832 | tf_op jit(solution)/shard_map/ppermute | solution.py:122
  223.2 18.3 %collective-permute-start.6 = (bf16[208,1024]{1,0:T(8,128)(2,1)S(1)}, bf16[208,1024]{1,0:T(8,128)(2,1)}, u32[]{:S(2)}, u32[]{:S(2)}) collective-permute-start(bf16[208,1024]{1,0:T(8,128)(2,1)S(1)} %get-tuple-element.379), channel_id=1, source_target_pairs={{0,1},{1,2},{2,3},{3,0},{4,5},{5,6},{6,7},{7,4},{8,9},{9,10},{10,1... | collective-permute-start | bytes 1277960 | tf_op jit(solution)/shard_map/ppermute | solution.py:122
  227.8 33.0 %collective-permute-start.7 = (bf16[208,1024]{1,0:T(8,128)(2,1)S(1)}, bf16[208,1024]{1,0:T(8,128)(2,1)}, u32[]{:S(2)}, u32[]{:S(2)}) collective-permute-start(bf16[208,1024]{1,0:T(8,128)(2,1)S(1)} %get-tuple-element.378), channel_id=1, source_target_pairs={{0,2},{1,3},{2,0},{3,1},{4,6},{5,7},{6,4},{7,5},{8,10},{9,11},{10,... | collective-permute-start | bytes 1277960 | tf_op jit(solution)/shard_map/ppermute | solution.py:122
  229.3 31.6 %collective-permute-start.8 = (bf16[208,1024]{1,0:T(8,128)(2,1)S(1)}, bf16[208,1024]{1,0:T(8,128)(2,1)}, u32[]{:S(2)}, u32[]{:S(2)}) collective-permute-start(bf16[208,1024]{1,0:T(8,128)(2,1)S(1)} %get-tuple-element.377), channel_id=1, source_target_pairs={{0,3},{1,0},{2,1},{3,2},{4,7},{5,4},{6,5},{7,6},{8,11},{9,8},{10,9... | collective-permute-start | bytes 1277960 | tf_op jit(solution)/shard_map/ppermute | solution.py:122
  355.6 201.2 %reduce-scatter.3.cloned.1.call-start = ((), (), s32[]{:S(2)}) async-start(), calls=%async_computation.16 | async-start | bytes 7962624 | tf_op jit(solution)/shard_map/reduce_scatter | solution.py:736
  389.2 20.4 %collective-permute-start.12 = (bf16[384,1024]{1,0:T(8,128)(2,1)S(1)}, bf16[384,1024]{1,0:T(8,128)(2,1)S(1)}, u32[]{:S(2)}, u32[]{:S(2)}) collective-permute-start(bf16[384,1024]{1,0:T(8,128)(2,1)S(1)} %get-tuple-element.371), channel_id=1, source_target_pairs={{0,24},{8,0},{16,8},{24,16},{1,25},{9,1},{17,9},{25,17},{2,26},{10... | collective-permute-start | bytes 2359304 | tf_op jit(solution)/shard_map/ppermute | solution.py:122
  389.8 36.5 %collective-permute-start.11 = (bf16[384,1024]{1,0:T(8,128)(2,1)S(1)}, bf16[384,1024]{1,0:T(8,128)(2,1)S(1)}, u32[]{:S(2)}, u32[]{:S(2)}) collective-permute-start(bf16[384,1024]{1,0:T(8,128)(2,1)S(1)} %get-tuple-element.372), channel_id=1, source_target_pairs={{0,16},{8,24},{16,0},{24,8},{1,17},{9,25},{17,1},{25,9},{2,18},{10... | collective-permute-start | bytes 2359304 | tf_op jit(solution)/shard_map/ppermute | solution.py:122
  391.3 35.0 %collective-permute-start.10 = (bf16[384,1024]{1,0:T(8,128)(2,1)S(1)}, bf16[384,1024]{1,0:T(8,128)(2,1)S(1)}, u32[]{:S(2)}, u32[]{:S(2)}) collective-permute-start(bf16[384,1024]{1,0:T(8,128)(2,1)S(1)} %get-tuple-element.370), channel_id=1, source_target_pairs={{0,8},{8,16},{16,24},{24,0},{1,9},{9,17},{17,25},{25,1},{2,10},{10... | collective-permute-start | bytes 2359304 | tf_op jit(solution)/shard_map/ppermute | solution.py:122
  427.6 18.3 %collective-permute-start.14 = (bf16[96,1024]{1,0:T(8,128)(2,1)S(1)}, bf16[96,1024]{1,0:T(8,128)(2,1)S(1)}, u32[]{:S(2)}, u32[]{:S(2)}) collective-permute-start(bf16[96,1024]{1,0:T(8,128)(2,1)S(1)} %get-tuple-element.416), channel_id=1, source_target_pairs={{0,2},{1,3},{2,0},{3,1},{4,6},{5,7},{6,4},{7,5},{8,10},{9,11},{10,... | collective-permute-start | bytes 589832 | tf_op jit(solution)/shard_map/ppermute | solution.py:122
  429.0 16.8 %collective-permute-start.13 = (bf16[96,1024]{1,0:T(8,128)(2,1)S(1)}, bf16[96,1024]{1,0:T(8,128)(2,1)S(1)}, u32[]{:S(2)}, u32[]{:S(2)}) collective-permute-start(bf16[96,1024]{1,0:T(8,128)(2,1)S(1)} %get-tuple-element.414), channel_id=1, source_target_pairs={{0,1},{1,2},{2,3},{3,0},{4,5},{5,6},{6,7},{7,4},{8,9},{9,10},{10,1... | collective-permute-start | bytes 589832 | tf_op jit(solution)/shard_map/ppermute | solution.py:122
  446.9 19.2 %collective-permute-start.17 = (bf16[96,1024]{1,0:T(8,128)(2,1)S(1)}, bf16[96,1024]{1,0:T(8,128)(2,1)S(1)}, u32[]{:S(2)}, u32[]{:S(2)}) collective-permute-start(bf16[96,1024]{1,0:T(8,128)(2,1)S(1)} %fusion.151), channel_id=1, source_target_pairs={{0,2},{1,3},{2,0},{3,1},{4,6},{5,7},{6,4},{7,5},{8,10},{9,11},{10,... | collective-permute-start | bytes 589832 | tf_op jit(solution)/shard_map/ppermute | solution.py:122
  448.5 17.6 %collective-permute-start.16 = (bf16[96,1024]{1,0:T(8,128)(2,1)S(1)}, bf16[96,1024]{1,0:T(8,128)(2,1)S(1)}, u32[]{:S(2)}, u32[]{:S(2)}) collective-permute-start(bf16[96,1024]{1,0:T(8,128)(2,1)S(1)} %fusion.151), channel_id=1, source_target_pairs={{0,1},{1,2},{2,3},{3,0},{4,5},{5,6},{6,7},{7,4},{8,9},{9,10},{10,1... | collective-permute-start | bytes 589832 | tf_op jit(solution)/shard_map/ppermute | solution.py:122
  477.3 202.0 %reduce-scatter.5.cloned.1.call-start = ((), (), s32[]{:S(2)}) async-start(), calls=%async_computation.17 | async-start | bytes 16515072 | tf_op jit(solution)/shard_map/reduce_scatter | solution.py:741
  484.6 16.5 %collective-permute-start.20 = (bf16[96,1024]{1,0:T(8,128)(2,1)S(1)}, bf16[96,1024]{1,0:T(8,128)(2,1)S(1)}, u32[]{:S(2)}, u32[]{:S(2)}) collective-permute-start(bf16[96,1024]{1,0:T(8,128)(2,1)S(1)} %get-tuple-element.413), channel_id=1, source_target_pairs={{0,2},{1,3},{2,0},{3,1},{4,6},{5,7},{6,4},{7,5},{8,10},{9,11},{10,... | collective-permute-start | bytes 589832 | tf_op jit(solution)/shard_map/ppermute | solution.py:122
  484.7 16.4 %collective-permute-start.19 = (bf16[96,1024]{1,0:T(8,128)(2,1)S(1)}, bf16[96,1024]{1,0:T(8,128)(2,1)S(1)}, u32[]{:S(2)}, u32[]{:S(2)}) collective-permute-start(bf16[96,1024]{1,0:T(8,128)(2,1)S(1)} %get-tuple-element.411), channel_id=1, source_target_pairs={{0,3},{1,0},{2,1},{3,2},{4,7},{5,4},{6,5},{7,6},{8,11},{9,8},{10,9... | collective-permute-start | bytes 589832 | tf_op jit(solution)/shard_map/ppermute | solution.py:122
  574.8 13.7 %all-to-all-start.8 = ((f32[32,1,352]{2,1,0:T(1,128)}), f32[32,1,352]{2,1,0:T(1,128)S(1)}, u32[]{:S(2)}, u32[]{:S(2)}) async-start(f32[32,1,352]{2,1,0:T(1,128)} %copy.120), calls=%async_computation.10 | async-start | bytes 98304 | tf_op jit(solution)/shard_map/all_to_all | solution.py:112
  589.1 67.2 %all-to-all-start.9 = ((bf16[32,24,1024]{2,1,0:T(8,128)(2,1)}), bf16[32,24,1024]{2,1,0:T(8,128)(2,1)}, u32[]{:S(2)}, u32[]{:S(2)}) async-start(bf16[32,24,1024]{2,1,0:T(8,128)(2,1)} %bitcast.120), calls=%async_computation.11 | async-start | bytes 3145728 | tf_op jit(solution)/shard_map/all_to_all | solution.py:112
  604.8 20.2 %collective-permute-start.27 = (bf16[144,1024]{1,0:T(8,128)(2,1)S(1)}, bf16[144,1024]{1,0:T(8,128)(2,1)S(1)}, u32[]{:S(2)}, u32[]{:S(2)}) collective-permute-start(bf16[144,1024]{1,0:T(8,128)(2,1)S(1)} %get-tuple-element.408), channel_id=1, source_target_pairs={{0,3},{1,0},{2,1},{3,2},{4,7},{5,4},{6,5},{7,6},{8,11},{9,8},{10,9... | collective-permute-start | bytes 884744 | tf_op jit(solution)/shard_map/ppermute | solution.py:122
  608.4 46.7 %collective-permute-start.26 = (bf16[144,1024]{1,0:T(8,128)(2,1)S(1)}, bf16[144,1024]{1,0:T(8,128)(2,1)S(1)}, u32[]{:S(2)}, u32[]{:S(2)}) collective-permute-start(bf16[144,1024]{1,0:T(8,128)(2,1)S(1)} %get-tuple-element.410), channel_id=1, source_target_pairs={{0,2},{1,3},{2,0},{3,1},{4,6},{5,7},{6,4},{7,5},{8,10},{9,11},{10,... | collective-permute-start | bytes 884744 | tf_op jit(solution)/shard_map/ppermute | solution.py:122
  608.4 46.7 %collective-permute-start.25 = (bf16[144,1024]{1,0:T(8,128)(2,1)S(1)}, bf16[144,1024]{1,0:T(8,128)(2,1)S(1)}, u32[]{:S(2)}, u32[]{:S(2)}) collective-permute-start(bf16[144,1024]{1,0:T(8,128)(2,1)S(1)} %get-tuple-element.409), channel_id=1, source_target_pairs={{0,1},{1,2},{2,3},{3,0},{4,5},{5,6},{6,7},{7,4},{8,9},{9,10},{10,1... | collective-permute-start | bytes 884744 | tf_op jit(solution)/shard_map/ppermute | solution.py:122
  682.4 15.8 %collective-permute-start.24 = (bf16[2,128,1024]{2,1,0:T(8,128)(2,1)S(1)}, bf16[2,128,1024]{2,1,0:T(8,128)(2,1)}, u32[]{:S(2)}, u32[]{:S(2)}) collective-permute-start(bf16[2,128,1024]{2,1,0:T(8,128)(2,1)S(1)} %get-tuple-element.374), channel_id=1, source_target_pairs={{0,3},{1,0},{2,1},{3,2},{4,7},{5,4},{6,5},{7,6},{8,11},{9,8},{10,9... | collective-permute-start | bytes 1572872 | tf_op jit(solution)/shard_map/ppermute | solution.py:122
  685.8 45.1 %collective-permute-start.23 = (bf16[2,128,1024]{2,1,0:T(8,128)(2,1)S(1)}, bf16[2,128,1024]{2,1,0:T(8,128)(2,1)}, u32[]{:S(2)}, u32[]{:S(2)}) collective-permute-start(bf16[2,128,1024]{2,1,0:T(8,128)(2,1)S(1)} %get-tuple-element.375), channel_id=1, source_target_pairs={{0,2},{1,3},{2,0},{3,1},{4,6},{5,7},{6,4},{7,5},{8,10},{9,11},{10,... | collective-permute-start | bytes 1572872 | tf_op jit(solution)/shard_map/ppermute | solution.py:122
  685.8 45.1 %collective-permute-start.22 = (bf16[2,128,1024]{2,1,0:T(8,128)(2,1)S(1)}, bf16[2,128,1024]{2,1,0:T(8,128)(2,1)}, u32[]{:S(2)}, u32[]{:S(2)}) collective-permute-start(bf16[2,128,1024]{2,1,0:T(8,128)(2,1)S(1)} %get-tuple-element.373), channel_id=1, source_target_pairs={{0,1},{1,2},{2,3},{3,0},{4,5},{5,6},{6,7},{7,4},{8,9},{9,10},{10,1... | collective-permute-start | bytes 1572872 | tf_op jit(solution)/shard_map/ppermute | solution.py:122
  759.0 14.7 %collective-permute-start.32 = (bf16[128,1024]{1,0:T(8,128)(2,1)S(1)}, bf16[128,1024]{1,0:T(8,128)(2,1)S(1)}, u32[]{:S(2)}, u32[]{:S(2)}) collective-permute-start(bf16[128,1024]{1,0:T(8,128)(2,1)S(1)} %get-tuple-element.442), channel_id=1, source_target_pairs={{0,16},{8,24},{16,0},{24,8},{1,17},{9,25},{17,1},{25,9},{2,18},{10... | collective-permute-start | bytes 786440 | tf_op jit(solution)/shard_map/ppermute | solution.py:122
  759.5 14.2 %collective-permute-start.33 = (bf16[128,1024]{1,0:T(8,128)(2,1)S(1)}, bf16[128,1024]{1,0:T(8,128)(2,1)S(1)}, u32[]{:S(2)}, u32[]{:S(2)}) collective-permute-start(bf16[128,1024]{1,0:T(8,128)(2,1)S(1)} %get-tuple-element.440), channel_id=1, source_target_pairs={{0,24},{8,0},{16,8},{24,16},{1,25},{9,1},{17,9},{25,17},{2,26},{10... | collective-permute-start | bytes 786440 | tf_op jit(solution)/shard_map/ppermute | solution.py:122
  763.6 15.2 %collective-permute-start.38 = (bf16[128,1024]{1,0:T(8,128)(2,1)S(1)}, bf16[128,1024]{1,0:T(8,128)(2,1)S(1)}, u32[]{:S(2)}, u32[]{:S(2)}) collective-permute-start(bf16[128,1024]{1,0:T(8,128)(2,1)S(1)} %get-tuple-element.403), channel_id=1, source_target_pairs={{0,24},{8,0},{16,8},{24,16},{1,25},{9,1},{17,9},{25,17},{2,26},{10... | collective-permute-start | bytes 786440 | tf_op jit(solution)/shard_map/ppermute | solution.py:122
  764.2 14.6 %collective-permute-start.37 = (bf16[128,1024]{1,0:T(8,128)(2,1)S(1)}, bf16[128,1024]{1,0:T(8,128)(2,1)S(1)}, u32[]{:S(2)}, u32[]{:S(2)}) collective-permute-start(bf16[128,1024]{1,0:T(8,128)(2,1)S(1)} %get-tuple-element.404), channel_id=1, source_target_pairs={{0,16},{8,24},{16,0},{24,8},{1,17},{9,25},{17,1},{25,9},{2,18},{10... | collective-permute-start | bytes 786440 | tf_op jit(solution)/shard_map/ppermute | solution.py:122
  768.4 16.5 %collective-permute-start.36 = (bf16[128,1024]{1,0:T(8,128)(2,1)S(1)}, bf16[128,1024]{1,0:T(8,128)(2,1)S(1)}, u32[]{:S(2)}, u32[]{:S(2)}) collective-permute-start(bf16[128,1024]{1,0:T(8,128)(2,1)S(1)} %get-tuple-element.402), channel_id=1, source_target_pairs={{0,8},{8,16},{16,24},{24,0},{1,9},{9,17},{17,25},{25,1},{2,10},{10... | collective-permute-start | bytes 786440 | tf_op jit(solution)/shard_map/ppermute | solution.py:122
  773.8 29.7 %collective-permute-start.34 = (bf16[512,1024]{1,0:T(8,128)(2,1)S(1)}, bf16[512,1024]{1,0:T(8,128)(2,1)S(1)}, u32[]{:S(2)}, u32[]{:S(2)}) collective-permute-start(bf16[512,1024]{1,0:T(8,128)(2,1)S(1)} %pad_maximum_fusion.4), channel_id=1, source_target_pairs={{0,4},{4,0},{1,5},{5,1},{2,6},{6,2},{3,7},{7,3},{8,12},{12,8},{9,1... | collective-permute-start | bytes 3145736 | tf_op jit(solution)/shard_map/ppermute | solution.py:162
  790.5 49.0 %collective-permute-start.30 = (bf16[2,32,1024]{2,1,0:T(8,128)(2,1)}, bf16[2,32,1024]{2,1,0:T(8,128)(2,1)S(1)}, u32[]{:S(2)}, u32[]{:S(2)}) collective-permute-start(bf16[2,32,1024]{2,1,0:T(8,128)(2,1)} %get-tuple-element.429), channel_id=1, source_target_pairs={{0,3},{1,0},{2,1},{3,2},{4,7},{5,4},{6,5},{7,6},{8,11},{9,8},{10,9... | collective-permute-start | bytes 393224 | tf_op jit(solution)/shard_map/ppermute | solution.py:122
  794.3 45.2 %collective-permute-start.29 = (bf16[2,32,1024]{2,1,0:T(8,128)(2,1)}, bf16[2,32,1024]{2,1,0:T(8,128)(2,1)S(1)}, u32[]{:S(2)}, u32[]{:S(2)}) collective-permute-start(bf16[2,32,1024]{2,1,0:T(8,128)(2,1)} %get-tuple-element.430), channel_id=1, source_target_pairs={{0,2},{1,3},{2,0},{3,1},{4,6},{5,7},{6,4},{7,5},{8,10},{9,11},{10,... | collective-permute-start | bytes 393224 | tf_op jit(solution)/shard_map/ppermute | solution.py:122
  799.9 39.6 %collective-permute-start.28 = (bf16[2,32,1024]{2,1,0:T(8,128)(2,1)}, bf16[2,32,1024]{2,1,0:T(8,128)(2,1)S(1)}, u32[]{:S(2)}, u32[]{:S(2)}) collective-permute-start(bf16[2,32,1024]{2,1,0:T(8,128)(2,1)} %get-tuple-element.431), channel_id=1, source_target_pairs={{0,1},{1,2},{2,3},{3,0},{4,5},{5,6},{6,7},{7,4},{8,9},{9,10},{10,1... | collective-permute-start | bytes 393224 | tf_op jit(solution)/shard_map/ppermute | solution.py:122
  844.3 30.6 %collective-permute-start.47 = (bf16[128,1024]{1,0:T(8,128)(2,1)}, bf16[128,1024]{1,0:T(8,128)(2,1)S(1)}, u32[]{:S(2)}, u32[]{:S(2)}) collective-permute-start(bf16[128,1024]{1,0:T(8,128)(2,1)} %get-tuple-element.395), channel_id=1, source_target_pairs={{0,8},{8,16},{16,24},{24,0},{1,9},{9,17},{17,25},{25,1},{2,10},{10... | collective-permute-start | bytes 786440 | tf_op jit(solution)/shard_map/ppermute | solution.py:122
  844.6 30.4 %collective-permute-start.46 = (bf16[128,1024]{1,0:T(8,128)(2,1)S(1)}, bf16[128,1024]{1,0:T(8,128)(2,1)}, u32[]{:S(2)}, u32[]{:S(2)}) collective-permute-start(bf16[128,1024]{1,0:T(8,128)(2,1)S(1)} %get-tuple-element.396), channel_id=1, source_target_pairs={{0,16},{8,24},{16,0},{24,8},{1,17},{9,25},{17,1},{25,9},{2,18},{10... | collective-permute-start | bytes 786440 | tf_op jit(solution)/shard_map/ppermute | solution.py:122
  845.6 29.4 %collective-permute-start.45 = (bf16[128,1024]{1,0:T(8,128)(2,1)S(1)}, bf16[128,1024]{1,0:T(8,128)(2,1)}, u32[]{:S(2)}, u32[]{:S(2)}) collective-permute-start(bf16[128,1024]{1,0:T(8,128)(2,1)S(1)} %get-tuple-element.397), channel_id=1, source_target_pairs={{0,24},{8,0},{16,8},{24,16},{1,25},{9,1},{17,9},{25,17},{2,26},{10... | collective-permute-start | bytes 786440 | tf_op jit(solution)/shard_map/ppermute | solution.py:122
  847.9 32.0 %collective-permute-start.53 = (bf16[144,1024]{1,0:T(8,128)(2,1)S(1)}, bf16[144,1024]{1,0:T(8,128)(2,1)S(1)}, u32[]{:S(2)}, u32[]{:S(2)}) collective-permute-start(bf16[144,1024]{1,0:T(8,128)(2,1)S(1)} %get-tuple-element.385), channel_id=1, source_target_pairs={{0,1},{1,2},{2,3},{3,0},{4,5},{5,6},{6,7},{7,4},{8,9},{9,10},{10,1... | collective-permute-start | bytes 884744 | tf_op jit(solution)/shard_map/ppermute | solution.py:122
  848.9 31.5 %collective-permute-start.52 = (bf16[144,1024]{1,0:T(8,128)(2,1)S(1)}, bf16[144,1024]{1,0:T(8,128)(2,1)S(1)}, u32[]{:S(2)}, u32[]{:S(2)}) collective-permute-start(bf16[144,1024]{1,0:T(8,128)(2,1)S(1)} %get-tuple-element.386), channel_id=1, source_target_pairs={{0,2},{1,3},{2,0},{3,1},{4,6},{5,7},{6,4},{7,5},{8,10},{9,11},{10,... | collective-permute-start | bytes 884744 | tf_op jit(solution)/shard_map/ppermute | solution.py:122
  877.9 16.5 %collective-permute-start.49 = (bf16[2,32,1024]{2,1,0:T(8,128)(2,1)S(1)}, bf16[2,32,1024]{2,1,0:T(8,128)(2,1)S(1)}, u32[]{:S(2)}, u32[]{:S(2)}) collective-permute-start(bf16[2,32,1024]{2,1,0:T(8,128)(2,1)S(1)} %get-tuple-element.438), channel_id=1, source_target_pairs={{0,2},{1,3},{2,0},{3,1},{4,6},{5,7},{6,4},{7,5},{8,10},{9,11},{10,... | collective-permute-start | bytes 393224 | tf_op jit(solution)/shard_map/ppermute | solution.py:122
  879.9 14.5 %collective-permute-start.48 = (bf16[2,32,1024]{2,1,0:T(8,128)(2,1)S(1)}, bf16[2,32,1024]{2,1,0:T(8,128)(2,1)S(1)}, u32[]{:S(2)}, u32[]{:S(2)}) collective-permute-start(bf16[2,32,1024]{2,1,0:T(8,128)(2,1)S(1)} %get-tuple-element.439), channel_id=1, source_target_pairs={{0,1},{1,2},{2,3},{3,0},{4,5},{5,6},{6,7},{7,4},{8,9},{9,10},{10,1... | collective-permute-start | bytes 393224 | tf_op jit(solution)/shard_map/ppermute | solution.py:122
  (193 other events, 2021.5 us)
Sparse Core Ops, SparseCore 0:
  11.6 131.7 all-gather.3
  145.8 47.5 all-gather.5
  221.8 89.6 all-gather.7
  477.4 63.1 reduce-scatter.2
  556.9 122.2 reduce-scatter.4

commit v9 on v8

--- a/solution.py
+++ b/solution.py
@@ -388,7 +388,7 @@
     return jnp.where(place == target, value, shares.astype(jnp.float32) * scale).astype(jnp.bfloat16)
 
 
-def grads_kernel(core_ref, target_ref, scale_ref, value_ref, shares_ref, table_ref, grads_ref):
+def grads_kernel(target_ref, scale_ref, value_ref, shares_ref, table_ref, grads_ref):
     place = lax.broadcasted_iota(jnp.int32, shares_ref.shape, 0)
     grads = logit_grads(place, target_ref[...], scale_ref[...], value_ref[...], shares_ref[...])
     grads_ref[...] = lax.dot_general(
@@ -396,24 +396,22 @@
     ).astype(jnp.bfloat16)
 
 
-def answer_grads(core, target, scale, value, shares, table, width):
+def answer_grads(half, target, scale, value, shares, table, width):
     rows, count = shares.shape
     steps = count // (2 * width)
-    row = pl.BlockSpec((1, width), lambda i, core_ref: (0, 2 * i + core_ref[0]))
+    first = half * steps
+    row = pl.BlockSpec((1, width), lambda i: (0, first + i))
     return pl.pallas_call(
         grads_kernel,
-        grid_spec=pltpu.PrefetchScalarGridSpec(
-            num_scalar_prefetch=1,
-            grid=(steps,),
-            in_specs=[
-                row,
-                row,
-                row,
-                pl.BlockSpec((rows, width), lambda i, core_ref: (0, 2 * i + core_ref[0])),
-                pl.BlockSpec((rows, D), lambda i, core_ref: (0, 0)),
-            ],
-            out_specs=pl.BlockSpec((width, D), lambda i, core_ref: (i, 0)),
-        ),
+        grid=(steps,),
+        in_specs=[
+            row,
+            row,
+            row,
+            pl.BlockSpec((rows, width), lambda i: (0, first + i)),
+            pl.BlockSpec((rows, D), lambda i: (0, 0)),
+        ],
+        out_specs=pl.BlockSpec((width, D), lambda i: (i, 0)),
         out_shape=jax.ShapeDtypeStruct((steps * width, D), jnp.bfloat16),
         compiler_params=pltpu.CompilerParams(vmem_limit_bytes=40 * 1024 * 1024),
         cost_estimate=pl.CostEstimate(
@@ -421,7 +419,7 @@
             bytes_accessed=2 * steps * width * (rows + D),
             transcendentals=0,
         ),
-    )(core.reshape(1), target, scale, value, shares, table)
+    )(target, scale, value, shares, table)
 
 
 def body(
@@ -596,48 +594,64 @@
     def wide_by_member(values):
         return jnp.pad(values, ((0, members - wides), (0, 0), (0, 0)))
 
-    moment_blocks = jnp.concatenate(
-        [
-            wide_by_member(wide_moment.astype(jnp.bfloat16)),
-            by_member(square_moment.astype(jnp.bfloat16)).reshape(members, -1, D),
-        ],
+    half_tokens = [
+        jnp.concatenate(gathered(piece, "chip"), axis=0) for piece in gathered(final_b, "vocab")
+    ]
+    response_tokens = jnp.concatenate(
+        half_tokens + [other_core(piece) for piece in half_tokens], axis=0
+    )
+    chips = groups // 2
+    chip = lax.axis_index("chip")
+    block_core = jnp.stack([core, 1 - core])[:, None, None]
+    block_member = ((member - jnp.arange(members)) % members)[None, :, None]
+    block_chip = ((chip - jnp.arange(chips)) % chips)[None, None, :]
+    block_device = ((block_chip * 2 + block_core) * members + block_member).reshape(-1)
+    device_block = jnp.sum(
+        jnp.where(
+            block_device[None, :] == jnp.arange(devices)[:, None], jnp.arange(devices)[None, :], 0
+        ),
         axis=1,
     )
-    final_b, moment_blocks = lax.optimization_barrier((final_b, moment_blocks))
-    response_tokens = lax.all_gather(final_b, ALL, axis=0, tiled=True)
-    response_tokens, moment_jobs = lax.optimization_barrier(
-        (response_tokens, handed_out(moment_blocks, "vocab"))
-    )
-    wide_moment_job = jnp.stack([piece[:wide_rows] for piece in moment_jobs])
-    square_moment_job = placed_before([piece[wide_rows:] for piece in moment_jobs], "vocab")
-    square_moment_job = square_moment_job.reshape(members, per_member, square_rows, D)
-    square_moment_job = square_moment_job.transpose(1, 0, 2, 3).reshape(per_member, group_rows, D)
-    local_target = jnp.where(targets // block_rows == device, targets % block_rows, -1)[None, :]
+    wide_moment_blocks, response_tokens = lax.optimization_barrier(
+        (wide_by_member(wide_moment.astype(jnp.bfloat16)), response_tokens)
+    )
+    wide_moment_job = handed_out(wide_moment_blocks, "vocab")
+    local_target = jnp.where(targets // block_rows == device, targets % block_rows, -1)
+    local_target = local_target.reshape(devices, RESP)[block_device].reshape(1, -1)
     shares, own_stats = answer_shares(local_target, response_tokens, table_b)
-    stats = own_stats[:3].reshape(3, devices, RESP).transpose(1, 0, 2)
+    own_stats, wide_moment_job = lax.optimization_barrier((own_stats, wide_moment_job))
+    wide_moment_job = jnp.stack(wide_moment_job)
+    stats = own_stats[:3].reshape(3, devices, RESP).transpose(1, 0, 2)[device_block]
     stats = exchanged(stats)
     top = jnp.max(stats[:, 0], axis=0)
     exp_total = jnp.sum(stats[:, 1] * jnp.exp(stats[:, 0] - top[None, :]), axis=0)
     own_log_total = top + jnp.log(exp_total)
     own_logp = jnp.sum(jnp.sum(stats[:, 2], axis=0) - own_log_total)
     joined = spread(jnp.concatenate([own_log_total, own_logp[None]]))
-    log_total = joined[:, :RESP].reshape(1, -1)
+    log_total = joined[:, :RESP][block_device].reshape(1, -1)
     margin = jnp.sum(pair_rows * joined[:, RESP][None, :], axis=1, keepdims=True)
     pair_loss = 0.5 * jnp.sum(jax.nn.softplus(-margin))
     grad_logp = chosen_sign * jax.nn.sigmoid(-margin) * (-pref_beta / RESP)
-    row_weight = jnp.broadcast_to(grad_logp, (devices, RESP)).reshape(1, -1)
+    row_weight = jnp.broadcast_to(grad_logp[block_device], (devices, RESP)).reshape(1, -1)
     share_scale = -row_weight * jnp.exp(own_stats[0:1] - log_total)
     target_value = row_weight * (1.0 - jnp.exp(own_stats[2:3] - log_total))
     given, kept = (
         answer_grads(
-            which, local_target, share_scale, target_value, shares, table_b, members * RESP
+            half, local_target, share_scale, target_value, shares, table_b, members * RESP
         )
-        for which in (1 - core, core)
+        for half in (1, 0)
     )
     grad_answer_pair = (kept.astype(jnp.float32) + other_core(given).astype(jnp.float32)).astype(
         jnp.bfloat16
     )
-    grad_answer_group = chip_sum(grad_answer_pair.reshape(groups // 2, members * RESP, D))
+    grad_answer_pair, square_moment_blocks = lax.optimization_barrier(
+        (grad_answer_pair, by_member(square_moment.astype(jnp.bfloat16)))
+    )
+    square_moment_job = handed_out(square_moment_blocks, "vocab")
+    grad_answer_pair = grad_answer_pair.reshape(members, chips, RESP, D)
+    grad_answer_group = added(
+        handed_back([grad_answer_pair[:, place] for place in range(chips)], "chip")
+    )
     grad_table = jnp.dot(
         logit_grads(
             jnp.arange(block_rows)[:, None], local_target, share_scale, target_value, shares
@@ -645,10 +659,12 @@
         response_tokens,
         preferred_element_type=jnp.float32,
     )
-    grad_answer_group, grad_table = lax.optimization_barrier(
-        (grad_answer_group.astype(jnp.bfloat16), grad_table)
-    )
-    grad_final = member_scatter(grad_answer_group.reshape(members, RESP, D))
+    grad_answer_group, grad_table, square_moment_job = lax.optimization_barrier(
+        (grad_answer_group.astype(jnp.bfloat16), grad_table, square_moment_job)
+    )
+    square_moment_job = placed_before(square_moment_job, "vocab")
+    square_moment_job = square_moment_job.transpose(1, 0, 2, 3).reshape(per_member, group_rows, D)
+    grad_final = member_return(list(grad_answer_group))
     grad_hidden3, grad_gain3 = norm_back(hidden3, gains[3], grad_final)
     grad_ffn_out = member_gather(grad_hidden3.astype(jnp.bfloat16))
     grad_inner = dense(grad_ffn_out, wide_b[2])

time: 914 us -> 890 us (0.974)
  waiting for transfers between devices: 414 us -> 331 us
  starting transfers between devices: 91.1 us -> 135 us
  other arithmetic: 99.9 us -> 111 us
    all_gather x1 -> x0, waiting for transfers between devices: 50.6 us -> none  [body(): response_tokens = lax.all_gather(final_b, ALL, axis=0, tiled=True)]
    ppermute x48 -> x66, starting transfers between devices: 59.3 us -> 103 us  [turned(): lax.ppermute(values, axis, [(i, (i + step) % count) for i in range(count)])]
    ppermute x48 -> x66, waiting for transfers between devices: 221 us -> 206 us  [turned(): lax.ppermute(values, axis, [(i, (i + step) % count) for i in range(count)])]
    unnamed x355 -> x393, local copies, waits for them, and re-layouts: 22.2 us -> 35.4 us
    add x0 -> x2, other arithmetic: none -> 12.4 us  [the longest x1 12.3 us: body(): grad_table + put(asked, returned_rows)]
    reduce_scatter x1, waiting for transfers between devices: 14.4 us -> 4.23 us  [body(): lax.psum_scatter(grad_square, DP, scatter_dimension=1, tiled=True)]
    all_gather x1, waiting for transfers between devices: 17 us -> 7.76 us  [body(): lax.all_gather(wide_master.astype(jnp.bfloat16), DP, axis=1, tiled=True)]
  transfers between devices with their start and end apart: 66 -> 87, of which waited for: 35 -> 37; matrix products, arithmetic and copies ran while one was open for 25% -> 27% of each run, Pallas kernels for 4% -> 7%
where the time goes in v9:
time: 890 us; the launch traced here: 882 us
  waiting for transfers between devices  331 us (37%)
  starting transfers between devices  135 us (15%)
  matrix products  135 us (15%)
  other arithmetic  111 us (12%)
  local copies, waits for them, and re-layouts  69.1 us (8%)
  Pallas kernels  68.9 us (8%)
  between operations  30.8 us (3%)
    ppermute x66, waiting for transfers between devices, turned(): lax.ppermute(values, axis, [(i, (i + step) % count) for i in range(count)])  206 us
    ppermute x66, starting transfers between devices, turned(): lax.ppermute(values, axis, [(i, (i + step) % count) for i in range(count)])  103 us
    all_to_all x5, waiting for transfers between devices, exchanged(): return lax.all_to_all(rows, ALL, 0, 0, tiled=True)  60 us
    all_gather x1, waiting for transfers between devices, body(): lax.all_gather(square_master.astype(jnp.bfloat16), ALL, axis=1, tiled=True)  38.6 us
    dot_general x14, matrix products, outer(): lax.dot_general(grads, inputs, (((0,), (0,)), ((), ())), preferred_elemen...  35.8 us
    unnamed x393, local copies, waits for them, and re-layouts  35.4 us
    dot_general x9, matrix products, back_dense(): return jnp.dot(grads, weight, preferred_element_type=jnp.float32)  32.2 us
    dot_general x10, matrix products, dense(): lax.dot_general(inputs, weight, (((1,), (1,)), ((), ())), preferred_eleme...  28.3 us
  transfers between devices with their start and end apart: 87, of which 37 were waited for; matrix products, arithmetic and copies ran while one was open for 27% of the time, Pallas kernels for 7%

profile of v9, /device:TPU:0, one launch (start us, length us, event | category | flops | bytes accessed | tf_op | source)
XLA Modules:
  0.0 881.7 jit_solution(3061324415165207944)
XLA Ops:
  19.5 7.3 all-to-all-start.4
  26.8 6.1 convert_element_type.420.table_ref
  35.3 6.8 fusion.67
  42.2 4.3 all-to-all-start.5
  55.6 45.7 %all-to-all-done.5 = bf16[32,24,1024]{2,1,0:T(8,128)(2,1)} async-done(((bf16[32,24,1024]{2,1,0:T(8,128)(2,1)}), bf16[32,24,1024]{2,1,0:T(8,128)(2,1)}, u32[]{:S(2)}, u32[]{:S(2)}) %all-to-all-start.5) | async-done | bytes 1572896 | tf_op jit(solution)/shard_map/all_to_all | solution.py:112
  104.7 38.6 %all-gather.3.cloned.1.call-done = bf16[7,1024,1024]{2,1,0:T(8,128)(2,1)} async-done(((bf16[7,32,1024]{2,1,0:T(8,128)(2,1)}), bf16[7,1024,1024]{2,1,0:T(8,128)(2,1)}) %all-gather.3.cloned.1.call-update) | async-done | bytes 14680080 | tf_op jit(solution)/shard_map/all_gather | solution.py:480
  146.4 5.7 fusion.171
  173.8 11.8 %collective-permute-start = (bf16[96,1024]{1,0:T(8,128)(2,1)S(1)}, bf16[96,1024]{1,0:T(8,128)(2,1)S(1)}, u32[]{:S(2)}, u32[]{:S(2)}) collective-permute-start(bf16[96,1024]{1,0:T(8,128)(2,1)S(1)} %multiply_convert_fusion.9), channel_id=1, source_target_pairs={{0,1},{1,2},{2,3},{3,0},{4,5},{5,6},{6,7},{7,4},{8,9},{9,10},{10,1... | collective-permute-start | bytes 589832 | tf_op jit(solution)/shard_map/ppermute | solution.py:122
  185.7 7.8 all-gather.5.cloned.1.call-done
  207.6 4.2 collective-permute-done.5
  211.8 7.8 collective-permute-done.4
  225.4 4.7 collective-permute-start.9
  277.7 3.8 collective-permute-start.26
  287.2 23.1 %shard_map.313 = (bf16[2048,3072]{1,0:T(8,128)(2,1)}, f32[8,3072]{1,0:T(8,128)S(1)}) custom-call(s32[1,3072]{1,0:T(1,128)S(1)} %reshape.940.target_ref, bf16[3072,1024]{1,0:T(8,128)(2,1)S(1)} %copy-done, bf16[2048,1024]{1,0:T(8,128)(2,1)S(1)} %copy-done.34), custom_call_target="tpu_custom_call" | custom-call | flops 12884901888 | bytes 18874368 | tf_op jit(solution)/shard_map/pallas_call | solution.py:361
  314.3 7.5 all-to-all-done.6
  326.4 7.1 all-to-all-done.7
  336.7 10.4 %shard_map.315 = bf16[1536,1024]{1,0:T(8,128)(2,1)S(1)} custom-call(s32[1,3072]{1,0:T(1,128)S(1)} %reshape.940.target_ref, f32[1,3072]{1,0:T(1,128)S(1)} %get-tuple-element.466.scale_ref, f32[1,3072]{1,0:T(1,128)S(1)} %get-tuple-element.465.value_ref, bf16[2048,3072]{1,0:T(8,128)(2,1)} %get-tuple-element.259.shares_ref, bf16[2048,1024]{1,0:T(8,128)(2,1)} %get-tuple-element.705), custom_call_target="tpu_custom_call" | custom-call | flops 6442450944 | bytes 9437184 | tf_op jit(solution)/shard_map/pallas_call | solution.py:404
  348.9 10.3 %shard_map.314 = bf16[1536,1024]{1,0:T(8,128)(2,1)S(1)} custom-call(s32[1,3072]{1,0:T(1,128)S(1)} %reshape.940.target_ref, f32[1,3072]{1,0:T(1,128)S(1)} %get-tuple-element.466.scale_ref, f32[1,3072]{1,0:T(1,128)S(1)} %get-tuple-element.465.value_ref, bf16[2048,3072]{1,0:T(8,128)(2,1)} %get-tuple-element.259.shares_ref, bf16[2048,1024]{1,0:T(8,128)(2,1)} %get-tuple-element.705), custom_call_target="tpu_custom_call" | custom-call | flops 6442450944 | bytes 9437184 | tf_op jit(solution)/shard_map/pallas_call | solution.py:404
  366.8 17.5 %fusion.12 = f32[2048,1024]{1,0:T(8,128)} fusion(bf16[3072,1024]{1,0:T(8,128)(2,1)} %constant_dynamic-update-slice_fusion.answers_ref, bf16[2048,3072]{1,0:T(8,128)(2,1)S(1)} %bitcast.547, f32[3072]{0:T(1024)S(1)} %bitcast.460, f32[3072]{0:T(1024)S(1)} %bitcast.459, s32[3072]{0:T(1024)S(1)} %eq.420), kind=kOutput, calls=%fused_computation.35 | convolution fusion | flops 12910067712 | bytes 27299840 | tf_op jit(solution)/shard_map/dot_general | solution.py:655
  388.9 11.2 %collective-permute-done.30 = bf16[4,96,1024]{2,1,0:T(8,128)(2,1)S(1)} collective-permute-done((bf16[4,96,1024]{2,1,0:T(8,128)(2,1)S(1)}, bf16[4,96,1024]{2,1,0:T(8,128)(2,1)S(1)}, u32[]{:S(2)}, u32[]{:S(2)}) %collective-permute-start.30) | collective-permute-done | bytes 786464 | tf_op jit(solution)/shard_map/ppermute | solution.py:122
  404.8 5.9 collective-permute-done.37
  410.7 7.0 collective-permute-done.36
  427.7 13.0 %collective-permute-done.39 = bf16[96,1024]{1,0:T(8,128)(2,1)S(1)} collective-permute-done((bf16[96,1024]{1,0:T(8,128)(2,1)S(1)}, bf16[96,1024]{1,0:T(8,128)(2,1)S(1)}, u32[]{:S(2)}, u32[]{:S(2)}) %collective-permute-start.39) | collective-permute-done | bytes 196640 | tf_op jit(solution)/shard_map/ppermute | solution.py:122
  463.6 5.1 collective-permute-done.43
  468.8 6.1 collective-permute-done.42
  502.3 7.5 multiply_reduce_fusion.1
  537.8 5.7 multiply_reduce_fusion.5
  549.0 6.4 all-to-all-start.8
  557.7 5.1 all-to-all-done.8
  576.1 22.6 %collective-permute-done.49 = bf16[144,1024]{1,0:T(8,128)(2,1)S(1)} collective-permute-done((bf16[144,1024]{1,0:T(8,128)(2,1)S(1)}, bf16[144,1024]{1,0:T(8,128)(2,1)S(1)}, u32[]{:S(2)}, u32[]{:S(2)}) %collective-permute-start.49) | collective-permute-done | bytes 294944 | tf_op jit(solution)/shard_map/ppermute | solution.py:122
  598.8 30.1 %collective-permute-done.48 = bf16[144,1024]{1,0:T(8,128)(2,1)S(1)} collective-permute-done((bf16[144,1024]{1,0:T(8,128)(2,1)S(1)}, bf16[144,1024]{1,0:T(8,128)(2,1)S(1)}, u32[]{:S(2)}, u32[]{:S(2)}) %collective-permute-start.48) | collective-permute-done | bytes 294944 | tf_op jit(solution)/shard_map/ppermute | solution.py:122
  629.0 7.8 fusion.17
  636.8 12.3 %add.1000 = f32[2048,1024]{1,0:T(8,128)} add(f32[2048,1024]{1,0:T(8,128)} %fusion.12, f32[2048,1024]{1,0:T(8,128)} %fusion.17) | non-fusion elementwise | flops 2097152 | bytes 25165824 | tf_op jit(solution)/shard_map/add | solution.py:783
  649.1 4.2 reduce-scatter.5.cloned.1.call-done
  662.2 6.1 multiply_reduce_fusion
  668.3 5.2 collective-permute-done.46
  673.5 32.6 %collective-permute-done.45 = bf16[2,128,1024]{2,1,0:T(8,128)(2,1)} collective-permute-done((bf16[2,128,1024]{2,1,0:T(8,128)(2,1)}, bf16[2,128,1024]{2,1,0:T(8,128)(2,1)}, u32[]{:S(2)}, u32[]{:S(2)}) %collective-permute-start.45) | collective-permute-done | bytes 524320 | tf_op jit(solution)/shard_map/ppermute | solution.py:122
  712.8 4.0 all-to-all-start.10
  717.4 6.4 all-to-all-done.10
  745.7 4.4 collective-permute-done.54
  750.3 5.0 collective-permute-done.60
  755.3 6.0 collective-permute-done.58
  771.3 4.9 collective-permute-done.62
  782.3 25.1 %shard_map.316 = bf16[1024,1024]{1,0:T(8,128)(2,1)S(1)} custom-call(s32[1]{0:T(128)} %bitcast.17.core_ref, bf16[512,1024]{1,0:T(8,128)(2,1)S(1)} %bitcast.458, bf16[512,1024]{1,0:T(8,128)(2,1)S(1)} %collective-permute-done.64.second_ref, f32[1024,1024]{1,0:T(8,128)S(1)} %fusion.173.square_ref), custom_call_target="tpu_custom_call" | custom-call | flops 19327352832 | bytes 6291456 | tf_op jit(solution)/shard_map/pallas_call | solution.py:306
  807.6 3.9 convolution_convert_fusion.4
  828.4 22.7 %add_multiply_fusion = (f32[2048,1024]{1,0:T(8,128)}, f32[2048,1024]{1,0:T(8,128)}, f32[2048,1024]{1,0:T(8,128)}) fusion(f32[2048,1024]{1,0:T(8,128)} %param.25, f32[]{:T(128)S(6)} %sub.276, f32[]{:T(128)S(6)} %sub.275, f32[2048,1024]{1,0:T(8,128)} %get-tuple-element.283, f32[]{:T(128)S(6)} %min.3, f32[2048,1024]{1,0:T(8,128)} %param.27, f32[2048,1024]{1,0:T(8,128)} %param.26), kind=kLoop, calls=%fused_computation.41 | loop fusion | flops 31457280 | bytes 58720268 | tf_op jit(solution)/shard_map/mul | solution.py:100
  856.6 4.4 collective-permute-done.73
  864.2 6.4 collective-permute-done.71
  (823 shorter events, 332.9 us)
Async XLA Ops:
  7.2 136.2 %all-gather.3.cloned.1.call-start = ((), (), s32[]{:S(2)}) async-start(), calls=%async_computation.13 | async-start | bytes 15138816 | tf_op jit(solution)/shard_map/all_gather | solution.py:480
  19.5 15.1 %all-to-all-start.4 = ((f32[32,1,349]{2,1,0:T(1,128)}), f32[32,1,349]{2,1,0:T(1,128)S(1)}, u32[]{:S(2)}, u32[]{:S(2)}) async-start(f32[32,1,349]{2,1,0:T(1,128)} %all_to_all.79), calls=%async_computation.4 | async-start | bytes 98304 | tf_op jit(solution)/shard_map/all_to_all | solution.py:112
  42.2 59.1 %all-to-all-start.5 = ((bf16[32,24,1024]{2,1,0:T(8,128)(2,1)}), bf16[32,24,1024]{2,1,0:T(8,128)(2,1)}, u32[]{:S(2)}, u32[]{:S(2)}) async-start(bf16[32,24,1024]{2,1,0:T(8,128)(2,1)} %bitcast.20), calls=%async_computation.5 | async-start | bytes 3145728 | tf_op jit(solution)/shard_map/all_to_all | solution.py:112
  46.5 147.0 %all-gather.5.cloned.1.call-start = ((), (), s32[]{:S(2)}) async-start(), calls=%async_computation.14 | async-start | bytes 7962624 | tf_op jit(solution)/shard_map/all_gather | solution.py:481
  171.8 21.6 %collective-permute-start.2 = (bf16[96,1024]{1,0:T(8,128)(2,1)S(1)}, bf16[96,1024]{1,0:T(8,128)(2,1)S(1)}, u32[]{:S(2)}, u32[]{:S(2)}) collective-permute-start(bf16[96,1024]{1,0:T(8,128)(2,1)S(1)} %multiply_convert_fusion.9), channel_id=1, source_target_pairs={{0,3},{1,0},{2,1},{3,2},{4,7},{5,4},{6,5},{7,6},{8,11},{9,8},{10,9... | collective-permute-start | bytes 589832 | tf_op jit(solution)/shard_map/ppermute | solution.py:122
  172.9 20.6 %collective-permute-start.1 = (bf16[96,1024]{1,0:T(8,128)(2,1)S(1)}, bf16[96,1024]{1,0:T(8,128)(2,1)S(1)}, u32[]{:S(2)}, u32[]{:S(2)}) collective-permute-start(bf16[96,1024]{1,0:T(8,128)(2,1)S(1)} %multiply_convert_fusion.9), channel_id=1, source_target_pairs={{0,2},{1,3},{2,0},{3,1},{4,6},{5,7},{6,4},{7,5},{8,10},{9,11},{10,... | collective-permute-start | bytes 589832 | tf_op jit(solution)/shard_map/ppermute | solution.py:122
  173.8 19.6 %collective-permute-start = (bf16[96,1024]{1,0:T(8,128)(2,1)S(1)}, bf16[96,1024]{1,0:T(8,128)(2,1)S(1)}, u32[]{:S(2)}, u32[]{:S(2)}) collective-permute-start(bf16[96,1024]{1,0:T(8,128)(2,1)S(1)} %multiply_convert_fusion.9), channel_id=1, source_target_pairs={{0,1},{1,2},{2,3},{3,0},{4,5},{5,6},{6,7},{7,4},{8,9},{9,10},{10,1... | collective-permute-start | bytes 589832 | tf_op jit(solution)/shard_map/ppermute | solution.py:122
  203.6 15.9 %collective-permute-start.4 = (bf16[96,1024]{1,0:T(8,128)(2,1)S(1)}, bf16[96,1024]{1,0:T(8,128)(2,1)S(1)}, u32[]{:S(2)}, u32[]{:S(2)}) collective-permute-start(bf16[96,1024]{1,0:T(8,128)(2,1)S(1)} %get-tuple-element.433), channel_id=1, source_target_pairs={{0,2},{1,3},{2,0},{3,1},{4,6},{5,7},{6,4},{7,5},{8,10},{9,11},{10,... | collective-permute-start | bytes 589832 | tf_op jit(solution)/shard_map/ppermute | solution.py:122
  222.8 14.9 %collective-permute-start.7 = (bf16[96,1024]{1,0:T(8,128)(2,1)S(1)}, bf16[96,1024]{1,0:T(8,128)(2,1)S(1)}, u32[]{:S(2)}, u32[]{:S(2)}) collective-permute-start(bf16[96,1024]{1,0:T(8,128)(2,1)S(1)} %get-tuple-element.372), channel_id=1, source_target_pairs={{0,16},{8,24},{16,0},{24,8},{1,17},{9,25},{17,1},{25,9},{2,18},{10... | collective-permute-start | bytes 589832 | tf_op jit(solution)/shard_map/ppermute | solution.py:122
  223.3 15.8 %collective-permute-start.8 = (bf16[96,1024]{1,0:T(8,128)(2,1)S(1)}, bf16[96,1024]{1,0:T(8,128)(2,1)S(1)}, u32[]{:S(2)}, u32[]{:S(2)}) collective-permute-start(bf16[96,1024]{1,0:T(8,128)(2,1)S(1)} %get-tuple-element.372), channel_id=1, source_target_pairs={{0,24},{8,0},{16,8},{24,16},{1,25},{9,1},{17,9},{25,17},{2,26},{10... | collective-permute-start | bytes 589832 | tf_op jit(solution)/shard_map/ppermute | solution.py:122
  256.2 15.0 %collective-permute-start.21 = (bf16[384,1024]{1,0:T(8,128)(2,1)S(1)}, bf16[384,1024]{1,0:T(8,128)(2,1)S(1)}, u32[]{:S(2)}, u32[]{:S(2)}) collective-permute-start(bf16[384,1024]{1,0:T(8,128)(2,1)S(1)} %pad_maximum_fusion.9), channel_id=1, source_target_pairs={{0,4},{4,0},{1,5},{5,1},{2,6},{6,2},{3,7},{7,3},{8,12},{12,8},{9,1... | collective-permute-start | bytes 2359304 | tf_op jit(solution)/shard_map/ppermute | solution.py:162
  256.2 15.9 %collective-permute-start.22 = (bf16[384,1024]{1,0:T(8,128)(2,1)S(1)}, bf16[384,1024]{1,0:T(8,128)(2,1)S(1)}, u32[]{:S(2)}, u32[]{:S(2)}) collective-permute-start(bf16[384,1024]{1,0:T(8,128)(2,1)S(1)} %pad_maximum_fusion.10), channel_id=1, source_target_pairs={{0,4},{4,0},{1,5},{5,1},{2,6},{6,2},{3,7},{7,3},{8,12},{12,8},{9,1... | collective-permute-start | bytes 2359304 | tf_op jit(solution)/shard_map/ppermute | solution.py:162
  275.7 34.5 %collective-permute-start.25 = (bf16[144,1024]{1,0:T(8,128)(2,1)S(1)}, bf16[144,1024]{1,0:T(8,128)(2,1)}, u32[]{:S(2)}, u32[]{:S(2)}) collective-permute-start(bf16[144,1024]{1,0:T(8,128)(2,1)S(1)} %get-tuple-element.402), channel_id=1, source_target_pairs={{0,1},{1,2},{2,3},{3,0},{4,5},{5,6},{6,7},{7,4},{8,9},{9,10},{10,1... | collective-permute-start | bytes 884744 | tf_op jit(solution)/shard_map/ppermute | solution.py:122
  277.7 32.6 %collective-permute-start.26 = (bf16[144,1024]{1,0:T(8,128)(2,1)S(1)}, bf16[144,1024]{1,0:T(8,128)(2,1)}, u32[]{:S(2)}, u32[]{:S(2)}) collective-permute-start(bf16[144,1024]{1,0:T(8,128)(2,1)S(1)} %get-tuple-element.401), channel_id=1, source_target_pairs={{0,2},{1,3},{2,0},{3,1},{4,6},{5,7},{6,4},{7,5},{8,10},{9,11},{10,... | collective-permute-start | bytes 884744 | tf_op jit(solution)/shard_map/ppermute | solution.py:122
  281.5 28.8 %collective-permute-start.27 = (bf16[144,1024]{1,0:T(8,128)(2,1)S(1)}, bf16[144,1024]{1,0:T(8,128)(2,1)}, u32[]{:S(2)}, u32[]{:S(2)}) collective-permute-start(bf16[144,1024]{1,0:T(8,128)(2,1)S(1)} %get-tuple-element.400), channel_id=1, source_target_pairs={{0,3},{1,0},{2,1},{3,2},{4,7},{5,4},{6,5},{7,6},{8,11},{9,8},{10,9... | collective-permute-start | bytes 884744 | tf_op jit(solution)/shard_map/ppermute | solution.py:122
  326.3 204.2 %reduce-scatter.3.cloned.1.call-start = ((), (), s32[]{:S(2)}) async-start(), calls=%async_computation.15 | async-start | bytes 7962624 | tf_op jit(solution)/shard_map/reduce_scatter | solution.py:752
  363.0 23.0 %collective-permute-start.31 = (bf16[4,96,1024]{2,1,0:T(8,128)(2,1)S(1)}, bf16[4,96,1024]{2,1,0:T(8,128)(2,1)S(1)}, u32[]{:S(2)}, u32[]{:S(2)}) collective-permute-start(bf16[4,96,1024]{2,1,0:T(8,128)(2,1)S(1)} %get-tuple-element.386), channel_id=1, source_target_pairs={{0,8},{8,16},{16,24},{24,0},{1,9},{9,17},{17,25},{25,1},{2,10},{10... | collective-permute-start | bytes 2359304 | tf_op jit(solution)/shard_map/ppermute | solution.py:122
  363.6 36.5 %collective-permute-start.30 = (bf16[4,96,1024]{2,1,0:T(8,128)(2,1)S(1)}, bf16[4,96,1024]{2,1,0:T(8,128)(2,1)S(1)}, u32[]{:S(2)}, u32[]{:S(2)}) collective-permute-start(bf16[4,96,1024]{2,1,0:T(8,128)(2,1)S(1)} %get-tuple-element.385), channel_id=1, source_target_pairs={{0,16},{8,24},{16,0},{24,8},{1,17},{9,25},{17,1},{25,9},{2,18},{10... | collective-permute-start | bytes 2359304 | tf_op jit(solution)/shard_map/ppermute | solution.py:122
  364.2 36.0 %collective-permute-start.29 = (bf16[4,96,1024]{2,1,0:T(8,128)(2,1)S(1)}, bf16[4,96,1024]{2,1,0:T(8,128)(2,1)S(1)}, u32[]{:S(2)}, u32[]{:S(2)}) collective-permute-start(bf16[4,96,1024]{2,1,0:T(8,128)(2,1)S(1)} %get-tuple-element.384), channel_id=1, source_target_pairs={{0,24},{8,0},{16,8},{24,16},{1,25},{9,1},{17,9},{25,17},{2,26},{10... | collective-permute-start | bytes 2359304 | tf_op jit(solution)/shard_map/ppermute | solution.py:122
  385.0 15.8 %collective-permute-start.32 = (bf16[2,32,1024]{2,1,0:T(8,128)(2,1)S(1)}, bf16[2,32,1024]{2,1,0:T(8,128)(2,1)S(1)}, u32[]{:S(2)}, u32[]{:S(2)}) collective-permute-start(bf16[2,32,1024]{2,1,0:T(8,128)(2,1)S(1)} %get-tuple-element.463), channel_id=1, source_target_pairs={{0,1},{1,2},{2,3},{3,0},{4,5},{5,6},{6,7},{7,4},{8,9},{9,10},{10,1... | collective-permute-start | bytes 393224 | tf_op jit(solution)/shard_map/ppermute | solution.py:122
  385.5 15.3 %collective-permute-start.33 = (bf16[2,32,1024]{2,1,0:T(8,128)(2,1)S(1)}, bf16[2,32,1024]{2,1,0:T(8,128)(2,1)S(1)}, u32[]{:S(2)}, u32[]{:S(2)}) collective-permute-start(bf16[2,32,1024]{2,1,0:T(8,128)(2,1)S(1)} %get-tuple-element.462), channel_id=1, source_target_pairs={{0,2},{1,3},{2,0},{3,1},{4,6},{5,7},{6,4},{7,5},{8,10},{9,11},{10,... | collective-permute-start | bytes 393224 | tf_op jit(solution)/shard_map/ppermute | solution.py:122
  386.0 14.8 %collective-permute-start.34 = (bf16[2,32,1024]{2,1,0:T(8,128)(2,1)S(1)}, bf16[2,32,1024]{2,1,0:T(8,128)(2,1)S(1)}, u32[]{:S(2)}, u32[]{:S(2)}) collective-permute-start(bf16[2,32,1024]{2,1,0:T(8,128)(2,1)S(1)} %get-tuple-element.461), channel_id=1, source_target_pairs={{0,3},{1,0},{2,1},{3,2},{4,7},{5,4},{6,5},{7,6},{8,11},{9,8},{10,9... | collective-permute-start | bytes 393224 | tf_op jit(solution)/shard_map/ppermute | solution.py:122
  401.4 16.2 %collective-permute-start.36 = (bf16[96,1024]{1,0:T(8,128)(2,1)S(1)}, bf16[96,1024]{1,0:T(8,128)(2,1)S(1)}, u32[]{:S(2)}, u32[]{:S(2)}) collective-permute-start(bf16[96,1024]{1,0:T(8,128)(2,1)S(1)} %get-tuple-element.430), channel_id=1, source_target_pairs={{0,2},{1,3},{2,0},{3,1},{4,6},{5,7},{6,4},{7,5},{8,10},{9,11},{10,... | collective-permute-start | bytes 589832 | tf_op jit(solution)/shard_map/ppermute | solution.py:122
  402.0 15.7 %collective-permute-start.35 = (bf16[96,1024]{1,0:T(8,128)(2,1)S(1)}, bf16[96,1024]{1,0:T(8,128)(2,1)S(1)}, u32[]{:S(2)}, u32[]{:S(2)}) collective-permute-start(bf16[96,1024]{1,0:T(8,128)(2,1)S(1)} %get-tuple-element.428), channel_id=1, source_target_pairs={{0,3},{1,0},{2,1},{3,2},{4,7},{5,4},{6,5},{7,6},{8,11},{9,8},{10,9... | collective-permute-start | bytes 589832 | tf_op jit(solution)/shard_map/ppermute | solution.py:122
  422.3 18.4 %collective-permute-start.39 = (bf16[96,1024]{1,0:T(8,128)(2,1)S(1)}, bf16[96,1024]{1,0:T(8,128)(2,1)S(1)}, u32[]{:S(2)}, u32[]{:S(2)}) collective-permute-start(bf16[96,1024]{1,0:T(8,128)(2,1)S(1)} %fusion.153), channel_id=1, source_target_pairs={{0,2},{1,3},{2,0},{3,1},{4,6},{5,7},{6,4},{7,5},{8,10},{9,11},{10,... | collective-permute-start | bytes 589832 | tf_op jit(solution)/shard_map/ppermute | solution.py:122
  424.1 16.7 %collective-permute-start.38 = (bf16[96,1024]{1,0:T(8,128)(2,1)S(1)}, bf16[96,1024]{1,0:T(8,128)(2,1)S(1)}, u32[]{:S(2)}, u32[]{:S(2)}) collective-permute-start(bf16[96,1024]{1,0:T(8,128)(2,1)S(1)} %fusion.153), channel_id=1, source_target_pairs={{0,1},{1,2},{2,3},{3,0},{4,5},{5,6},{6,7},{7,4},{8,9},{9,10},{10,1... | collective-permute-start | bytes 589832 | tf_op jit(solution)/shard_map/ppermute | solution.py:122
  452.0 201.4 %reduce-scatter.5.cloned.1.call-start = ((), (), s32[]{:S(2)}) async-start(), calls=%async_computation.16 | async-start | bytes 16515072 | tf_op jit(solution)/shard_map/reduce_scatter | solution.py:757
  459.1 15.8 %collective-permute-start.42 = (bf16[96,1024]{1,0:T(8,128)(2,1)S(1)}, bf16[96,1024]{1,0:T(8,128)(2,1)S(1)}, u32[]{:S(2)}, u32[]{:S(2)}) collective-permute-start(bf16[96,1024]{1,0:T(8,128)(2,1)S(1)} %get-tuple-element.427), channel_id=1, source_target_pairs={{0,2},{1,3},{2,0},{3,1},{4,6},{5,7},{6,4},{7,5},{8,10},{9,11},{10,... | collective-permute-start | bytes 589832 | tf_op jit(solution)/shard_map/ppermute | solution.py:122
  459.9 15.1 %collective-permute-start.41 = (bf16[96,1024]{1,0:T(8,128)(2,1)S(1)}, bf16[96,1024]{1,0:T(8,128)(2,1)S(1)}, u32[]{:S(2)}, u32[]{:S(2)}) collective-permute-start(bf16[96,1024]{1,0:T(8,128)(2,1)S(1)} %get-tuple-element.425), channel_id=1, source_target_pairs={{0,3},{1,0},{2,1},{3,2},{4,7},{5,4},{6,5},{7,6},{8,11},{9,8},{10,9... | collective-permute-start | bytes 589832 | tf_op jit(solution)/shard_map/ppermute | solution.py:122
  562.8 66.2 %all-to-all-start.9 = ((bf16[32,24,1024]{2,1,0:T(8,128)(2,1)}), bf16[32,24,1024]{2,1,0:T(8,128)(2,1)}, u32[]{:S(2)}, u32[]{:S(2)}) async-start(bf16[32,24,1024]{2,1,0:T(8,128)(2,1)} %bitcast.124), calls=%async_computation.11 | async-start | bytes 3145728 | tf_op jit(solution)/shard_map/all_to_all | solution.py:112
  569.3 29.5 %collective-permute-start.49 = (bf16[144,1024]{1,0:T(8,128)(2,1)S(1)}, bf16[144,1024]{1,0:T(8,128)(2,1)S(1)}, u32[]{:S(2)}, u32[]{:S(2)}) collective-permute-start(bf16[144,1024]{1,0:T(8,128)(2,1)S(1)} %get-tuple-element.422), channel_id=1, source_target_pairs={{0,3},{1,0},{2,1},{3,2},{4,7},{5,4},{6,5},{7,6},{8,11},{9,8},{10,9... | collective-permute-start | bytes 884744 | tf_op jit(solution)/shard_map/ppermute | solution.py:122
  572.9 56.0 %collective-permute-start.48 = (bf16[144,1024]{1,0:T(8,128)(2,1)S(1)}, bf16[144,1024]{1,0:T(8,128)(2,1)S(1)}, u32[]{:S(2)}, u32[]{:S(2)}) collective-permute-start(bf16[144,1024]{1,0:T(8,128)(2,1)S(1)} %get-tuple-element.424), channel_id=1, source_target_pairs={{0,2},{1,3},{2,0},{3,1},{4,6},{5,7},{6,4},{7,5},{8,10},{9,11},{10,... | collective-permute-start | bytes 884744 | tf_op jit(solution)/shard_map/ppermute | solution.py:122
  572.9 56.0 %collective-permute-start.47 = (bf16[144,1024]{1,0:T(8,128)(2,1)S(1)}, bf16[144,1024]{1,0:T(8,128)(2,1)S(1)}, u32[]{:S(2)}, u32[]{:S(2)}) collective-permute-start(bf16[144,1024]{1,0:T(8,128)(2,1)S(1)} %get-tuple-element.423), channel_id=1, source_target_pairs={{0,1},{1,2},{2,3},{3,0},{4,5},{5,6},{6,7},{7,4},{8,9},{9,10},{10,1... | collective-permute-start | bytes 884744 | tf_op jit(solution)/shard_map/ppermute | solution.py:122
  657.5 16.0 %collective-permute-start.46 = (bf16[2,128,1024]{2,1,0:T(8,128)(2,1)}, bf16[2,128,1024]{2,1,0:T(8,128)(2,1)}, u32[]{:S(2)}, u32[]{:S(2)}) collective-permute-start(bf16[2,128,1024]{2,1,0:T(8,128)(2,1)} %get-tuple-element.388), channel_id=1, source_target_pairs={{0,3},{1,0},{2,1},{3,2},{4,7},{5,4},{6,5},{7,6},{8,11},{9,8},{10,9... | collective-permute-start | bytes 1572872 | tf_op jit(solution)/shard_map/ppermute | solution.py:122
  660.8 45.3 %collective-permute-start.45 = (bf16[2,128,1024]{2,1,0:T(8,128)(2,1)}, bf16[2,128,1024]{2,1,0:T(8,128)(2,1)}, u32[]{:S(2)}, u32[]{:S(2)}) collective-permute-start(bf16[2,128,1024]{2,1,0:T(8,128)(2,1)} %get-tuple-element.389), channel_id=1, source_target_pairs={{0,2},{1,3},{2,0},{3,1},{4,6},{5,7},{6,4},{7,5},{8,10},{9,11},{10,... | collective-permute-start | bytes 1572872 | tf_op jit(solution)/shard_map/ppermute | solution.py:122
  660.9 45.3 %collective-permute-start.44 = (bf16[2,128,1024]{2,1,0:T(8,128)(2,1)}, bf16[2,128,1024]{2,1,0:T(8,128)(2,1)}, u32[]{:S(2)}, u32[]{:S(2)}) collective-permute-start(bf16[2,128,1024]{2,1,0:T(8,128)(2,1)} %get-tuple-element.387), channel_id=1, source_target_pairs={{0,1},{1,2},{2,3},{3,0},{4,5},{5,6},{6,7},{7,4},{8,9},{9,10},{10,1... | collective-permute-start | bytes 1572872 | tf_op jit(solution)/shard_map/ppermute | solution.py:122
  740.1 15.2 %collective-permute-start.60 = (bf16[128,1024]{1,0:T(8,128)(2,1)S(1)}, bf16[128,1024]{1,0:T(8,128)(2,1)S(1)}, u32[]{:S(2)}, u32[]{:S(2)}) collective-permute-start(bf16[128,1024]{1,0:T(8,128)(2,1)S(1)} %get-tuple-element.417), channel_id=1, source_target_pairs={{0,24},{8,0},{16,8},{24,16},{1,25},{9,1},{17,9},{25,17},{2,26},{10... | collective-permute-start | bytes 786440 | tf_op jit(solution)/shard_map/ppermute | solution.py:122
  744.9 16.4 %collective-permute-start.58 = (bf16[128,1024]{1,0:T(8,128)(2,1)S(1)}, bf16[128,1024]{1,0:T(8,128)(2,1)S(1)}, u32[]{:S(2)}, u32[]{:S(2)}) collective-permute-start(bf16[128,1024]{1,0:T(8,128)(2,1)S(1)} %get-tuple-element.416), channel_id=1, source_target_pairs={{0,8},{8,16},{16,24},{24,0},{1,9},{9,17},{17,25},{25,1},{2,10},{10... | collective-permute-start | bytes 786440 | tf_op jit(solution)/shard_map/ppermute | solution.py:122
  750.2 29.6 %collective-permute-start.56 = (bf16[512,1024]{1,0:T(8,128)(2,1)S(1)}, bf16[512,1024]{1,0:T(8,128)(2,1)S(1)}, u32[]{:S(2)}, u32[]{:S(2)}) collective-permute-start(bf16[512,1024]{1,0:T(8,128)(2,1)S(1)} %pad_maximum_fusion.4), channel_id=1, source_target_pairs={{0,4},{4,0},{1,5},{5,1},{2,6},{6,2},{3,7},{7,3},{8,12},{12,8},{9,1... | collective-permute-start | bytes 3145736 | tf_op jit(solution)/shard_map/ppermute | solution.py:162
  766.9 48.9 %collective-permute-start.52 = (bf16[2,32,1024]{2,1,0:T(8,128)(2,1)}, bf16[2,32,1024]{2,1,0:T(8,128)(2,1)S(1)}, u32[]{:S(2)}, u32[]{:S(2)}) collective-permute-start(bf16[2,32,1024]{2,1,0:T(8,128)(2,1)} %get-tuple-element.443), channel_id=1, source_target_pairs={{0,3},{1,0},{2,1},{3,2},{4,7},{5,4},{6,5},{7,6},{8,11},{9,8},{10,9... | collective-permute-start | bytes 393224 | tf_op jit(solution)/shard_map/ppermute | solution.py:122
  770.8 45.0 %collective-permute-start.51 = (bf16[2,32,1024]{2,1,0:T(8,128)(2,1)}, bf16[2,32,1024]{2,1,0:T(8,128)(2,1)S(1)}, u32[]{:S(2)}, u32[]{:S(2)}) collective-permute-start(bf16[2,32,1024]{2,1,0:T(8,128)(2,1)} %get-tuple-element.444), channel_id=1, source_target_pairs={{0,2},{1,3},{2,0},{3,1},{4,6},{5,7},{6,4},{7,5},{8,10},{9,11},{10,... | collective-permute-start | bytes 393224 | tf_op jit(solution)/shard_map/ppermute | solution.py:122
  776.2 39.6 %collective-permute-start.50 = (bf16[2,32,1024]{2,1,0:T(8,128)(2,1)}, bf16[2,32,1024]{2,1,0:T(8,128)(2,1)S(1)}, u32[]{:S(2)}, u32[]{:S(2)}) collective-permute-start(bf16[2,32,1024]{2,1,0:T(8,128)(2,1)} %get-tuple-element.445), channel_id=1, source_target_pairs={{0,1},{1,2},{2,3},{3,0},{4,5},{5,6},{6,7},{7,4},{8,9},{9,10},{10,1... | collective-permute-start | bytes 393224 | tf_op jit(solution)/shard_map/ppermute | solution.py:122
  820.6 30.6 %collective-permute-start.69 = (bf16[128,1024]{1,0:T(8,128)(2,1)}, bf16[128,1024]{1,0:T(8,128)(2,1)S(1)}, u32[]{:S(2)}, u32[]{:S(2)}) collective-permute-start(bf16[128,1024]{1,0:T(8,128)(2,1)} %get-tuple-element.409), channel_id=1, source_target_pairs={{0,8},{8,16},{16,24},{24,0},{1,9},{9,17},{17,25},{25,1},{2,10},{10... | collective-permute-start | bytes 786440 | tf_op jit(solution)/shard_map/ppermute | solution.py:122
  820.9 30.3 %collective-permute-start.68 = (bf16[128,1024]{1,0:T(8,128)(2,1)S(1)}, bf16[128,1024]{1,0:T(8,128)(2,1)}, u32[]{:S(2)}, u32[]{:S(2)}) collective-permute-start(bf16[128,1024]{1,0:T(8,128)(2,1)S(1)} %get-tuple-element.410), channel_id=1, source_target_pairs={{0,16},{8,24},{16,0},{24,8},{1,17},{9,25},{17,1},{25,9},{2,18},{10... | collective-permute-start | bytes 786440 | tf_op jit(solution)/shard_map/ppermute | solution.py:122
  821.9 29.4 %collective-permute-start.67 = (bf16[128,1024]{1,0:T(8,128)(2,1)S(1)}, bf16[128,1024]{1,0:T(8,128)(2,1)}, u32[]{:S(2)}, u32[]{:S(2)}) collective-permute-start(bf16[128,1024]{1,0:T(8,128)(2,1)S(1)} %get-tuple-element.411), channel_id=1, source_target_pairs={{0,24},{8,0},{16,8},{24,16},{1,25},{9,1},{17,9},{25,17},{2,26},{10... | collective-permute-start | bytes 786440 | tf_op jit(solution)/shard_map/ppermute | solution.py:122
  824.2 31.9 %collective-permute-start.75 = (bf16[144,1024]{1,0:T(8,128)(2,1)S(1)}, bf16[144,1024]{1,0:T(8,128)(2,1)S(1)}, u32[]{:S(2)}, u32[]{:S(2)}) collective-permute-start(bf16[144,1024]{1,0:T(8,128)(2,1)S(1)} %get-tuple-element.395), channel_id=1, source_target_pairs={{0,1},{1,2},{2,3},{3,0},{4,5},{5,6},{6,7},{7,4},{8,9},{9,10},{10,1... | collective-permute-start | bytes 884744 | tf_op jit(solution)/shard_map/ppermute | solution.py:122
  825.1 31.5 %collective-permute-start.74 = (bf16[144,1024]{1,0:T(8,128)(2,1)S(1)}, bf16[144,1024]{1,0:T(8,128)(2,1)S(1)}, u32[]{:S(2)}, u32[]{:S(2)}) collective-permute-start(bf16[144,1024]{1,0:T(8,128)(2,1)S(1)} %get-tuple-element.396), channel_id=1, source_target_pairs={{0,2},{1,3},{2,0},{3,1},{4,6},{5,7},{6,4},{7,5},{8,10},{9,11},{10,... | collective-permute-start | bytes 884744 | tf_op jit(solution)/shard_map/ppermute | solution.py:122
  854.1 16.5 %collective-permute-start.71 = (bf16[2,32,1024]{2,1,0:T(8,128)(2,1)S(1)}, bf16[2,32,1024]{2,1,0:T(8,128)(2,1)S(1)}, u32[]{:S(2)}, u32[]{:S(2)}) collective-permute-start(bf16[2,32,1024]{2,1,0:T(8,128)(2,1)S(1)} %get-tuple-element.452), channel_id=1, source_target_pairs={{0,2},{1,3},{2,0},{3,1},{4,6},{5,7},{6,4},{7,5},{8,10},{9,11},{10,... | collective-permute-start | bytes 393224 | tf_op jit(solution)/shard_map/ppermute | solution.py:122
  (224 other events, 3552.1 us)
Sparse Core Ops, SparseCore 0:
  11.6 131.6 all-gather.2
  145.8 47.5 all-gather.4
  452.1 63.6 reduce-scatter.2
  530.7 122.6 reduce-scatter.4

commit v10 on v9

--- a/solution.py
+++ b/solution.py
@@ -736,11 +736,9 @@
     grad_norm0, grad_gain0 = norm_back(hidden0, gains[0], grad_act1)
     grad_embed_b = (grad_hidden1 + grad_norm0).astype(jnp.bfloat16)
 
+    grad_first = (*grad_inner_w, grad_mixer_w)
     grad_square = jnp.stack(
-        [
-            part.astype(jnp.bfloat16)
-            for part in (*grad_inner_w, grad_mixer_w, grad_query_w, grad_pair_w, grad_out_w)
-        ]
+        [part.astype(jnp.bfloat16) for part in (grad_query_w, grad_pair_w, grad_out_w)]
     )
     grad_vector = jnp.stack(
         [grad_gain0, grad_gain1, grad_gain2, grad_gain3, grad_tap0, grad_tap1, grad_tap2]
@@ -755,7 +753,21 @@
     share_wide = share_wide_b.astype(jnp.float32)
     wide_grad_job = jnp.stack(handed_out(wide_by_member(share_wide_b), "vocab"))
     group_square = lax.psum_scatter(grad_square, DP, scatter_dimension=1, tiled=True)
-    square_grad_job = member_scatter(by_member(group_square))
+
+    def permuted_sum(values):
+        blocks = values.astype(jnp.bfloat16).reshape(chips, 2, group_rows, D)
+        given = lax.dynamic_index_in_dim(blocks, 1 - core, 1, keepdims=False)
+        kept = lax.dynamic_index_in_dim(blocks, core, 1, keepdims=False)
+        pair = kept.astype(jnp.float32) + other_core(given).astype(jnp.float32)
+        return chip_sum(pair.astype(jnp.bfloat16)).astype(jnp.bfloat16)
+
+    group_square = jnp.pad(group_square, ((0, per_member * members - squares), (0, 0), (0, 0)))
+    square_grad_job = jnp.stack(
+        [
+            member_scatter(jnp.stack([permuted_sum(part) for part in grad_first])),
+            member_scatter(group_square),
+        ]
+    )
 
     def from_members(values):
         values = values.reshape(per_member, members, square_rows, D).transpose(1, 0, 2, 3)

time: 890 us -> 935 us (1.051)
  starting transfers between devices: 135 us -> 156 us
  other arithmetic: 111 us -> 131 us
  matrix products: 135 us -> 121 us
  waiting for transfers between devices: 331 us -> 341 us
    ppermute x66 -> x81, starting transfers between devices: 103 us -> 123 us  [turned(): lax.ppermute(values, axis, [(i, (i + step) % count) for i in range(count)])]
    ppermute x66 -> x81, waiting for transfers between devices: 206 us -> 213 us  [turned(): lax.ppermute(values, axis, [(i, (i + step) % count) for i in range(count)])]
    unnamed x393 -> x425, local copies, waits for them, and re-layouts: 35.4 us -> 35.6 us
  transfers between devices with their start and end apart: 87 -> 106, of which waited for: 37 -> 42; matrix products, arithmetic and copies ran while one was open for 27% -> 27% of each run, Pallas kernels for 7% -> 6%
where the time goes in v10:
time: 935 us; the launch traced here: 926 us
  waiting for transfers between devices  341 us (36%)
  starting transfers between devices  156 us (17%)
  other arithmetic  131 us (14%)
  matrix products  121 us (13%)
  local copies, waits for them, and re-layouts  76.2 us (8%)
  Pallas kernels  68.9 us (7%)
  between operations  31 us (3%)
    ppermute x81, waiting for transfers between devices, turned(): lax.ppermute(values, axis, [(i, (i + step) % count) for i in range(count)])  213 us
    ppermute x81, starting transfers between devices, turned(): lax.ppermute(values, axis, [(i, (i + step) % count) for i in range(count)])  123 us
    all_to_all x5, waiting for transfers between devices, exchanged(): return lax.all_to_all(rows, ALL, 0, 0, tiled=True)  67 us
    all_gather x1, waiting for transfers between devices, body(): lax.all_gather(square_master.astype(jnp.bfloat16), ALL, axis=1, tiled=True)  38.6 us
    unnamed x425, local copies, waits for them, and re-layouts  35.6 us
    dot_general x10, matrix products, dense(): lax.dot_general(inputs, weight, (((1,), (1,)), ((), ())), preferred_eleme...  28.3 us
    dot_general x14, matrix products, outer(): lax.dot_general(grads, inputs, (((0,), (0,)), ((), ())), preferred_elemen...  27.7 us
    dot_general x9, matrix products, back_dense(): return jnp.dot(grads, weight, preferred_element_type=jnp.float32)  26.6 us
  transfers between devices with their start and end apart: 106, of which 42 were waited for; matrix products, arithmetic and copies ran while one was open for 27% of the time, Pallas kernels for 6%

profile of v10, /device:TPU:0, one launch (start us, length us, event | category | flops | bytes accessed | tf_op | source)
XLA Modules:
  0.0 925.8 jit_solution(8639482889785253435)
XLA Ops:
  19.5 7.3 all-to-all-start.4
  26.8 6.1 convert_element_type.556.table_ref
  35.4 6.8 fusion.71
  42.2 4.2 all-to-all-start.5
  55.6 45.7 %all-to-all-done.5 = bf16[32,24,1024]{2,1,0:T(8,128)(2,1)} async-done(((bf16[32,24,1024]{2,1,0:T(8,128)(2,1)}), bf16[32,24,1024]{2,1,0:T(8,128)(2,1)}, u32[]{:S(2)}, u32[]{:S(2)}) %all-to-all-start.5) | async-done | bytes 1572896 | tf_op jit(solution)/shard_map/all_to_all | solution.py:112
  104.7 38.6 %all-gather.3.cloned.1.call-done = bf16[7,1024,1024]{2,1,0:T(8,128)(2,1)} async-done(((bf16[7,32,1024]{2,1,0:T(8,128)(2,1)}), bf16[7,1024,1024]{2,1,0:T(8,128)(2,1)}) %all-gather.3.cloned.1.call-update) | async-done | bytes 14680080 | tf_op jit(solution)/shard_map/all_gather | solution.py:480
  146.4 5.7 fusion.196
  173.4 11.8 %collective-permute-start = (bf16[96,1024]{1,0:T(8,128)(2,1)S(1)}, bf16[96,1024]{1,0:T(8,128)(2,1)S(1)}, u32[]{:S(2)}, u32[]{:S(2)}) collective-permute-start(bf16[96,1024]{1,0:T(8,128)(2,1)S(1)} %multiply_convert_fusion.9), channel_id=1, source_target_pairs={{0,1},{1,2},{2,3},{3,0},{4,5},{5,6},{6,7},{7,4},{8,9},{9,10},{10,1... | collective-permute-start | bytes 589832 | tf_op jit(solution)/shard_map/ppermute | solution.py:122
  185.2 8.2 all-gather.5.cloned.1.call-done
  207.6 4.2 collective-permute-done.5
  211.8 7.7 collective-permute-done.4
  225.4 4.7 collective-permute-start.9
  287.2 23.1 %shard_map.313 = (bf16[2048,3072]{1,0:T(8,128)(2,1)}, f32[8,3072]{1,0:T(8,128)S(1)}) custom-call(s32[1,3072]{1,0:T(1,128)S(1)} %reshape.966.target_ref, bf16[3072,1024]{1,0:T(8,128)(2,1)S(1)} %copy-done, bf16[2048,1024]{1,0:T(8,128)(2,1)S(1)} %copy-done.33), custom_call_target="tpu_custom_call" | custom-call | flops 12884901888 | bytes 18874368 | tf_op jit(solution)/shard_map/pallas_call | solution.py:361
  314.3 7.5 all-to-all-done.6
  326.4 7.0 all-to-all-done.7
  336.6 10.4 %shard_map.315 = bf16[1536,1024]{1,0:T(8,128)(2,1)S(1)} custom-call(s32[1,3072]{1,0:T(1,128)S(1)} %reshape.966.target_ref, f32[1,3072]{1,0:T(1,128)S(1)} %get-tuple-element.477.scale_ref, f32[1,3072]{1,0:T(1,128)S(1)} %get-tuple-element.476.value_ref, bf16[2048,3072]{1,0:T(8,128)(2,1)} %get-tuple-element.259.shares_ref, bf16[2048,1024]{1,0:T(8,128)(2,1)} %get-tuple-element.718), custom_call_target="tpu_custom_call" | custom-call | flops 6442450944 | bytes 9437184 | tf_op jit(solution)/shard_map/pallas_call | solution.py:404
  348.8 10.3 %shard_map.314 = bf16[1536,1024]{1,0:T(8,128)(2,1)S(1)} custom-call(s32[1,3072]{1,0:T(1,128)S(1)} %reshape.966.target_ref, f32[1,3072]{1,0:T(1,128)S(1)} %get-tuple-element.477.scale_ref, f32[1,3072]{1,0:T(1,128)S(1)} %get-tuple-element.476.value_ref, bf16[2048,3072]{1,0:T(8,128)(2,1)} %get-tuple-element.259.shares_ref, bf16[2048,1024]{1,0:T(8,128)(2,1)} %get-tuple-element.718), custom_call_target="tpu_custom_call" | custom-call | flops 6442450944 | bytes 9437184 | tf_op jit(solution)/shard_map/pallas_call | solution.py:404
  366.7 17.5 %fusion.12 = f32[2048,1024]{1,0:T(8,128)} fusion(bf16[3072,1024]{1,0:T(8,128)(2,1)} %constant_dynamic-update-slice_fusion.answers_ref, bf16[2048,3072]{1,0:T(8,128)(2,1)S(1)} %bitcast.645, f32[3072]{0:T(1024)S(1)} %bitcast.540, f32[3072]{0:T(1024)S(1)} %bitcast.539, s32[3072]{0:T(1024)S(1)} %eq.440), kind=kOutput, calls=%fused_computation.35 | convolution fusion | flops 12910067712 | bytes 27299840 | tf_op jit(solution)/shard_map/dot_general | solution.py:655
  388.3 11.8 %collective-permute-done.30 = bf16[4,96,1024]{2,1,0:T(8,128)(2,1)S(1)} collective-permute-done((bf16[4,96,1024]{2,1,0:T(8,128)(2,1)S(1)}, bf16[4,96,1024]{2,1,0:T(8,128)(2,1)S(1)}, u32[]{:S(2)}, u32[]{:S(2)}) %collective-permute-start.30) | collective-permute-done | bytes 786464 | tf_op jit(solution)/shard_map/ppermute | solution.py:122
  404.7 5.9 collective-permute-done.37
  410.6 7.0 collective-permute-done.36
  427.6 13.1 %collective-permute-done.39 = bf16[96,1024]{1,0:T(8,128)(2,1)S(1)} collective-permute-done((bf16[96,1024]{1,0:T(8,128)(2,1)S(1)}, bf16[96,1024]{1,0:T(8,128)(2,1)S(1)}, u32[]{:S(2)}, u32[]{:S(2)}) %collective-permute-start.39) | collective-permute-done | bytes 196640 | tf_op jit(solution)/shard_map/ppermute | solution.py:122
  468.9 6.4 collective-permute-done.42
  516.0 7.9 multiply_reduce_fusion.1
  525.8 4.2 multiply_convert_fusion.2
  566.0 6.3 all-to-all-start.8
  576.4 12.1 %all-to-all-done.8 = f32[32,1,352]{2,1,0:T(1,128)S(1)} async-done(((f32[32,1,352]{2,1,0:T(1,128)}), f32[32,1,352]{2,1,0:T(1,128)S(1)}, u32[]{:S(2)}, u32[]{:S(2)}) %all-to-all-start.8) | async-done | bytes 45088 | tf_op jit(solution)/shard_map/all_to_all | solution.py:112
  603.7 20.6 %collective-permute-done.53 = bf16[128,1024]{1,0:T(8,128)(2,1)S(1)} collective-permute-done((bf16[128,1024]{1,0:T(8,128)(2,1)S(1)}, bf16[128,1024]{1,0:T(8,128)(2,1)S(1)}, u32[]{:S(2)}, u32[]{:S(2)}) %collective-permute-start.53) | collective-permute-done | bytes 262176 | tf_op jit(solution)/shard_map/ppermute | solution.py:122
  624.8 7.3 collective-permute-done.51
  638.9 4.5 collective-permute-done.47
  643.4 6.0 collective-permute-done.45
  661.0 15.6 %collective-permute-done.61 = bf16[128,1024]{1,0:T(8,128)(2,1)} collective-permute-done((bf16[128,1024]{1,0:T(8,128)(2,1)S(1)}, bf16[128,1024]{1,0:T(8,128)(2,1)}, u32[]{:S(2)}, u32[]{:S(2)}) %collective-permute-start.61) | collective-permute-done | bytes 262176 | tf_op jit(solution)/shard_map/ppermute | solution.py:122
  687.3 20.0 %collective-permute-done.67 = bf16[144,1024]{1,0:T(8,128)(2,1)S(1)} collective-permute-done((bf16[144,1024]{1,0:T(8,128)(2,1)S(1)}, bf16[144,1024]{1,0:T(8,128)(2,1)S(1)}, u32[]{:S(2)}, u32[]{:S(2)}) %collective-permute-start.67) | collective-permute-done | bytes 294944 | tf_op jit(solution)/shard_map/ppermute | solution.py:122
  707.5 7.3 fusion.17
  714.8 12.2 %add.1152 = f32[2048,1024]{1,0:T(8,128)} add(f32[2048,1024]{1,0:T(8,128)} %fusion.12, f32[2048,1024]{1,0:T(8,128)} %fusion.17) | non-fusion elementwise | flops 2097152 | bytes 25165824 | tf_op jit(solution)/shard_map/add | solution.py:795
  731.2 6.2 multiply_reduce_fusion
  737.4 15.1 %collective-permute-done.64 = bf16[128,1024]{1,0:T(8,128)(2,1)} collective-permute-done((bf16[128,1024]{1,0:T(8,128)(2,1)}, bf16[128,1024]{1,0:T(8,128)(2,1)}, u32[]{:S(2)}, u32[]{:S(2)}) %collective-permute-start.64) | collective-permute-done | bytes 262176 | tf_op jit(solution)/shard_map/ppermute | solution.py:122
  762.5 6.4 all-to-all-done.10
  784.3 4.5 collective-permute-done.72
  789.6 4.4 collective-permute-done.73
  795.1 4.0 collective-permute-done.79
  799.2 6.1 collective-permute-done.77
  810.7 3.9 collective-permute-done.82
  815.2 4.9 collective-permute-done.81
  826.5 25.1 %shard_map.316 = bf16[1024,1024]{1,0:T(8,128)(2,1)S(1)} custom-call(s32[1]{0:T(128)} %bitcast.17.core_ref, bf16[512,1024]{1,0:T(8,128)(2,1)S(1)} %bitcast.538, bf16[512,1024]{1,0:T(8,128)(2,1)S(1)} %collective-permute-done.83.second_ref, f32[1024,1024]{1,0:T(8,128)S(1)} %fusion.198.square_ref), custom_call_target="tpu_custom_call" | custom-call | flops 19327352832 | bytes 6291456 | tf_op jit(solution)/shard_map/pallas_call | solution.py:306
  872.6 22.7 %add_multiply_fusion = (f32[2048,1024]{1,0:T(8,128)}, f32[2048,1024]{1,0:T(8,128)}, f32[2048,1024]{1,0:T(8,128)}) fusion(f32[2048,1024]{1,0:T(8,128)} %param.25, f32[]{:T(128)S(6)} %sub.280, f32[]{:T(128)S(6)} %sub.279, f32[2048,1024]{1,0:T(8,128)} %get-tuple-element.283, f32[]{:T(128)S(6)} %min.3, f32[2048,1024]{1,0:T(8,128)} %param.27, f32[2048,1024]{1,0:T(8,128)} %param.26), kind=kLoop, calls=%fused_computation.41 | loop fusion | flops 31457280 | bytes 58720268 | tf_op jit(solution)/shard_map/mul | solution.py:100
  900.8 4.4 collective-permute-done.92
  908.3 6.5 collective-permute-done.90
  (916 shorter events, 385.5 us)
Async XLA Ops:
  7.2 136.1 %all-gather.3.cloned.1.call-start = ((), (), s32[]{:S(2)}) async-start(), calls=%async_computation.13 | async-start | bytes 15138816 | tf_op jit(solution)/shard_map/all_gather | solution.py:480
  42.2 59.1 %all-to-all-start.5 = ((bf16[32,24,1024]{2,1,0:T(8,128)(2,1)}), bf16[32,24,1024]{2,1,0:T(8,128)(2,1)}, u32[]{:S(2)}, u32[]{:S(2)}) async-start(bf16[32,24,1024]{2,1,0:T(8,128)(2,1)} %bitcast.20), calls=%async_computation.5 | async-start | bytes 3145728 | tf_op jit(solution)/shard_map/all_to_all | solution.py:112
  46.5 146.9 %all-gather.5.cloned.1.call-start = ((), (), s32[]{:S(2)}) async-start(), calls=%async_computation.14 | async-start | bytes 7962624 | tf_op jit(solution)/shard_map/all_gather | solution.py:481
  171.3 22.1 %collective-permute-start.2 = (bf16[96,1024]{1,0:T(8,128)(2,1)S(1)}, bf16[96,1024]{1,0:T(8,128)(2,1)S(1)}, u32[]{:S(2)}, u32[]{:S(2)}) collective-permute-start(bf16[96,1024]{1,0:T(8,128)(2,1)S(1)} %multiply_convert_fusion.9), channel_id=1, source_target_pairs={{0,3},{1,0},{2,1},{3,2},{4,7},{5,4},{6,5},{7,6},{8,11},{9,8},{10,9... | collective-permute-start | bytes 589832 | tf_op jit(solution)/shard_map/ppermute | solution.py:122
  172.4 21.0 %collective-permute-start.1 = (bf16[96,1024]{1,0:T(8,128)(2,1)S(1)}, bf16[96,1024]{1,0:T(8,128)(2,1)S(1)}, u32[]{:S(2)}, u32[]{:S(2)}) collective-permute-start(bf16[96,1024]{1,0:T(8,128)(2,1)S(1)} %multiply_convert_fusion.9), channel_id=1, source_target_pairs={{0,2},{1,3},{2,0},{3,1},{4,6},{5,7},{6,4},{7,5},{8,10},{9,11},{10,... | collective-permute-start | bytes 589832 | tf_op jit(solution)/shard_map/ppermute | solution.py:122
  173.4 20.1 %collective-permute-start = (bf16[96,1024]{1,0:T(8,128)(2,1)S(1)}, bf16[96,1024]{1,0:T(8,128)(2,1)S(1)}, u32[]{:S(2)}, u32[]{:S(2)}) collective-permute-start(bf16[96,1024]{1,0:T(8,128)(2,1)S(1)} %multiply_convert_fusion.9), channel_id=1, source_target_pairs={{0,1},{1,2},{2,3},{3,0},{4,5},{5,6},{6,7},{7,4},{8,9},{9,10},{10,1... | collective-permute-start | bytes 589832 | tf_op jit(solution)/shard_map/ppermute | solution.py:122
  275.7 34.5 %collective-permute-start.25 = (bf16[144,1024]{1,0:T(8,128)(2,1)S(1)}, bf16[144,1024]{1,0:T(8,128)(2,1)}, u32[]{:S(2)}, u32[]{:S(2)}) collective-permute-start(bf16[144,1024]{1,0:T(8,128)(2,1)S(1)} %get-tuple-element.395), channel_id=1, source_target_pairs={{0,1},{1,2},{2,3},{3,0},{4,5},{5,6},{6,7},{7,4},{8,9},{9,10},{10,1... | collective-permute-start | bytes 884744 | tf_op jit(solution)/shard_map/ppermute | solution.py:122
  277.7 32.6 %collective-permute-start.26 = (bf16[144,1024]{1,0:T(8,128)(2,1)S(1)}, bf16[144,1024]{1,0:T(8,128)(2,1)}, u32[]{:S(2)}, u32[]{:S(2)}) collective-permute-start(bf16[144,1024]{1,0:T(8,128)(2,1)S(1)} %get-tuple-element.394), channel_id=1, source_target_pairs={{0,2},{1,3},{2,0},{3,1},{4,6},{5,7},{6,4},{7,5},{8,10},{9,11},{10,... | collective-permute-start | bytes 884744 | tf_op jit(solution)/shard_map/ppermute | solution.py:122
  281.5 28.8 %collective-permute-start.27 = (bf16[144,1024]{1,0:T(8,128)(2,1)S(1)}, bf16[144,1024]{1,0:T(8,128)(2,1)}, u32[]{:S(2)}, u32[]{:S(2)}) collective-permute-start(bf16[144,1024]{1,0:T(8,128)(2,1)S(1)} %get-tuple-element.393), channel_id=1, source_target_pairs={{0,3},{1,0},{2,1},{3,2},{4,7},{5,4},{6,5},{7,6},{8,11},{9,8},{10,9... | collective-permute-start | bytes 884744 | tf_op jit(solution)/shard_map/ppermute | solution.py:122
  326.4 197.5 %reduce-scatter.3.cloned.1.call-start = ((), (), s32[]{:S(2)}) async-start(), calls=%async_computation.15 | async-start | bytes 7962624 | tf_op jit(solution)/shard_map/reduce_scatter | solution.py:750
  362.9 22.5 %collective-permute-start.31 = (bf16[4,96,1024]{2,1,0:T(8,128)(2,1)S(1)}, bf16[4,96,1024]{2,1,0:T(8,128)(2,1)S(1)}, u32[]{:S(2)}, u32[]{:S(2)}) collective-permute-start(bf16[4,96,1024]{2,1,0:T(8,128)(2,1)S(1)} %get-tuple-element.382), channel_id=1, source_target_pairs={{0,8},{8,16},{16,24},{24,0},{1,9},{9,17},{17,25},{25,1},{2,10},{10... | collective-permute-start | bytes 2359304 | tf_op jit(solution)/shard_map/ppermute | solution.py:122
  363.5 36.5 %collective-permute-start.30 = (bf16[4,96,1024]{2,1,0:T(8,128)(2,1)S(1)}, bf16[4,96,1024]{2,1,0:T(8,128)(2,1)S(1)}, u32[]{:S(2)}, u32[]{:S(2)}) collective-permute-start(bf16[4,96,1024]{2,1,0:T(8,128)(2,1)S(1)} %get-tuple-element.381), channel_id=1, source_target_pairs={{0,16},{8,24},{16,0},{24,8},{1,17},{9,25},{17,1},{25,9},{2,18},{10... | collective-permute-start | bytes 2359304 | tf_op jit(solution)/shard_map/ppermute | solution.py:122
  364.1 36.0 %collective-permute-start.29 = (bf16[4,96,1024]{2,1,0:T(8,128)(2,1)S(1)}, bf16[4,96,1024]{2,1,0:T(8,128)(2,1)S(1)}, u32[]{:S(2)}, u32[]{:S(2)}) collective-permute-start(bf16[4,96,1024]{2,1,0:T(8,128)(2,1)S(1)} %get-tuple-element.380), channel_id=1, source_target_pairs={{0,24},{8,0},{16,8},{24,16},{1,25},{9,1},{17,9},{25,17},{2,26},{10... | collective-permute-start | bytes 2359304 | tf_op jit(solution)/shard_map/ppermute | solution.py:122
  422.3 18.5 %collective-permute-start.39 = (bf16[96,1024]{1,0:T(8,128)(2,1)S(1)}, bf16[96,1024]{1,0:T(8,128)(2,1)S(1)}, u32[]{:S(2)}, u32[]{:S(2)}) collective-permute-start(bf16[96,1024]{1,0:T(8,128)(2,1)S(1)} %fusion.180), channel_id=1, source_target_pairs={{0,2},{1,3},{2,0},{3,1},{4,6},{5,7},{6,4},{7,5},{8,10},{9,11},{10,... | collective-permute-start | bytes 589832 | tf_op jit(solution)/shard_map/ppermute | solution.py:122
  452.0 275.0 %reduce-scatter.5.cloned.1.call-start = ((), (), s32[]{:S(2)}) async-start(), calls=%async_computation.16 | async-start | bytes 7077888 | tf_op jit(solution)/shard_map/reduce_scatter | solution.py:755
  509.3 42.7 %collective-permute-start.56 = (bf16[4,128,1024]{2,1,0:T(8,128)(2,1)}, bf16[4,128,1024]{2,1,0:T(8,128)(2,1)}, u32[]{:S(2)}, u32[]{:S(2)}) collective-permute-start(bf16[4,128,1024]{2,1,0:T(8,128)(2,1)} %dynamic-slice_bitcast_fusion.1), channel_id=1, source_target_pairs={{0,4},{4,0},{1,5},{5,1},{2,6},{6,2},{3,7},{7,3},{8,12},{12,8},{9,1... | collective-permute-start | bytes 3145736 | tf_op jit(solution)/shard_map/ppermute | solution.py:162
  533.6 25.2 %collective-permute-start.52 = (bf16[4,128,1024]{2,1,0:T(8,128)(2,1)}, bf16[4,128,1024]{2,1,0:T(8,128)(2,1)}, u32[]{:S(2)}, u32[]{:S(2)}) collective-permute-start(bf16[4,128,1024]{2,1,0:T(8,128)(2,1)} %dynamic-slice_bitcast_fusion.2), channel_id=1, source_target_pairs={{0,4},{4,0},{1,5},{5,1},{2,6},{6,2},{3,7},{7,3},{8,12},{12,8},{9,1... | collective-permute-start | bytes 3145736 | tf_op jit(solution)/shard_map/ppermute | solution.py:162
  536.2 25.8 %collective-permute-start.48 = (bf16[4,128,1024]{2,1,0:T(8,128)(2,1)}, bf16[4,128,1024]{2,1,0:T(8,128)(2,1)}, u32[]{:S(2)}, u32[]{:S(2)}) collective-permute-start(bf16[4,128,1024]{2,1,0:T(8,128)(2,1)} %dynamic-slice_bitcast_fusion.3), channel_id=1, source_target_pairs={{0,4},{4,0},{1,5},{5,1},{2,6},{6,2},{3,7},{7,3},{8,12},{12,8},{9,1... | collective-permute-start | bytes 3145736 | tf_op jit(solution)/shard_map/ppermute | solution.py:162
  539.2 35.4 %collective-permute-start.44 = (bf16[4,128,1024]{2,1,0:T(8,128)(2,1)}, bf16[4,128,1024]{2,1,0:T(8,128)(2,1)}, u32[]{:S(2)}, u32[]{:S(2)}) collective-permute-start(bf16[4,128,1024]{2,1,0:T(8,128)(2,1)} %dynamic-slice_bitcast_fusion.4), channel_id=1, source_target_pairs={{0,4},{4,0},{1,5},{5,1},{2,6},{6,2},{3,7},{7,3},{8,12},{12,8},{9,1... | collective-permute-start | bytes 3145736 | tf_op jit(solution)/shard_map/ppermute | solution.py:162
  555.5 39.0 %collective-permute-start.59 = (bf16[128,1024]{1,0:T(8,128)(2,1)}, bf16[128,1024]{1,0:T(8,128)(2,1)}, u32[]{:S(2)}, u32[]{:S(2)}) collective-permute-start(bf16[128,1024]{1,0:T(8,128)(2,1)} %get-tuple-element.425), channel_id=1, source_target_pairs={{0,24},{8,0},{16,8},{24,16},{1,25},{9,1},{17,9},{25,17},{2,26},{10... | collective-permute-start | bytes 786440 | tf_op jit(solution)/shard_map/ppermute | solution.py:122
  558.3 38.0 %collective-permute-start.58 = (bf16[128,1024]{1,0:T(8,128)(2,1)}, bf16[128,1024]{1,0:T(8,128)(2,1)}, u32[]{:S(2)}, u32[]{:S(2)}) collective-permute-start(bf16[128,1024]{1,0:T(8,128)(2,1)} %get-tuple-element.426), channel_id=1, source_target_pairs={{0,16},{8,24},{16,0},{24,8},{1,17},{9,25},{17,1},{25,9},{2,18},{10... | collective-permute-start | bytes 786440 | tf_op jit(solution)/shard_map/ppermute | solution.py:122
  558.9 38.7 %collective-permute-start.57 = (bf16[128,1024]{1,0:T(8,128)(2,1)}, bf16[128,1024]{1,0:T(8,128)(2,1)}, u32[]{:S(2)}, u32[]{:S(2)}) collective-permute-start(bf16[128,1024]{1,0:T(8,128)(2,1)} %get-tuple-element.424), channel_id=1, source_target_pairs={{0,8},{8,16},{16,24},{24,0},{1,9},{9,17},{17,25},{25,1},{2,10},{10... | collective-permute-start | bytes 786440 | tf_op jit(solution)/shard_map/ppermute | solution.py:122
  562.0 37.3 %collective-permute-start.55 = (bf16[128,1024]{1,0:T(8,128)(2,1)}, bf16[128,1024]{1,0:T(8,128)(2,1)S(1)}, u32[]{:S(2)}, u32[]{:S(2)}) collective-permute-start(bf16[128,1024]{1,0:T(8,128)(2,1)} %get-tuple-element.422), channel_id=1, source_target_pairs={{0,24},{8,0},{16,8},{24,16},{1,25},{9,1},{17,9},{25,17},{2,26},{10... | collective-permute-start | bytes 786440 | tf_op jit(solution)/shard_map/ppermute | solution.py:122
  566.0 22.5 %all-to-all-start.8 = ((f32[32,1,352]{2,1,0:T(1,128)}), f32[32,1,352]{2,1,0:T(1,128)S(1)}, u32[]{:S(2)}, u32[]{:S(2)}) async-start(f32[32,1,352]{2,1,0:T(1,128)} %copy.146), calls=%async_computation.10 | async-start | bytes 98304 | tf_op jit(solution)/shard_map/all_to_all | solution.py:112
  574.6 26.6 %collective-permute-start.54 = (bf16[128,1024]{1,0:T(8,128)(2,1)}, bf16[128,1024]{1,0:T(8,128)(2,1)}, u32[]{:S(2)}, u32[]{:S(2)}) collective-permute-start(bf16[128,1024]{1,0:T(8,128)(2,1)} %get-tuple-element.423), channel_id=1, source_target_pairs={{0,16},{8,24},{16,0},{24,8},{1,17},{9,25},{17,1},{25,9},{2,18},{10... | collective-permute-start | bytes 786440 | tf_op jit(solution)/shard_map/ppermute | solution.py:122
  588.5 119.0 %all-to-all-start.9 = ((bf16[32,24,1024]{2,1,0:T(8,128)(2,1)}), bf16[32,24,1024]{2,1,0:T(8,128)(2,1)}, u32[]{:S(2)}, u32[]{:S(2)}) async-start(bf16[32,24,1024]{2,1,0:T(8,128)(2,1)} %bitcast.587), calls=%async_computation.11 | async-start | bytes 3145728 | tf_op jit(solution)/shard_map/all_to_all | solution.py:112
  594.5 29.8 %collective-permute-start.53 = (bf16[128,1024]{1,0:T(8,128)(2,1)S(1)}, bf16[128,1024]{1,0:T(8,128)(2,1)S(1)}, u32[]{:S(2)}, u32[]{:S(2)}) collective-permute-start(bf16[128,1024]{1,0:T(8,128)(2,1)S(1)} %copy-done.93), channel_id=1, source_target_pairs={{0,8},{8,16},{16,24},{24,0},{1,9},{9,17},{17,25},{25,1},{2,10},{10... | collective-permute-start | bytes 786440 | tf_op jit(solution)/shard_map/ppermute | solution.py:122
  596.3 35.8 %collective-permute-start.51 = (bf16[128,1024]{1,0:T(8,128)(2,1)S(1)}, bf16[128,1024]{1,0:T(8,128)(2,1)S(1)}, u32[]{:S(2)}, u32[]{:S(2)}) collective-permute-start(bf16[128,1024]{1,0:T(8,128)(2,1)S(1)} %get-tuple-element.419), channel_id=1, source_target_pairs={{0,24},{8,0},{16,8},{24,16},{1,25},{9,1},{17,9},{25,17},{2,26},{10... | collective-permute-start | bytes 786440 | tf_op jit(solution)/shard_map/ppermute | solution.py:122
  597.5 37.4 %collective-permute-start.50 = (bf16[128,1024]{1,0:T(8,128)(2,1)S(1)}, bf16[128,1024]{1,0:T(8,128)(2,1)S(1)}, u32[]{:S(2)}, u32[]{:S(2)}) collective-permute-start(bf16[128,1024]{1,0:T(8,128)(2,1)S(1)} %get-tuple-element.420), channel_id=1, source_target_pairs={{0,16},{8,24},{16,0},{24,8},{1,17},{9,25},{17,1},{25,9},{2,18},{10... | collective-permute-start | bytes 786440 | tf_op jit(solution)/shard_map/ppermute | solution.py:122
  599.3 39.4 %collective-permute-start.49 = (bf16[128,1024]{1,0:T(8,128)(2,1)S(1)}, bf16[128,1024]{1,0:T(8,128)(2,1)S(1)}, u32[]{:S(2)}, u32[]{:S(2)}) collective-permute-start(bf16[128,1024]{1,0:T(8,128)(2,1)S(1)} %get-tuple-element.418), channel_id=1, source_target_pairs={{0,8},{8,16},{16,24},{24,0},{1,9},{9,17},{17,25},{25,1},{2,10},{10... | collective-permute-start | bytes 786440 | tf_op jit(solution)/shard_map/ppermute | solution.py:122
  601.2 42.2 %collective-permute-start.47 = (bf16[128,1024]{1,0:T(8,128)(2,1)S(1)}, bf16[128,1024]{1,0:T(8,128)(2,1)S(1)}, u32[]{:S(2)}, u32[]{:S(2)}) collective-permute-start(bf16[128,1024]{1,0:T(8,128)(2,1)S(1)} %get-tuple-element.416), channel_id=1, source_target_pairs={{0,24},{8,0},{16,8},{24,16},{1,25},{9,1},{17,9},{25,17},{2,26},{10... | collective-permute-start | bytes 786440 | tf_op jit(solution)/shard_map/ppermute | solution.py:122
  624.3 19.1 %collective-permute-start.46 = (bf16[128,1024]{1,0:T(8,128)(2,1)S(1)}, bf16[128,1024]{1,0:T(8,128)(2,1)S(1)}, u32[]{:S(2)}, u32[]{:S(2)}) collective-permute-start(bf16[128,1024]{1,0:T(8,128)(2,1)S(1)} %get-tuple-element.417), channel_id=1, source_target_pairs={{0,16},{8,24},{16,0},{24,8},{1,17},{9,25},{17,1},{25,9},{2,18},{10... | collective-permute-start | bytes 786440 | tf_op jit(solution)/shard_map/ppermute | solution.py:122
  632.1 17.3 %collective-permute-start.45 = (bf16[128,1024]{1,0:T(8,128)(2,1)S(1)}, bf16[128,1024]{1,0:T(8,128)(2,1)S(1)}, u32[]{:S(2)}, u32[]{:S(2)}) collective-permute-start(bf16[128,1024]{1,0:T(8,128)(2,1)S(1)} %get-tuple-element.415), channel_id=1, source_target_pairs={{0,8},{8,16},{16,24},{24,0},{1,9},{9,17},{17,25},{25,1},{2,10},{10... | collective-permute-start | bytes 786440 | tf_op jit(solution)/shard_map/ppermute | solution.py:122
  653.9 22.7 %collective-permute-start.61 = (bf16[128,1024]{1,0:T(8,128)(2,1)S(1)}, bf16[128,1024]{1,0:T(8,128)(2,1)}, u32[]{:S(2)}, u32[]{:S(2)}) collective-permute-start(bf16[128,1024]{1,0:T(8,128)(2,1)S(1)} %get-tuple-element.414), channel_id=1, source_target_pairs={{0,2},{1,3},{2,0},{3,1},{4,6},{5,7},{6,4},{7,5},{8,10},{9,11},{10,... | collective-permute-start | bytes 786440 | tf_op jit(solution)/shard_map/ppermute | solution.py:122
  653.9 22.7 %collective-permute-start.60 = (bf16[128,1024]{1,0:T(8,128)(2,1)S(1)}, bf16[128,1024]{1,0:T(8,128)(2,1)}, u32[]{:S(2)}, u32[]{:S(2)}) collective-permute-start(bf16[128,1024]{1,0:T(8,128)(2,1)S(1)} %get-tuple-element.412), channel_id=1, source_target_pairs={{0,1},{1,2},{2,3},{3,0},{4,5},{5,6},{6,7},{7,4},{8,9},{9,10},{10,1... | collective-permute-start | bytes 786440 | tf_op jit(solution)/shard_map/ppermute | solution.py:122
  679.4 27.9 %collective-permute-start.67 = (bf16[144,1024]{1,0:T(8,128)(2,1)S(1)}, bf16[144,1024]{1,0:T(8,128)(2,1)S(1)}, u32[]{:S(2)}, u32[]{:S(2)}) collective-permute-start(bf16[144,1024]{1,0:T(8,128)(2,1)S(1)} %get-tuple-element.432), channel_id=1, source_target_pairs={{0,2},{1,3},{2,0},{3,1},{4,6},{5,7},{6,4},{7,5},{8,10},{9,11},{10,... | collective-permute-start | bytes 884744 | tf_op jit(solution)/shard_map/ppermute | solution.py:122
  682.1 25.3 %collective-permute-start.66 = (bf16[144,1024]{1,0:T(8,128)(2,1)S(1)}, bf16[144,1024]{1,0:T(8,128)(2,1)S(1)}, u32[]{:S(2)}, u32[]{:S(2)}) collective-permute-start(bf16[144,1024]{1,0:T(8,128)(2,1)S(1)} %get-tuple-element.431), channel_id=1, source_target_pairs={{0,1},{1,2},{2,3},{3,0},{4,5},{5,6},{6,7},{7,4},{8,9},{9,10},{10,1... | collective-permute-start | bytes 884744 | tf_op jit(solution)/shard_map/ppermute | solution.py:122
  728.9 23.6 %collective-permute-start.64 = (bf16[128,1024]{1,0:T(8,128)(2,1)}, bf16[128,1024]{1,0:T(8,128)(2,1)}, u32[]{:S(2)}, u32[]{:S(2)}) collective-permute-start(bf16[128,1024]{1,0:T(8,128)(2,1)} %get-tuple-element.434), channel_id=1, source_target_pairs={{0,2},{1,3},{2,0},{3,1},{4,6},{5,7},{6,4},{7,5},{8,10},{9,11},{10,... | collective-permute-start | bytes 786440 | tf_op jit(solution)/shard_map/ppermute | solution.py:122
  728.9 23.6 %collective-permute-start.63 = (bf16[128,1024]{1,0:T(8,128)(2,1)}, bf16[128,1024]{1,0:T(8,128)(2,1)}, u32[]{:S(2)}, u32[]{:S(2)}) collective-permute-start(bf16[128,1024]{1,0:T(8,128)(2,1)} %get-tuple-element.433), channel_id=1, source_target_pairs={{0,1},{1,2},{2,3},{3,0},{4,5},{5,6},{6,7},{7,4},{8,9},{9,10},{10,1... | collective-permute-start | bytes 786440 | tf_op jit(solution)/shard_map/ppermute | solution.py:122
  795.1 27.6 %collective-permute-start.75 = (bf16[512,1024]{1,0:T(8,128)(2,1)}, bf16[512,1024]{1,0:T(8,128)(2,1)}, u32[]{:S(2)}, u32[]{:S(2)}) collective-permute-start(bf16[512,1024]{1,0:T(8,128)(2,1)} %pad_maximum_fusion.8), channel_id=1, source_target_pairs={{0,4},{4,0},{1,5},{5,1},{2,6},{6,2},{3,7},{7,3},{8,12},{12,8},{9,1... | collective-permute-start | bytes 3145736 | tf_op jit(solution)/shard_map/ppermute | solution.py:162
  810.2 49.9 %collective-permute-start.71 = (bf16[2,32,1024]{2,1,0:T(8,128)(2,1)S(1)}, bf16[2,32,1024]{2,1,0:T(8,128)(2,1)S(1)}, u32[]{:S(2)}, u32[]{:S(2)}) collective-permute-start(bf16[2,32,1024]{2,1,0:T(8,128)(2,1)S(1)} %get-tuple-element.454), channel_id=1, source_target_pairs={{0,3},{1,0},{2,1},{3,2},{4,7},{5,4},{6,5},{7,6},{8,11},{9,8},{10,9... | collective-permute-start | bytes 393224 | tf_op jit(solution)/shard_map/ppermute | solution.py:122
  814.7 45.4 %collective-permute-start.70 = (bf16[2,32,1024]{2,1,0:T(8,128)(2,1)S(1)}, bf16[2,32,1024]{2,1,0:T(8,128)(2,1)S(1)}, u32[]{:S(2)}, u32[]{:S(2)}) collective-permute-start(bf16[2,32,1024]{2,1,0:T(8,128)(2,1)S(1)} %get-tuple-element.455), channel_id=1, source_target_pairs={{0,2},{1,3},{2,0},{3,1},{4,6},{5,7},{6,4},{7,5},{8,10},{9,11},{10,... | collective-permute-start | bytes 393224 | tf_op jit(solution)/shard_map/ppermute | solution.py:122
  820.1 40.0 %collective-permute-start.69 = (bf16[2,32,1024]{2,1,0:T(8,128)(2,1)S(1)}, bf16[2,32,1024]{2,1,0:T(8,128)(2,1)S(1)}, u32[]{:S(2)}, u32[]{:S(2)}) collective-permute-start(bf16[2,32,1024]{2,1,0:T(8,128)(2,1)S(1)} %get-tuple-element.456), channel_id=1, source_target_pairs={{0,1},{1,2},{2,3},{3,0},{4,5},{5,6},{6,7},{7,4},{8,9},{9,10},{10,1... | collective-permute-start | bytes 393224 | tf_op jit(solution)/shard_map/ppermute | solution.py:122
  864.9 30.5 %collective-permute-start.88 = (bf16[128,1024]{1,0:T(8,128)(2,1)}, bf16[128,1024]{1,0:T(8,128)(2,1)S(1)}, u32[]{:S(2)}, u32[]{:S(2)}) collective-permute-start(bf16[128,1024]{1,0:T(8,128)(2,1)} %get-tuple-element.402), channel_id=1, source_target_pairs={{0,8},{8,16},{16,24},{24,0},{1,9},{9,17},{17,25},{25,1},{2,10},{10... | collective-permute-start | bytes 786440 | tf_op jit(solution)/shard_map/ppermute | solution.py:122
  865.2 30.2 %collective-permute-start.87 = (bf16[128,1024]{1,0:T(8,128)(2,1)S(1)}, bf16[128,1024]{1,0:T(8,128)(2,1)}, u32[]{:S(2)}, u32[]{:S(2)}) collective-permute-start(bf16[128,1024]{1,0:T(8,128)(2,1)S(1)} %get-tuple-element.403), channel_id=1, source_target_pairs={{0,16},{8,24},{16,0},{24,8},{1,17},{9,25},{17,1},{25,9},{2,18},{10... | collective-permute-start | bytes 786440 | tf_op jit(solution)/shard_map/ppermute | solution.py:122
  866.1 29.3 %collective-permute-start.86 = (bf16[128,1024]{1,0:T(8,128)(2,1)S(1)}, bf16[128,1024]{1,0:T(8,128)(2,1)}, u32[]{:S(2)}, u32[]{:S(2)}) collective-permute-start(bf16[128,1024]{1,0:T(8,128)(2,1)S(1)} %get-tuple-element.404), channel_id=1, source_target_pairs={{0,24},{8,0},{16,8},{24,16},{1,25},{9,1},{17,9},{25,17},{2,26},{10... | collective-permute-start | bytes 786440 | tf_op jit(solution)/shard_map/ppermute | solution.py:122
  868.5 31.8 %collective-permute-start.94 = (bf16[144,1024]{1,0:T(8,128)(2,1)S(1)}, bf16[144,1024]{1,0:T(8,128)(2,1)S(1)}, u32[]{:S(2)}, u32[]{:S(2)}) collective-permute-start(bf16[144,1024]{1,0:T(8,128)(2,1)S(1)} %get-tuple-element.388), channel_id=1, source_target_pairs={{0,1},{1,2},{2,3},{3,0},{4,5},{5,6},{6,7},{7,4},{8,9},{9,10},{10,1... | collective-permute-start | bytes 884744 | tf_op jit(solution)/shard_map/ppermute | solution.py:122
  869.3 31.5 %collective-permute-start.93 = (bf16[144,1024]{1,0:T(8,128)(2,1)S(1)}, bf16[144,1024]{1,0:T(8,128)(2,1)S(1)}, u32[]{:S(2)}, u32[]{:S(2)}) collective-permute-start(bf16[144,1024]{1,0:T(8,128)(2,1)S(1)} %get-tuple-element.389), channel_id=1, source_target_pairs={{0,2},{1,3},{2,0},{3,1},{4,6},{5,7},{6,4},{7,5},{8,10},{9,11},{10,... | collective-permute-start | bytes 884744 | tf_op jit(solution)/shard_map/ppermute | solution.py:122
  (259 other events, 3717.4 us)
Sparse Core Ops, SparseCore 0:
  11.6 131.6 all-gather.2
  145.8 47.5 all-gather.4
  452.1 63.5 reduce-scatter.2
  524.1 117.3 reduce-scatter.4

commit v11 on v9

--- a/solution.py
+++ b/solution.py
@@ -861,23 +861,21 @@
     rest_b = ortho_rest(core, wide_first, wide_second, square_gram)
     power = leading_coefficient**NS_ITERS
     wide_rest = jnp.where(core == 0, rest_b, other_core(rest_b))
-    back_square = square_product(square_job, rest_b).astype(jnp.bfloat16)
     half_rows = square_half.shape[0]
-    back_square = jnp.where(
-        core == 0, other_core(back_square[half_rows:]), back_square[:half_rows]
-    )
+    given = square_product(square_job[half_rows:], rest_b).astype(jnp.bfloat16)
+    kept = square_product(square_half, rest_b).astype(jnp.bfloat16)
+    back_square = jnp.where(core == 0, other_core(given), kept)
     back_wide = square_product(wide_job, wide_rest).astype(jnp.bfloat16)
-    share_table, back_square, back_wide = lax.optimization_barrier(
-        (share_table, back_square, back_wide)
-    )
+    back_square, back_wide = lax.optimization_barrier((back_square, back_wide))
+    back_square = handed_back(list(back_square.reshape(-1, group_rows, D)), "chip")
+    share_table, back_square = lax.optimization_barrier((share_table, back_square))
     table_step, table_first_new, table_second_new = adam_step(
         table_master, table_first, table_second, share_table, factor, adam_count
     )
-    back_square = handed_back(list(back_square.reshape(-1, group_rows, D)), "chip")
     back_square = placed_after(back_square, "chip")[:per_member]
+    back_square = from_members(back_square)
     back_wide = handed_back(list(back_wide.reshape(members, wide_rows, D)), "vocab")
     back_wide = placed_after(back_wide, "vocab")[:wides]
-    back_square = from_members(back_square)
     ortho_wide = power * ortho_wide + back_wide.astype(jnp.float32)
     ortho_square = power * ortho_square + back_square
     wide_scale = jnp.array([math.sqrt(FF / D), math.sqrt(FF / D), 1.0], jnp.float32)

time: 890 us -> 887 us (level)
  waiting for transfers between devices: 331 us -> 322 us
    unnamed x393 -> x405, local copies, waits for them, and re-layouts: 35.4 us -> 35.3 us
  transfers between devices with their start and end apart: 87 -> 87, of which waited for: 37 -> 36; matrix products, arithmetic and copies ran while one was open for 27% -> 27% of each run, Pallas kernels for 7% -> 7%
where the time goes in v11:
time: 887 us; the launch traced here: 879 us
  waiting for transfers between devices  322 us (36%)
  starting transfers between devices  141 us (16%)
  matrix products  134 us (15%)
  other arithmetic  113 us (13%)
  Pallas kernels  68.9 us (8%)
  local copies, waits for them, and re-layouts  68.8 us (8%)
  between operations  30.8 us (3%)
    ppermute x66, waiting for transfers between devices, turned(): lax.ppermute(values, axis, [(i, (i + step) % count) for i in range(count)])  198 us
    ppermute x66, starting transfers between devices, turned(): lax.ppermute(values, axis, [(i, (i + step) % count) for i in range(count)])  109 us
    all_to_all x5, waiting for transfers between devices, exchanged(): return lax.all_to_all(rows, ALL, 0, 0, tiled=True)  60 us
    all_gather x1, waiting for transfers between devices, body(): lax.all_gather(square_master.astype(jnp.bfloat16), ALL, axis=1, tiled=True)  38.6 us
    dot_general x14, matrix products, outer(): lax.dot_general(grads, inputs, (((0,), (0,)), ((), ())), preferred_elemen...  35.9 us
    unnamed x405, local copies, waits for them, and re-layouts  35.3 us
    dot_general x9, matrix products, back_dense(): return jnp.dot(grads, weight, preferred_element_type=jnp.float32)  32.1 us
    dot_general x10, matrix products, dense(): lax.dot_general(inputs, weight, (((1,), (1,)), ((), ())), preferred_eleme...  28.3 us
  transfers between devices with their start and end apart: 87, of which 36 were waited for; matrix products, arithmetic and copies ran while one was open for 27% of the time, Pallas kernels for 7%

profile of v11, /device:TPU:0, one launch (start us, length us, event | category | flops | bytes accessed | tf_op | source)
XLA Modules:
  0.0 878.6 jit_solution(10868813954794122814)
XLA Ops:
  19.5 7.3 all-to-all-start.4
  26.8 6.1 convert_element_type.423.table_ref
  35.4 6.8 fusion.67
  42.2 4.2 all-to-all-start.5
  55.6 45.7 %all-to-all-done.5 = bf16[32,24,1024]{2,1,0:T(8,128)(2,1)} async-done(((bf16[32,24,1024]{2,1,0:T(8,128)(2,1)}), bf16[32,24,1024]{2,1,0:T(8,128)(2,1)}, u32[]{:S(2)}, u32[]{:S(2)}) %all-to-all-start.5) | async-done | bytes 1572896 | tf_op jit(solution)/shard_map/all_to_all | solution.py:112
  104.7 38.6 %all-gather.3.cloned.1.call-done = bf16[7,1024,1024]{2,1,0:T(8,128)(2,1)} async-done(((bf16[7,32,1024]{2,1,0:T(8,128)(2,1)}), bf16[7,1024,1024]{2,1,0:T(8,128)(2,1)}) %all-gather.3.cloned.1.call-update) | async-done | bytes 14680080 | tf_op jit(solution)/shard_map/all_gather | solution.py:480
  146.4 5.7 fusion.172
  152.1 3.6 multiply_convert_fusion.4
  173.9 11.8 %collective-permute-start = (bf16[96,1024]{1,0:T(8,128)(2,1)S(1)}, bf16[96,1024]{1,0:T(8,128)(2,1)S(1)}, u32[]{:S(2)}, u32[]{:S(2)}) collective-permute-start(bf16[96,1024]{1,0:T(8,128)(2,1)S(1)} %multiply_convert_fusion.9), channel_id=1, source_target_pairs={{0,1},{1,2},{2,3},{3,0},{4,5},{5,6},{6,7},{7,4},{8,9},{9,10},{10,1... | collective-permute-start | bytes 589832 | tf_op jit(solution)/shard_map/ppermute | solution.py:122
  185.7 7.7 all-gather.5.cloned.1.call-done
  207.6 4.2 collective-permute-done.5
  211.8 7.8 collective-permute-done.4
  225.4 4.7 collective-permute-start.9
  256.7 3.6 collective-permute-done.18
  277.7 3.8 collective-permute-start.26
  287.2 23.1 %shard_map.313 = (bf16[2048,3072]{1,0:T(8,128)(2,1)}, f32[8,3072]{1,0:T(8,128)S(1)}) custom-call(s32[1,3072]{1,0:T(1,128)S(1)} %reshape.941.target_ref, bf16[3072,1024]{1,0:T(8,128)(2,1)S(1)} %copy-done, bf16[2048,1024]{1,0:T(8,128)(2,1)S(1)} %copy-done.34), custom_call_target="tpu_custom_call" | custom-call | flops 12884901888 | bytes 18874368 | tf_op jit(solution)/shard_map/pallas_call | solution.py:361
  314.2 7.5 all-to-all-done.6
  326.4 7.1 all-to-all-done.7
  336.6 10.4 %shard_map.315 = bf16[1536,1024]{1,0:T(8,128)(2,1)S(1)} custom-call(s32[1,3072]{1,0:T(1,128)S(1)} %reshape.941.target_ref, f32[1,3072]{1,0:T(1,128)S(1)} %get-tuple-element.474.scale_ref, f32[1,3072]{1,0:T(1,128)S(1)} %get-tuple-element.473.value_ref, bf16[2048,3072]{1,0:T(8,128)(2,1)} %get-tuple-element.263.shares_ref, bf16[2048,1024]{1,0:T(8,128)(2,1)} %get-tuple-element.713), custom_call_target="tpu_custom_call" | custom-call | flops 6442450944 | bytes 9437184 | tf_op jit(solution)/shard_map/pallas_call | solution.py:404
  348.8 10.3 %shard_map.314 = bf16[1536,1024]{1,0:T(8,128)(2,1)S(1)} custom-call(s32[1,3072]{1,0:T(1,128)S(1)} %reshape.941.target_ref, f32[1,3072]{1,0:T(1,128)S(1)} %get-tuple-element.474.scale_ref, f32[1,3072]{1,0:T(1,128)S(1)} %get-tuple-element.473.value_ref, bf16[2048,3072]{1,0:T(8,128)(2,1)} %get-tuple-element.263.shares_ref, bf16[2048,1024]{1,0:T(8,128)(2,1)} %get-tuple-element.713), custom_call_target="tpu_custom_call" | custom-call | flops 6442450944 | bytes 9437184 | tf_op jit(solution)/shard_map/pallas_call | solution.py:404
  366.7 17.5 %fusion.12 = f32[2048,1024]{1,0:T(8,128)} fusion(bf16[3072,1024]{1,0:T(8,128)(2,1)} %constant_dynamic-update-slice_fusion.answers_ref, bf16[2048,3072]{1,0:T(8,128)(2,1)S(1)} %bitcast.543, f32[3072]{0:T(1024)S(1)} %bitcast.460, f32[3072]{0:T(1024)S(1)} %bitcast.459, s32[3072]{0:T(1024)S(1)} %eq.420), kind=kOutput, calls=%fused_computation.35 | convolution fusion | flops 12910067712 | bytes 27299840 | tf_op jit(solution)/shard_map/dot_general | solution.py:655
  388.8 11.2 %collective-permute-done.30 = bf16[4,96,1024]{2,1,0:T(8,128)(2,1)S(1)} collective-permute-done((bf16[4,96,1024]{2,1,0:T(8,128)(2,1)S(1)}, bf16[4,96,1024]{2,1,0:T(8,128)(2,1)S(1)}, u32[]{:S(2)}, u32[]{:S(2)}) %collective-permute-start.30) | collective-permute-done | bytes 786464 | tf_op jit(solution)/shard_map/ppermute | solution.py:122
  404.7 5.9 collective-permute-done.37
  410.6 7.0 collective-permute-done.36
  418.5 3.7 collective-permute-start.40
  427.6 13.0 %collective-permute-done.39 = bf16[96,1024]{1,0:T(8,128)(2,1)S(1)} collective-permute-done((bf16[96,1024]{1,0:T(8,128)(2,1)S(1)}, bf16[96,1024]{1,0:T(8,128)(2,1)S(1)}, u32[]{:S(2)}, u32[]{:S(2)}) %collective-permute-start.39) | collective-permute-done | bytes 196640 | tf_op jit(solution)/shard_map/ppermute | solution.py:122
  463.6 5.1 collective-permute-done.43
  468.7 6.2 collective-permute-done.42
  502.3 7.5 multiply_reduce_fusion.1
  537.7 5.7 multiply_reduce_fusion.5
  545.2 3.7 fusion.35
  548.9 6.3 all-to-all-start.8
  557.5 5.1 all-to-all-done.8
  576.4 22.2 %collective-permute-done.49 = bf16[144,1024]{1,0:T(8,128)(2,1)S(1)} collective-permute-done((bf16[144,1024]{1,0:T(8,128)(2,1)S(1)}, bf16[144,1024]{1,0:T(8,128)(2,1)S(1)}, u32[]{:S(2)}, u32[]{:S(2)}) %collective-permute-start.49) | collective-permute-done | bytes 294944 | tf_op jit(solution)/shard_map/ppermute | solution.py:122
  598.6 30.1 %collective-permute-done.48 = bf16[144,1024]{1,0:T(8,128)(2,1)S(1)} collective-permute-done((bf16[144,1024]{1,0:T(8,128)(2,1)S(1)}, bf16[144,1024]{1,0:T(8,128)(2,1)S(1)}, u32[]{:S(2)}, u32[]{:S(2)}) %collective-permute-start.48) | collective-permute-done | bytes 294944 | tf_op jit(solution)/shard_map/ppermute | solution.py:122
  628.9 7.8 fusion.17
  636.6 12.3 %add.1000 = f32[2048,1024]{1,0:T(8,128)} add(f32[2048,1024]{1,0:T(8,128)} %fusion.12, f32[2048,1024]{1,0:T(8,128)} %fusion.17) | non-fusion elementwise | flops 2097152 | bytes 25165824 | tf_op jit(solution)/shard_map/add | solution.py:783
  649.0 4.2 reduce-scatter.5.cloned.1.call-done
  662.0 6.1 multiply_reduce_fusion
  668.1 5.2 collective-permute-done.46
  673.4 32.6 %collective-permute-done.45 = bf16[2,128,1024]{2,1,0:T(8,128)(2,1)} collective-permute-done((bf16[2,128,1024]{2,1,0:T(8,128)(2,1)}, bf16[2,128,1024]{2,1,0:T(8,128)(2,1)}, u32[]{:S(2)}, u32[]{:S(2)}) %collective-permute-start.45) | collective-permute-done | bytes 524320 | tf_op jit(solution)/shard_map/ppermute | solution.py:122
  712.6 4.0 all-to-all-start.10
  717.3 6.4 all-to-all-done.10
  750.3 5.3 collective-permute-done.60
  755.6 5.4 collective-permute-done.59
  771.0 5.0 collective-permute-done.62
  782.3 25.1 %shard_map.316 = bf16[1024,1024]{1,0:T(8,128)(2,1)S(1)} custom-call(s32[1]{0:T(128)} %bitcast.17.core_ref, bf16[512,1024]{1,0:T(8,128)(2,1)S(1)} %bitcast.458, bf16[512,1024]{1,0:T(8,128)(2,1)S(1)} %collective-permute-done.64.second_ref, f32[1024,1024]{1,0:T(8,128)S(1)} %fusion.174.square_ref), custom_call_target="tpu_custom_call" | custom-call | flops 19327352832 | bytes 6291456 | tf_op jit(solution)/shard_map/pallas_call | solution.py:306
  835.7 22.9 %add_multiply_fusion = (f32[2048,1024]{1,0:T(8,128)}, f32[2048,1024]{1,0:T(8,128)}, f32[2048,1024]{1,0:T(8,128)}) fusion(f32[2048,1024]{1,0:T(8,128)} %param.25, f32[]{:T(128)S(6)} %sub.276, f32[]{:T(128)S(6)} %sub.275, f32[2048,1024]{1,0:T(8,128)} %get-tuple-element.291, f32[]{:T(128)S(6)} %min.3, f32[2048,1024]{1,0:T(8,128)} %param.27, f32[2048,1024]{1,0:T(8,128)} %param.26), kind=kLoop, calls=%fused_computation.41 | loop fusion | flops 31457280 | bytes 58720268 | tf_op jit(solution)/shard_map/mul | solution.py:100
  (835 shorter events, 335.1 us)
Async XLA Ops:
  7.2 136.1 %all-gather.3.cloned.1.call-start = ((), (), s32[]{:S(2)}) async-start(), calls=%async_computation.13 | async-start | bytes 15138816 | tf_op jit(solution)/shard_map/all_gather | solution.py:480
  19.5 15.1 %all-to-all-start.4 = ((f32[32,1,349]{2,1,0:T(1,128)}), f32[32,1,349]{2,1,0:T(1,128)S(1)}, u32[]{:S(2)}, u32[]{:S(2)}) async-start(f32[32,1,349]{2,1,0:T(1,128)} %all_to_all.79), calls=%async_computation.4 | async-start | bytes 98304 | tf_op jit(solution)/shard_map/all_to_all | solution.py:112
  42.2 59.1 %all-to-all-start.5 = ((bf16[32,24,1024]{2,1,0:T(8,128)(2,1)}), bf16[32,24,1024]{2,1,0:T(8,128)(2,1)}, u32[]{:S(2)}, u32[]{:S(2)}) async-start(bf16[32,24,1024]{2,1,0:T(8,128)(2,1)} %bitcast.20), calls=%async_computation.5 | async-start | bytes 3145728 | tf_op jit(solution)/shard_map/all_to_all | solution.py:112
  46.5 146.9 %all-gather.5.cloned.1.call-start = ((), (), s32[]{:S(2)}) async-start(), calls=%async_computation.14 | async-start | bytes 7962624 | tf_op jit(solution)/shard_map/all_gather | solution.py:481
  171.8 21.6 %collective-permute-start.2 = (bf16[96,1024]{1,0:T(8,128)(2,1)S(1)}, bf16[96,1024]{1,0:T(8,128)(2,1)S(1)}, u32[]{:S(2)}, u32[]{:S(2)}) collective-permute-start(bf16[96,1024]{1,0:T(8,128)(2,1)S(1)} %multiply_convert_fusion.9), channel_id=1, source_target_pairs={{0,3},{1,0},{2,1},{3,2},{4,7},{5,4},{6,5},{7,6},{8,11},{9,8},{10,9... | collective-permute-start | bytes 589832 | tf_op jit(solution)/shard_map/ppermute | solution.py:122
  172.9 20.5 %collective-permute-start.1 = (bf16[96,1024]{1,0:T(8,128)(2,1)S(1)}, bf16[96,1024]{1,0:T(8,128)(2,1)S(1)}, u32[]{:S(2)}, u32[]{:S(2)}) collective-permute-start(bf16[96,1024]{1,0:T(8,128)(2,1)S(1)} %multiply_convert_fusion.9), channel_id=1, source_target_pairs={{0,2},{1,3},{2,0},{3,1},{4,6},{5,7},{6,4},{7,5},{8,10},{9,11},{10,... | collective-permute-start | bytes 589832 | tf_op jit(solution)/shard_map/ppermute | solution.py:122
  173.9 19.6 %collective-permute-start = (bf16[96,1024]{1,0:T(8,128)(2,1)S(1)}, bf16[96,1024]{1,0:T(8,128)(2,1)S(1)}, u32[]{:S(2)}, u32[]{:S(2)}) collective-permute-start(bf16[96,1024]{1,0:T(8,128)(2,1)S(1)} %multiply_convert_fusion.9), channel_id=1, source_target_pairs={{0,1},{1,2},{2,3},{3,0},{4,5},{5,6},{6,7},{7,4},{8,9},{9,10},{10,1... | collective-permute-start | bytes 589832 | tf_op jit(solution)/shard_map/ppermute | solution.py:122
  203.6 15.9 %collective-permute-start.4 = (bf16[96,1024]{1,0:T(8,128)(2,1)S(1)}, bf16[96,1024]{1,0:T(8,128)(2,1)S(1)}, u32[]{:S(2)}, u32[]{:S(2)}) collective-permute-start(bf16[96,1024]{1,0:T(8,128)(2,1)S(1)} %get-tuple-element.441), channel_id=1, source_target_pairs={{0,2},{1,3},{2,0},{3,1},{4,6},{5,7},{6,4},{7,5},{8,10},{9,11},{10,... | collective-permute-start | bytes 589832 | tf_op jit(solution)/shard_map/ppermute | solution.py:122
  222.8 14.9 %collective-permute-start.7 = (bf16[96,1024]{1,0:T(8,128)(2,1)S(1)}, bf16[96,1024]{1,0:T(8,128)(2,1)S(1)}, u32[]{:S(2)}, u32[]{:S(2)}) collective-permute-start(bf16[96,1024]{1,0:T(8,128)(2,1)S(1)} %get-tuple-element.380), channel_id=1, source_target_pairs={{0,16},{8,24},{16,0},{24,8},{1,17},{9,25},{17,1},{25,9},{2,18},{10... | collective-permute-start | bytes 589832 | tf_op jit(solution)/shard_map/ppermute | solution.py:122
  223.3 15.7 %collective-permute-start.8 = (bf16[96,1024]{1,0:T(8,128)(2,1)S(1)}, bf16[96,1024]{1,0:T(8,128)(2,1)S(1)}, u32[]{:S(2)}, u32[]{:S(2)}) collective-permute-start(bf16[96,1024]{1,0:T(8,128)(2,1)S(1)} %get-tuple-element.380), channel_id=1, source_target_pairs={{0,24},{8,0},{16,8},{24,16},{1,25},{9,1},{17,9},{25,17},{2,26},{10... | collective-permute-start | bytes 589832 | tf_op jit(solution)/shard_map/ppermute | solution.py:122
  256.2 15.0 %collective-permute-start.21 = (bf16[384,1024]{1,0:T(8,128)(2,1)S(1)}, bf16[384,1024]{1,0:T(8,128)(2,1)S(1)}, u32[]{:S(2)}, u32[]{:S(2)}) collective-permute-start(bf16[384,1024]{1,0:T(8,128)(2,1)S(1)} %pad_maximum_fusion.9), channel_id=1, source_target_pairs={{0,4},{4,0},{1,5},{5,1},{2,6},{6,2},{3,7},{7,3},{8,12},{12,8},{9,1... | collective-permute-start | bytes 2359304 | tf_op jit(solution)/shard_map/ppermute | solution.py:162
  256.2 15.9 %collective-permute-start.22 = (bf16[384,1024]{1,0:T(8,128)(2,1)S(1)}, bf16[384,1024]{1,0:T(8,128)(2,1)S(1)}, u32[]{:S(2)}, u32[]{:S(2)}) collective-permute-start(bf16[384,1024]{1,0:T(8,128)(2,1)S(1)} %pad_maximum_fusion.10), channel_id=1, source_target_pairs={{0,4},{4,0},{1,5},{5,1},{2,6},{6,2},{3,7},{7,3},{8,12},{12,8},{9,1... | collective-permute-start | bytes 2359304 | tf_op jit(solution)/shard_map/ppermute | solution.py:162
  275.7 34.5 %collective-permute-start.25 = (bf16[144,1024]{1,0:T(8,128)(2,1)S(1)}, bf16[144,1024]{1,0:T(8,128)(2,1)}, u32[]{:S(2)}, u32[]{:S(2)}) collective-permute-start(bf16[144,1024]{1,0:T(8,128)(2,1)S(1)} %get-tuple-element.410), channel_id=1, source_target_pairs={{0,1},{1,2},{2,3},{3,0},{4,5},{5,6},{6,7},{7,4},{8,9},{9,10},{10,1... | collective-permute-start | bytes 884744 | tf_op jit(solution)/shard_map/ppermute | solution.py:122
  277.7 32.6 %collective-permute-start.26 = (bf16[144,1024]{1,0:T(8,128)(2,1)S(1)}, bf16[144,1024]{1,0:T(8,128)(2,1)}, u32[]{:S(2)}, u32[]{:S(2)}) collective-permute-start(bf16[144,1024]{1,0:T(8,128)(2,1)S(1)} %get-tuple-element.409), channel_id=1, source_target_pairs={{0,2},{1,3},{2,0},{3,1},{4,6},{5,7},{6,4},{7,5},{8,10},{9,11},{10,... | collective-permute-start | bytes 884744 | tf_op jit(solution)/shard_map/ppermute | solution.py:122
  281.4 28.8 %collective-permute-start.27 = (bf16[144,1024]{1,0:T(8,128)(2,1)S(1)}, bf16[144,1024]{1,0:T(8,128)(2,1)}, u32[]{:S(2)}, u32[]{:S(2)}) collective-permute-start(bf16[144,1024]{1,0:T(8,128)(2,1)S(1)} %get-tuple-element.408), channel_id=1, source_target_pairs={{0,3},{1,0},{2,1},{3,2},{4,7},{5,4},{6,5},{7,6},{8,11},{9,8},{10,9... | collective-permute-start | bytes 884744 | tf_op jit(solution)/shard_map/ppermute | solution.py:122
  326.3 204.1 %reduce-scatter.3.cloned.1.call-start = ((), (), s32[]{:S(2)}) async-start(), calls=%async_computation.15 | async-start | bytes 7962624 | tf_op jit(solution)/shard_map/reduce_scatter | solution.py:752
  362.9 23.0 %collective-permute-start.31 = (bf16[4,96,1024]{2,1,0:T(8,128)(2,1)S(1)}, bf16[4,96,1024]{2,1,0:T(8,128)(2,1)S(1)}, u32[]{:S(2)}, u32[]{:S(2)}) collective-permute-start(bf16[4,96,1024]{2,1,0:T(8,128)(2,1)S(1)} %get-tuple-element.394), channel_id=1, source_target_pairs={{0,8},{8,16},{16,24},{24,0},{1,9},{9,17},{17,25},{25,1},{2,10},{10... | collective-permute-start | bytes 2359304 | tf_op jit(solution)/shard_map/ppermute | solution.py:122
  363.5 36.5 %collective-permute-start.30 = (bf16[4,96,1024]{2,1,0:T(8,128)(2,1)S(1)}, bf16[4,96,1024]{2,1,0:T(8,128)(2,1)S(1)}, u32[]{:S(2)}, u32[]{:S(2)}) collective-permute-start(bf16[4,96,1024]{2,1,0:T(8,128)(2,1)S(1)} %get-tuple-element.393), channel_id=1, source_target_pairs={{0,16},{8,24},{16,0},{24,8},{1,17},{9,25},{17,1},{25,9},{2,18},{10... | collective-permute-start | bytes 2359304 | tf_op jit(solution)/shard_map/ppermute | solution.py:122
  364.1 36.0 %collective-permute-start.29 = (bf16[4,96,1024]{2,1,0:T(8,128)(2,1)S(1)}, bf16[4,96,1024]{2,1,0:T(8,128)(2,1)S(1)}, u32[]{:S(2)}, u32[]{:S(2)}) collective-permute-start(bf16[4,96,1024]{2,1,0:T(8,128)(2,1)S(1)} %get-tuple-element.392), channel_id=1, source_target_pairs={{0,24},{8,0},{16,8},{24,16},{1,25},{9,1},{17,9},{25,17},{2,26},{10... | collective-permute-start | bytes 2359304 | tf_op jit(solution)/shard_map/ppermute | solution.py:122
  384.9 15.8 %collective-permute-start.32 = (bf16[2,32,1024]{2,1,0:T(8,128)(2,1)S(1)}, bf16[2,32,1024]{2,1,0:T(8,128)(2,1)S(1)}, u32[]{:S(2)}, u32[]{:S(2)}) collective-permute-start(bf16[2,32,1024]{2,1,0:T(8,128)(2,1)S(1)} %get-tuple-element.471), channel_id=1, source_target_pairs={{0,1},{1,2},{2,3},{3,0},{4,5},{5,6},{6,7},{7,4},{8,9},{9,10},{10,1... | collective-permute-start | bytes 393224 | tf_op jit(solution)/shard_map/ppermute | solution.py:122
  385.4 15.3 %collective-permute-start.33 = (bf16[2,32,1024]{2,1,0:T(8,128)(2,1)S(1)}, bf16[2,32,1024]{2,1,0:T(8,128)(2,1)S(1)}, u32[]{:S(2)}, u32[]{:S(2)}) collective-permute-start(bf16[2,32,1024]{2,1,0:T(8,128)(2,1)S(1)} %get-tuple-element.470), channel_id=1, source_target_pairs={{0,2},{1,3},{2,0},{3,1},{4,6},{5,7},{6,4},{7,5},{8,10},{9,11},{10,... | collective-permute-start | bytes 393224 | tf_op jit(solution)/shard_map/ppermute | solution.py:122
  385.9 14.8 %collective-permute-start.34 = (bf16[2,32,1024]{2,1,0:T(8,128)(2,1)S(1)}, bf16[2,32,1024]{2,1,0:T(8,128)(2,1)S(1)}, u32[]{:S(2)}, u32[]{:S(2)}) collective-permute-start(bf16[2,32,1024]{2,1,0:T(8,128)(2,1)S(1)} %get-tuple-element.469), channel_id=1, source_target_pairs={{0,3},{1,0},{2,1},{3,2},{4,7},{5,4},{6,5},{7,6},{8,11},{9,8},{10,9... | collective-permute-start | bytes 393224 | tf_op jit(solution)/shard_map/ppermute | solution.py:122
  401.4 16.2 %collective-permute-start.36 = (bf16[96,1024]{1,0:T(8,128)(2,1)S(1)}, bf16[96,1024]{1,0:T(8,128)(2,1)S(1)}, u32[]{:S(2)}, u32[]{:S(2)}) collective-permute-start(bf16[96,1024]{1,0:T(8,128)(2,1)S(1)} %get-tuple-element.438), channel_id=1, source_target_pairs={{0,2},{1,3},{2,0},{3,1},{4,6},{5,7},{6,4},{7,5},{8,10},{9,11},{10,... | collective-permute-start | bytes 589832 | tf_op jit(solution)/shard_map/ppermute | solution.py:122
  401.9 15.7 %collective-permute-start.35 = (bf16[96,1024]{1,0:T(8,128)(2,1)S(1)}, bf16[96,1024]{1,0:T(8,128)(2,1)S(1)}, u32[]{:S(2)}, u32[]{:S(2)}) collective-permute-start(bf16[96,1024]{1,0:T(8,128)(2,1)S(1)} %get-tuple-element.436), channel_id=1, source_target_pairs={{0,3},{1,0},{2,1},{3,2},{4,7},{5,4},{6,5},{7,6},{8,11},{9,8},{10,9... | collective-permute-start | bytes 589832 | tf_op jit(solution)/shard_map/ppermute | solution.py:122
  422.2 18.4 %collective-permute-start.39 = (bf16[96,1024]{1,0:T(8,128)(2,1)S(1)}, bf16[96,1024]{1,0:T(8,128)(2,1)S(1)}, u32[]{:S(2)}, u32[]{:S(2)}) collective-permute-start(bf16[96,1024]{1,0:T(8,128)(2,1)S(1)} %fusion.153), channel_id=1, source_target_pairs={{0,2},{1,3},{2,0},{3,1},{4,6},{5,7},{6,4},{7,5},{8,10},{9,11},{10,... | collective-permute-start | bytes 589832 | tf_op jit(solution)/shard_map/ppermute | solution.py:122
  424.0 16.7 %collective-permute-start.38 = (bf16[96,1024]{1,0:T(8,128)(2,1)S(1)}, bf16[96,1024]{1,0:T(8,128)(2,1)S(1)}, u32[]{:S(2)}, u32[]{:S(2)}) collective-permute-start(bf16[96,1024]{1,0:T(8,128)(2,1)S(1)} %fusion.153), channel_id=1, source_target_pairs={{0,1},{1,2},{2,3},{3,0},{4,5},{5,6},{6,7},{7,4},{8,9},{9,10},{10,1... | collective-permute-start | bytes 589832 | tf_op jit(solution)/shard_map/ppermute | solution.py:122
  451.9 201.3 %reduce-scatter.5.cloned.1.call-start = ((), (), s32[]{:S(2)}) async-start(), calls=%async_computation.16 | async-start | bytes 16515072 | tf_op jit(solution)/shard_map/reduce_scatter | solution.py:757
  459.0 15.9 %collective-permute-start.42 = (bf16[96,1024]{1,0:T(8,128)(2,1)S(1)}, bf16[96,1024]{1,0:T(8,128)(2,1)S(1)}, u32[]{:S(2)}, u32[]{:S(2)}) collective-permute-start(bf16[96,1024]{1,0:T(8,128)(2,1)S(1)} %get-tuple-element.435), channel_id=1, source_target_pairs={{0,2},{1,3},{2,0},{3,1},{4,6},{5,7},{6,4},{7,5},{8,10},{9,11},{10,... | collective-permute-start | bytes 589832 | tf_op jit(solution)/shard_map/ppermute | solution.py:122
  459.8 15.1 %collective-permute-start.41 = (bf16[96,1024]{1,0:T(8,128)(2,1)S(1)}, bf16[96,1024]{1,0:T(8,128)(2,1)S(1)}, u32[]{:S(2)}, u32[]{:S(2)}) collective-permute-start(bf16[96,1024]{1,0:T(8,128)(2,1)S(1)} %get-tuple-element.433), channel_id=1, source_target_pairs={{0,3},{1,0},{2,1},{3,2},{4,7},{5,4},{6,5},{7,6},{8,11},{9,8},{10,9... | collective-permute-start | bytes 589832 | tf_op jit(solution)/shard_map/ppermute | solution.py:122
  562.6 66.2 %all-to-all-start.9 = ((bf16[32,24,1024]{2,1,0:T(8,128)(2,1)}), bf16[32,24,1024]{2,1,0:T(8,128)(2,1)}, u32[]{:S(2)}, u32[]{:S(2)}) async-start(bf16[32,24,1024]{2,1,0:T(8,128)(2,1)} %bitcast.124), calls=%async_computation.11 | async-start | bytes 3145728 | tf_op jit(solution)/shard_map/all_to_all | solution.py:112
  569.6 29.0 %collective-permute-start.49 = (bf16[144,1024]{1,0:T(8,128)(2,1)S(1)}, bf16[144,1024]{1,0:T(8,128)(2,1)S(1)}, u32[]{:S(2)}, u32[]{:S(2)}) collective-permute-start(bf16[144,1024]{1,0:T(8,128)(2,1)S(1)} %get-tuple-element.430), channel_id=1, source_target_pairs={{0,3},{1,0},{2,1},{3,2},{4,7},{5,4},{6,5},{7,6},{8,11},{9,8},{10,9... | collective-permute-start | bytes 884744 | tf_op jit(solution)/shard_map/ppermute | solution.py:122
  573.2 55.5 %collective-permute-start.48 = (bf16[144,1024]{1,0:T(8,128)(2,1)S(1)}, bf16[144,1024]{1,0:T(8,128)(2,1)S(1)}, u32[]{:S(2)}, u32[]{:S(2)}) collective-permute-start(bf16[144,1024]{1,0:T(8,128)(2,1)S(1)} %get-tuple-element.432), channel_id=1, source_target_pairs={{0,2},{1,3},{2,0},{3,1},{4,6},{5,7},{6,4},{7,5},{8,10},{9,11},{10,... | collective-permute-start | bytes 884744 | tf_op jit(solution)/shard_map/ppermute | solution.py:122
  573.2 55.5 %collective-permute-start.47 = (bf16[144,1024]{1,0:T(8,128)(2,1)S(1)}, bf16[144,1024]{1,0:T(8,128)(2,1)S(1)}, u32[]{:S(2)}, u32[]{:S(2)}) collective-permute-start(bf16[144,1024]{1,0:T(8,128)(2,1)S(1)} %get-tuple-element.431), channel_id=1, source_target_pairs={{0,1},{1,2},{2,3},{3,0},{4,5},{5,6},{6,7},{7,4},{8,9},{9,10},{10,1... | collective-permute-start | bytes 884744 | tf_op jit(solution)/shard_map/ppermute | solution.py:122
  657.3 16.0 %collective-permute-start.46 = (bf16[2,128,1024]{2,1,0:T(8,128)(2,1)}, bf16[2,128,1024]{2,1,0:T(8,128)(2,1)}, u32[]{:S(2)}, u32[]{:S(2)}) collective-permute-start(bf16[2,128,1024]{2,1,0:T(8,128)(2,1)} %get-tuple-element.396), channel_id=1, source_target_pairs={{0,3},{1,0},{2,1},{3,2},{4,7},{5,4},{6,5},{7,6},{8,11},{9,8},{10,9... | collective-permute-start | bytes 1572872 | tf_op jit(solution)/shard_map/ppermute | solution.py:122
  660.7 45.3 %collective-permute-start.45 = (bf16[2,128,1024]{2,1,0:T(8,128)(2,1)}, bf16[2,128,1024]{2,1,0:T(8,128)(2,1)}, u32[]{:S(2)}, u32[]{:S(2)}) collective-permute-start(bf16[2,128,1024]{2,1,0:T(8,128)(2,1)} %get-tuple-element.397), channel_id=1, source_target_pairs={{0,2},{1,3},{2,0},{3,1},{4,6},{5,7},{6,4},{7,5},{8,10},{9,11},{10,... | collective-permute-start | bytes 1572872 | tf_op jit(solution)/shard_map/ppermute | solution.py:122
  660.7 45.3 %collective-permute-start.44 = (bf16[2,128,1024]{2,1,0:T(8,128)(2,1)}, bf16[2,128,1024]{2,1,0:T(8,128)(2,1)}, u32[]{:S(2)}, u32[]{:S(2)}) collective-permute-start(bf16[2,128,1024]{2,1,0:T(8,128)(2,1)} %get-tuple-element.395), channel_id=1, source_target_pairs={{0,1},{1,2},{2,3},{3,0},{4,5},{5,6},{6,7},{7,4},{8,9},{9,10},{10,1... | collective-permute-start | bytes 1572872 | tf_op jit(solution)/shard_map/ppermute | solution.py:122
  739.5 16.1 %collective-permute-start.60 = (bf16[128,1024]{1,0:T(8,128)(2,1)S(1)}, bf16[128,1024]{1,0:T(8,128)(2,1)S(1)}, u32[]{:S(2)}, u32[]{:S(2)}) collective-permute-start(bf16[128,1024]{1,0:T(8,128)(2,1)S(1)} %get-tuple-element.425), channel_id=1, source_target_pairs={{0,24},{8,0},{16,8},{24,16},{1,25},{9,1},{17,9},{25,17},{2,26},{10... | collective-permute-start | bytes 786440 | tf_op jit(solution)/shard_map/ppermute | solution.py:122
  741.9 19.0 %collective-permute-start.59 = (bf16[128,1024]{1,0:T(8,128)(2,1)S(1)}, bf16[128,1024]{1,0:T(8,128)(2,1)S(1)}, u32[]{:S(2)}, u32[]{:S(2)}) collective-permute-start(bf16[128,1024]{1,0:T(8,128)(2,1)S(1)} %get-tuple-element.426), channel_id=1, source_target_pairs={{0,16},{8,24},{16,0},{24,8},{1,17},{9,25},{17,1},{25,9},{2,18},{10... | collective-permute-start | bytes 786440 | tf_op jit(solution)/shard_map/ppermute | solution.py:122
  744.3 16.7 %collective-permute-start.58 = (bf16[128,1024]{1,0:T(8,128)(2,1)S(1)}, bf16[128,1024]{1,0:T(8,128)(2,1)S(1)}, u32[]{:S(2)}, u32[]{:S(2)}) collective-permute-start(bf16[128,1024]{1,0:T(8,128)(2,1)S(1)} %get-tuple-element.424), channel_id=1, source_target_pairs={{0,8},{8,16},{16,24},{24,0},{1,9},{9,17},{17,25},{25,1},{2,10},{10... | collective-permute-start | bytes 786440 | tf_op jit(solution)/shard_map/ppermute | solution.py:122
  750.2 29.5 %collective-permute-start.56 = (bf16[512,1024]{1,0:T(8,128)(2,1)S(1)}, bf16[512,1024]{1,0:T(8,128)(2,1)S(1)}, u32[]{:S(2)}, u32[]{:S(2)}) collective-permute-start(bf16[512,1024]{1,0:T(8,128)(2,1)S(1)} %pad_maximum_fusion.4), channel_id=1, source_target_pairs={{0,4},{4,0},{1,5},{5,1},{2,6},{6,2},{3,7},{7,3},{8,12},{12,8},{9,1... | collective-permute-start | bytes 3145736 | tf_op jit(solution)/shard_map/ppermute | solution.py:162
  767.5 43.4 %collective-permute-start.52 = (bf16[2,32,1024]{2,1,0:T(8,128)(2,1)}, bf16[2,32,1024]{2,1,0:T(8,128)(2,1)}, u32[]{:S(2)}, u32[]{:S(2)}) collective-permute-start(bf16[2,32,1024]{2,1,0:T(8,128)(2,1)} %get-tuple-element.451), channel_id=1, source_target_pairs={{0,3},{1,0},{2,1},{3,2},{4,7},{5,4},{6,5},{7,6},{8,11},{9,8},{10,9... | collective-permute-start | bytes 393224 | tf_op jit(solution)/shard_map/ppermute | solution.py:122
  770.4 40.5 %collective-permute-start.51 = (bf16[2,32,1024]{2,1,0:T(8,128)(2,1)}, bf16[2,32,1024]{2,1,0:T(8,128)(2,1)}, u32[]{:S(2)}, u32[]{:S(2)}) collective-permute-start(bf16[2,32,1024]{2,1,0:T(8,128)(2,1)} %get-tuple-element.452), channel_id=1, source_target_pairs={{0,2},{1,3},{2,0},{3,1},{4,6},{5,7},{6,4},{7,5},{8,10},{9,11},{10,... | collective-permute-start | bytes 393224 | tf_op jit(solution)/shard_map/ppermute | solution.py:122
  776.1 34.8 %collective-permute-start.50 = (bf16[2,32,1024]{2,1,0:T(8,128)(2,1)}, bf16[2,32,1024]{2,1,0:T(8,128)(2,1)}, u32[]{:S(2)}, u32[]{:S(2)}) collective-permute-start(bf16[2,32,1024]{2,1,0:T(8,128)(2,1)} %get-tuple-element.453), channel_id=1, source_target_pairs={{0,1},{1,2},{2,3},{3,0},{4,5},{5,6},{6,7},{7,4},{8,9},{9,10},{10,1... | collective-permute-start | bytes 393224 | tf_op jit(solution)/shard_map/ppermute | solution.py:122
  820.6 38.0 %collective-permute-start.75 = (bf16[144,1024]{1,0:T(8,128)(2,1)}, bf16[144,1024]{1,0:T(8,128)(2,1)S(1)}, u32[]{:S(2)}, u32[]{:S(2)}) collective-permute-start(bf16[144,1024]{1,0:T(8,128)(2,1)} %get-tuple-element.403), channel_id=1, source_target_pairs={{0,1},{1,2},{2,3},{3,0},{4,5},{5,6},{6,7},{7,4},{8,9},{9,10},{10,1... | collective-permute-start | bytes 884744 | tf_op jit(solution)/shard_map/ppermute | solution.py:122
  821.5 37.8 %collective-permute-start.74 = (bf16[144,1024]{1,0:T(8,128)(2,1)}, bf16[144,1024]{1,0:T(8,128)(2,1)}, u32[]{:S(2)}, u32[]{:S(2)}) collective-permute-start(bf16[144,1024]{1,0:T(8,128)(2,1)} %get-tuple-element.404), channel_id=1, source_target_pairs={{0,2},{1,3},{2,0},{3,1},{4,6},{5,7},{6,4},{7,5},{8,10},{9,11},{10,... | collective-permute-start | bytes 884744 | tf_op jit(solution)/shard_map/ppermute | solution.py:122
  824.8 34.5 %collective-permute-start.73 = (bf16[144,1024]{1,0:T(8,128)(2,1)S(1)}, bf16[144,1024]{1,0:T(8,128)(2,1)}, u32[]{:S(2)}, u32[]{:S(2)}) collective-permute-start(bf16[144,1024]{1,0:T(8,128)(2,1)S(1)} %get-tuple-element.405), channel_id=1, source_target_pairs={{0,3},{1,0},{2,1},{3,2},{4,7},{5,4},{6,5},{7,6},{8,11},{9,8},{10,9... | collective-permute-start | bytes 884744 | tf_op jit(solution)/shard_map/ppermute | solution.py:122
  832.4 31.3 %collective-permute-start.72 = (bf16[2,32,1024]{2,1,0:T(8,128)(2,1)}, bf16[2,32,1024]{2,1,0:T(8,128)(2,1)}, u32[]{:S(2)}, u32[]{:S(2)}) collective-permute-start(bf16[2,32,1024]{2,1,0:T(8,128)(2,1)} %get-tuple-element.459), channel_id=1, source_target_pairs={{0,3},{1,0},{2,1},{3,2},{4,7},{5,4},{6,5},{7,6},{8,11},{9,8},{10,9... | collective-permute-start | bytes 393224 | tf_op jit(solution)/shard_map/ppermute | solution.py:122
  835.7 27.9 %collective-permute-start.71 = (bf16[2,32,1024]{2,1,0:T(8,128)(2,1)}, bf16[2,32,1024]{2,1,0:T(8,128)(2,1)}, u32[]{:S(2)}, u32[]{:S(2)}) collective-permute-start(bf16[2,32,1024]{2,1,0:T(8,128)(2,1)} %get-tuple-element.460), channel_id=1, source_target_pairs={{0,2},{1,3},{2,0},{3,1},{4,6},{5,7},{6,4},{7,5},{8,10},{9,11},{10,... | collective-permute-start | bytes 393224 | tf_op jit(solution)/shard_map/ppermute | solution.py:122
  (230 other events, 3616.5 us)
Sparse Core Ops, SparseCore 0:
  11.6 131.6 all-gather.2
  145.8 47.5 all-gather.4
  452.0 63.6 reduce-scatter.2
  530.6 122.5 reduce-scatter.4

commit v12 on v11

--- a/solution.py
+++ b/solution.py
@@ -192,6 +192,21 @@
 
 def member_scatter(blocks):
     return added(handed_out(blocks, "vocab"))
+
+
+def member_scatter_halves(blocks):
+    if blocks.shape[0] != 4:
+        return member_scatter(blocks)
+    member = lax.axis_index("vocab")
+    near, half = member % 2, member // 2
+    far_first = (1 - half) * 2
+    neighbours = [(0, 1), (1, 0), (2, 3), (3, 2)]
+    across = [(0, 2), (2, 0), (1, 3), (3, 1)]
+    far = lax.ppermute(block_at(blocks, far_first + 1 - near), "vocab", neighbours)
+    far = added([block_at(blocks, far_first + near), far]).astype(jnp.bfloat16)
+    far = lax.ppermute(far, "vocab", across)
+    close = lax.ppermute(block_at(blocks, half * 2 + 1 - near), "vocab", neighbours)
+    return added([block_at(blocks, member), close, far])
 
 
 def onehot_rows(index, count):
@@ -755,7 +770,6 @@
     share_wide = share_wide_b.astype(jnp.float32)
     wide_grad_job = jnp.stack(handed_out(wide_by_member(share_wide_b), "vocab"))
     group_square = lax.psum_scatter(grad_square, DP, scatter_dimension=1, tiled=True)
-    square_grad_job = member_scatter(by_member(group_square))
 
     def from_members(values):
         values = values.reshape(per_member, members, square_rows, D).transpose(1, 0, 2, 3)
@@ -763,7 +777,6 @@
         values = values.transpose(1, 0, 2, 3).reshape(per_member * members, square_rows, D)
         return values[:squares].astype(jnp.float32)
 
-    share_square = from_members(square_grad_job)
 
     def returned(row_keys, count):
         rows = outer(onehot_rows(row_keys, count), grad_embed_b)
@@ -790,6 +803,9 @@
         ],
         axis=1,
     )
+    group_square, share_table = lax.optimization_barrier((group_square, share_table))
+    square_grad_job = member_scatter_halves(by_member(group_square))
+    share_square = from_members(square_grad_job)
     vector_notes = jnp.sum(exchanged(vector_notes), axis=0)
     share_vector = vector_notes[: vector_master.size].reshape(vector_master.shape)
     gains_total = vector_notes[vector_master.size :].reshape(grad_head_gains.shape)

time: 887 us -> 893 us (level); the launches traced: 879 us -> 904 us
  waiting for transfers between devices: 322 us -> 304 us
  blocking collectives: 0 us -> 15.2 us
  matrix products: 134 us -> 148 us
  starting transfers between devices: 141 us -> 150 us
    all_to_all x5 -> x8, waiting for transfers between devices: 60 us -> 108 us  [exchanged(): return lax.all_to_all(rows, ALL, 0, 0, tiled=True)]
    ppermute x66 -> x63, waiting for transfers between devices: 198 us -> 156 us  [turned(): lax.ppermute(values, axis, [(i, (i + step) % count) for i in range(count)])]
    all_gather x1, waiting for transfers between devices: 38.6 us -> 0.92 us  [body(): lax.all_gather(square_master.astype(jnp.bfloat16), ALL, axis=1, tiled=True)]
    ppermute x0 -> x3, waiting for transfers between devices: none -> 17.3 us  [the longest x1 13 us: member_scatter_halves(): lax.ppermute(block_at(blocks, half * 2 + 1 - near), 'vocab', neighbours)]
    all_to_all x0 -> x1, blocking collectives: none -> 15.2 us  [exchanged(): return lax.all_to_all(rows, ALL, 0, 0, tiled=True)]
    dot_general x14 -> x16, matrix products: 35.9 us -> 44.9 us  [outer(): lax.dot_general(grads, inputs, (((0,), (0,)), ((), ())), preferred_elemen...]
    all_to_all x5 -> x8, starting transfers between devices: 23.9 us -> 32.6 us  [exchanged(): return lax.all_to_all(rows, ALL, 0, 0, tiled=True)]
    ppermute x66 -> x63, starting transfers between devices: 109 us -> 104 us  [turned(): lax.ppermute(values, axis, [(i, (i + step) % count) for i in range(count)])]
  transfers between devices with their start and end apart: 87 -> 90, of which waited for: 36 -> 39; matrix products, arithmetic and copies ran while one was open for 27% -> 29% of each run, Pallas kernels for 7% -> 7%
where the time goes in v12:
time: 893 us; the launch traced here: 904 us
  waiting for transfers between devices  304 us (34%)
  starting transfers between devices  150 us (17%)
  matrix products  148 us (17%)
  other arithmetic  115 us (13%)
  local copies, waits for them, and re-layouts  73.4 us (8%)
  Pallas kernels  69.2 us (8%)
  between operations  30.6 us (3%)
  blocking collectives  15.2 us (2%)
    ppermute x63, waiting for transfers between devices, turned(): lax.ppermute(values, axis, [(i, (i + step) % count) for i in range(count)])  156 us
    all_to_all x8, waiting for transfers between devices, exchanged(): return lax.all_to_all(rows, ALL, 0, 0, tiled=True)  108 us
    ppermute x63, starting transfers between devices, turned(): lax.ppermute(values, axis, [(i, (i + step) % count) for i in range(count)])  104 us
    dot_general x16, matrix products, outer(): lax.dot_general(grads, inputs, (((0,), (0,)), ((), ())), preferred_elemen...  44.9 us
    unnamed x401, local copies, waits for them, and re-layouts  34.5 us
    all_to_all x8, starting transfers between devices, exchanged(): return lax.all_to_all(rows, ALL, 0, 0, tiled=True)  32.6 us
    dot_general x9, matrix products, back_dense(): return jnp.dot(grads, weight, preferred_element_type=jnp.float32)  30.6 us
    dot_general x10, matrix products, dense(): lax.dot_general(inputs, weight, (((1,), (1,)), ((), ())), preferred_eleme...  28.3 us
  transfers between devices with their start and end apart: 90, of which 39 were waited for; matrix products, arithmetic and copies ran while one was open for 29% of the time, Pallas kernels for 7%

profile of v12, /device:TPU:0, one launch (start us, length us, event | category | flops | bytes accessed | tf_op | source)
XLA Modules:
  0.0 904.4 jit_solution(14711790373565480088)
XLA Ops:
  19.5 7.3 all-to-all-start.4
  26.8 6.1 convert_element_type.432.table_ref
  35.3 6.8 fusion.67
  42.2 4.3 all-to-all-start.5
  55.6 45.7 %all-to-all-done.5 = bf16[32,24,1024]{2,1,0:T(8,128)(2,1)} async-done(((bf16[32,24,1024]{2,1,0:T(8,128)(2,1)}), bf16[32,24,1024]{2,1,0:T(8,128)(2,1)}, u32[]{:S(2)}, u32[]{:S(2)}) %all-to-all-start.5) | async-done | bytes 1572896 | tf_op jit(solution)/shard_map/all_to_all | solution.py:112
  103.7 49.1 %while.24 = (s32[]{:T(128)}, f32[512,1024]{1,0:T(8,128)S(1)}, s32[]{:T(128)}, s32[512]{0:T(512)S(1)}, s32[512]{0:T(512)S(1)}, /*index=5*/pred[512]{0:T(512)(128)...) while((s32[]{:T(128)}, f32[512,1024]{1,0:T(8,128)S(1)}, ...), condition=%wide.region_9.10_spmd, body=%wide.region_7.9_spmd.sunk | while | flops 1344147456 | bytes 11039421 | solution.py:544
  104.1 15.2 %all_to_all.113 = s32[32,8,1]{1,2,0:T(1,128)S(1)} all-to-all(s32[32,8,1]{1,2,0:T(1,128)S(1)} %bitcast.503), channel_id=1, replica_groups=mesh['chip'=4,'core'=2,'vocab'=4] {'chip','core','vocab'}, dimensions={0} | all-to-all | bytes 2048 | tf_op jit(solution)/shard_map/while/body/all_to_all | solution.py:112
  120.6 4.3 fusion.232
  127.5 24.3 %all-to-all-done.1 = bf16[32,8,1024]{2,1,0:T(8,128)(2,1)S(1)} async-done(((bf16[32,8,1024]{2,1,0:T(8,128)(2,1)}), bf16[32,8,1024]{2,1,0:T(8,128)(2,1)S(1)}, u32[]{:S(2)}, u32[]{:S(2)}) %all-to-all-start.1) | async-done | bytes 524320 | tf_op jit(solution)/shard_map/while/body/all_to_all | solution.py:112
  157.4 5.7 fusion.171
  186.4 10.4 %collective-permute-start = (bf16[96,1024]{1,0:T(8,128)(2,1)S(1)}, bf16[96,1024]{1,0:T(8,128)(2,1)S(1)}, u32[]{:S(2)}, u32[]{:S(2)}) collective-permute-start(bf16[96,1024]{1,0:T(8,128)(2,1)S(1)} %multiply_convert_fusion.9), channel_id=1, source_target_pairs={{0,1},{1,2},{2,3},{3,0},{4,5},{5,6},{6,7},{7,4},{8,9},{9,10},{10,1... | collective-permute-start | bytes 589832 | tf_op jit(solution)/shard_map/ppermute | solution.py:122
  196.9 7.7 all-gather.5.cloned.1.call-done
  218.8 4.2 collective-permute-done.5
  223.0 7.8 collective-permute-done.4
  236.6 4.7 collective-permute-start.9
  288.9 3.8 collective-permute-start.26
  298.4 23.1 %shard_map.313 = (bf16[2048,3072]{1,0:T(8,128)(2,1)}, f32[8,3072]{1,0:T(8,128)S(1)}) custom-call(s32[1,3072]{1,0:T(1,128)S(1)} %reshape.943.target_ref, bf16[3072,1024]{1,0:T(8,128)(2,1)S(1)} %copy-done, bf16[2048,1024]{1,0:T(8,128)(2,1)S(1)} %copy-done.35), custom_call_target="tpu_custom_call" | custom-call | flops 12884901888 | bytes 18874368 | tf_op jit(solution)/shard_map/pallas_call | solution.py:376
  325.6 7.5 all-to-all-done.6
  337.7 7.0 all-to-all-done.7
  347.9 10.4 %shard_map.315 = bf16[1536,1024]{1,0:T(8,128)(2,1)S(1)} custom-call(s32[1,3072]{1,0:T(1,128)S(1)} %reshape.943.target_ref, f32[1,3072]{1,0:T(1,128)S(1)} %get-tuple-element.477.scale_ref, f32[1,3072]{1,0:T(1,128)S(1)} %get-tuple-element.476.value_ref, bf16[2048,3072]{1,0:T(8,128)(2,1)} %get-tuple-element.265.shares_ref, bf16[2048,1024]{1,0:T(8,128)(2,1)} %get-tuple-element.716), custom_call_target="tpu_custom_call" | custom-call | flops 6442450944 | bytes 9437184 | tf_op jit(solution)/shard_map/pallas_call | solution.py:419
  360.0 10.3 %shard_map.314 = bf16[1536,1024]{1,0:T(8,128)(2,1)S(1)} custom-call(s32[1,3072]{1,0:T(1,128)S(1)} %reshape.943.target_ref, f32[1,3072]{1,0:T(1,128)S(1)} %get-tuple-element.477.scale_ref, f32[1,3072]{1,0:T(1,128)S(1)} %get-tuple-element.476.value_ref, bf16[2048,3072]{1,0:T(8,128)(2,1)} %get-tuple-element.265.shares_ref, bf16[2048,1024]{1,0:T(8,128)(2,1)} %get-tuple-element.716), custom_call_target="tpu_custom_call" | custom-call | flops 6442450944 | bytes 9437184 | tf_op jit(solution)/shard_map/pallas_call | solution.py:419
  377.9 17.6 %fusion.12 = f32[2048,1024]{1,0:T(8,128)} fusion(bf16[3072,1024]{1,0:T(8,128)(2,1)} %constant_dynamic-update-slice_fusion.answers_ref, bf16[2048,3072]{1,0:T(8,128)(2,1)S(1)} %bitcast.559, f32[3072]{0:T(1024)S(1)} %bitcast.470, f32[3072]{0:T(1024)S(1)} %bitcast.469, s32[3072]{0:T(1024)S(1)} %eq.421), kind=kOutput, calls=%fused_computation.35 | convolution fusion | flops 12910067712 | bytes 27299840 | tf_op jit(solution)/shard_map/dot_general | solution.py:670
  400.1 11.2 %collective-permute-done.30 = bf16[4,96,1024]{2,1,0:T(8,128)(2,1)S(1)} collective-permute-done((bf16[4,96,1024]{2,1,0:T(8,128)(2,1)S(1)}, bf16[4,96,1024]{2,1,0:T(8,128)(2,1)S(1)}, u32[]{:S(2)}, u32[]{:S(2)}) %collective-permute-start.30) | collective-permute-done | bytes 786464 | tf_op jit(solution)/shard_map/ppermute | solution.py:122
  415.9 5.9 collective-permute-done.37
  421.8 7.0 collective-permute-done.36
  438.9 13.0 %collective-permute-done.39 = bf16[96,1024]{1,0:T(8,128)(2,1)S(1)} collective-permute-done((bf16[96,1024]{1,0:T(8,128)(2,1)S(1)}, bf16[96,1024]{1,0:T(8,128)(2,1)S(1)}, u32[]{:S(2)}, u32[]{:S(2)}) %collective-permute-start.39) | collective-permute-done | bytes 196640 | tf_op jit(solution)/shard_map/ppermute | solution.py:122
  474.8 5.1 collective-permute-done.43
  479.9 6.2 collective-permute-done.42
  512.0 8.4 multiply_reduce_fusion.1
  554.2 7.7 all-to-all-start.8
  575.1 19.5 %collective-permute-done.46 = bf16[144,1024]{1,0:T(8,128)(2,1)S(1)} collective-permute-done((bf16[144,1024]{1,0:T(8,128)(2,1)}, bf16[144,1024]{1,0:T(8,128)(2,1)S(1)}, u32[]{:S(2)}, u32[]{:S(2)}) %collective-permute-start.46) | collective-permute-done | bytes 294944 | tf_op jit(solution)/shard_map/ppermute | solution.py:122
  594.6 30.1 %collective-permute-done.45 = bf16[144,1024]{1,0:T(8,128)(2,1)} collective-permute-done((bf16[144,1024]{1,0:T(8,128)(2,1)}, bf16[144,1024]{1,0:T(8,128)(2,1)}, u32[]{:S(2)}, u32[]{:S(2)}) %collective-permute-start.45) | collective-permute-done | bytes 294944 | tf_op jit(solution)/shard_map/ppermute | solution.py:122
  626.9 7.3 fusion.17
  634.2 12.3 %add.1018 = f32[2048,1024]{1,0:T(8,128)} add(f32[2048,1024]{1,0:T(8,128)} %fusion.12, f32[2048,1024]{1,0:T(8,128)} %fusion.17) | non-fusion elementwise | flops 2097152 | bytes 25165824 | tf_op jit(solution)/shard_map/add | solution.py:796
  646.4 36.0 %while.25 = (s32[]{:T(128)}, f32[2048,1024]{1,0:T(8,128)}, s32[]{:T(128)}, s32[512]{0:T(512)S(1)}, s32[512]{0:T(512)S(1)}, /*index=5*/pred[512]{0:T(512)(128)(4,...) while((s32[]{:T(128)}, f32[2048,1024]{1,0:T(8,128)}, ...), condition=%wide.region_39.40_spmd, body=%wide.region_37.39_spmd.sunk | while | flops 1345720320 | bytes 20508380 | solution.py:795
  651.6 5.7 all-to-all-done.2
  661.2 13.1 %all-to-all-done.3 = bf16[32,8,1024]{2,1,0:T(8,128)(2,1)S(1)} async-done(((bf16[32,8,1024]{2,1,0:T(8,128)(2,1)}), bf16[32,8,1024]{2,1,0:T(8,128)(2,1)S(1)}, u32[]{:S(2)}, u32[]{:S(2)}) %all-to-all-start.3) | async-done | bytes 524320 | tf_op jit(solution)/shard_map/while/body/all_to_all | solution.py:112
  674.3 8.2 convolution_add_fusion.5
  693.2 10.4 %all-to-all-done.9 = f32[32,1,352]{2,1,0:T(1,128)S(1)} async-done(((f32[32,1,352]{2,1,0:T(1,128)}), f32[32,1,352]{2,1,0:T(1,128)S(1)}, u32[]{:S(2)}, u32[]{:S(2)}) %all-to-all-start.9) | async-done | bytes 45088 | tf_op jit(solution)/shard_map/all_to_all | solution.py:112
  709.8 6.2 multiply_reduce_fusion
  716.0 13.0 %collective-permute-done.47 = bf16[2,128,1024]{2,1,0:T(8,128)(2,1)S(1)} collective-permute-done((bf16[2,128,1024]{2,1,0:T(8,128)(2,1)S(1)}, bf16[2,128,1024]{2,1,0:T(8,128)(2,1)S(1)}, u32[]{:S(2)}, u32[]{:S(2)}) %collective-permute-start.47) | collective-permute-done | bytes 524320 | tf_op jit(solution)/shard_map/ppermute | solution.py:208
  728.9 4.4 collective-permute-done.49
  742.3 6.4 all-to-all-done.10
  776.3 4.5 collective-permute-done.60
  780.8 5.4 collective-permute-done.59
  796.2 4.9 collective-permute-done.62
  807.3 25.3 %shard_map.316 = bf16[1024,1024]{1,0:T(8,128)(2,1)S(1)} custom-call(s32[1]{0:T(128)} %bitcast.17.core_ref, bf16[512,1024]{1,0:T(8,128)(2,1)S(1)} %bitcast.468, bf16[512,1024]{1,0:T(8,128)(2,1)S(1)} %collective-permute-done.64.second_ref, f32[1024,1024]{1,0:T(8,128)S(1)} %fusion.173.square_ref), custom_call_target="tpu_custom_call" | custom-call | flops 19327352832 | bytes 6291456 | tf_op jit(solution)/shard_map/pallas_call | solution.py:321
  861.5 23.0 %add_multiply_fusion = (f32[2048,1024]{1,0:T(8,128)}, f32[2048,1024]{1,0:T(8,128)}, f32[2048,1024]{1,0:T(8,128)}) fusion(f32[2048,1024]{1,0:T(8,128)} %param.25, f32[]{:T(128)S(6)} %sub.292, f32[]{:T(128)S(6)} %sub.291, f32[2048,1024]{1,0:T(8,128)} %get-tuple-element.295, f32[]{:T(128)S(6)} %min.3, f32[2048,1024]{1,0:T(8,128)} %param.27, f32[2048,1024]{1,0:T(8,128)} %param.26), kind=kLoop, calls=%fused_computation.41 | loop fusion | flops 31457280 | bytes 58720268 | tf_op jit(solution)/shard_map/mul | solution.py:100
  (857 shorter events, 375.0 us)
Async XLA Ops:
  7.2 147.2 %all-gather.3.cloned.1.call-start = ((), (), s32[]{:S(2)}) async-start(), calls=%async_computation.13 | async-start | bytes 15138816 | tf_op jit(solution)/shard_map/all_gather | solution.py:495
  19.5 15.1 %all-to-all-start.4 = ((f32[32,1,349]{2,1,0:T(1,128)}), f32[32,1,349]{2,1,0:T(1,128)S(1)}, u32[]{:S(2)}, u32[]{:S(2)}) async-start(f32[32,1,349]{2,1,0:T(1,128)} %all_to_all.79), calls=%async_computation.4 | async-start | bytes 98304 | tf_op jit(solution)/shard_map/all_to_all | solution.py:112
  42.2 59.1 %all-to-all-start.5 = ((bf16[32,24,1024]{2,1,0:T(8,128)(2,1)}), bf16[32,24,1024]{2,1,0:T(8,128)(2,1)}, u32[]{:S(2)}, u32[]{:S(2)}) async-start(bf16[32,24,1024]{2,1,0:T(8,128)(2,1)} %bitcast.20), calls=%async_computation.5 | async-start | bytes 3145728 | tf_op jit(solution)/shard_map/all_to_all | solution.py:112
  46.5 158.2 %all-gather.5.cloned.1.call-start = ((), (), s32[]{:S(2)}) async-start(), calls=%async_computation.14 | async-start | bytes 7962624 | tf_op jit(solution)/shard_map/all_gather | solution.py:496
  124.9 26.9 %all-to-all-start.1 = ((bf16[32,8,1024]{2,1,0:T(8,128)(2,1)}), bf16[32,8,1024]{2,1,0:T(8,128)(2,1)S(1)}, u32[]{:S(2)}, u32[]{:S(2)}) async-start(bf16[32,8,1024]{2,1,0:T(8,128)(2,1)} %fusion.232), calls=%async_computation.1 | async-start | bytes 1048576 | tf_op jit(solution)/shard_map/while/body/all_to_all | solution.py:112
  182.9 21.8 %collective-permute-start.2 = (bf16[96,1024]{1,0:T(8,128)(2,1)S(1)}, bf16[96,1024]{1,0:T(8,128)(2,1)S(1)}, u32[]{:S(2)}, u32[]{:S(2)}) collective-permute-start(bf16[96,1024]{1,0:T(8,128)(2,1)S(1)} %multiply_convert_fusion.9), channel_id=1, source_target_pairs={{0,3},{1,0},{2,1},{3,2},{4,7},{5,4},{6,5},{7,6},{8,11},{9,8},{10,9... | collective-permute-start | bytes 589832 | tf_op jit(solution)/shard_map/ppermute | solution.py:122
  184.9 19.8 %collective-permute-start.1 = (bf16[96,1024]{1,0:T(8,128)(2,1)S(1)}, bf16[96,1024]{1,0:T(8,128)(2,1)S(1)}, u32[]{:S(2)}, u32[]{:S(2)}) collective-permute-start(bf16[96,1024]{1,0:T(8,128)(2,1)S(1)} %multiply_convert_fusion.9), channel_id=1, source_target_pairs={{0,2},{1,3},{2,0},{3,1},{4,6},{5,7},{6,4},{7,5},{8,10},{9,11},{10,... | collective-permute-start | bytes 589832 | tf_op jit(solution)/shard_map/ppermute | solution.py:122
  186.4 18.2 %collective-permute-start = (bf16[96,1024]{1,0:T(8,128)(2,1)S(1)}, bf16[96,1024]{1,0:T(8,128)(2,1)S(1)}, u32[]{:S(2)}, u32[]{:S(2)}) collective-permute-start(bf16[96,1024]{1,0:T(8,128)(2,1)S(1)} %multiply_convert_fusion.9), channel_id=1, source_target_pairs={{0,1},{1,2},{2,3},{3,0},{4,5},{5,6},{6,7},{7,4},{8,9},{9,10},{10,1... | collective-permute-start | bytes 589832 | tf_op jit(solution)/shard_map/ppermute | solution.py:122
  214.8 15.9 %collective-permute-start.4 = (bf16[96,1024]{1,0:T(8,128)(2,1)S(1)}, bf16[96,1024]{1,0:T(8,128)(2,1)S(1)}, u32[]{:S(2)}, u32[]{:S(2)}) collective-permute-start(bf16[96,1024]{1,0:T(8,128)(2,1)S(1)} %get-tuple-element.444), channel_id=1, source_target_pairs={{0,2},{1,3},{2,0},{3,1},{4,6},{5,7},{6,4},{7,5},{8,10},{9,11},{10,... | collective-permute-start | bytes 589832 | tf_op jit(solution)/shard_map/ppermute | solution.py:122
  234.6 15.8 %collective-permute-start.8 = (bf16[96,1024]{1,0:T(8,128)(2,1)S(1)}, bf16[96,1024]{1,0:T(8,128)(2,1)S(1)}, u32[]{:S(2)}, u32[]{:S(2)}) collective-permute-start(bf16[96,1024]{1,0:T(8,128)(2,1)S(1)} %get-tuple-element.382), channel_id=1, source_target_pairs={{0,24},{8,0},{16,8},{24,16},{1,25},{9,1},{17,9},{25,17},{2,26},{10... | collective-permute-start | bytes 589832 | tf_op jit(solution)/shard_map/ppermute | solution.py:122
  267.4 15.0 %collective-permute-start.21 = (bf16[384,1024]{1,0:T(8,128)(2,1)S(1)}, bf16[384,1024]{1,0:T(8,128)(2,1)S(1)}, u32[]{:S(2)}, u32[]{:S(2)}) collective-permute-start(bf16[384,1024]{1,0:T(8,128)(2,1)S(1)} %pad_maximum_fusion.9), channel_id=1, source_target_pairs={{0,4},{4,0},{1,5},{5,1},{2,6},{6,2},{3,7},{7,3},{8,12},{12,8},{9,1... | collective-permute-start | bytes 2359304 | tf_op jit(solution)/shard_map/ppermute | solution.py:162
  267.4 15.9 %collective-permute-start.22 = (bf16[384,1024]{1,0:T(8,128)(2,1)S(1)}, bf16[384,1024]{1,0:T(8,128)(2,1)S(1)}, u32[]{:S(2)}, u32[]{:S(2)}) collective-permute-start(bf16[384,1024]{1,0:T(8,128)(2,1)S(1)} %pad_maximum_fusion.10), channel_id=1, source_target_pairs={{0,4},{4,0},{1,5},{5,1},{2,6},{6,2},{3,7},{7,3},{8,12},{12,8},{9,1... | collective-permute-start | bytes 2359304 | tf_op jit(solution)/shard_map/ppermute | solution.py:162
  286.9 34.6 %collective-permute-start.25 = (bf16[144,1024]{1,0:T(8,128)(2,1)S(1)}, bf16[144,1024]{1,0:T(8,128)(2,1)}, u32[]{:S(2)}, u32[]{:S(2)}) collective-permute-start(bf16[144,1024]{1,0:T(8,128)(2,1)S(1)} %get-tuple-element.413), channel_id=1, source_target_pairs={{0,1},{1,2},{2,3},{3,0},{4,5},{5,6},{6,7},{7,4},{8,9},{9,10},{10,1... | collective-permute-start | bytes 884744 | tf_op jit(solution)/shard_map/ppermute | solution.py:122
  288.9 32.6 %collective-permute-start.26 = (bf16[144,1024]{1,0:T(8,128)(2,1)S(1)}, bf16[144,1024]{1,0:T(8,128)(2,1)}, u32[]{:S(2)}, u32[]{:S(2)}) collective-permute-start(bf16[144,1024]{1,0:T(8,128)(2,1)S(1)} %get-tuple-element.412), channel_id=1, source_target_pairs={{0,2},{1,3},{2,0},{3,1},{4,6},{5,7},{6,4},{7,5},{8,10},{9,11},{10,... | collective-permute-start | bytes 884744 | tf_op jit(solution)/shard_map/ppermute | solution.py:122
  292.7 28.9 %collective-permute-start.27 = (bf16[144,1024]{1,0:T(8,128)(2,1)S(1)}, bf16[144,1024]{1,0:T(8,128)(2,1)}, u32[]{:S(2)}, u32[]{:S(2)}) collective-permute-start(bf16[144,1024]{1,0:T(8,128)(2,1)S(1)} %get-tuple-element.411), channel_id=1, source_target_pairs={{0,3},{1,0},{2,1},{3,2},{4,7},{5,4},{6,5},{7,6},{8,11},{9,8},{10,9... | collective-permute-start | bytes 884744 | tf_op jit(solution)/shard_map/ppermute | solution.py:122
  337.6 203.5 %reduce-scatter.3.cloned.1.call-start = ((), (), s32[]{:S(2)}) async-start(), calls=%async_computation.15 | async-start | bytes 7962624 | tf_op jit(solution)/shard_map/reduce_scatter | solution.py:767
  374.2 23.1 %collective-permute-start.31 = (bf16[4,96,1024]{2,1,0:T(8,128)(2,1)S(1)}, bf16[4,96,1024]{2,1,0:T(8,128)(2,1)S(1)}, u32[]{:S(2)}, u32[]{:S(2)}) collective-permute-start(bf16[4,96,1024]{2,1,0:T(8,128)(2,1)S(1)} %get-tuple-element.398), channel_id=1, source_target_pairs={{0,8},{8,16},{16,24},{24,0},{1,9},{9,17},{17,25},{25,1},{2,10},{10... | collective-permute-start | bytes 2359304 | tf_op jit(solution)/shard_map/ppermute | solution.py:122
  374.8 36.5 %collective-permute-start.30 = (bf16[4,96,1024]{2,1,0:T(8,128)(2,1)S(1)}, bf16[4,96,1024]{2,1,0:T(8,128)(2,1)S(1)}, u32[]{:S(2)}, u32[]{:S(2)}) collective-permute-start(bf16[4,96,1024]{2,1,0:T(8,128)(2,1)S(1)} %get-tuple-element.397), channel_id=1, source_target_pairs={{0,16},{8,24},{16,0},{24,8},{1,17},{9,25},{17,1},{25,9},{2,18},{10... | collective-permute-start | bytes 2359304 | tf_op jit(solution)/shard_map/ppermute | solution.py:122
  375.3 36.0 %collective-permute-start.29 = (bf16[4,96,1024]{2,1,0:T(8,128)(2,1)S(1)}, bf16[4,96,1024]{2,1,0:T(8,128)(2,1)S(1)}, u32[]{:S(2)}, u32[]{:S(2)}) collective-permute-start(bf16[4,96,1024]{2,1,0:T(8,128)(2,1)S(1)} %get-tuple-element.396), channel_id=1, source_target_pairs={{0,24},{8,0},{16,8},{24,16},{1,25},{9,1},{17,9},{25,17},{2,26},{10... | collective-permute-start | bytes 2359304 | tf_op jit(solution)/shard_map/ppermute | solution.py:122
  396.2 15.8 %collective-permute-start.32 = (bf16[2,32,1024]{2,1,0:T(8,128)(2,1)S(1)}, bf16[2,32,1024]{2,1,0:T(8,128)(2,1)S(1)}, u32[]{:S(2)}, u32[]{:S(2)}) collective-permute-start(bf16[2,32,1024]{2,1,0:T(8,128)(2,1)S(1)} %get-tuple-element.474), channel_id=1, source_target_pairs={{0,1},{1,2},{2,3},{3,0},{4,5},{5,6},{6,7},{7,4},{8,9},{9,10},{10,1... | collective-permute-start | bytes 393224 | tf_op jit(solution)/shard_map/ppermute | solution.py:122
  396.7 15.3 %collective-permute-start.33 = (bf16[2,32,1024]{2,1,0:T(8,128)(2,1)S(1)}, bf16[2,32,1024]{2,1,0:T(8,128)(2,1)S(1)}, u32[]{:S(2)}, u32[]{:S(2)}) collective-permute-start(bf16[2,32,1024]{2,1,0:T(8,128)(2,1)S(1)} %get-tuple-element.473), channel_id=1, source_target_pairs={{0,2},{1,3},{2,0},{3,1},{4,6},{5,7},{6,4},{7,5},{8,10},{9,11},{10,... | collective-permute-start | bytes 393224 | tf_op jit(solution)/shard_map/ppermute | solution.py:122
  412.6 16.2 %collective-permute-start.36 = (bf16[96,1024]{1,0:T(8,128)(2,1)S(1)}, bf16[96,1024]{1,0:T(8,128)(2,1)S(1)}, u32[]{:S(2)}, u32[]{:S(2)}) collective-permute-start(bf16[96,1024]{1,0:T(8,128)(2,1)S(1)} %get-tuple-element.441), channel_id=1, source_target_pairs={{0,2},{1,3},{2,0},{3,1},{4,6},{5,7},{6,4},{7,5},{8,10},{9,11},{10,... | collective-permute-start | bytes 589832 | tf_op jit(solution)/shard_map/ppermute | solution.py:122
  413.2 15.6 %collective-permute-start.35 = (bf16[96,1024]{1,0:T(8,128)(2,1)S(1)}, bf16[96,1024]{1,0:T(8,128)(2,1)S(1)}, u32[]{:S(2)}, u32[]{:S(2)}) collective-permute-start(bf16[96,1024]{1,0:T(8,128)(2,1)S(1)} %get-tuple-element.439), channel_id=1, source_target_pairs={{0,3},{1,0},{2,1},{3,2},{4,7},{5,4},{6,5},{7,6},{8,11},{9,8},{10,9... | collective-permute-start | bytes 589832 | tf_op jit(solution)/shard_map/ppermute | solution.py:122
  433.5 18.4 %collective-permute-start.39 = (bf16[96,1024]{1,0:T(8,128)(2,1)S(1)}, bf16[96,1024]{1,0:T(8,128)(2,1)S(1)}, u32[]{:S(2)}, u32[]{:S(2)}) collective-permute-start(bf16[96,1024]{1,0:T(8,128)(2,1)S(1)} %fusion.153), channel_id=1, source_target_pairs={{0,2},{1,3},{2,0},{3,1},{4,6},{5,7},{6,4},{7,5},{8,10},{9,11},{10,... | collective-permute-start | bytes 589832 | tf_op jit(solution)/shard_map/ppermute | solution.py:122
  435.2 16.7 %collective-permute-start.38 = (bf16[96,1024]{1,0:T(8,128)(2,1)S(1)}, bf16[96,1024]{1,0:T(8,128)(2,1)S(1)}, u32[]{:S(2)}, u32[]{:S(2)}) collective-permute-start(bf16[96,1024]{1,0:T(8,128)(2,1)S(1)} %fusion.153), channel_id=1, source_target_pairs={{0,1},{1,2},{2,3},{3,0},{4,5},{5,6},{6,7},{7,4},{8,9},{9,10},{10,1... | collective-permute-start | bytes 589832 | tf_op jit(solution)/shard_map/ppermute | solution.py:122
  463.1 219.3 %reduce-scatter.5.cloned.1.call-start = ((), (), s32[]{:S(2)}) async-start(), calls=%async_computation.16 | async-start | bytes 16515072 | tf_op jit(solution)/shard_map/reduce_scatter | solution.py:772
  470.2 15.9 %collective-permute-start.42 = (bf16[96,1024]{1,0:T(8,128)(2,1)S(1)}, bf16[96,1024]{1,0:T(8,128)(2,1)S(1)}, u32[]{:S(2)}, u32[]{:S(2)}) collective-permute-start(bf16[96,1024]{1,0:T(8,128)(2,1)S(1)} %get-tuple-element.438), channel_id=1, source_target_pairs={{0,2},{1,3},{2,0},{3,1},{4,6},{5,7},{6,4},{7,5},{8,10},{9,11},{10,... | collective-permute-start | bytes 589832 | tf_op jit(solution)/shard_map/ppermute | solution.py:122
  471.0 15.1 %collective-permute-start.41 = (bf16[96,1024]{1,0:T(8,128)(2,1)S(1)}, bf16[96,1024]{1,0:T(8,128)(2,1)S(1)}, u32[]{:S(2)}, u32[]{:S(2)}) collective-permute-start(bf16[96,1024]{1,0:T(8,128)(2,1)S(1)} %get-tuple-element.436), channel_id=1, source_target_pairs={{0,3},{1,0},{2,1},{3,2},{4,7},{5,4},{6,5},{7,6},{8,11},{9,8},{10,9... | collective-permute-start | bytes 589832 | tf_op jit(solution)/shard_map/ppermute | solution.py:122
  554.2 72.7 %all-to-all-start.8 = ((bf16[32,24,1024]{2,1,0:T(8,128)(2,1)}), bf16[32,24,1024]{2,1,0:T(8,128)(2,1)}, u32[]{:S(2)}, u32[]{:S(2)}) async-start(bf16[32,24,1024]{2,1,0:T(8,128)(2,1)} %bitcast.504), calls=%async_computation.10 | async-start | bytes 3145728 | tf_op jit(solution)/shard_map/all_to_all | solution.py:112
  563.1 31.5 %collective-permute-start.46 = (bf16[144,1024]{1,0:T(8,128)(2,1)}, bf16[144,1024]{1,0:T(8,128)(2,1)S(1)}, u32[]{:S(2)}, u32[]{:S(2)}) collective-permute-start(bf16[144,1024]{1,0:T(8,128)(2,1)} %get-tuple-element.433), channel_id=1, source_target_pairs={{0,3},{1,0},{2,1},{3,2},{4,7},{5,4},{6,5},{7,6},{8,11},{9,8},{10,9... | collective-permute-start | bytes 884744 | tf_op jit(solution)/shard_map/ppermute | solution.py:122
  566.7 58.0 %collective-permute-start.45 = (bf16[144,1024]{1,0:T(8,128)(2,1)}, bf16[144,1024]{1,0:T(8,128)(2,1)}, u32[]{:S(2)}, u32[]{:S(2)}) collective-permute-start(bf16[144,1024]{1,0:T(8,128)(2,1)} %get-tuple-element.435), channel_id=1, source_target_pairs={{0,2},{1,3},{2,0},{3,1},{4,6},{5,7},{6,4},{7,5},{8,10},{9,11},{10,... | collective-permute-start | bytes 884744 | tf_op jit(solution)/shard_map/ppermute | solution.py:122
  566.7 58.0 %collective-permute-start.44 = (bf16[144,1024]{1,0:T(8,128)(2,1)S(1)}, bf16[144,1024]{1,0:T(8,128)(2,1)}, u32[]{:S(2)}, u32[]{:S(2)}) collective-permute-start(bf16[144,1024]{1,0:T(8,128)(2,1)S(1)} %get-tuple-element.434), channel_id=1, source_target_pairs={{0,1},{1,2},{2,3},{3,0},{4,5},{5,6},{6,7},{7,4},{8,9},{9,10},{10,1... | collective-permute-start | bytes 884744 | tf_op jit(solution)/shard_map/ppermute | solution.py:122
  657.3 17.0 %all-to-all-start.3 = ((bf16[32,8,1024]{2,1,0:T(8,128)(2,1)}), bf16[32,8,1024]{2,1,0:T(8,128)(2,1)S(1)}, u32[]{:S(2)}, u32[]{:S(2)}) async-start(bf16[32,8,1024]{2,1,0:T(8,128)(2,1)} %fusion.235), calls=%async_computation.3 | async-start | bytes 1048576 | tf_op jit(solution)/shard_map/while/body/all_to_all | solution.py:112
  686.5 19.7 %collective-permute-start.48 = (bf16[2,128,1024]{2,1,0:T(8,128)(2,1)}, bf16[2,128,1024]{2,1,0:T(8,128)(2,1)}, u32[]{:S(2)}, u32[]{:S(2)}) collective-permute-start(bf16[2,128,1024]{2,1,0:T(8,128)(2,1)} %get-tuple-element.400), channel_id=1, source_target_pairs={{0,1},{1,0},{2,3},{3,2},{4,5},{5,4},{6,7},{7,6},{8,9},{9,8},{10,11... | collective-permute-start | bytes 1572872 | tf_op jit(solution)/shard_map/ppermute | solution.py:205
  705.8 23.1 %collective-permute-start.47 = (bf16[2,128,1024]{2,1,0:T(8,128)(2,1)S(1)}, bf16[2,128,1024]{2,1,0:T(8,128)(2,1)S(1)}, u32[]{:S(2)}, u32[]{:S(2)}) collective-permute-start(bf16[2,128,1024]{2,1,0:T(8,128)(2,1)S(1)} %copy-done.83), channel_id=1, source_target_pairs={{0,1},{1,0},{2,3},{3,2},{4,5},{5,4},{6,7},{7,6},{8,9},{9,8},{10,11... | collective-permute-start | bytes 1572872 | tf_op jit(solution)/shard_map/ppermute | solution.py:208
  707.4 25.9 %collective-permute-start.49 = (bf16[2,128,1024]{2,1,0:T(8,128)(2,1)S(1)}, bf16[2,128,1024]{2,1,0:T(8,128)(2,1)S(1)}, u32[]{:S(2)}, u32[]{:S(2)}) collective-permute-start(bf16[2,128,1024]{2,1,0:T(8,128)(2,1)S(1)} %fusion.87), channel_id=1, source_target_pairs={{0,2},{2,0},{1,3},{3,1},{4,6},{6,4},{5,7},{7,5},{8,10},{10,8},{9,1... | collective-permute-start | bytes 1572872 | tf_op jit(solution)/shard_map/ppermute | solution.py:207
  765.0 15.7 %collective-permute-start.60 = (bf16[128,1024]{1,0:T(8,128)(2,1)S(1)}, bf16[128,1024]{1,0:T(8,128)(2,1)S(1)}, u32[]{:S(2)}, u32[]{:S(2)}) collective-permute-start(bf16[128,1024]{1,0:T(8,128)(2,1)S(1)} %get-tuple-element.428), channel_id=1, source_target_pairs={{0,24},{8,0},{16,8},{24,16},{1,25},{9,1},{17,9},{25,17},{2,26},{10... | collective-permute-start | bytes 786440 | tf_op jit(solution)/shard_map/ppermute | solution.py:122
  767.4 18.7 %collective-permute-start.59 = (bf16[128,1024]{1,0:T(8,128)(2,1)S(1)}, bf16[128,1024]{1,0:T(8,128)(2,1)S(1)}, u32[]{:S(2)}, u32[]{:S(2)}) collective-permute-start(bf16[128,1024]{1,0:T(8,128)(2,1)S(1)} %get-tuple-element.429), channel_id=1, source_target_pairs={{0,16},{8,24},{16,0},{24,8},{1,17},{9,25},{17,1},{25,9},{2,18},{10... | collective-permute-start | bytes 786440 | tf_op jit(solution)/shard_map/ppermute | solution.py:122
  769.5 16.7 %collective-permute-start.58 = (bf16[128,1024]{1,0:T(8,128)(2,1)S(1)}, bf16[128,1024]{1,0:T(8,128)(2,1)S(1)}, u32[]{:S(2)}, u32[]{:S(2)}) collective-permute-start(bf16[128,1024]{1,0:T(8,128)(2,1)S(1)} %get-tuple-element.427), channel_id=1, source_target_pairs={{0,8},{8,16},{16,24},{24,0},{1,9},{9,17},{17,25},{25,1},{2,10},{10... | collective-permute-start | bytes 786440 | tf_op jit(solution)/shard_map/ppermute | solution.py:122
  776.3 27.3 %collective-permute-start.56 = (bf16[512,1024]{1,0:T(8,128)(2,1)}, bf16[512,1024]{1,0:T(8,128)(2,1)}, u32[]{:S(2)}, u32[]{:S(2)}) collective-permute-start(bf16[512,1024]{1,0:T(8,128)(2,1)} %pad_maximum_fusion.4), channel_id=1, source_target_pairs={{0,4},{4,0},{1,5},{5,1},{2,6},{6,2},{3,7},{7,3},{8,12},{12,8},{9,1... | collective-permute-start | bytes 3145736 | tf_op jit(solution)/shard_map/ppermute | solution.py:162
  792.7 44.7 %collective-permute-start.52 = (bf16[2,32,1024]{2,1,0:T(8,128)(2,1)}, bf16[2,32,1024]{2,1,0:T(8,128)(2,1)S(1)}, u32[]{:S(2)}, u32[]{:S(2)}) collective-permute-start(bf16[2,32,1024]{2,1,0:T(8,128)(2,1)} %get-tuple-element.454), channel_id=1, source_target_pairs={{0,3},{1,0},{2,1},{3,2},{4,7},{5,4},{6,5},{7,6},{8,11},{9,8},{10,9... | collective-permute-start | bytes 393224 | tf_op jit(solution)/shard_map/ppermute | solution.py:122
  795.6 41.8 %collective-permute-start.51 = (bf16[2,32,1024]{2,1,0:T(8,128)(2,1)}, bf16[2,32,1024]{2,1,0:T(8,128)(2,1)S(1)}, u32[]{:S(2)}, u32[]{:S(2)}) collective-permute-start(bf16[2,32,1024]{2,1,0:T(8,128)(2,1)} %get-tuple-element.455), channel_id=1, source_target_pairs={{0,2},{1,3},{2,0},{3,1},{4,6},{5,7},{6,4},{7,5},{8,10},{9,11},{10,... | collective-permute-start | bytes 393224 | tf_op jit(solution)/shard_map/ppermute | solution.py:122
  801.2 36.3 %collective-permute-start.50 = (bf16[2,32,1024]{2,1,0:T(8,128)(2,1)}, bf16[2,32,1024]{2,1,0:T(8,128)(2,1)}, u32[]{:S(2)}, u32[]{:S(2)}) collective-permute-start(bf16[2,32,1024]{2,1,0:T(8,128)(2,1)} %get-tuple-element.456), channel_id=1, source_target_pairs={{0,1},{1,2},{2,3},{3,0},{4,5},{5,6},{6,7},{7,4},{8,9},{9,10},{10,1... | collective-permute-start | bytes 393224 | tf_op jit(solution)/shard_map/ppermute | solution.py:122
  847.1 37.5 %collective-permute-start.75 = (bf16[144,1024]{1,0:T(8,128)(2,1)}, bf16[144,1024]{1,0:T(8,128)(2,1)S(1)}, u32[]{:S(2)}, u32[]{:S(2)}) collective-permute-start(bf16[144,1024]{1,0:T(8,128)(2,1)} %get-tuple-element.406), channel_id=1, source_target_pairs={{0,1},{1,2},{2,3},{3,0},{4,5},{5,6},{6,7},{7,4},{8,9},{9,10},{10,1... | collective-permute-start | bytes 884744 | tf_op jit(solution)/shard_map/ppermute | solution.py:122
  847.7 37.5 %collective-permute-start.74 = (bf16[144,1024]{1,0:T(8,128)(2,1)}, bf16[144,1024]{1,0:T(8,128)(2,1)}, u32[]{:S(2)}, u32[]{:S(2)}) collective-permute-start(bf16[144,1024]{1,0:T(8,128)(2,1)} %get-tuple-element.407), channel_id=1, source_target_pairs={{0,2},{1,3},{2,0},{3,1},{4,6},{5,7},{6,4},{7,5},{8,10},{9,11},{10,... | collective-permute-start | bytes 884744 | tf_op jit(solution)/shard_map/ppermute | solution.py:122
  851.2 34.0 %collective-permute-start.73 = (bf16[144,1024]{1,0:T(8,128)(2,1)S(1)}, bf16[144,1024]{1,0:T(8,128)(2,1)}, u32[]{:S(2)}, u32[]{:S(2)}) collective-permute-start(bf16[144,1024]{1,0:T(8,128)(2,1)S(1)} %get-tuple-element.408), channel_id=1, source_target_pairs={{0,3},{1,0},{2,1},{3,2},{4,7},{5,4},{6,5},{7,6},{8,11},{9,8},{10,9... | collective-permute-start | bytes 884744 | tf_op jit(solution)/shard_map/ppermute | solution.py:122
  858.1 31.7 %collective-permute-start.72 = (bf16[2,32,1024]{2,1,0:T(8,128)(2,1)S(1)}, bf16[2,32,1024]{2,1,0:T(8,128)(2,1)S(1)}, u32[]{:S(2)}, u32[]{:S(2)}) collective-permute-start(bf16[2,32,1024]{2,1,0:T(8,128)(2,1)S(1)} %get-tuple-element.462), channel_id=1, source_target_pairs={{0,3},{1,0},{2,1},{3,2},{4,7},{5,4},{6,5},{7,6},{8,11},{9,8},{10,9... | collective-permute-start | bytes 393224 | tf_op jit(solution)/shard_map/ppermute | solution.py:122
  861.5 28.3 %collective-permute-start.71 = (bf16[2,32,1024]{2,1,0:T(8,128)(2,1)S(1)}, bf16[2,32,1024]{2,1,0:T(8,128)(2,1)}, u32[]{:S(2)}, u32[]{:S(2)}) collective-permute-start(bf16[2,32,1024]{2,1,0:T(8,128)(2,1)S(1)} %get-tuple-element.463), channel_id=1, source_target_pairs={{0,2},{1,3},{2,0},{3,1},{4,6},{5,7},{6,4},{7,5},{8,10},{9,11},{10,... | collective-permute-start | bytes 393224 | tf_op jit(solution)/shard_map/ppermute | solution.py:122
  (231 other events, 3631.7 us)
Sparse Core Ops, SparseCore 0:
  11.6 142.7 all-gather.2
  156.8 47.7 all-gather.4
  463.2 63.6 reduce-scatter.2
  541.3 112.8 reduce-scatter.4
